TPU v7x, 32 devices: a whole 2x2x4 slice. The times are simulated.
32 devices in a mesh: grp: 2 (over core), blk: 16 (over z, y, x).
Axes of the slice: x: 2, y: 2, z: 4, core: 2. Of those that a mesh axis runs over, the one named last changes fastest.
Arguments:
- hidden_in: bfloat16 [4352, 1024], P(('grp', 'blk')), may hold values from -6 to 6
- segment_ids: int32 [4352], P(('grp', 'blk')), may hold values from 0 to 3, as said below
- order_ids: int32 [4352], P(('grp', 'blk')), may hold values from 0 to 127
- box_ids: int32 [2, 4352], P(None, ('grp', 'blk')), may hold values from 0 to 63
- qkv_weight: bfloat16 [3, 1024, 1024], P(None, ('grp', 'blk')), may hold values from -0.25 to 0.25
- qkv_bias: bfloat16 [2, 1024], P(None, ('grp', 'blk')), may hold values from -0.59765625 to 0.59765625
- rel_tables: bfloat16 [3, 128, 1024], P(None, None, ('grp', 'blk')), may hold values from -8 to 8
- out_weight: bfloat16 [1024, 1024], P(('grp', 'blk')), may hold values from -0.75 to 0.75
- branch_bias: bfloat16 [2, 1024], P(None, ('grp', 'blk')), may hold values from -1.796875 to 1.796875
- norm_gains: bfloat16 [2, 1024], P(None, ('grp', 'blk')), may hold values from 0.25 to 1.75
- norm_shifts: bfloat16 [2, 1024], P(None, ('grp', 'blk')), may hold values from -1.796875 to 1.796875
- ffn_in: bfloat16 [1024, 4096], P(('grp', 'blk')), may hold values from -0.1875 to 0.1875
- ffn_in_bias: bfloat16 [4096], P(('grp', 'blk')), may hold values from -1.796875 to 1.796875
- ffn_out: bfloat16 [4096, 1024], P(('grp', 'blk')), may hold values from -0.125 to 0.125
- out_grad: bfloat16 [4352, 1024], P(('grp', 'blk')), may hold values from -6 to 6
Outputs:
- hidden_out: bfloat16 [4352, 1024], P(('grp', 'blk'))
- hidden_grad: bfloat16 [4352, 1024], P(('grp', 'blk'))
- qkv_weight_grad: float32 [3, 1024, 1024], P(None, ('grp', 'blk'))
- qkv_bias_grad: float32 [2, 1024], P(None, ('grp', 'blk'))
- rel_tables_grad: float32 [3, 128, 1024], P(None, None, ('grp', 'blk'))
- out_weight_grad: float32 [1024, 1024], P(('grp', 'blk'))
- branch_bias_grad: float32 [2, 1024], P(None, ('grp', 'blk'))
- norm_gains_grad: float32 [2, 1024], P(None, ('grp', 'blk'))
- norm_shifts_grad: float32 [2, 1024], P(None, ('grp', 'blk'))
- ffn_in_grad: float32 [1024, 4096], P(('grp', 'blk'))
- ffn_in_bias_grad: float32 [4096], P(('grp', 'blk'))
- ffn_out_grad: float32 [4096, 1024], P(('grp', 'blk'))
Inputs may be any that keep to these rules, and one draw needn't show every extreme that they name: `segment_ids`: one label for each page of 544 consecutive tokens; pages of a batch group with equal labels form one document; in every batch group the first and the last page carry the same label, and some page carries another.
All inputs are finite; a program needn't handle non-finite values.
Results may differ from a plain program's by a relative error of at most 0.02.
Values may be sent and summed in bfloat16 or wider, within the bound.
A program may use at most 256 MiB of HBM per device.

v0:
```python
import math

import jax
import jax.numpy as jnp
from jax import lax
from jax.sharding import PartitionSpec as P

H = 16
HD = 64
NB = 128
ORDER_RANGE = 128
BOX_RANGE = 64


NEGATIVE = -1e30
EPSILON = 1e-05


def shifted(x, axis, by):
    devices = lax.axis_size(axis)
    return lax.ppermute(x, axis, [(i, (i + by) % devices) for i in range(devices)])


def block_size(row_count):
    chosen = 1
    for option in range(1, min(row_count, 544) + 1):
        if row_count % option == 0:
            chosen = option
    return chosen


def kind_ranges():
    return (ORDER_RANGE, BOX_RANGE, BOX_RANGE)


def query_maps(layout_ids):
    maps_out = []
    for column, extent in enumerate(kind_ranges()):
        offsets = layout_ids[:, column][:, None] - jnp.arange(extent, dtype=jnp.int32)[None, :]
        bucket = jnp.clip(offsets, -(NB // 2), NB // 2 - 1) + NB // 2
        maps_out.append(bucket[:, :, None] == jnp.arange(NB, dtype=jnp.int32)[None, None, :])
    return maps_out


def key_onehot(key_ids):
    pieces_out = []
    for column, extent in enumerate(kind_ranges()):
        pieces_out.append(
            key_ids[:, column + 1][:, None] == jnp.arange(extent, dtype=jnp.int32)[None, :]
        )
    return jnp.concatenate(pieces_out, axis=1).astype(jnp.bfloat16)


def norm_forward(values_in, norm_gain, norm_shift):
    center = values_in - jnp.mean(values_in, axis=-1, keepdims=True)
    inverse = lax.rsqrt(jnp.mean(center * center, axis=-1, keepdims=True) + EPSILON)
    normed = center * inverse
    return (normed * norm_gain + norm_shift, normed, inverse)


def norm_backward(upstream, normed, inverse, norm_gain):
    scaled = upstream * norm_gain
    inner_part = (
        scaled
        - jnp.mean(scaled, axis=-1, keepdims=True)
        - normed * jnp.mean(scaled * normed, axis=-1, keepdims=True)
    )
    return (inner_part * inverse, jnp.sum(upstream * normed, axis=0), jnp.sum(upstream, axis=0))


def block_logits(query_heads, selector, query_seg, key_part, meta_part, scaling):
    key_ids = meta_part.astype(jnp.int32)
    row_count = key_part.shape[0]
    key_heads = key_part.reshape(row_count, H, HD)
    content = jnp.einsum("thd,khd->htk", query_heads, key_heads, preferred_element_type=jnp.float32)
    onehot = key_onehot(key_ids)
    rel_bias = jnp.einsum("thv,kv->htk", selector, onehot, preferred_element_type=jnp.float32)
    allowed = query_seg[:, None] == key_ids[None, :, 0]
    logits = jnp.where(allowed[None], (content + rel_bias) * scaling, NEGATIVE)
    return (logits, allowed, onehot, key_heads)


def over_blocks(advance, carry, piece, start):
    row_count = piece[0].shape[0]
    stride = block_size(row_count)

    def one_step(block_index, running):
        portion = tuple(
            (lax.dynamic_slice_in_dim(member, block_index * stride, stride, 0) for member in piece)
        )
        return advance(running, portion, start + block_index * stride)

    return lax.fori_loop(0, row_count // stride, one_step, carry)


def shards(
    hidden_in,
    segment_ids,
    order_ids,
    box_ids,
    qkv_weight,
    qkv_bias,
    rel_tables,
    out_weight,
    branch_bias,
    norm_gains,
    norm_shifts,
    ffn_in,
    ffn_in_bias,
    ffn_out,
    out_grad,
):
    gathered = (
        lax.all_gather(qkv_weight, ("grp", "blk"), axis=1, tiled=True),
        lax.all_gather(qkv_bias, ("grp", "blk"), axis=1, tiled=True),
        lax.all_gather(rel_tables, ("grp", "blk"), axis=2, tiled=True),
        lax.all_gather(out_weight, ("grp", "blk"), axis=0, tiled=True),
        lax.all_gather(branch_bias, ("grp", "blk"), axis=1, tiled=True),
        lax.all_gather(norm_gains, ("grp", "blk"), axis=1, tiled=True),
        lax.all_gather(norm_shifts, ("grp", "blk"), axis=1, tiled=True),
        lax.all_gather(ffn_in, ("grp", "blk"), axis=0, tiled=True),
        lax.all_gather(ffn_in_bias, ("grp", "blk"), axis=0, tiled=True),
        lax.all_gather(ffn_out, ("grp", "blk"), axis=0, tiled=True),
    )
    w_qkv, b_qkv, w_rel, w_out, b_branch, gains, shifts, w_in, b_in, w_down = gathered
    row_count = hidden_in.shape[0]
    width = hidden_in.shape[1]
    scaling = 1.0 / math.sqrt(4.0 * HD)
    select_width = ORDER_RANGE + 2 * BOX_RANGE
    projected = jnp.einsum("td,cde->cte", hidden_in, w_qkv, preferred_element_type=jnp.float32)
    bias_qkv = b_qkv.astype(jnp.float32)
    query_rows = (projected[0] + bias_qkv[0]).astype(jnp.bfloat16)
    key_rows = projected[1].astype(jnp.bfloat16)
    value_rows = (projected[2] + bias_qkv[1]).astype(jnp.bfloat16)
    layout_ids = jnp.stack([order_ids, box_ids[0], box_ids[1]], axis=1)
    key_meta = jnp.stack([segment_ids, order_ids, box_ids[0], box_ids[1]], axis=1).astype(
        jnp.bfloat16
    )
    query_heads = query_rows.reshape(row_count, H, HD)
    rel_heads = w_rel.reshape(3, NB, H, HD)
    tables = jnp.einsum(
        "thd,nbhd->thnb", query_heads, rel_heads, preferred_element_type=jnp.float32
    ).astype(jnp.bfloat16)
    maps_list = query_maps(layout_ids)
    selector = jnp.concatenate(
        [
            jnp.einsum(
                "thb,tvb->thv",
                tables[:, :, column],
                maps_list[column].astype(jnp.bfloat16),
                preferred_element_type=jnp.float32,
            )
            for column in range(3)
        ],
        axis=2,
    ).astype(jnp.bfloat16)

    def forward_step(running, portion, offset):
        row_top, row_total, weighted = running
        key_part, value_part, meta_part = portion
        logits, allowed, onehot, key_heads = block_logits(
            query_heads, selector, segment_ids, key_part, meta_part, scaling
        )
        new_top = jnp.maximum(row_top, jnp.max(logits, axis=2))
        rescale = jnp.exp(row_top - new_top)
        weights = jnp.where(allowed[None], jnp.exp(logits - new_top[:, :, None]), 0.0)
        value_heads = value_part.reshape(value_part.shape[0], H, HD)
        weighted = weighted * rescale.T[:, :, None] + jnp.einsum(
            "htk,khd->thd",
            weights.astype(jnp.bfloat16),
            value_heads,
            preferred_element_type=jnp.float32,
        )
        return (new_top, row_total * rescale + jnp.sum(weights, axis=2), weighted)

    start_state = (
        jnp.full((H, row_count), NEGATIVE, jnp.float32),
        jnp.zeros((H, row_count), jnp.float32),
        jnp.zeros((row_count, H, HD), jnp.float32),
    )
    row_top, row_total, weighted = over_blocks(
        forward_step,
        start_state,
        (
            lax.all_gather(key_rows, "blk", axis=0, tiled=True),
            lax.all_gather(value_rows, "blk", axis=0, tiled=True),
            lax.all_gather(key_meta, "blk", axis=0, tiled=True),
        ),
        jnp.int32(0),
    )
    context_full = weighted / row_total.T[:, :, None]
    log_total = row_top + jnp.log(row_total)
    context = context_full.reshape(row_count, width).astype(jnp.bfloat16)
    branch = jnp.dot(context, w_out, preferred_element_type=jnp.float32) + b_branch[0].astype(
        jnp.float32
    )
    first, normed_one, inverse_one = norm_forward(
        hidden_in.astype(jnp.float32) + branch,
        gains[0].astype(jnp.float32),
        shifts[0].astype(jnp.float32),
    )
    first_low = first.astype(jnp.bfloat16)
    inner_pre = jnp.dot(first_low, w_in, preferred_element_type=jnp.float32) + b_in.astype(
        jnp.float32
    )
    activated, gelu_pull = jax.vjp(
        lambda pre_act: jax.nn.gelu(pre_act, approximate=False), inner_pre
    )
    activated_low = activated.astype(jnp.bfloat16)
    second = jnp.dot(activated_low, w_down, preferred_element_type=jnp.float32) + b_branch[
        1
    ].astype(jnp.float32)
    result, normed_two, inverse_two = norm_forward(
        first + second, gains[1].astype(jnp.float32), shifts[1].astype(jnp.float32)
    )
    hidden_out = result.astype(jnp.bfloat16)
    grad_sum2, gain_grad2, shift_grad2 = norm_backward(
        out_grad.astype(jnp.float32), normed_two, inverse_two, gains[1].astype(jnp.float32)
    )
    grad_second = grad_sum2.astype(jnp.bfloat16)
    grad_w_down = jnp.einsum(
        "tf,td->fd", activated_low, grad_second, preferred_element_type=jnp.float32
    )
    grad_bias_two = jnp.sum(grad_second.astype(jnp.float32), axis=0)
    grad_act = jnp.einsum("td,fd->tf", grad_second, w_down, preferred_element_type=jnp.float32)
    grad_inner = gelu_pull(grad_act)[0].astype(jnp.bfloat16)
    grad_b_in = jnp.sum(grad_inner.astype(jnp.float32), axis=0)
    grad_w_in = jnp.einsum("td,tf->df", first_low, grad_inner, preferred_element_type=jnp.float32)
    grad_first = grad_sum2 + jnp.einsum(
        "tf,df->td", grad_inner, w_in, preferred_element_type=jnp.float32
    )
    grad_sum1, gain_grad1, shift_grad1 = norm_backward(
        grad_first, normed_one, inverse_one, gains[0].astype(jnp.float32)
    )
    grad_branch = grad_sum1.astype(jnp.bfloat16)
    grad_w_out = jnp.einsum("td,te->de", context, grad_branch, preferred_element_type=jnp.float32)
    grad_bias_one = jnp.sum(grad_branch.astype(jnp.float32), axis=0)
    grad_context = jnp.einsum(
        "te,de->td", grad_branch, w_out, preferred_element_type=jnp.float32
    ).astype(jnp.bfloat16)
    grad_heads = grad_context.reshape(row_count, H, HD)
    delta = jnp.einsum("thd,thd->ht", grad_heads.astype(jnp.float32), context_full)

    def backward_core(grad_query, grad_select, portion):
        key_part, value_part, meta_part = portion
        logits, allowed, onehot, key_heads = block_logits(
            query_heads, selector, segment_ids, key_part, meta_part, scaling
        )
        probs = jnp.where(allowed[None], jnp.exp(logits - log_total[:, :, None]), 0.0)
        part_rows = key_part.shape[0]
        value_heads = value_part.reshape(part_rows, H, HD)
        grad_probs = jnp.einsum(
            "thd,khd->htk", grad_heads, value_heads, preferred_element_type=jnp.float32
        )
        grad_logits = (probs * (grad_probs - delta[:, :, None])).astype(jnp.bfloat16)
        grad_query = grad_query + scaling * jnp.einsum(
            "htk,khd->thd", grad_logits, key_heads, preferred_element_type=jnp.float32
        )
        grad_select = grad_select + scaling * jnp.einsum(
            "htk,kv->thv", grad_logits, onehot, preferred_element_type=jnp.float32
        )
        grad_key = scaling * jnp.einsum(
            "htk,thd->khd", grad_logits, query_heads, preferred_element_type=jnp.float32
        )
        grad_value = jnp.einsum(
            "htk,thd->khd",
            probs.astype(jnp.bfloat16),
            grad_heads,
            preferred_element_type=jnp.float32,
        )
        update = jnp.concatenate(
            [grad_key.reshape(part_rows, width), grad_value.reshape(part_rows, width)], axis=1
        )
        return (grad_query, grad_select, update)

    query_zero = jnp.zeros((row_count, H, HD), jnp.float32)
    select_zero = jnp.zeros((row_count, H, select_width), jnp.float32)

    def cycle_turn(turn, carry):
        grad_query, grad_select, key_part, value_part, meta_part, carried = carry
        portion = (key_part, value_part, meta_part)
        grad_query, grad_select, update = backward_core(grad_query, grad_select, portion)
        carried = carried + update
        key_part, value_part, meta_part = shifted((key_part, value_part, meta_part), "blk", 1)
        carried = shifted(carried.astype(jnp.bfloat16), "blk", 1).astype(carried.dtype)
        return (grad_query, grad_select, key_part, value_part, meta_part, carried)

    cycle_start = (
        query_zero,
        select_zero,
        key_rows,
        value_rows,
        key_meta,
        jnp.zeros((row_count, 2 * width), jnp.float32),
    )
    cycle_end = lax.fori_loop(0, lax.axis_size("blk"), cycle_turn, cycle_start)
    grad_query, grad_select, own_pairs = (cycle_end[0], cycle_end[1], cycle_end[5])
    grad_key_rows = own_pairs[:, :width].astype(jnp.bfloat16)
    grad_value_rows = own_pairs[:, width:].astype(jnp.bfloat16)
    cursor = 0
    table_parts = []
    for column, extent in enumerate(kind_ranges()):
        table_parts.append(
            jnp.einsum(
                "thv,tvb->thb",
                grad_select[:, :, cursor : cursor + extent],
                maps_list[column].astype(jnp.float32),
                precision=lax.Precision.HIGHEST,
            )
        )
        cursor = cursor + extent
    grad_tables = jnp.stack(table_parts, axis=2).astype(jnp.bfloat16)
    grad_query_total = grad_query + jnp.einsum(
        "thnb,nbhd->thd", grad_tables, rel_heads, preferred_element_type=jnp.float32
    )
    grad_query_rows = grad_query_total.reshape(row_count, width).astype(jnp.bfloat16)
    grad_rel = jnp.einsum(
        "thnb,thd->nbhd", grad_tables, query_heads, preferred_element_type=jnp.float32
    ).reshape(3, NB, width)
    grad_stack = jnp.stack([grad_query_rows, grad_key_rows, grad_value_rows])
    grad_w_qkv = jnp.einsum(
        "td,cte->cde", hidden_in, grad_stack, preferred_element_type=jnp.float32
    )
    grad_b_qkv = jnp.stack(
        [
            jnp.sum(grad_query_rows.astype(jnp.float32), axis=0),
            jnp.sum(grad_value_rows.astype(jnp.float32), axis=0),
        ]
    )
    grad_input = grad_sum1 + jnp.einsum(
        "cte,cde->td", grad_stack, w_qkv, preferred_element_type=jnp.float32
    )
    summed = (
        lax.psum_scatter(grad_w_qkv, ("grp", "blk"), scatter_dimension=1, tiled=True),
        lax.psum_scatter(grad_b_qkv, ("grp", "blk"), scatter_dimension=1, tiled=True),
        lax.psum_scatter(grad_rel, ("grp", "blk"), scatter_dimension=2, tiled=True),
        lax.psum_scatter(grad_w_out, ("grp", "blk"), scatter_dimension=0, tiled=True),
        lax.psum_scatter(
            jnp.stack([grad_bias_one, grad_bias_two]),
            ("grp", "blk"),
            scatter_dimension=1,
            tiled=True,
        ),
        lax.psum_scatter(
            jnp.stack([gain_grad1, gain_grad2]), ("grp", "blk"), scatter_dimension=1, tiled=True
        ),
        lax.psum_scatter(
            jnp.stack([shift_grad1, shift_grad2]), ("grp", "blk"), scatter_dimension=1, tiled=True
        ),
        lax.psum_scatter(grad_w_in, ("grp", "blk"), scatter_dimension=0, tiled=True),
        lax.psum_scatter(grad_b_in, ("grp", "blk"), scatter_dimension=0, tiled=True),
        lax.psum_scatter(grad_w_down, ("grp", "blk"), scatter_dimension=0, tiled=True),
    )
    return (
        hidden_out,
        grad_input.astype(jnp.bfloat16),
        summed[0],
        summed[1],
        summed[2],
        summed[3],
        summed[4],
        summed[5],
        summed[6],
        summed[7],
        summed[8],
        summed[9],
    )


def solution(mesh):
    return jax.shard_map(
        shards,
        mesh=mesh,
        in_specs=(
            P(("grp", "blk"), None),
            P(("grp", "blk")),
            P(("grp", "blk")),
            P(None, ("grp", "blk")),
            P(None, ("grp", "blk"), None),
            P(None, ("grp", "blk")),
            P(None, None, ("grp", "blk")),
            P(("grp", "blk"), None),
            P(None, ("grp", "blk")),
            P(None, ("grp", "blk")),
            P(None, ("grp", "blk")),
            P(("grp", "blk"), None),
            P(("grp", "blk")),
            P(("grp", "blk"), None),
            P(("grp", "blk"), None),
        ),
        out_specs=(
            P(("grp", "blk"), None),
            P(("grp", "blk"), None),
            P(None, ("grp", "blk"), None),
            P(None, ("grp", "blk")),
            P(None, None, ("grp", "blk")),
            P(("grp", "blk"), None),
            P(None, ("grp", "blk")),
            P(None, ("grp", "blk")),
            P(None, ("grp", "blk")),
            P(("grp", "blk"), None),
            P(("grp", "blk")),
            P(("grp", "blk"), None),
        ),
        check_vma=False,
    )
```

profile of v0, /device:TPU:1, one launch (start us, length us, event | category | flops | bytes accessed | tf_op | source)
XLA Modules:
  0.0 3210.1 jit_solution(13710692740422065837)
XLA Ops:
  8.0 74.7 %all-gather.14.cloned.1.call-done = bf16[3,1024,1024]{2,1,0:T(8,128)(2,1)} async-done(((bf16[3,32,1024]{2,1,0:T(8,128)(2,1)}), bf16[3,1024,1024]{2,1,0:T(8,128)(2,1)}) %all-gather.14.cloned.1.call-update) | async-done | bytes 6291472 | tf_op jit(solution)/shard_map/all_gather | solution.py:114
  87.5 66.3 %all-gather.2 = bf16[32,32,2]{1,2,0:T(2,128)(2,1)S(1)} all-gather(bf16[1,32,2]{1,2,0:T(2,128)(2,1)S(1)} %bitcast.326), channel_id=1, replica_groups=mesh['grp'=2,'blk'=16] {'grp','blk'}, dimensions={0}, use_global_device_ids=true | all-gather | bytes 4224 | tf_op jit(solution)/shard_map/all_gather | solution.py:115
  158.0 63.0 %all-gather.3 = bf16[32,32,2]{1,2,0:T(2,128)(2,1)S(1)} all-gather(bf16[1,32,2]{1,2,0:T(2,128)(2,1)S(1)} %bitcast.327), channel_id=1, replica_groups=mesh['grp'=2,'blk'=16] {'grp','blk'}, dimensions={0}, use_global_device_ids=true | all-gather | bytes 4224 | tf_op jit(solution)/shard_map/all_gather | solution.py:118
  221.8 65.7 %all-gather.6 = bf16[32,1,128]{2,1,0:T(2,128)(2,1)S(1)} all-gather(bf16[1,1,128]{2,1,0:T(2,128)(2,1)S(1)} %bitcast.328), channel_id=1, replica_groups=mesh['grp'=2,'blk'=16] {'grp','blk'}, dimensions={0}, use_global_device_ids=true | all-gather | bytes 8448 | tf_op jit(solution)/shard_map/all_gather | solution.py:122
  288.1 29.2 all-gather.1
  317.6 79.8 %all_gather.43 = bf16[3,128,1024]{1,2,0:T(8,128)(2,1)S(1)} all-gather(bf16[3,128,32]{1,2,0:T(8,128)(2,1)S(1)} %copy-done.53), channel_id=1, replica_groups=mesh['grp'=2,'blk'=16] {'grp','blk'}, dimensions={2}, use_global_device_ids=true | all-gather | bytes 811008 | tf_op jit(solution)/shard_map/all_gather | solution.py:116
  397.6 63.2 %all-gather.5 = bf16[32,32,2]{1,2,0:T(2,128)(2,1)S(1)} all-gather(bf16[1,32,2]{1,2,0:T(2,128)(2,1)S(1)} %bitcast.329), channel_id=1, replica_groups=mesh['grp'=2,'blk'=16] {'grp','blk'}, dimensions={0}, use_global_device_ids=true | all-gather | bytes 4224 | tf_op jit(solution)/shard_map/all_gather | solution.py:120
  461.5 65.5 %all-gather.4 = bf16[32,32,2]{1,2,0:T(2,128)(2,1)S(1)} all-gather(bf16[1,32,2]{1,2,0:T(2,128)(2,1)S(1)} %bitcast.330), channel_id=1, replica_groups=mesh['grp'=2,'blk'=16] {'grp','blk'}, dimensions={0}, use_global_device_ids=true | all-gather | bytes 4224 | tf_op jit(solution)/shard_map/all_gather | solution.py:119
  543.4 114.7 %while.39 = (s32[]{:T(128)}, f32[16,136]{1,0:T(8,128)}, f32[16,136]{1,0:T(8,128)}, f32[136,16,64]{0,2,1:T(8,128)}, s32[136]{0:T(256)}, /*index=5*/bf16[2176,4]{0...) while((s32[]{:T(128)}, f32[16,136]{1,0:T(8,128)}, ...), condition=%wide.region_3.4_spmd.clone, body=%wide.region_0.3_spmd.clone.sunk | while | flops 921877632 | bytes 38616212 | solution.py:93
  552.7 7.2 fusion.187
  581.1 7.2 fusion.187
  609.8 7.2 fusion.187
  638.6 7.2 fusion.187
  662.1 6.2 convolution_add_fusion
  668.3 10.0 fusion.119
  680.0 8.4 convert_reduce_fusion
  697.5 643.3 %while.40 = (s32[]{:T(128)}, f32[136,16,64]{0,2,1:T(8,128)}, f32[136,16,256]{2,0,1:T(8,128)}, bf16[136,1024]{0,1:T(8,128)(2,1)}, bf16[136,1024]{0,1:T(8,128)(2,1...) while((s32[]{:T(128)}, f32[136,16,64]{0,2,1:T(8,128)}, ...), condition=%wide.region_13.14_spmd.clone, body=%wide.region_12.13_spmd.clone.sunk | while | flops 498914912 | bytes 58318884 | solution.py:296
  720.0 20.8 collective-permute-done.3
  765.9 19.2 collective-permute-done.3
  810.2 18.2 collective-permute-done.3
  853.6 17.3 collective-permute-done.3
  896.0 16.4 collective-permute-done.3
  937.6 15.5 collective-permute-done.3
  978.2 14.6 collective-permute-done.3
  1017.9 13.7 collective-permute-done.3
  1056.7 13.3 collective-permute-done.3
  1095.0 13.3 collective-permute-done.3
  1133.4 13.3 collective-permute-done.3
  1171.8 13.3 collective-permute-done.3
  1210.2 13.3 collective-permute-done.3
  1248.6 13.2 collective-permute-done.3
  1287.0 13.3 collective-permute-done.3
  1325.4 13.3 collective-permute-done.3
  1349.8 6.1 fusion.71
  1364.4 6.4 convolution_bitcast_fusion
  1370.8 18.4 copy.139
  1396.8 8.3 fusion.110
  1406.8 10.1 fusion.104
  1417.7 43.4 %all-reduce.1 = f32[4096]{0:T(1024)S(1)} all-reduce(f32[4096]{0:T(1024)S(1)} %copy-done.55), channel_id=11, replica_groups=mesh['grp'=2,'blk'=16] {'grp','blk'}, use_global_device_ids=true, to_apply=%region_31.32.clone | all-reduce | flops 4096 | bytes 32768
  1467.4 34.0 %reduce-scatter.25.cloned.1.call-done = f32[32,2]{1,0:T(8,128)} async-done(((f32[1024,2]{1,0:T(8,128)}), f32[32,2]{1,0:T(8,128)}) %reduce-scatter.25.cloned.1.call-update) | async-done | bytes 272
  1502.8 135.0 %reduce-scatter.27.cloned.1.call-done = f32[32,2]{1,0:T(8,128)} async-done(((f32[1024,2]{1,0:T(8,128)}), f32[32,2]{1,0:T(8,128)}) %reduce-scatter.27.cloned.1.call-update) | async-done | bytes 272
  1639.2 135.0 %reduce-scatter.29.cloned.1.call-done = f32[32,2]{1,0:T(8,128)} async-done(((f32[1024,2]{1,0:T(8,128)}), f32[32,2]{1,0:T(8,128)}) %reduce-scatter.29.cloned.1.call-update) | async-done | bytes 272
  1775.6 134.9 %reduce-scatter.31.cloned.1.call-done = f32[32,2]{1,0:T(8,128)} async-done(((f32[1024,2]{1,0:T(8,128)}), f32[32,2]{1,0:T(8,128)}) %reduce-scatter.31.cloned.1.call-update) | async-done | bytes 272
  1911.8 278.9 %all-reduce.4.cloned.1.call-done = f32[3,1024,1024]{2,0,1:T(4,128)} async-done(((f32[3,1024,1024]{2,0,1:T(4,128)}), f32[3,1024,1024]{2,0,1:T(4,128)}) %all-reduce.4.cloned.1.call-update) | async-done | bytes 12582928
  2192.8 142.2 %reduce-scatter.17.cloned.1.call-done = f32[3,128,32]{1,2,0:T(8,128)} async-done(((f32[3,128,1024]{1,2,0:T(8,128)}), f32[3,128,32]{1,2,0:T(8,128)}) %reduce-scatter.17.cloned.1.call-update) | async-done | bytes 49168 | tf_op jit(solution)/shard_map/reduce_scatter | solution.py:336
  2335.0 146.4 %reduce-scatter.19.cloned.1.call-done = f32[32,1024]{1,0:T(8,128)} async-done(((f32[1024,1024]{1,0:T(8,128)}), f32[32,1024]{1,0:T(8,128)}) %reduce-scatter.19.cloned.1.call-update) | async-done | bytes 131088 | tf_op jit(solution)/shard_map/reduce_scatter | solution.py:337
  2481.4 358.9 %reduce-scatter.21.cloned.1.call-done = f32[32,4096]{1,0:T(8,128)} async-done(((f32[1024,4096]{1,0:T(8,128)}), f32[32,4096]{1,0:T(8,128)}) %reduce-scatter.21.cloned.1.call-update) | async-done | bytes 524304 | tf_op jit(solution)/shard_map/reduce_scatter | solution.py:350
  2840.3 362.9 %reduce-scatter.23.cloned.1.call-done = f32[128,1024]{1,0:T(8,128)} async-done(((f32[4096,1024]{1,0:T(8,128)}), f32[128,1024]{1,0:T(8,128)}) %reduce-scatter.23.cloned.1.call-update) | async-done | bytes 524304 | tf_op jit(solution)/shard_map/reduce_scatter | solution.py:352
  (933 shorter events, 568.0 us)
Async XLA Ops:
  7.2 75.4 %all-gather.14.cloned.1.call-start = ((), (), s32[]{:S(2)}) async-start(), calls=%async_computation.8 | async-start | bytes 6488064 | tf_op jit(solution)/shard_map/all_gather | solution.py:114
  7.9 535.4 %all-gather.24.cloned.1.call-start = ((), (), s32[]{:S(2)}) async-start(), calls=%async_computation.17 | async-start | bytes 4734976 | tf_op jit(solution)/shard_map/all_gather | solution.py:185
  87.4 456.0 %all-gather.16.cloned.1.call-start = ((), (), s32[]{:S(2)}) async-start(), calls=%async_computation.9 | async-start | bytes 4734976 | tf_op jit(solution)/shard_map/all_gather | solution.py:186
  154.7 504.7 %all-gather.18.cloned.1.call-start = ((), (), s32[]{:S(2)}) async-start(), calls=%async_computation.10 | async-start | bytes 2162688 | tf_op jit(solution)/shard_map/all_gather | solution.py:117
  155.3 506.8 %all-gather.20.cloned.1.call-start = ((), (), s32[]{:S(2)}) async-start(), calls=%async_computation.11 | async-start | bytes 8650752 | tf_op jit(solution)/shard_map/all_gather | solution.py:121
  155.9 512.4 %all-gather.22.cloned.1.call-start = ((), (), s32[]{:S(2)}) async-start(), calls=%async_computation.12 | async-start | bytes 8650752 | tf_op jit(solution)/shard_map/all_gather | solution.py:123
  156.4 1345.0 %reduce-scatter.25.cloned.1.call-start = ((), (), s32[]{:S(2)}) async-start(), calls=%async_computation.18 | async-start | bytes 540672
  700.0 42.9 %collective-permute-start = (bf16[136,1024]{0,1:T(8,128)(2,1)}, bf16[136,1024]{0,1:T(8,128)(2,1)}, u32[]{:S(2)}, u32[]{:S(2)}) collective-permute-start(bf16[136,1024]{0,1:T(8,128)(2,1)} %copy.223), channel_id=1, source_target_pairs={{0,1},{1,2},{2,3},{3,4},{4,5},{5,6},{6,7},{7,8},{8,9},{9,10},{10,1... | collective-permute-start | bytes 835592 | tf_op jit(solution)/shard_map/while/body/eval_jaxpr/ppermute | solution.py:21
  701.9 41.1 %collective-permute-start.1 = (bf16[136,1024]{0,1:T(8,128)(2,1)}, bf16[136,1024]{0,1:T(8,128)(2,1)}, u32[]{:S(2)}, u32[]{:S(2)}) collective-permute-start(bf16[136,1024]{0,1:T(8,128)(2,1)} %copy.224), channel_id=1, source_target_pairs={{0,1},{1,2},{2,3},{3,4},{4,5},{5,6},{6,7},{7,8},{8,9},{9,10},{10,1... | collective-permute-start | bytes 835592 | tf_op jit(solution)/shard_map/while/body/eval_jaxpr/ppermute | solution.py:21
  701.9 41.0 %collective-permute-start.2 = (bf16[136,4]{0,1:T(4,128)(2,1)S(1)}, bf16[136,4]{0,1:T(4,128)(2,1)S(1)}, u32[]{:S(2)}, u32[]{:S(2)}) collective-permute-start(bf16[136,4]{0,1:T(4,128)(2,1)S(1)} %copy.225), channel_id=1, source_target_pairs={{0,1},{1,2},{2,3},{3,4},{4,5},{5,6},{6,7},{7,8},{8,9},{9,10},{10,1... | collective-permute-start | bytes 3272 | tf_op jit(solution)/shard_map/while/body/eval_jaxpr/ppermute | solution.py:21
  745.2 42.0 %collective-permute-start = (bf16[136,1024]{0,1:T(8,128)(2,1)}, bf16[136,1024]{0,1:T(8,128)(2,1)}, u32[]{:S(2)}, u32[]{:S(2)}) collective-permute-start(bf16[136,1024]{0,1:T(8,128)(2,1)} %copy.223), channel_id=1, source_target_pairs={{0,1},{1,2},{2,3},{3,4},{4,5},{5,6},{6,7},{7,8},{8,9},{9,10},{10,1... | collective-permute-start | bytes 835592 | tf_op jit(solution)/shard_map/while/body/eval_jaxpr/ppermute | solution.py:21
  747.1 40.2 %collective-permute-start.1 = (bf16[136,1024]{0,1:T(8,128)(2,1)}, bf16[136,1024]{0,1:T(8,128)(2,1)}, u32[]{:S(2)}, u32[]{:S(2)}) collective-permute-start(bf16[136,1024]{0,1:T(8,128)(2,1)} %copy.224), channel_id=1, source_target_pairs={{0,1},{1,2},{2,3},{3,4},{4,5},{5,6},{6,7},{7,8},{8,9},{9,10},{10,1... | collective-permute-start | bytes 835592 | tf_op jit(solution)/shard_map/while/body/eval_jaxpr/ppermute | solution.py:21
  747.1 40.2 %collective-permute-start.2 = (bf16[136,4]{0,1:T(4,128)(2,1)S(1)}, bf16[136,4]{0,1:T(4,128)(2,1)S(1)}, u32[]{:S(2)}, u32[]{:S(2)}) collective-permute-start(bf16[136,4]{0,1:T(4,128)(2,1)S(1)} %copy.225), channel_id=1, source_target_pairs={{0,1},{1,2},{2,3},{3,4},{4,5},{5,6},{6,7},{7,8},{8,9},{9,10},{10,1... | collective-permute-start | bytes 3272 | tf_op jit(solution)/shard_map/while/body/eval_jaxpr/ppermute | solution.py:21
  789.5 41.1 %collective-permute-start = (bf16[136,1024]{0,1:T(8,128)(2,1)}, bf16[136,1024]{0,1:T(8,128)(2,1)}, u32[]{:S(2)}, u32[]{:S(2)}) collective-permute-start(bf16[136,1024]{0,1:T(8,128)(2,1)} %copy.223), channel_id=1, source_target_pairs={{0,1},{1,2},{2,3},{3,4},{4,5},{5,6},{6,7},{7,8},{8,9},{9,10},{10,1... | collective-permute-start | bytes 835592 | tf_op jit(solution)/shard_map/while/body/eval_jaxpr/ppermute | solution.py:21
  791.4 39.2 %collective-permute-start.1 = (bf16[136,1024]{0,1:T(8,128)(2,1)}, bf16[136,1024]{0,1:T(8,128)(2,1)}, u32[]{:S(2)}, u32[]{:S(2)}) collective-permute-start(bf16[136,1024]{0,1:T(8,128)(2,1)} %copy.224), channel_id=1, source_target_pairs={{0,1},{1,2},{2,3},{3,4},{4,5},{5,6},{6,7},{7,8},{8,9},{9,10},{10,1... | collective-permute-start | bytes 835592 | tf_op jit(solution)/shard_map/while/body/eval_jaxpr/ppermute | solution.py:21
  791.4 39.2 %collective-permute-start.2 = (bf16[136,4]{0,1:T(4,128)(2,1)S(1)}, bf16[136,4]{0,1:T(4,128)(2,1)S(1)}, u32[]{:S(2)}, u32[]{:S(2)}) collective-permute-start(bf16[136,4]{0,1:T(4,128)(2,1)S(1)} %copy.225), channel_id=1, source_target_pairs={{0,1},{1,2},{2,3},{3,4},{4,5},{5,6},{6,7},{7,8},{8,9},{9,10},{10,1... | collective-permute-start | bytes 3272 | tf_op jit(solution)/shard_map/while/body/eval_jaxpr/ppermute | solution.py:21
  832.9 40.2 %collective-permute-start = (bf16[136,1024]{0,1:T(8,128)(2,1)}, bf16[136,1024]{0,1:T(8,128)(2,1)}, u32[]{:S(2)}, u32[]{:S(2)}) collective-permute-start(bf16[136,1024]{0,1:T(8,128)(2,1)} %copy.223), channel_id=1, source_target_pairs={{0,1},{1,2},{2,3},{3,4},{4,5},{5,6},{6,7},{7,8},{8,9},{9,10},{10,1... | collective-permute-start | bytes 835592 | tf_op jit(solution)/shard_map/while/body/eval_jaxpr/ppermute | solution.py:21
  834.8 38.3 %collective-permute-start.1 = (bf16[136,1024]{0,1:T(8,128)(2,1)}, bf16[136,1024]{0,1:T(8,128)(2,1)}, u32[]{:S(2)}, u32[]{:S(2)}) collective-permute-start(bf16[136,1024]{0,1:T(8,128)(2,1)} %copy.224), channel_id=1, source_target_pairs={{0,1},{1,2},{2,3},{3,4},{4,5},{5,6},{6,7},{7,8},{8,9},{9,10},{10,1... | collective-permute-start | bytes 835592 | tf_op jit(solution)/shard_map/while/body/eval_jaxpr/ppermute | solution.py:21
  834.8 38.3 %collective-permute-start.2 = (bf16[136,4]{0,1:T(4,128)(2,1)S(1)}, bf16[136,4]{0,1:T(4,128)(2,1)S(1)}, u32[]{:S(2)}, u32[]{:S(2)}) collective-permute-start(bf16[136,4]{0,1:T(4,128)(2,1)S(1)} %copy.225), channel_id=1, source_target_pairs={{0,1},{1,2},{2,3},{3,4},{4,5},{5,6},{6,7},{7,8},{8,9},{9,10},{10,1... | collective-permute-start | bytes 3272 | tf_op jit(solution)/shard_map/while/body/eval_jaxpr/ppermute | solution.py:21
  875.4 39.3 %collective-permute-start = (bf16[136,1024]{0,1:T(8,128)(2,1)}, bf16[136,1024]{0,1:T(8,128)(2,1)}, u32[]{:S(2)}, u32[]{:S(2)}) collective-permute-start(bf16[136,1024]{0,1:T(8,128)(2,1)} %copy.223), channel_id=1, source_target_pairs={{0,1},{1,2},{2,3},{3,4},{4,5},{5,6},{6,7},{7,8},{8,9},{9,10},{10,1... | collective-permute-start | bytes 835592 | tf_op jit(solution)/shard_map/while/body/eval_jaxpr/ppermute | solution.py:21
  877.2 37.4 %collective-permute-start.1 = (bf16[136,1024]{0,1:T(8,128)(2,1)}, bf16[136,1024]{0,1:T(8,128)(2,1)}, u32[]{:S(2)}, u32[]{:S(2)}) collective-permute-start(bf16[136,1024]{0,1:T(8,128)(2,1)} %copy.224), channel_id=1, source_target_pairs={{0,1},{1,2},{2,3},{3,4},{4,5},{5,6},{6,7},{7,8},{8,9},{9,10},{10,1... | collective-permute-start | bytes 835592 | tf_op jit(solution)/shard_map/while/body/eval_jaxpr/ppermute | solution.py:21
  877.2 37.4 %collective-permute-start.2 = (bf16[136,4]{0,1:T(4,128)(2,1)S(1)}, bf16[136,4]{0,1:T(4,128)(2,1)S(1)}, u32[]{:S(2)}, u32[]{:S(2)}) collective-permute-start(bf16[136,4]{0,1:T(4,128)(2,1)S(1)} %copy.225), channel_id=1, source_target_pairs={{0,1},{1,2},{2,3},{3,4},{4,5},{5,6},{6,7},{7,8},{8,9},{9,10},{10,1... | collective-permute-start | bytes 3272 | tf_op jit(solution)/shard_map/while/body/eval_jaxpr/ppermute | solution.py:21
  916.9 38.3 %collective-permute-start = (bf16[136,1024]{0,1:T(8,128)(2,1)}, bf16[136,1024]{0,1:T(8,128)(2,1)}, u32[]{:S(2)}, u32[]{:S(2)}) collective-permute-start(bf16[136,1024]{0,1:T(8,128)(2,1)} %copy.223), channel_id=1, source_target_pairs={{0,1},{1,2},{2,3},{3,4},{4,5},{5,6},{6,7},{7,8},{8,9},{9,10},{10,1... | collective-permute-start | bytes 835592 | tf_op jit(solution)/shard_map/while/body/eval_jaxpr/ppermute | solution.py:21
  918.8 36.5 %collective-permute-start.1 = (bf16[136,1024]{0,1:T(8,128)(2,1)}, bf16[136,1024]{0,1:T(8,128)(2,1)}, u32[]{:S(2)}, u32[]{:S(2)}) collective-permute-start(bf16[136,1024]{0,1:T(8,128)(2,1)} %copy.224), channel_id=1, source_target_pairs={{0,1},{1,2},{2,3},{3,4},{4,5},{5,6},{6,7},{7,8},{8,9},{9,10},{10,1... | collective-permute-start | bytes 835592 | tf_op jit(solution)/shard_map/while/body/eval_jaxpr/ppermute | solution.py:21
  918.8 36.5 %collective-permute-start.2 = (bf16[136,4]{0,1:T(4,128)(2,1)S(1)}, bf16[136,4]{0,1:T(4,128)(2,1)S(1)}, u32[]{:S(2)}, u32[]{:S(2)}) collective-permute-start(bf16[136,4]{0,1:T(4,128)(2,1)S(1)} %copy.225), channel_id=1, source_target_pairs={{0,1},{1,2},{2,3},{3,4},{4,5},{5,6},{6,7},{7,8},{8,9},{9,10},{10,1... | collective-permute-start | bytes 3272 | tf_op jit(solution)/shard_map/while/body/eval_jaxpr/ppermute | solution.py:21
  957.5 37.4 %collective-permute-start = (bf16[136,1024]{0,1:T(8,128)(2,1)}, bf16[136,1024]{0,1:T(8,128)(2,1)}, u32[]{:S(2)}, u32[]{:S(2)}) collective-permute-start(bf16[136,1024]{0,1:T(8,128)(2,1)} %copy.223), channel_id=1, source_target_pairs={{0,1},{1,2},{2,3},{3,4},{4,5},{5,6},{6,7},{7,8},{8,9},{9,10},{10,1... | collective-permute-start | bytes 835592 | tf_op jit(solution)/shard_map/while/body/eval_jaxpr/ppermute | solution.py:21
  959.4 35.6 %collective-permute-start.1 = (bf16[136,1024]{0,1:T(8,128)(2,1)}, bf16[136,1024]{0,1:T(8,128)(2,1)}, u32[]{:S(2)}, u32[]{:S(2)}) collective-permute-start(bf16[136,1024]{0,1:T(8,128)(2,1)} %copy.224), channel_id=1, source_target_pairs={{0,1},{1,2},{2,3},{3,4},{4,5},{5,6},{6,7},{7,8},{8,9},{9,10},{10,1... | collective-permute-start | bytes 835592 | tf_op jit(solution)/shard_map/while/body/eval_jaxpr/ppermute | solution.py:21
  959.4 35.5 %collective-permute-start.2 = (bf16[136,4]{0,1:T(4,128)(2,1)S(1)}, bf16[136,4]{0,1:T(4,128)(2,1)S(1)}, u32[]{:S(2)}, u32[]{:S(2)}) collective-permute-start(bf16[136,4]{0,1:T(4,128)(2,1)S(1)} %copy.225), channel_id=1, source_target_pairs={{0,1},{1,2},{2,3},{3,4},{4,5},{5,6},{6,7},{7,8},{8,9},{9,10},{10,1... | collective-permute-start | bytes 3272 | tf_op jit(solution)/shard_map/while/body/eval_jaxpr/ppermute | solution.py:21
  997.2 36.5 %collective-permute-start = (bf16[136,1024]{0,1:T(8,128)(2,1)}, bf16[136,1024]{0,1:T(8,128)(2,1)}, u32[]{:S(2)}, u32[]{:S(2)}) collective-permute-start(bf16[136,1024]{0,1:T(8,128)(2,1)} %copy.223), channel_id=1, source_target_pairs={{0,1},{1,2},{2,3},{3,4},{4,5},{5,6},{6,7},{7,8},{8,9},{9,10},{10,1... | collective-permute-start | bytes 835592 | tf_op jit(solution)/shard_map/while/body/eval_jaxpr/ppermute | solution.py:21
  999.1 34.6 %collective-permute-start.1 = (bf16[136,1024]{0,1:T(8,128)(2,1)}, bf16[136,1024]{0,1:T(8,128)(2,1)}, u32[]{:S(2)}, u32[]{:S(2)}) collective-permute-start(bf16[136,1024]{0,1:T(8,128)(2,1)} %copy.224), channel_id=1, source_target_pairs={{0,1},{1,2},{2,3},{3,4},{4,5},{5,6},{6,7},{7,8},{8,9},{9,10},{10,1... | collective-permute-start | bytes 835592 | tf_op jit(solution)/shard_map/while/body/eval_jaxpr/ppermute | solution.py:21
  999.1 34.6 %collective-permute-start.2 = (bf16[136,4]{0,1:T(4,128)(2,1)S(1)}, bf16[136,4]{0,1:T(4,128)(2,1)S(1)}, u32[]{:S(2)}, u32[]{:S(2)}) collective-permute-start(bf16[136,4]{0,1:T(4,128)(2,1)S(1)} %copy.225), channel_id=1, source_target_pairs={{0,1},{1,2},{2,3},{3,4},{4,5},{5,6},{6,7},{7,8},{8,9},{9,10},{10,1... | collective-permute-start | bytes 3272 | tf_op jit(solution)/shard_map/while/body/eval_jaxpr/ppermute | solution.py:21
  1036.0 36.1 %collective-permute-start = (bf16[136,1024]{0,1:T(8,128)(2,1)}, bf16[136,1024]{0,1:T(8,128)(2,1)}, u32[]{:S(2)}, u32[]{:S(2)}) collective-permute-start(bf16[136,1024]{0,1:T(8,128)(2,1)} %copy.223), channel_id=1, source_target_pairs={{0,1},{1,2},{2,3},{3,4},{4,5},{5,6},{6,7},{7,8},{8,9},{9,10},{10,1... | collective-permute-start | bytes 835592 | tf_op jit(solution)/shard_map/while/body/eval_jaxpr/ppermute | solution.py:21
  1074.4 36.1 %collective-permute-start = (bf16[136,1024]{0,1:T(8,128)(2,1)}, bf16[136,1024]{0,1:T(8,128)(2,1)}, u32[]{:S(2)}, u32[]{:S(2)}) collective-permute-start(bf16[136,1024]{0,1:T(8,128)(2,1)} %copy.223), channel_id=1, source_target_pairs={{0,1},{1,2},{2,3},{3,4},{4,5},{5,6},{6,7},{7,8},{8,9},{9,10},{10,1... | collective-permute-start | bytes 835592 | tf_op jit(solution)/shard_map/while/body/eval_jaxpr/ppermute | solution.py:21
  1076.2 34.2 %collective-permute-start.1 = (bf16[136,1024]{0,1:T(8,128)(2,1)}, bf16[136,1024]{0,1:T(8,128)(2,1)}, u32[]{:S(2)}, u32[]{:S(2)}) collective-permute-start(bf16[136,1024]{0,1:T(8,128)(2,1)} %copy.224), channel_id=1, source_target_pairs={{0,1},{1,2},{2,3},{3,4},{4,5},{5,6},{6,7},{7,8},{8,9},{9,10},{10,1... | collective-permute-start | bytes 835592 | tf_op jit(solution)/shard_map/while/body/eval_jaxpr/ppermute | solution.py:21
  1112.8 36.1 %collective-permute-start = (bf16[136,1024]{0,1:T(8,128)(2,1)}, bf16[136,1024]{0,1:T(8,128)(2,1)}, u32[]{:S(2)}, u32[]{:S(2)}) collective-permute-start(bf16[136,1024]{0,1:T(8,128)(2,1)} %copy.223), channel_id=1, source_target_pairs={{0,1},{1,2},{2,3},{3,4},{4,5},{5,6},{6,7},{7,8},{8,9},{9,10},{10,1... | collective-permute-start | bytes 835592 | tf_op jit(solution)/shard_map/while/body/eval_jaxpr/ppermute | solution.py:21
  1151.1 36.1 %collective-permute-start = (bf16[136,1024]{0,1:T(8,128)(2,1)}, bf16[136,1024]{0,1:T(8,128)(2,1)}, u32[]{:S(2)}, u32[]{:S(2)}) collective-permute-start(bf16[136,1024]{0,1:T(8,128)(2,1)} %copy.223), channel_id=1, source_target_pairs={{0,1},{1,2},{2,3},{3,4},{4,5},{5,6},{6,7},{7,8},{8,9},{9,10},{10,1... | collective-permute-start | bytes 835592 | tf_op jit(solution)/shard_map/while/body/eval_jaxpr/ppermute | solution.py:21
  1189.5 36.1 %collective-permute-start = (bf16[136,1024]{0,1:T(8,128)(2,1)}, bf16[136,1024]{0,1:T(8,128)(2,1)}, u32[]{:S(2)}, u32[]{:S(2)}) collective-permute-start(bf16[136,1024]{0,1:T(8,128)(2,1)} %copy.223), channel_id=1, source_target_pairs={{0,1},{1,2},{2,3},{3,4},{4,5},{5,6},{6,7},{7,8},{8,9},{9,10},{10,1... | collective-permute-start | bytes 835592 | tf_op jit(solution)/shard_map/while/body/eval_jaxpr/ppermute | solution.py:21
  1227.9 36.1 %collective-permute-start = (bf16[136,1024]{0,1:T(8,128)(2,1)}, bf16[136,1024]{0,1:T(8,128)(2,1)}, u32[]{:S(2)}, u32[]{:S(2)}) collective-permute-start(bf16[136,1024]{0,1:T(8,128)(2,1)} %copy.223), channel_id=1, source_target_pairs={{0,1},{1,2},{2,3},{3,4},{4,5},{5,6},{6,7},{7,8},{8,9},{9,10},{10,1... | collective-permute-start | bytes 835592 | tf_op jit(solution)/shard_map/while/body/eval_jaxpr/ppermute | solution.py:21
  1266.3 36.1 %collective-permute-start = (bf16[136,1024]{0,1:T(8,128)(2,1)}, bf16[136,1024]{0,1:T(8,128)(2,1)}, u32[]{:S(2)}, u32[]{:S(2)}) collective-permute-start(bf16[136,1024]{0,1:T(8,128)(2,1)} %copy.223), channel_id=1, source_target_pairs={{0,1},{1,2},{2,3},{3,4},{4,5},{5,6},{6,7},{7,8},{8,9},{9,10},{10,1... | collective-permute-start | bytes 835592 | tf_op jit(solution)/shard_map/while/body/eval_jaxpr/ppermute | solution.py:21
  1304.7 36.1 %collective-permute-start = (bf16[136,1024]{0,1:T(8,128)(2,1)}, bf16[136,1024]{0,1:T(8,128)(2,1)}, u32[]{:S(2)}, u32[]{:S(2)}) collective-permute-start(bf16[136,1024]{0,1:T(8,128)(2,1)} %copy.223), channel_id=1, source_target_pairs={{0,1},{1,2},{2,3},{3,4},{4,5},{5,6},{6,7},{7,8},{8,9},{9,10},{10,1... | collective-permute-start | bytes 835592 | tf_op jit(solution)/shard_map/while/body/eval_jaxpr/ppermute | solution.py:21
  1360.7 277.1 %reduce-scatter.27.cloned.1.call-start = ((), (), s32[]{:S(2)}) async-start(), calls=%async_computation.19 | async-start | bytes 540672
  1361.9 412.4 %reduce-scatter.29.cloned.1.call-start = ((), (), s32[]{:S(2)}) async-start(), calls=%async_computation.20 | async-start | bytes 540672
  1363.0 547.5 %reduce-scatter.31.cloned.1.call-start = ((), (), s32[]{:S(2)}) async-start(), calls=%async_computation.21 | async-start | bytes 540672
  1364.3 826.4 %all-reduce.4.cloned.1.call-start = ((), (), s32[]{:S(2)}) async-start(), calls=%async_computation.22 | async-start | bytes 33554432
  1389.2 945.8 %reduce-scatter.17.cloned.1.call-start = ((), (), s32[]{:S(2)}) async-start(), calls=%async_computation.13 | async-start | bytes 1622016 | tf_op jit(solution)/shard_map/reduce_scatter | solution.py:336
  1392.3 1089.1 %reduce-scatter.19.cloned.1.call-start = ((), (), s32[]{:S(2)}) async-start(), calls=%async_computation.14 | async-start | bytes 4325376 | tf_op jit(solution)/shard_map/reduce_scatter | solution.py:337
  1395.4 1444.9 %reduce-scatter.21.cloned.1.call-start = ((), (), s32[]{:S(2)}) async-start(), calls=%async_computation.15 | async-start | bytes 17301504 | tf_op jit(solution)/shard_map/reduce_scatter | solution.py:350
  1405.1 1798.1 %reduce-scatter.23.cloned.1.call-start = ((), (), s32[]{:S(2)}) async-start(), calls=%async_computation.16 | async-start | bytes 17301504 | tf_op jit(solution)/shard_map/reduce_scatter | solution.py:352
  (192 other events, 4458.7 us)
Sparse Core Ops, SparseCore 0:
  10.9 71.6 all-gather.13
  87.5 75.7 all-gather.23
  166.6 76.8 all-gather.15
  246.2 56.5 all-gather.17
  305.5 83.6 all-gather.19
  391.9 77.0 all-gather.21
  1360.8 140.5 reduce-scatter.24
  1503.7 134.0 reduce-scatter.26
  1640.1 134.1 reduce-scatter.28
  1776.4 134.0 reduce-scatter.30
  1916.5 274.1 all-reduce.3
  2193.4 141.5 reduce-scatter.16
  2338.0 143.4 reduce-scatter.18
  2484.3 355.9 reduce-scatter.20
  2843.1 360.0 reduce-scatter.22
where the time goes:
time: 3220 us; the launch traced here: 3210 us
  waiting for transfers between devices  2050 us (64%)
  blocking collectives  476 us (15%)
  matrix products  338 us (10%)
  local copies, waits for them, and re-layouts  199 us (6%)
  other arithmetic  130 us (4%)
    unnamed x20, waiting for transfers between devices  720 us
    reduce_scatter x1, waiting for transfers between devices, shards(): lax.psum_scatter(grad_w_down, ('grp', 'blk'), scatter_dimension=0, tiled=...  363 us
    reduce_scatter x1, waiting for transfers between devices, shards(): lax.psum_scatter(grad_w_in, ('grp', 'blk'), scatter_dimension=0, tiled=True)  359 us
    ppermute x64, waiting for transfers between devices, shifted(): lax.ppermute(x, axis, [(i, (i + by) % devices) for i in range(devices)])  242 us
    reduce_scatter x1, waiting for transfers between devices, shards(): lax.psum_scatter(grad_w_out, ('grp', 'blk'), scatter_dimension=0, tiled=T...  146 us
    reduce_scatter x1, waiting for transfers between devices, shards(): lax.psum_scatter(grad_rel, ('grp', 'blk'), scatter_dimension=2, tiled=True)  142 us
    while x260, local copies, waits for them, and re-layouts  90.9 us
    all_gather x1, blocking collectives, shards(): lax.all_gather(rel_tables, ('grp', 'blk'), axis=2, tiled=True)  79.8 us
  transfers between devices with their start and end apart: 79, of which 26 were waited for; matrix products, arithmetic and copies ran while one was open for 17% of the time, Pallas kernels for 0%

commit v1 on v0

--- a/solution.py
+++ b/solution.py
@@ -1,8 +1,11 @@
+import functools
 import math
 
 import jax
 import jax.numpy as jnp
 from jax import lax
+from jax.experimental import pallas as pl
+from jax.experimental.pallas import tpu as pltpu
 from jax.sharding import PartitionSpec as P
 
 H = 16
@@ -367,9 +370,1151 @@
     )
 
 
+MESH = pl.DeviceIdType.MESH
+LOW = jnp.bfloat16
+HIGH = jnp.float32
+CHIPS = 16
+HALF = 8
+BLOCK = 256
+MASKED = -1e30
+VMEM_LIMIT = 60 * 2**20
+
+
+def dot(left, right, dims=((1,), (0,))):
+    return lax.dot_general(left, right, (dims, ((), ())), preferred_element_type=HIGH)
+
+
+NT = ((1,), (1,))
+TN = ((0,), (0,))
+
+
+def place():
+    core = lax.axis_index("grp")
+    chip = lax.axis_index("blk")
+    return core, chip
+
+
+def coordinates(chip):
+    return lax.div(chip, 4), lax.rem(lax.div(chip, 2), 2), lax.rem(chip, 2)
+
+
+def chip_at(z, y, x):
+    return z * 4 + y * 2 + x
+
+
+def meet():
+    core, chip = place()
+    me = core * CHIPS + chip
+    barrier = pltpu.get_barrier_semaphore()
+
+    def greet(ahead, carry):
+        other = lax.rem(me + ahead, 2 * CHIPS)
+        pl.semaphore_signal(
+            barrier,
+            inc=1,
+            device_id=(lax.div(other, CHIPS), lax.rem(other, CHIPS)),
+            device_id_type=MESH,
+        )
+        return carry
+
+    lax.fori_loop(1, 2 * CHIPS, greet, 0)
+    pl.semaphore_wait(barrier, 2 * CHIPS - 1)
+
+
+def remote(source, target, send, recv, device):
+    return pltpu.make_async_remote_copy(
+        src_ref=source,
+        dst_ref=target,
+        send_sem=send,
+        recv_sem=recv,
+        device_id=device,
+        device_id_type=MESH,
+    )
+
+
+def gather_steps(pick, send, recv, across):
+    core, chip = place()
+    z, y, x = coordinates(chip)
+    started = []
+
+    def flip(far_p, far_q, ahead):
+        p_y, p_x = (0, far_p) if across == "x" else (far_p, 0)
+        q_y, q_x = (far_q, 0) if across == "x" else (0, far_q)
+        y_to = 1 - y if p_y + q_y else y
+        x_to = 1 - x if p_x + q_x else x
+        return chip_at(lax.rem(z + ahead, 4), y_to, x_to)
+
+    def ship(slot, to):
+        copy = remote(
+            pick(slot), pick(slot), send.at[len(started)], recv.at[slot], (core, to)
+        )
+        copy.start()
+        started.append(copy)
+
+    def landed(slot):
+        remote(pick(slot), pick(slot), send.at[0], recv.at[slot], (core, flip(1, 0, 0))).wait_recv()
+
+    def own():
+        for ahead in (1, 3, 2):
+            ship(chip, flip(0, 0, ahead))
+        ship(chip, flip(1, 0, 0))
+        ship(chip, flip(0, 1, 0))
+
+    def line(ahead):
+        slot = flip(0, 0, ahead)
+        landed(slot)
+        ship(slot, flip(1, 0, 0))
+        ship(slot, flip(0, 1, 0))
+
+    def side(ahead):
+        slot = flip(1, 0, ahead)
+        landed(slot)
+        ship(slot, flip(0, 1, 0))
+
+    def finish():
+        for ahead in (0, 1, 3, 2):
+            for far_p in (0, 1):
+                landed(flip(far_p, 1, ahead))
+        for copy in started:
+            copy.wait_send()
+
+    return [
+        own,
+        lambda: side(0),
+        lambda: line(1),
+        lambda: side(1),
+        lambda: line(3),
+        lambda: side(3),
+        lambda: line(2),
+        lambda: side(2),
+        finish,
+    ]
+
+
+def run_together(*plans):
+    for steps in zip(*plans):
+        for step in steps:
+            step()
+
+
+def to_tokens(source, target, send, recv):
+    core, chip = place()
+    to_core = lax.div(chip, HALF)
+    mine = core * HALF + lax.rem(chip, HALF)
+    here = to_core == core
+
+    def copy_to(ahead):
+        chip_to = lax.rem(chip + ahead, CHIPS)
+        return remote(
+            source.at[chip_to], target.at[mine], send.at[ahead], recv.at[mine], (to_core, chip_to)
+        )
+
+    @pl.when(here)
+    def _():
+        pltpu.make_async_copy(source.at[chip], target.at[mine], recv.at[mine]).start()
+
+    @pl.when(jnp.logical_not(here))
+    def _():
+        copy_to(0).start()
+
+    for ahead in range(1, CHIPS):
+        copy_to(ahead).start()
+
+    def finish():
+        for slot in range(CHIPS):
+            pltpu.make_async_copy(source.at[slot], target.at[slot], recv.at[slot]).wait()
+
+        @pl.when(jnp.logical_not(here))
+        def _():
+            copy_to(0).wait_send()
+
+        for ahead in range(1, CHIPS):
+            copy_to(ahead).wait_send()
+
+    return finish
+
+
+def to_heads(source, target, send, recv):
+    core, chip = place()
+
+    def copy_to(group, ahead):
+        head = lax.rem(chip + ahead, HALF)
+        return remote(
+            source.at[group * HALF + head],
+            target.at[chip],
+            send.at[group * HALF + ahead],
+            recv.at[chip],
+            (group, core * HALF + head),
+        )
+
+    here = lax.div(chip, HALF) == core
+
+    def each(act):
+        for group in range(2):
+            for ahead in range(HALF):
+                if ahead == 0:
+                    itself = jnp.logical_and(here, core == group)
+                    pl.when(jnp.logical_not(itself))(lambda: act(copy_to(group, 0)))
+                else:
+                    act(copy_to(group, ahead))
+
+    @pl.when(here)
+    def _():
+        pltpu.make_async_copy(
+            source.at[core * HALF + lax.rem(chip, HALF)], target.at[chip], recv.at[chip]
+        ).start()
+
+    each(lambda copy: copy.start())
+
+    def finish():
+        for slot in range(CHIPS):
+            pltpu.make_async_copy(source.at[slot], target.at[slot], recv.at[slot]).wait()
+        each(lambda copy: copy.wait_send())
+
+    return finish
+
+
+def lanes(rows, width=128):
+    return lax.broadcasted_iota(jnp.int32, (rows, width), 1)
+
+
+def fold(rows_in):
+    half = rows_in.shape[0] // 2
+    both = jnp.where(lanes(half) < HD, rows_in[:half], pltpu.roll(rows_in[half:], HD, 1))
+    pad = -half % 16
+    if pad:
+        both = jnp.concatenate([both, jnp.zeros((pad, 128), HIGH)], axis=0)
+    return both.astype(LOW)
+
+
+def gather_tokens(slot_rows, x_in, w_in, rel_in, x_all, w_all, rel_all, *sems):
+    x_send, x_recv, w_send, w_recv, rel_send, rel_recv, pair_sem, own_sem = sems
+    core, chip = place()
+    me = core * CHIPS + chip
+    to_chip = lax.div(me, 2)
+    side = lax.rem(chip, 2)
+    depth = rel_in.shape[0]
+    half = x_in.shape[1] // 2
+    own_x = pltpu.make_async_copy(x_in, x_all.at[pl.ds(chip * slot_rows, slot_rows)], own_sem.at[0])
+    own_w = pltpu.make_async_copy(w_in.at[chip], w_all.at[me], own_sem.at[1])
+    own_x.start()
+    own_w.start()
+    meet()
+    rel_slot = rel_all.at[pl.ds(side * depth, depth)]
+
+    def rel_copy(to_core):
+        return remote(
+            rel_in, rel_slot, rel_send.at[to_core], rel_recv.at[side], (to_core, to_chip)
+        )
+
+    def rel_each(act_remote, act_own):
+        for to_core in range(2):
+            itself = jnp.logical_and(to_chip == chip, core == to_core)
+            pl.when(jnp.logical_not(itself))(lambda: act_remote(rel_copy(to_core)))
+            if act_own is not None:
+                pl.when(itself)(act_own)
+
+    rel_each(
+        lambda copy: copy.start(),
+        lambda: pltpu.make_async_copy(rel_in, rel_slot, rel_recv.at[side]).start(),
+    )
+
+    def w_copy(ahead):
+        chip_to = lax.rem(chip + ahead, CHIPS)
+        return remote(w_in.at[chip_to], w_all.at[me], w_send.at[ahead], w_recv.at[chip], (core, chip_to))
+
+    for ahead in range(1, CHIPS):
+        w_copy(ahead).start()
+
+    def pick(part):
+        return lambda slot: x_all.at[
+            pl.ds(pl.multiple_of(slot * slot_rows, 16), slot_rows), pl.ds(part * half, half)
+        ]
+
+    own_x.wait()
+    run_together(
+        gather_steps(pick(0), x_send.at[0], x_recv.at[0], "x"),
+        gather_steps(pick(1), x_send.at[1], x_recv.at[1], "y"),
+    )
+    own_w.wait()
+    for ahead in range(1, CHIPS):
+        chip_from = lax.rem(chip + ahead, CHIPS)
+        remote(
+            w_in.at[0], w_all.at[core * CHIPS + chip_from], w_send.at[0], w_recv.at[chip_from], (core, chip_from)
+        ).wait_recv()
+    mine = w_all.at[pl.ds(core * CHIPS, CHIPS)]
+    pair = remote(mine, mine, pair_sem.at[0], pair_sem.at[1], (1 - core, chip))
+    pair.start()
+    for ahead in range(1, CHIPS):
+        w_copy(ahead).wait_send()
+    rel_each(lambda copy: copy.wait_send(), None)
+    for slot in range(2):
+        pltpu.make_async_copy(
+            rel_in, rel_all.at[pl.ds(slot * depth, depth)], rel_recv.at[slot]
+        ).wait()
+    pair.wait()
+
+
+def gather_weights(in_in, down_in, out_in, qkv_in, small_in, w_in, w_down, w_out, w_qkv, small, *sems):
+    in_send, in_recv, down_send, down_recv, out_send, out_recv, qkv_send, qkv_recv, pair_sem, own_sem = sems
+    core, chip = place()
+    other = 1 - core
+    wide = in_in.shape[1] // 2
+    narrow = qkv_in.shape[2] // 2
+
+    def columns(half, width):
+        return pl.ds(pl.multiple_of(half * width, 128), width)
+
+    own = [
+        pltpu.make_async_copy(in_in.at[:, columns(core, wide)], w_in.at[core, chip], own_sem.at[0]),
+        pltpu.make_async_copy(qkv_in.at[:, :, columns(core, narrow)], w_qkv.at[:, core, chip], own_sem.at[1]),
+        pltpu.make_async_copy(down_in, w_down.at[chip], own_sem.at[2]),
+        pltpu.make_async_copy(out_in, w_out.at[chip], own_sem.at[3]),
+        pltpu.make_async_copy(small_in, small.at[core], own_sem.at[4]),
+    ]
+    for copy in own:
+        copy.start()
+    meet()
+    pair = [
+        remote(in_in.at[:, columns(other, wide)], w_in.at[core, chip], pair_sem.at[0], pair_sem.at[1], (other, chip)),
+        remote(
+            qkv_in.at[:, :, columns(other, narrow)],
+            w_qkv.at[:, core, chip],
+            pair_sem.at[2],
+            pair_sem.at[3],
+            (other, chip),
+        ),
+        remote(small_in, small.at[core], pair_sem.at[4], pair_sem.at[5], (other, chip)),
+    ]
+    for copy in pair:
+        copy.start()
+    for copy in own:
+        copy.wait()
+    plans = (
+        gather_steps(lambda slot: w_out.at[slot], out_send, out_recv, "x"),
+        gather_steps(lambda slot: w_down.at[slot], down_send, down_recv, "y"),
+        gather_steps(lambda slot: w_in.at[:, slot], in_send, in_recv, "x"),
+        gather_steps(lambda slot: w_qkv.at[:, :, slot], qkv_send, qkv_recv, "y"),
+    )
+    plans[0][0]()
+    plans[1][0]()
+    for copy in pair:
+        copy.wait()
+    plans[2][0]()
+    plans[3][0]()
+    run_together(*(plan[1:] for plan in plans))
+
+
+def attend_forward(
+    slot_rows, token_rows, x_all, w_all, rel_all, left, right, right_t, value, value_t, kept, arrived, *scratch
+):
+    meta, message, send, recv = scratch
+    total = x_all.shape[0]
+    eye = (
+        lax.broadcasted_iota(jnp.int32, (slot_rows, 2 * 128), 0)
+        == lax.broadcasted_iota(jnp.int32, (slot_rows, 2 * 128), 1)
+    ).astype(LOW)
+    for slot in range(CHIPS):
+        end = (slot + 1) * slot_rows
+        labels = x_all[end - 16 : end, 0:256]
+        meta[end - slot_rows : end, 0:16] = dot(eye, labels, NT)
+    rel = rel_all[...]
+    table_t = rel[:, 0 : 3 * NB]
+    depth = rel.shape[0]
+    eye_small = lax.broadcasted_iota(jnp.int32, (depth, 128), 0) == lax.broadcasted_iota(
+        jnp.int32, (depth, 128), 1
+    )
+    eye_next = lax.broadcasted_iota(jnp.int32, (depth, 128), 0) + depth == lax.broadcasted_iota(
+        jnp.int32, (depth, 128), 1
+    )
+    extra = rel[:, 3 * NB : 4 * NB].astype(HIGH)
+    bias = jnp.sum(
+        jnp.where(eye_small, extra[:, 0:1], 0.0) + jnp.where(eye_next, extra[:, 1:2], 0.0),
+        axis=0,
+        keepdims=True,
+    )
+    lane = lanes(BLOCK)
+    first_half = lane < HD
+    scale = 1.0 / math.sqrt(4.0 * HD)
+
+    def prepare(index, carry):
+        rows = pl.ds(pl.multiple_of(index * BLOCK, BLOCK), BLOCK)
+        projected = dot(x_all[rows, :], w_all[...])
+        query_value = (projected[:, 0:128] + bias).astype(LOW).astype(HIGH)
+        key = projected[:, 128:256].astype(LOW).astype(HIGH)
+        query = query_value[:, 0:HD].astype(LOW)
+        tables = dot(query, table_t).astype(LOW).astype(HIGH)
+        ids = meta[rows, 8:12].astype(jnp.int32)
+        segment, order, box_x, box_y = ids[:, 0:1], ids[:, 1:2], ids[:, 2:3], ids[:, 3:4]
+
+        def selected(column, ids_of, values):
+            bucket = jnp.clip(ids_of - values, -(NB // 2), NB // 2 - 1) + NB // 2
+            return jnp.take_along_axis(tables[:, column * NB : (column + 1) * NB], bucket, axis=1)
+
+        wide = selected(0, order, lane)
+        narrow = jnp.where(
+            first_half, selected(1, box_x, lane), selected(2, box_y, lane - HD)
+        )
+        label = lane - HD
+        query_side = jnp.where(
+            first_half,
+            query_value * scale,
+            jnp.where(jnp.logical_and(label != segment, label < 8), MASKED, 0.0),
+        )
+        key_side = jnp.where(first_half, key, (label == segment).astype(HIGH))
+        left[rows, 0:128] = (wide * scale).astype(LOW)
+        left[rows, 128:256] = (narrow * scale).astype(LOW)
+        left[rows, 256:384] = query_side.astype(LOW)
+        order_hot = (lane == order).astype(HIGH)
+        box_hot = (jnp.where(first_half, box_x, box_y + HD) == lane).astype(HIGH)
+        right[rows, 0:128] = order_hot.astype(LOW)
+        right[rows, 128:256] = box_hot.astype(LOW)
+        right[rows, 256:384] = key_side.astype(LOW)
+        right_t[0:128, rows] = order_hot.T.astype(LOW)
+        right_t[128:256, rows] = box_hot.T.astype(LOW)
+        right_t[256:384, rows] = key_side.T.astype(LOW)
+        held = jnp.where(first_half, pltpu.roll(query_value, HD, 1), (label == 0).astype(HIGH))
+        value[rows, :] = held.astype(LOW)
+        value_t[:, rows] = held.T.astype(LOW)
+        return carry
+
+    lax.fori_loop(0, total // BLOCK, prepare, 0)
+
+    def attend(index, carry):
+        rows = pl.ds(pl.multiple_of(index * BLOCK, BLOCK), BLOCK)
+        logits = dot(left[rows, :], right_t[...])
+        top = jnp.max(logits, axis=1, keepdims=True)
+        weights = jnp.exp(logits - top).astype(LOW)
+        mixed = dot(weights, value[...])
+        row_sum = mixed[:, HD : HD + 1]
+        ids = meta[rows, 8:12]
+        facts = jnp.where(lane == HD, top + jnp.log(row_sum), ids[:, 3:4])
+        facts = jnp.where(lane == HD + 1, ids[:, 1:2], facts)
+        facts = jnp.where(lane == HD + 2, ids[:, 2:3], facts)
+        kept[rows, :] = jnp.where(first_half, mixed / row_sum, facts)
+        return carry
+
+    lax.fori_loop(0, total // BLOCK, attend, 0)
+    for slot in range(CHIPS):
+        message[slot] = fold(kept[slot * slot_rows : (slot + 1) * slot_rows, :])
+    meet()
+    to_tokens(message, arrived, send, recv)()
+
+
+def gelu_parts(pre):
+    cdf = 0.5 * (1.0 + lax.erf(pre * math.sqrt(0.5)))
+    density = jnp.exp(-0.5 * pre * pre) * (1.0 / math.sqrt(2.0 * math.pi))
+    return pre * cdf, cdf + pre * density
+
+
+def feed_forward(slot_rows, *refs):
+    inputs, refs = refs[:8], refs[8:]
+    outputs, refs = refs[:7], refs[7:]
+    context_in, x_in, grad_in, vectors, bias_in, w_in, w_down, w_out = inputs
+    out, d_sum1, g_in, g_down, g_out, g_small, arrived = outputs
+    (context_wide, context, low_first, act, slope, d_second, d_inner, d_branch) = refs[:8]
+    (out_part, in_part, d_message, pair_send, pair_recv, send, recv) = refs[8:]
+    core, chip = place()
+    own = pl.ds(pl.multiple_of(core * slot_rows, 16), slot_rows)
+    far = pl.ds(pl.multiple_of((1 - core) * slot_rows, 16), slot_rows)
+    width = x_in.shape[1]
+    hidden = w_in.shape[1]
+    tile = 512
+    half = slot_rows // 2
+    meet()
+    count = [0]
+
+    def swap(source, target):
+        copy = remote(
+            source, target, pair_send.at[count[0]], pair_recv.at[count[0]], (1 - core, chip)
+        )
+        count[0] += 1
+        copy.start()
+        return copy
+
+    def swap_sum(index, full):
+        copy = swap(out_part.at[index], in_part.at[index])
+        copy.wait()
+        return full[...] + in_part[index]
+
+    left_half = lanes(half) < HD
+    for group in range(2):
+        for pair in range(HALF // 2):
+            even = context_in[group * HALF + 2 * pair].astype(HIGH)[:half]
+            odd = context_in[group * HALF + 2 * pair + 1].astype(HIGH)[:half]
+            top = group * slot_rows
+            columns = slice(pair * 128, pair * 128 + 128)
+            context_wide[top : top + half, columns] = jnp.where(left_half, even, pltpu.roll(odd, HD, 1))
+            context_wide[top + half : top + slot_rows, columns] = jnp.where(
+                left_half, pltpu.roll(even, HD, 1), odd
+            )
+    context[...] = context_wide[...].astype(LOW)
+
+    def product(index, lhs, rhs):
+        out_part[index] = dot(lhs[far, :], rhs[...])
+        copy = swap(out_part.at[index], in_part.at[index])
+        mine = dot(lhs[own, :], rhs[...])
+        copy.wait()
+        return mine + in_part[index]
+
+    def normalize(v, gain, shift):
+        center = v - jnp.mean(v, axis=1, keepdims=True)
+        inverse = lax.rsqrt(jnp.mean(center * center, axis=1, keepdims=True) + EPSILON)
+        normed = center * inverse
+        return normed * gain + shift, normed, inverse
+
+    def normalize_back(c, normed, inverse, gain):
+        scaled = c * gain
+        inner = (
+            scaled
+            - jnp.mean(scaled, axis=1, keepdims=True)
+            - normed * jnp.mean(scaled * normed, axis=1, keepdims=True)
+        )
+        return inner * inverse
+
+    def column_sums(v):
+        return jnp.sum(v, axis=0, keepdims=True)
+
+    branch = product(0, context, w_out) + vectors[0:1]
+    first, normed1, inverse1 = normalize(x_in[...].astype(HIGH) + branch, vectors[2:3], vectors[4:5])
+    low_first[own, :] = first.astype(LOW)
+    swap(low_first.at[own], low_first.at[own]).wait()
+
+    def widen(index, carry):
+        columns = pl.ds(pl.multiple_of(index * tile, tile), tile)
+        pre = dot(low_first[...], w_in[:, columns]) + bias_in[:, columns]
+        value, derivative = gelu_parts(pre)
+        act[:, columns] = value.astype(LOW)
+        slope[:, columns] = derivative
+        return carry
+
+    lax.fori_loop(0, hidden // tile, widen, 0)
+    second = product(1, act, w_down) + vectors[1:2]
+    result, normed2, inverse2 = normalize(first + second, vectors[3:4], vectors[5:6])
+    out[...] = result.astype(LOW)
+    upstream = grad_in[...].astype(HIGH)
+    g_small[...] = jnp.zeros_like(g_small)
+    d_sum2 = normalize_back(upstream, normed2, inverse2, vectors[3:4])
+    low_second = d_sum2.astype(LOW)
+    d_second[own, :] = low_second
+    copy = swap(d_second.at[own], d_second.at[own])
+    g_small[1:2, 0:width] = column_sums(low_second.astype(HIGH))
+    g_small[3:4, 0:width] = column_sums(upstream * normed2)
+    g_small[5:6, 0:width] = column_sums(upstream)
+    copy.wait()
+
+    def narrow_back(index, carry):
+        columns = pl.ds(pl.multiple_of(index * tile, tile), tile)
+        d_act = dot(d_second[...], w_down[columns, :], NT)
+        low = (d_act * slope[:, columns]).astype(LOW)
+        d_inner[:, columns] = low
+        g_small[pl.ds(8, 1), columns] = column_sums(low.astype(HIGH))
+        g_down[columns, :] = dot(act[:, columns], d_second[...], TN).astype(LOW)
+        return carry
+
+    lax.fori_loop(0, hidden // tile, narrow_back, 0)
+    out_part[2] = dot(d_inner[far, :], w_in[...], NT)
+    copy = swap(out_part.at[2], in_part.at[2])
+    mine = dot(d_inner[own, :], w_in[...], NT)
+
+    def widen_grad(index, carry):
+        rows = pl.ds(pl.multiple_of(index * 256, 256), 256)
+        g_in[rows, :] = dot(low_first[:, rows], d_inner[...], TN).astype(LOW)
+        return carry
+
+    lax.fori_loop(0, width // 256, widen_grad, 0)
+    copy.wait()
+    d_first = d_sum2 + mine + in_part[2]
+    grad1 = normalize_back(d_first, normed1, inverse1, vectors[2:3])
+    d_sum1[...] = grad1
+    low_branch = grad1.astype(LOW)
+    d_branch[own, :] = low_branch
+    copy = swap(d_branch.at[own], d_branch.at[own])
+    g_small[0:1, 0:width] = column_sums(low_branch.astype(HIGH))
+    g_small[2:3, 0:width] = column_sums(d_first * normed1)
+    g_small[4:5, 0:width] = column_sums(d_first)
+    copy.wait()
+    context_wide[...] = dot(d_branch[...], w_out[...], NT)
+    for group in range(2):
+        for pair in range(HALF // 2):
+            both = context_wide[
+                group * slot_rows : (group + 1) * slot_rows, pair * 128 : pair * 128 + 128
+            ]
+            d_message[group * HALF + 2 * pair] = fold(both)
+            d_message[group * HALF + 2 * pair + 1] = fold(pltpu.roll(both, HD, 1))
+    finish = to_heads(d_message, arrived, send, recv)
+    g_out[...] = dot(context[...], d_branch[...], TN).astype(LOW)
+    finish()
+
+
+def attend_backward(slot_rows, *refs):
+    left, right, right_t, value_t, kept, rel_all, x_all, message_in = refs[:8]
+    tokens_out, w_out, rel_out = refs[8:11]
+    d_context, d_query, d_query_t, d_pair_t, rel_grad, message, w_mine, w_far, w_low = refs[11:20]
+    rel_far, rel_sum, send, recv, w_send, w_recv, pair_sem, rel_sem, own_sem = refs[20:]
+    core, chip = place()
+    total = x_all.shape[0]
+    width = x_all.shape[1]
+    half = slot_rows // 2
+    scale = 1.0 / math.sqrt(4.0 * HD)
+    left_half = lanes(half) < HD
+    for slot in range(CHIPS):
+        both = message_in[slot].astype(HIGH)[:half]
+        top = slot * slot_rows
+        d_context[top : top + half, :] = jnp.where(left_half, both, 0.0)
+        d_context[top + half : top + slot_rows, :] = jnp.where(left_half, pltpu.roll(both, HD, 1), 0.0)
+    table_t = rel_all[:, 0 : 3 * NB]
+    lane = lanes(BLOCK)
+    first_half = lane < HD
+    d_pair_t[...] = jnp.zeros_like(d_pair_t)
+    rel_grad[...] = jnp.zeros_like(rel_grad)
+
+    def step(index, carry):
+        rows = pl.ds(pl.multiple_of(index * BLOCK, BLOCK), BLOCK)
+        facts = kept[rows, :]
+        grad = d_context[rows, :]
+        delta = jnp.sum(grad * facts, axis=1, keepdims=True)
+        probs = jnp.exp(dot(left[rows, :], right_t[...]) - facts[:, HD : HD + 1])
+        d_probs = dot(grad.astype(LOW), value_t[...])
+        d_logits = (probs * (d_probs - delta)).astype(LOW)
+        query_t = jnp.where(first_half, left[rows, 256:384].astype(HIGH), 0.0).T[0:HD]
+        d_pair_t[0:HD, :] += dot(grad.T[0:HD].astype(LOW), probs.astype(LOW))
+        d_pair_t[HD : 2 * HD, :] += dot(query_t.astype(LOW), d_logits)
+        back = dot(d_logits, right[...]) * scale
+        ids = facts.astype(jnp.int32)
+        order, box_x, box_y = (ids[:, HD + k : HD + k + 1] for k in (1, 2, 3))
+
+        def placed(column, ids_of, extent, start):
+            value = ids_of + NB // 2 - lane
+            found = jnp.take_along_axis(
+                back[:, column * 128 : column * 128 + 128], jnp.clip(value, 0, extent - 1) + start, axis=1
+            )
+            return jnp.where(jnp.logical_and(value >= 0, value < extent), found, 0.0)
+
+        wide = back[:, 0:128]
+        low_end = jnp.sum(jnp.where(lane >= order + NB // 2, wide, 0.0), axis=1, keepdims=True)
+        high_end = jnp.sum(jnp.where(lane <= order - (NB // 2 - 1), wide, 0.0), axis=1, keepdims=True)
+        first = placed(0, order, ORDER_RANGE, 0)
+        first = jnp.where(lane == 0, low_end, jnp.where(lane == NB - 1, high_end, first))
+        d_tables = jnp.concatenate(
+            [first, placed(1, box_x, BOX_RANGE, 0), placed(1, box_y, BOX_RANGE, BOX_RANGE)], axis=1
+        ).astype(LOW)
+        from_tables = dot(d_tables, table_t, NT)
+        content = back[:, 256:384]
+        d_query[rows, :] = jnp.where(
+            first_half, content + jnp.concatenate([from_tables, from_tables], axis=1), 0.0
+        )
+        d_query_t[0:HD, rows] = d_query[rows, :].T[0:HD].astype(LOW)
+        rel_grad[:, 0 : 3 * NB] += dot((query_t / scale).astype(LOW), d_tables)
+        return carry
+
+    lax.fori_loop(0, total // BLOCK, step, 0)
+    d_query_t[HD : 3 * HD, :] = d_pair_t[...].astype(LOW)
+    d_columns = d_query_t[...]
+    sums = jnp.sum(d_columns[0 : 2 * HD].astype(HIGH), axis=1, keepdims=True)
+    rel_grad[:, 3 * NB : 4 * NB] = jnp.where(
+        lanes(HD) == 0, sums[0:HD], jnp.where(lanes(HD) == 1, sums[HD : 2 * HD], 0.0)
+    )
+    slot_lane = lanes(slot_rows)
+    for slot in range(CHIPS):
+        top = slot * slot_rows
+        if slot % 8 == 0:
+            turned = d_pair_t[:, top : top + 8 * slot_rows].T
+        pair = turned[(slot % 8) * slot_rows : (slot % 8 + 1) * slot_rows]
+        turned_pair = pltpu.roll(pair, HD, 1)
+        message[slot, 0:slot_rows, :] = jnp.where(
+            slot_lane < HD, d_query[top : top + slot_rows, :], pair
+        ).astype(LOW)
+        message[slot, slot_rows:, :] = fold(pair)
+    meet()
+    finish_tokens = to_tokens(message, tokens_out, send, recv)
+    w_grad = dot(d_columns, x_all[...])
+    half_width = width // 2
+    for part in range(2):
+        w_mine[part] = w_grad[:, part * half_width : (part + 1) * half_width]
+    w_pair = remote(w_mine.at[1 - core], w_far, pair_sem.at[0], pair_sem.at[1], (1 - core, chip))
+    w_pair.start()
+    depth = rel_sum.shape[0]
+    rel_rows = pl.ds(pl.multiple_of((1 - core) * depth, 8), depth)
+    rel_pair = remote(rel_grad.at[rel_rows], rel_far, pair_sem.at[2], pair_sem.at[3], (1 - core, chip))
+    rel_pair.start()
+    w_pair.wait()
+    w_sum = (w_mine[core] + w_far[...]).T
+    rows_each = w_low.shape[1]
+    for slot in range(CHIPS):
+        w_low[slot] = w_sum[slot * rows_each : (slot + 1) * rows_each].astype(LOW)
+
+    def w_copy(ahead):
+        to = lax.rem(chip + ahead, CHIPS)
+        return remote(w_low.at[to], w_out.at[chip], w_send.at[ahead], w_recv.at[chip], (core, to))
+
+    own_w = pltpu.make_async_copy(w_low.at[chip], w_out.at[chip], own_sem.at[0])
+    own_w.start()
+    for ahead in range(1, CHIPS):
+        w_copy(ahead).start()
+    rel_pair.wait()
+    rel_sum[...] = rel_grad[pl.ds(pl.multiple_of(core * depth, 8), depth), :] + rel_far[...]
+    rel_to = (lax.div(chip, HALF), lax.rem(2 * chip + core, CHIPS))
+    itself = jnp.logical_and(rel_to[0] == core, rel_to[1] == chip)
+    rel_copy = remote(rel_sum, rel_out, rel_sem.at[0], rel_sem.at[1], rel_to)
+    own_rel = pltpu.make_async_copy(rel_sum, rel_out, rel_sem.at[1])
+    pl.when(itself)(lambda: own_rel.start())
+    pl.when(jnp.logical_not(itself))(lambda: rel_copy.start())
+    own_rel.wait()
+    pl.when(jnp.logical_not(itself))(lambda: rel_copy.wait_send())
+    own_w.wait()
+    for ahead in range(1, CHIPS):
+        came = lax.rem(chip + ahead, CHIPS)
+        remote(w_low.at[0], w_out.at[came], w_send.at[0], w_recv.at[came], (core, came)).wait_recv()
+        w_copy(ahead).wait_send()
+    finish_tokens()
+
+
+def input_gradient(slot_rows, message_in, w_qkv, d_sum1, out, wide, low, out_part, in_part, sems):
+    core, chip = place()
+    own = pl.ds(pl.multiple_of(core * slot_rows, 16), slot_rows)
+    far = pl.ds(pl.multiple_of((1 - core) * slot_rows, 16), slot_rows)
+    half = slot_rows // 2
+    pad = message_in.shape[1] - slot_rows
+    lane_all = lanes(slot_rows) < HD
+    lane_half = lanes(half) < HD
+    for group in range(2):
+        top = group * slot_rows
+        for pair in range(HALF // 2):
+            columns = slice(pair * 128, pair * 128 + 128)
+            even = message_in[group * HALF + 2 * pair].astype(HIGH)
+            odd = message_in[group * HALF + 2 * pair + 1].astype(HIGH)
+            even_main, odd_main = even[:slot_rows], odd[:slot_rows]
+            wide[0, top : top + slot_rows, columns] = jnp.where(
+                lane_all, even_main, pltpu.roll(odd_main, HD, 1)
+            )
+            wide[1, top : top + slot_rows, columns] = jnp.where(
+                lane_all, pltpu.roll(even_main, HD, 1), odd_main
+            )
+            even_last, odd_last = even[slot_rows : slot_rows + half], odd[slot_rows : slot_rows + half]
+            wide[2, top : top + half, columns] = jnp.where(
+                lane_half, even_last, pltpu.roll(odd_last, HD, 1)
+            )
+            wide[2, top + half : top + slot_rows, columns] = jnp.where(
+                lane_half, pltpu.roll(even_last, HD, 1), odd_last
+            )
+    low[...] = wide[...].astype(LOW)
+    meet()
+
+    def part(rows):
+        return (
+            dot(low[0, rows, :], w_qkv[0], NT)
+            + dot(low[1, rows, :], w_qkv[1], NT)
+            + dot(low[2, rows, :], w_qkv[2], NT)
+        )
+
+    out_part[...] = part(far)
+    copy = remote(out_part, in_part, sems.at[0], sems.at[1], (1 - core, chip))
+    copy.start()
+    mine = part(own) + d_sum1[...]
+    copy.wait()
+    out[...] = (mine + in_part[...]).astype(LOW)
+
+
+def reduce_steps(own, slot_of, stages, send, recv, across, result):
+    core, chip = place()
+    z, y, x = coordinates(chip)
+    first, second, third = stages
+    started = []
+    order = (1, 3, 2, 0)
+
+    def at(far_p, far_q, ahead):
+        far_y, far_x = (far_q, far_p) if across == "x" else (far_p, far_q)
+        return chip_at(lax.rem(z + ahead, 4), 1 - y if far_y else y, 1 - x if far_x else x)
+
+    def ship(source, target, slot, to):
+        copy = remote(source, target, send.at[len(started)], recv.at[slot], (core, to))
+        copy.start()
+        started.append(copy)
+
+    def landed(target, slot):
+        remote(target, target, send.at[0], recv.at[slot], (core, at(1, 0, 0))).wait_recv()
+
+    def start():
+        for ahead in order:
+            for far_p in (1, 0):
+                place_at = ahead * 2 + far_p
+                ship(slot_of(own, at(far_p, 1, ahead)), first.at[place_at], place_at, at(0, 1, 0))
+
+    def side(ahead):
+        place_at = ahead * 2 + 1
+        landed(first.at[place_at], place_at)
+        mine = slot_of(own, at(1, 0, ahead))
+        first[place_at] = (first[place_at].astype(HIGH) + mine[...].astype(HIGH)).astype(LOW)
+        ship(first.at[place_at], second.at[ahead], 8 + ahead, at(1, 0, 0))
+
+    def line(ahead):
+        place_at = ahead * 2
+        landed(first.at[place_at], place_at)
+        landed(second.at[ahead], 8 + ahead)
+        mine = slot_of(own, at(0, 0, ahead))
+        total = (
+            first[place_at].astype(HIGH) + second[ahead].astype(HIGH) + mine[...].astype(HIGH)
+        )
+        if ahead:
+            first[place_at] = total.astype(LOW)
+            ship(first.at[place_at], third.at[ahead - 1], 11 + ahead, at(0, 0, ahead))
+        else:
+            result[...] = total
+
+    def finish():
+        for ahead in (1, 3, 2):
+            landed(third.at[ahead - 1], 11 + ahead)
+            result[...] += third[ahead - 1].astype(HIGH)
+        for copy in started:
+            copy.wait_send()
+
+    return [start] + [step for ahead in order for step in (functools.partial(side, ahead), functools.partial(line, ahead))] + [finish]
+
+
+def reduce_gradients(*refs):
+    g_in, g_down, g_out, g_small = refs[:4]
+    in_result, down_result, out_result, small_result = refs[4:8]
+    in_stages, down_stages, out_stages, refs = refs[8:11], refs[11:14], refs[14:17], refs[17:]
+    in_total, in_far, small_sum, small_in = refs[:4]
+    in_send, in_recv, down_send, down_recv, out_send, out_recv, small_send, small_recv, pair_sem = refs[4:]
+    core, chip = place()
+    z, y, x = coordinates(chip)
+    meet()
+    plans = (
+        reduce_steps(g_down, lambda ref, slot: ref.at[slot], down_stages, down_send, down_recv, "y", down_result),
+        reduce_steps(g_in, lambda ref, slot: ref.at[:, slot], in_stages, in_send, in_recv, "x", in_total),
+        reduce_steps(g_out, lambda ref, slot: ref.at[slot], out_stages, out_send, out_recv, "y", out_result),
+    )
+    small_sum[...] = g_small[...]
+    waiting = []
+
+    def small_ship(index, device):
+        copy = remote(small_sum, small_in.at[index], small_send.at[index], small_recv.at[index], device)
+        copy.start()
+        return copy
+
+    def small_pair():
+        copy = small_ship(0, (1 - core, chip))
+        copy.wait()
+        small_sum[0:8, :] += small_in[0, 0:8, :]
+
+    def small_side(index, to):
+        copy = small_ship(index, (core, to))
+        copy.wait()
+        small_sum[...] += small_in[index]
+
+    def small_line():
+        copies = [small_ship(2 + ahead, (core, chip_at(lax.rem(z + ahead, 4), y, x))) for ahead in (1, 2, 3)]
+        for copy in copies:
+            copy.wait()
+        small_result[...] = small_sum[...] + small_in[3] + small_in[4] + small_in[5]
+
+    nothing = lambda: None
+    small_steps = [
+        nothing,
+        small_pair,
+        nothing,
+        lambda: small_side(1, chip_at(z, 1 - y, x)),
+        nothing,
+        lambda: small_side(2, chip_at(z, y, 1 - x)),
+        nothing,
+        small_line,
+        nothing,
+        nothing,
+    ]
+    run_together(*plans, small_steps)
+    pair = remote(in_total.at[1 - core], in_far, pair_sem.at[0], pair_sem.at[1], (1 - core, chip))
+    pair.start()
+    wide = in_total.shape[2]
+
+    def columns(half):
+        return pl.ds(pl.multiple_of(half * wide, 128), wide)
+
+    in_result[:, columns(core)] = in_total[core]
+    pair.wait()
+    in_result[:, columns(1 - core)] = in_far[...]
+
+
+def communicate(kernel, name, number, outputs, scratch, in_memory, out_memory):
+    return pl.pallas_call(
+        kernel,
+        out_shape=outputs,
+        in_specs=[pl.BlockSpec(memory_space=space) for space in in_memory],
+        out_specs=[pl.BlockSpec(memory_space=space) for space in out_memory],
+        scratch_shapes=scratch,
+        compiler_params=pltpu.CompilerParams(
+            collective_id=number, has_side_effects=True, vmem_limit_bytes=VMEM_LIMIT
+        ),
+        name=name,
+    )
+
+
+def head_shards(
+    hidden_in,
+    segment_ids,
+    order_ids,
+    box_ids,
+    qkv_weight,
+    qkv_bias,
+    rel_tables,
+    out_weight,
+    branch_bias,
+    norm_gains,
+    norm_shifts,
+    ffn_in,
+    ffn_in_bias,
+    ffn_out,
+    out_grad,
+):
+    rows, width = hidden_in.shape
+    slot_rows = -(-(rows + 5) // 16) * 16
+    total = CHIPS * slot_rows
+    depth = qkv_weight.shape[1]
+    hidden = ffn_in.shape[1]
+    half_hidden, half_width = hidden // 2, width // 2
+    down_rows = ffn_out.shape[0]
+    core = lax.axis_index("grp")
+    chip = lax.axis_index("blk")
+    shape = jax.ShapeDtypeStruct
+    any_, vmem = pl.ANY, pltpu.VMEM
+    dma = pltpu.SemaphoreType.DMA
+
+    def row(values):
+        return jnp.pad(values.astype(LOW), (0, width - values.shape[0]))[None]
+
+    pad_label = jnp.full((slot_rows - rows,), 4, jnp.int32)
+    extra = jnp.concatenate(
+        [
+            row(jnp.concatenate([segment_ids, pad_label])),
+            row(order_ids),
+            row(box_ids[0]),
+            row(box_ids[1]),
+            row(
+                jnp.concatenate(
+                    [branch_bias.reshape(-1), norm_gains.reshape(-1), norm_shifts.reshape(-1), ffn_in_bias]
+                )
+            ),
+            jnp.zeros((slot_rows - rows - 5, width), LOW),
+        ],
+        axis=0,
+    )
+    x_slot = jnp.concatenate([hidden_in, extra], axis=0)
+    w_heads = jnp.concatenate(
+        [
+            qkv_weight[0].reshape(depth, H, HD),
+            qkv_weight[2].reshape(depth, H, HD),
+            qkv_weight[1].reshape(depth, H, HD),
+            jnp.zeros((depth, H, HD), LOW),
+        ],
+        axis=2,
+    ).transpose(1, 0, 2)
+    rel_part = jnp.concatenate(
+        [
+            rel_tables.reshape(3 * NB, depth).T,
+            qkv_bias.T,
+            jnp.zeros((depth, NB - 2), LOW),
+        ],
+        axis=1,
+    )
+    x_all, w_all, rel_all = communicate(
+        functools.partial(gather_tokens, slot_rows),
+        "gather_tokens",
+        0,
+        (
+            shape((total, width), LOW),
+            shape((2 * CHIPS, depth, 4 * HD), LOW),
+            shape((2 * depth, 4 * NB), LOW),
+        ),
+        [dma((2, 16)), dma((2, 16)), dma((16,)), dma((16,)), dma((2,)), dma((2,)), dma((2,)), dma((2,))],
+        [any_] * 3,
+        [any_] * 3,
+    )(x_slot, w_heads, rel_part)
+    small_in = x_all.reshape(CHIPS, slot_rows, width)[:, rows + 4, : 6 * depth + down_rows]
+    w_in, w_down, w_out, w_qkv, small = communicate(
+        gather_weights,
+        "gather_weights",
+        1,
+        (
+            shape((2, CHIPS, depth, half_hidden), LOW),
+            shape((CHIPS, down_rows, width), LOW),
+            shape((CHIPS, depth, width), LOW),
+            shape((3, 2, CHIPS, depth, half_width), LOW),
+            shape((2,) + small_in.shape, LOW),
+        ),
+        [dma((16,))] * 8 + [dma((6,)), dma((5,))],
+        [any_] * 5,
+        [any_] * 5,
+    )(ffn_in, ffn_out, out_weight, qkv_weight, small_in)
+    left, right, right_t, value, value_t, kept, context = communicate(
+        functools.partial(attend_forward, slot_rows, rows),
+        "attend_forward",
+        2,
+        (
+            shape((total, 384), LOW),
+            shape((total, 384), LOW),
+            shape((384, total), LOW),
+            shape((total, 128), LOW),
+            shape((128, total), LOW),
+            shape((total, 128), HIGH),
+            shape((CHIPS, 80, 128), LOW),
+        ),
+        [vmem((total, 128), HIGH), vmem((CHIPS, 80, 128), LOW), dma((16,)), dma((16,))],
+        [vmem] * 3,
+        [vmem] * 7,
+    )(x_all, w_all.reshape(width, 4 * HD), rel_all)
+    vectors = (
+        small[:, :, : 6 * depth].astype(HIGH).reshape(2, CHIPS, 6, depth).transpose(2, 0, 1, 3).reshape(6, width)
+    )
+    vectors = jnp.pad(vectors, ((0, 2), (0, 0)))
+    bias_in = small_in[:, 6 * depth :].astype(HIGH).reshape(1, half_hidden)
+    pad_rows = ((0, slot_rows - rows), (0, 0))
+    both = 2 * slot_rows
+    hidden_out, d_sum1, g_in, g_down, g_out, g_small, d_context = communicate(
+        functools.partial(feed_forward, slot_rows),
+        "feed_forward",
+        3,
+        (
+            shape((slot_rows, width), LOW),
+            shape((slot_rows, width), HIGH),
+            shape((width, half_hidden), LOW),
+            shape((half_hidden, width), LOW),
+            shape((half_width, width), LOW),
+            shape((16, half_hidden), HIGH),
+            shape((CHIPS, 80, 128), LOW),
+        ),
+        [
+            vmem((both, half_width), HIGH),
+            vmem((both, half_width), LOW),
+            vmem((both, width), LOW),
+            vmem((both, half_hidden), LOW),
+            vmem((both, half_hidden), HIGH),
+            vmem((both, width), LOW),
+            vmem((both, half_hidden), LOW),
+            vmem((both, width), LOW),
+            vmem((3, slot_rows, width), HIGH),
+            vmem((3, slot_rows, width), HIGH),
+            vmem((CHIPS, 80, 128), LOW),
+            dma((6,)),
+            dma((6,)),
+            dma((16,)),
+            dma((16,)),
+        ],
+        [vmem] * 8,
+        [vmem] * 7,
+    )(
+        context,
+        jnp.pad(hidden_in, pad_rows),
+        jnp.pad(out_grad, pad_rows),
+        vectors,
+        bias_in,
+        w_in.reshape(width, half_hidden),
+        w_down.reshape(half_hidden, width),
+        w_out.reshape(half_width, width),
+    )
+    token_grads, w_grad, rel_grad = communicate(
+        functools.partial(attend_backward, slot_rows),
+        "attend_backward",
+        4,
+        (
+            shape((CHIPS, slot_rows + 80, 128), LOW),
+            shape((CHIPS, depth, 3 * HD), LOW),
+            shape((depth, 4 * NB), HIGH),
+        ),
+        [
+            vmem((total, 128), HIGH),
+            vmem((total, 128), HIGH),
+            vmem((3 * HD, total), LOW),
+            vmem((2 * HD, total), HIGH),
+            vmem((2 * depth, 4 * NB), HIGH),
+            vmem((CHIPS, slot_rows + 80, 128), LOW),
+            vmem((2, 3 * HD, half_width), HIGH),
+            vmem((3 * HD, half_width), HIGH),
+            vmem((CHIPS, depth, 3 * HD), LOW),
+            vmem((depth, 4 * NB), HIGH),
+            vmem((depth, 4 * NB), HIGH),
+            dma((16,)),
+            dma((16,)),
+            dma((16,)),
+            dma((16,)),
+            dma((4,)),
+            dma((2,)),
+            dma((1,)),
+        ],
+        [vmem] * 8,
+        [vmem] * 3,
+    )(left, right, right_t, value_t, kept, rel_all, x_all, d_context)
+    hidden_grad = communicate(
+        functools.partial(input_gradient, slot_rows),
+        "input_gradient",
+        5,
+        (shape((slot_rows, width), LOW),),
+        [
+            vmem((3, both, half_width), HIGH),
+            vmem((3, both, half_width), LOW),
+            vmem((slot_rows, width), HIGH),
+            vmem((slot_rows, width), HIGH),
+            dma((2,)),
+        ],
+        [vmem] * 3,
+        [vmem],
+    )(token_grads, w_qkv.reshape(3, width, half_width), d_sum1)[0]
+
+    def stages(block):
+        return [vmem((count,) + block, LOW) for count in (8, 4, 3)]
+
+    in_grad, down_grad, out_w_grad, small_grad = communicate(
+        reduce_gradients,
+        "reduce_gradients",
+        6,
+        (
+            shape((depth, hidden), HIGH),
+            shape((down_rows, width), HIGH),
+            shape((depth, width), HIGH),
+            shape((16, half_hidden), HIGH),
+        ),
+        stages((2, depth, half_hidden))
+        + stages((down_rows, width))
+        + stages((depth, width))
+        + [
+            vmem((2, depth, half_hidden), HIGH),
+            vmem((depth, half_hidden), HIGH),
+            vmem((16, half_hidden), HIGH),
+            vmem((6, 16, half_hidden), HIGH),
+        ]
+        + [dma((16,))] * 6
+        + [dma((6,)), dma((6,)), dma((2,))],
+        [vmem] * 4,
+        [vmem] * 4,
+    )(
+        g_in.reshape(2, CHIPS, depth, half_hidden),
+        g_down.reshape(CHIPS, down_rows, width),
+        g_out.reshape(CHIPS, depth, width),
+        g_small,
+    )
+    qkv_grad = w_grad.reshape(H, depth, 3, HD).transpose(2, 1, 0, 3).reshape(3, depth, width).astype(HIGH)
+    mine = lax.dynamic_slice_in_dim(small_grad[0:6], (core * CHIPS + chip) * depth, depth, 1)
+    bias_grad = lax.dynamic_slice_in_dim(small_grad[8], chip * down_rows, down_rows, 0)
+    return (
+        hidden_out[:rows],
+        hidden_grad[:rows],
+        jnp.stack([qkv_grad[0], qkv_grad[2], qkv_grad[1]]),
+        rel_grad[:, 3 * NB : 3 * NB + 2].T,
+        rel_grad[:, : 3 * NB].T.reshape(3, NB, depth),
+        out_w_grad,
+        mine[0:2],
+        mine[2:4],
+        mine[4:6],
+        in_grad,
+        bias_grad,
+        down_grad,
+    )
+
+
 def solution(mesh):
+    by_heads = mesh.shape["grp"] == 2 and mesh.shape["blk"] == CHIPS == H
     return jax.shard_map(
-        shards,
+        head_shards if by_heads else shards,
         mesh=mesh,
         in_specs=(
             P(("grp", "blk"), None),

time: 3220 us -> 551 us (0.17)
  waiting for transfers between devices: 2050 us -> 0 us
  Pallas kernels: 0 us -> 519 us
  blocking collectives: 476 us -> 0 us
  matrix products: 338 us -> 0 us
  local copies, waits for them, and re-layouts: 199 us -> 23.5 us
  other arithmetic: 130 us -> 7.04 us
    reduce_scatter x4 -> x0, waiting for transfers between devices: 1010 us -> none  [the longest x1 363 us: shards(): lax.psum_scatter(grad_w_down, ('grp', 'blk'), scatter_dimension=0, tiled=...]
    unnamed x20 -> x0, waiting for transfers between devices: 720 us -> none
    pallas_call x0 -> x7, Pallas kernels: none -> 519 us  [the longest x1 134 us: head_shards(): communicate(reduce_gradients, 'reduce_gradients', 6, (shape((depth, hidde...]
    all_gather x7 -> x0, blocking collectives: 433 us -> none  [the longest x1 79.8 us: shards(): lax.all_gather(rel_tables, ('grp', 'blk'), axis=2, tiled=True)]
    dot_general x145 -> x0, matrix products: 338 us -> none  [the longest x20 56.1 us: block_logits(): jnp.einsum('thd,khd->htk', query_heads, key_heads, preferred_element_type...]
    ppermute x64 -> x0, waiting for transfers between devices: 242 us -> none  [shifted(): lax.ppermute(x, axis, [(i, (i + by) % devices) for i in range(devices)])]
    while x261 -> x0, local copies, waits for them, and re-layouts: 93.3 us -> none
    convert_element_type x58 -> x1, other arithmetic: 80.6 us -> 0.68 us  [row(): return jnp.pad(values.astype(LOW), (0, width - values.shape[0]))[None]]
  transfers between devices with their start and end apart: 79 -> 0, of which waited for: 26 -> 0; matrix products, arithmetic and copies ran while one was open for 17% -> 0% of each run, Pallas kernels for 0% -> 0%
where the time goes in v1:
time: 551 us
  Pallas kernels  519 us (94%)
  local copies, waits for them, and re-layouts  23.5 us (4%)
  other arithmetic  7.04 us (1%)
    pallas_call x1, Pallas kernels, head_shards(): communicate(reduce_gradients, 'reduce_gradients', 6, (shape((depth, hidde...  134 us
    pallas_call x1, Pallas kernels, head_shards(): communicate(gather_weights, 'gather_weights', 1, (shape((2, CHIPS, depth,...  130 us
    pallas_call x1, Pallas kernels, head_shards(): communicate(functools.partial(feed_forward, slot_rows), 'feed_forward', 3...  72.2 us
    pallas_call x1, Pallas kernels, head_shards(): communicate(functools.partial(attend_backward, slot_rows), 'attend_backwa...  68.2 us
    pallas_call x1, Pallas kernels, head_shards(): communicate(functools.partial(gather_tokens, slot_rows), 'gather_tokens',...  57.8 us
    pallas_call x1, Pallas kernels, head_shards(): communicate(functools.partial(attend_forward, slot_rows, rows), 'attend_f...  46.2 us

profile of v1, /device:TPU:1, one launch (start us, length us, event | category | flops | bytes accessed | tf_op | source)
XLA Modules:
  0.0 550.5 jit_solution(8497071734786263990)
XLA Ops:
  0.7 0.9 fusion.9
  1.6 0.1 reshape_squeeze.9
  1.8 0.1 reshape_squeeze.10
  2.0 0.1 reshape_squeeze.11
  2.2 0.9 maximum_bitcast_fusion.w_in
  3.1 0.7 convert.17
  3.9 0.7 reshape.90
  4.6 0.7 reshape.91
  5.3 0.7 reshape.92
  6.1 0.7 fusion.7
  6.8 0.7 convert.16
  7.5 0.7 convert_element_type.37
  8.2 3.2 concatenate.17.x_in
  11.4 0.7 copy.48
  12.3 0.6 maximum_maximum_fusion.rel_in
  12.9 57.8 %gather_tokens.1 = (bf16[2304,1024]{1,0:T(8,128)(2,1)}, bf16[32,32,256]{2,1,0:T(8,128)(2,1)}, bf16[64,512]{1,0:T(8,128)(2,1)}) custom-call(bf16[144,1024]{1,0:T(8,128)(2,1)} %concatenate.17.x_in, bf16[16,32,256]{2,1,0:T(8,128)(2,1)} %maximum_bitcast_fusion.w_in, bf16[32,512]{1,0:T(8,128)(2,1)} %maximum_maximum_fusion.rel_in), custom_call_target="tpu_custom_call" | custom-call | tf_op jit(solution)/shard_map/gather_tokens/pallas_call | solution.py:1320
  70.7 46.2 %attend_forward.1 = (bf16[2304,384]{1,0:T(8,128)(2,1)}, bf16[2304,384]{1,0:T(8,128)(2,1)}, bf16[384,2304]{1,0:T(8,128)(2,1)}, bf16[2304,128]{1,0:T(8,128)(2,1)},...) custom-call(bf16[2304,1024]{1,0:T(8,128)(2,1)} %get-tuple-element.40.x_all.refs_6_, ...), custom_call_target="tpu_custom_call" | custom-call | tf_op jit(solution)/shard_map/attend_forward/pallas_call | solution.py:1349
  116.9 0.9 slice.96
  117.8 0.6 copy.62
  118.4 130.0 %gather_weights.1 = (bf16[2,16,32,2048]{3,2,1,0:T(8,128)(2,1)}, bf16[16,128,1024]{2,1,0:T(8,128)(2,1)}, bf16[16,32,1024]{2,1,0:T(8,128)(2,1)}, bf16[3,2,16,32,512]{4,3,2,1,0:T(8,128)(2,1)}, bf16[2,16,320]{2,1,0:T(8,128)(2,1)}) custom-call(bf16[32,4096]{1,0:T(8,128)(2,1)} %in_in.1, bf16[128,1024]{1,0:T(8,128)(2,1)} %down_in.1, bf16[32,1024]{1,0:T(8,128)(2,1)} %out_in.1, ...), custom_call_target="tpu_custom_call" | custom-call | tf_op jit(solution)/shard_map/gather_weights/pallas_call | solution.py:1334
  248.4 0.7 slice.77
  249.4 0.6 pad_convert_fusion.refs_3_
  250.0 1.4 slice_convert_fusion
  251.4 0.7 pad.38.refs_1_
  252.1 0.7 pad.39.refs_2_
  252.8 72.2 %feed_forward.1 = (bf16[144,1024]{1,0:T(8,128)(2,1)}, f32[144,1024]{1,0:T(8,128)}, bf16[1024,2048]{1,0:T(8,128)(2,1)}, bf16[2048,1024]{1,0:T(8,128)(2,1)}, bf16[...) custom-call(bf16[16,80,128]{2,1,0:T(8,128)(2,1)} %get-tuple-element.43.refs_0_, ...), custom_call_target="tpu_custom_call" | custom-call | tf_op jit(solution)/shard_map/feed_forward/pallas_call | solution.py:1373
  325.1 134.0 %reduce_gradients.1 = (f32[32,4096]{1,0:T(8,128)}, f32[128,1024]{1,0:T(8,128)}, f32[32,1024]{1,0:T(8,128)}, f32[16,2048]{1,0:T(8,128)}) custom-call(bf16[2,16,32,2048]{3,2,1,0:T(8,128)(2,1)} %bitcast.44, bf16[16,128,1024]{2,1,0:T(8,128)(2,1)} %bitcast.45, bf16[16,32,1024]{2,1,0:T(8,128)(2,1)} %bitcast.51, f32[16,2048]{1,0:T(8,128)} %get-tuple-element.63.refs_3_), custom_call_target="tpu_custom_call" | custom-call | tf_op jit(solution)/shard_map/reduce_gradients/pallas_call | solution.py:1466
  459.1 0.8 slice.89
  460.0 0.6 fusion.10
  460.6 0.8 slice.93
  461.5 0.5 dynamic-slice_bitcast_fusion
  462.0 68.2 %attend_backward.1 = (bf16[16,224,128]{2,1,0:T(8,128)(2,1)}, bf16[16,32,192]{2,1,0:T(8,128)(2,1)}, f32[32,512]{1,0:T(8,128)}) custom-call(bf16[2304,384]{1,0:T(8,128)(2,1)} %get-tuple-element.49.refs_0_, bf16[2304,384]{1,0:T(8,128)(2,1)} %get-tuple-element.50.refs_1_, bf16[384,2304]{1,0:T(8,128)(2,1)} %get-tuple-element.51.refs_2_, ...), custom_call_target="tpu_custom_call" | custom-call | tf_op jit(solution)/shard_map/attend_backward/pallas_call | solution.py:1415
  530.2 1.5 reshape.110
  531.6 0.6 fusion.8
  532.3 0.2 copy.51
  532.6 0.2 copy.52
  532.7 0.1 slice.84
  532.9 0.2 copy.53
  533.0 0.1 slice.86
  533.2 0.8 pad_maximum_fusion
  533.9 10.6 %input_gradient.1 = bf16[144,1024]{1,0:T(8,128)(2,1)} custom-call(bf16[16,224,128]{2,1,0:T(8,128)(2,1)} %get-tuple-element.55.message_in, bf16[3,1024,512]{2,1,0:T(8,128)(2,1)} %bitcast.49, f32[144,1024]{1,0:T(8,128)} %get-tuple-element.57.d_sum1), custom_call_target="tpu_custom_call" | custom-call | tf_op jit(solution)/shard_map/input_gradient/pallas_call | solution.py:1447
  544.6 1.7 slice.80
  546.3 0.6 copy_bitcast_fusion
  546.9 0.6 copy.54
  547.5 0.7 slice.79
  548.3 0.7 copy.66
  548.9 0.8 copy.67
  549.7 0.8 copy.68
  (41 shorter events, 0.8 us)
Async XLA Ops:
  0.6 10.8 %copy-start = (bf16[3,128,32]{1,2,0:T(8,128)(2,1)S(1)}, bf16[3,128,32]{1,2,0:T(8,128)(2,1)}, u32[]{:S(2)}) copy-start(bf16[3,128,32]{1,2,0:T(8,128)(2,1)} %param.21) | copy-start | bytes 73732
  2.2 249.1 %copy-start.1 = (bf16[136,1024]{1,0:T(8,128)(2,1)S(1)}, bf16[136,1024]{1,0:T(8,128)(2,1)}, u32[]{:S(2)}) copy-start(bf16[136,1024]{1,0:T(8,128)(2,1)} %param.15) | copy-start | bytes 835588
  8.2 243.9 %copy-start.4 = (bf16[136,1024]{1,0:T(8,128)(2,1)S(1)}, bf16[136,1024]{1,0:T(8,128)(2,1)}, u32[]{:S(2)}) copy-start(bf16[136,1024]{1,0:T(8,128)(2,1)} %param.29) | copy-start | bytes 835588
  532.4 13.8 %copy-start.7 = (f32[32,512]{1,0:T(8,128)S(1)}, f32[32,512]{1,0:T(8,128)}, u32[]{:S(2)}) copy-start(f32[32,512]{1,0:T(8,128)} %get-tuple-element.59) | copy-start | bytes 196612
  532.6 15.0 %copy-start.5 = (bf16[144,1024]{1,0:T(8,128)(2,1)S(1)}, bf16[144,1024]{1,0:T(8,128)(2,1)}, u32[]{:S(2)}) copy-start(bf16[144,1024]{1,0:T(8,128)(2,1)} %get-tuple-element.48) | copy-start | bytes 884740
  532.7 15.5 %copy-start.6 = (f32[32,1024]{1,0:T(8,128)S(1)}, f32[32,1024]{1,0:T(8,128)}, u32[]{:S(2)}) copy-start(f32[32,1024]{1,0:T(8,128)} %get-tuple-element.132) | copy-start | bytes 393220
  532.7 16.2 %copy-start.3 = (f32[32,4096]{1,0:T(8,128)S(1)}, f32[32,4096]{1,0:T(8,128)}, u32[]{:S(2)}) copy-start(f32[32,4096]{1,0:T(8,128)} %get-tuple-element.136) | copy-start | bytes 1572868
  533.2 16.6 %copy-start.2 = (f32[128,1024]{1,0:T(8,128)S(1)}, f32[128,1024]{1,0:T(8,128)}, u32[]{:S(2)}) copy-start(f32[128,1024]{1,0:T(8,128)} %get-tuple-element.138) | copy-start | bytes 1572868

commit v2 on v0

--- a/solution.py
+++ b/solution.py
@@ -1,8 +1,12 @@
+import functools
 import math
+import types
 
 import jax
 import jax.numpy as jnp
 from jax import lax
+from jax.experimental import pallas as pl
+from jax.experimental.pallas import tpu as pltpu
 from jax.sharding import PartitionSpec as P
 
 H = 16
@@ -367,9 +371,1378 @@
     )
 
 
+MESH = pl.DeviceIdType.MESH
+LOW = jnp.bfloat16
+HIGH = jnp.float32
+CHIPS = 16
+HALF = 8
+BLOCK = 256
+MASKED = -1e30
+VMEM_LIMIT = 62 * 2**20
+NT = ((1,), (1,))
+TN = ((0,), (0,))
+
+
+def dot(left, right, dims=((1,), (0,))):
+    return lax.dot_general(left, right, (dims, ((), ())), preferred_element_type=HIGH)
+
+
+def place():
+    return lax.axis_index("grp"), lax.axis_index("blk")
+
+
+def coordinates(chip):
+    return lax.div(chip, 4), lax.rem(lax.div(chip, 2), 2), lax.rem(chip, 2)
+
+
+def meet():
+    core, chip = place()
+    me = core * CHIPS + chip
+    barrier = pltpu.get_barrier_semaphore()
+
+    def greet(ahead, carry):
+        other = lax.rem(me + ahead, 2 * CHIPS)
+        pl.semaphore_signal(
+            barrier,
+            inc=1,
+            device_id=(lax.div(other, CHIPS), lax.rem(other, CHIPS)),
+            device_id_type=MESH,
+        )
+        return carry
+
+    lax.fori_loop(1, 2 * CHIPS, greet, 0)
+    pl.semaphore_wait(barrier, 2 * CHIPS - 1)
+
+
+def remote(source, target, send, recv, device):
+    return pltpu.make_async_remote_copy(
+        src_ref=source,
+        dst_ref=target,
+        send_sem=send,
+        recv_sem=recv,
+        device_id=device,
+        device_id_type=MESH,
+    )
+
+
+def local(source, target, sem):
+    return pltpu.make_async_copy(source, target, sem)
+
+
+def neighbours(across):
+    core, chip = place()
+    z, y, x = coordinates(chip)
+    planes = (z + 1 - 2 * lax.rem(z, 2), 2 - lax.div(z, 2), 3 - 3 * lax.div(z, 2))
+
+    def slot(far_p, far_q, line):
+        far_y, far_x = (far_q, far_p) if across == "x" else (far_p, far_q)
+        plane = z if line is None else planes[line]
+        return plane * 4 + (1 - y if far_y else y) * 2 + (1 - x if far_x else x)
+
+    return slot
+
+
+class Shipments:
+    def __init__(self, send, recv):
+        self.send, self.recv, self.made = send, recv, []
+        self.core = lax.axis_index("grp")
+
+    def ship(self, source, target, recv_index, to):
+        index = len(self.made)
+
+        def make():
+            return remote(
+                source(), target(), self.send.at[index], self.recv.at[recv_index()], (self.core, to())
+            )
+
+        self.made.append(make)
+        make().start()
+
+    def landed(self, target, recv_index, near):
+        remote(target, target, self.send.at[0], self.recv.at[recv_index], (self.core, near)).wait_recv()
+
+    def all_sent(self):
+        assert len(self.made) == 15
+        for make in self.made:
+            make().wait_send()
+
+
+class Gather:
+    def __init__(self, pick, send, recv, across):
+        self.pick, self.at = pick, neighbours(across)
+        self.moves = Shipments(send, recv)
+
+    def ship(self, what, to):
+        slot = lambda: self.at(*what)
+        ref = lambda: self.pick(slot())
+        self.moves.ship(ref, ref, slot, lambda: self.at(*to))
+
+    def landed(self, *what):
+        slot = self.at(*what)
+        self.moves.landed(self.pick(slot), slot, self.at(1, 0, None))
+
+    def own_line(self, line):
+        self.ship((0, 0, None), (0, 0, line))
+
+    def own_plane(self):
+        self.ship((0, 0, None), (1, 0, None))
+        self.ship((0, 0, None), (0, 1, None))
+
+    def line(self, line):
+        self.landed(0, 0, line)
+        self.ship((0, 0, line), (1, 0, None))
+        self.ship((0, 0, line), (0, 1, None))
+
+    def side(self, line):
+        self.landed(1, 0, line)
+        self.ship((1, 0, line), (0, 1, None))
+
+    def arrive(self):
+        for line in (None, 0, 1, 2):
+            for far_p in (0, 1):
+                self.landed(far_p, 1, line)
+
+    def finish(self):
+        self.moves.all_sent()
+
+
+class Reduce:
+    def __init__(self, sent, own, pick, stages, send, recv, across):
+        self.sent, self.own, self.pick, self.at = sent, own, pick, neighbours(across)
+        self.first, self.second, self.third = stages
+        self.moves = Shipments(send, recv)
+
+    @staticmethod
+    def number(line):
+        return 3 if line is None else line
+
+    def ship(self, source, target, index, to):
+        self.moves.ship(source, target, lambda: index, lambda: self.at(*to))
+
+    def landed(self, target, index):
+        self.moves.landed(target, index, self.at(1, 0, None))
+
+    def start(self, line):
+        for far_p in (1, 0):
+            index = self.number(line) * 2 + far_p
+            self.ship(
+                lambda far_p=far_p: self.pick(self.sent, self.at(far_p, 1, line)),
+                lambda index=index: self.first.at[index],
+                index,
+                (0, 1, None),
+            )
+
+    def mine(self, *what):
+        return self.pick(self.own, self.at(*what))[...].astype(HIGH)
+
+    def side(self, line):
+        number = self.number(line)
+        index = number * 2 + 1
+        self.landed(self.first.at[index], index)
+        self.first[index] = (self.first[index].astype(HIGH) + self.mine(1, 0, line)).astype(LOW)
+        self.ship(
+            lambda: self.first.at[index], lambda: self.second.at[number], 8 + number, (1, 0, None)
+        )
+
+    def line(self, line):
+        number = self.number(line)
+        index = number * 2
+        self.landed(self.first.at[index], index)
+        self.landed(self.second.at[number], 8 + number)
+        total = (
+            self.first[index].astype(HIGH)
+            + self.second[number].astype(HIGH)
+            + self.mine(0, 0, line)
+        )
+        if line is None:
+            return total
+        self.first[index] = total.astype(LOW)
+        ahead = lambda: lax.rem(lax.div(self.at(0, 0, None), 4) - lax.div(self.at(0, 0, line), 4) + 4, 4) - 1
+        self.moves.ship(
+            lambda: self.first.at[index],
+            lambda: self.third.at[ahead()],
+            lambda: 12 + ahead(),
+            lambda: self.at(0, 0, line),
+        )
+
+    def finish(self, result):
+        result[...] = self.line(None)
+        for ahead in range(3):
+            self.landed(self.third.at[ahead], 12 + ahead)
+            result[...] += self.third[ahead].astype(HIGH)
+        self.moves.all_sent()
+
+
+def each(plans, act, *arguments):
+    for plan in plans:
+        act(plan, *arguments)
+
+
+def to_tokens(source, target, send, recv):
+    core, chip = place()
+    to_core = lax.div(chip, HALF)
+    mine = core * HALF + lax.rem(chip, HALF)
+    here = to_core == core
+
+    def copy_to(ahead):
+        chip_to = lax.rem(chip + ahead, CHIPS)
+        return remote(
+            source.at[chip_to], target.at[mine], send.at[ahead], recv.at[mine], (to_core, chip_to)
+        )
+
+    pl.when(here)(lambda: local(source.at[chip], target.at[mine], recv.at[mine]).start())
+    pl.when(jnp.logical_not(here))(lambda: copy_to(0).start())
+    for ahead in range(1, CHIPS):
+        copy_to(ahead).start()
+
+    def arrive():
+        for slot in range(CHIPS):
+            local(source.at[slot], target.at[slot], recv.at[slot]).wait()
+
+    def finish():
+        pl.when(jnp.logical_not(here))(lambda: copy_to(0).wait_send())
+        for ahead in range(1, CHIPS):
+            copy_to(ahead).wait_send()
+
+    return arrive, finish
+
+
+def to_heads(source, target, send, recv):
+    core, chip = place()
+    here = lax.div(chip, HALF) == core
+
+    def copy_to(group, ahead):
+        head = lax.rem(chip + ahead, HALF)
+        return remote(
+            source.at[group * HALF + head],
+            target.at[chip],
+            send.at[group * HALF + ahead],
+            recv.at[chip],
+            (group, core * HALF + head),
+        )
+
+    def every(act):
+        for group in range(2):
+            for ahead in range(HALF):
+                if ahead == 0:
+                    itself = jnp.logical_and(here, core == group)
+                    pl.when(jnp.logical_not(itself))(lambda: act(copy_to(group, 0)))
+                else:
+                    act(copy_to(group, ahead))
+
+    pl.when(here)(
+        lambda: local(
+            source.at[core * HALF + lax.rem(chip, HALF)], target.at[chip], recv.at[chip]
+        ).start()
+    )
+    every(lambda copy: copy.start())
+
+    def arrive():
+        for slot in range(CHIPS):
+            local(source.at[slot], target.at[slot], recv.at[slot]).wait()
+
+    return arrive, lambda: every(lambda copy: copy.wait_send())
+
+
+def lanes(rows, width=128):
+    return lax.broadcasted_iota(jnp.int32, (rows, width), 1)
+
+
+def turn(values):
+    return pltpu.roll(values, HD, 1)
+
+
+def fold(rows_in):
+    half = rows_in.shape[0] // 2
+    both = jnp.where(lanes(half) < HD, rows_in[:half], turn(rows_in[half:]))
+    pad = -half % 16
+    if pad:
+        both = jnp.concatenate([both, jnp.zeros((pad, 128), HIGH)], axis=0)
+    return both.astype(LOW)
+
+
+def column_sums(v):
+    return jnp.sum(v, axis=0, keepdims=True)
+
+
+def gelu_parts(pre):
+    cdf = 0.5 * (1.0 + lax.erf(pre * math.sqrt(0.5)))
+    density = jnp.exp(-0.5 * pre * pre) * (1.0 / math.sqrt(2.0 * math.pi))
+    return pre * cdf, cdf + pre * density
+
+
+def normalize(v, gain, shift):
+    center = v - jnp.mean(v, axis=1, keepdims=True)
+    inverse = lax.rsqrt(jnp.mean(center * center, axis=1, keepdims=True) + EPSILON)
+    normed = center * inverse
+    return normed * gain + shift, normed, inverse
+
+
+def normalize_back(c, normed, inverse, gain):
+    scaled = c * gain
+    inner = (
+        scaled
+        - jnp.mean(scaled, axis=1, keepdims=True)
+        - normed * jnp.mean(scaled * normed, axis=1, keepdims=True)
+    )
+    return inner * inverse
+
+
+def at_steps(index, steps):
+    for number, acts in steps.items():
+
+        def run(acts=acts):
+            for act in acts:
+                act()
+
+        pl.when(index == number)(run)
+
+
+def columns_of(half, width):
+    return pl.ds(pl.multiple_of(half * width, 128), width)
+
+
+LABEL_AT, BRANCH_AT, GAIN_AT, SHIFT_AT, BIAS_AT = 0, 256, 384, 512, 640
+
+
+def first_kernel(names, *refs):
+    r = types.SimpleNamespace(**dict(zip(names, refs)))
+    hidden, x_all, w_all, rel_all = r.hidden_in, r.x_vmem, r.w_all, r.rel_all
+    token_rows, width = hidden.shape
+    total = x_all.shape[0]
+    slot_rows = total // CHIPS
+    depth = r.out_weight.shape[0]
+    w_in, w_down, w_out, w_qkv = r.w_in, r.w_down, r.w_out, r.w_qkv
+    half_hidden = w_in.shape[3]
+    half_width = width // 2
+    core, chip = place()
+    other = 1 - core
+    me = core * CHIPS + chip
+    keep = r.keep_sem
+
+    loads = [
+        local(r.ffn_in.at[:, columns_of(core, half_hidden)], w_in.at[core, chip], keep.at[0]),
+        local(r.ffn_out, w_down.at[chip], keep.at[1]),
+        local(r.out_weight, w_out.at[chip], keep.at[2]),
+        local(r.qkv_any.at[:, :, columns_of(core, half_width)], w_qkv.at[:, core, chip], keep.at[3]),
+    ]
+    for copy in loads:
+        copy.start()
+
+    own_slot = pl.ds(pl.multiple_of(chip * slot_rows, 16), slot_rows)
+    extra = r.extra
+    extra[...] = jnp.zeros_like(extra)
+    extra[0:1, 0:256] = jnp.full((1, 256), 4.0, HIGH)
+    extra[0:1, 0:token_rows] = r.segment_ids[...].astype(HIGH)
+    extra[1:2, 0:token_rows] = r.order_ids[...].astype(HIGH)
+    extra[2:4, 0:token_rows] = r.box_ids[...].astype(HIGH)
+    for start, pair in ((BRANCH_AT, r.branch_bias), (GAIN_AT, r.norm_gains), (SHIFT_AT, r.norm_shifts)):
+        extra[0:2, start : start + depth] = pair[...].astype(HIGH)
+    extra[0:1, BIAS_AT : BIAS_AT + 128] = r.ffn_in_bias[...].astype(HIGH)
+    tail = token_rows - token_rows % 16
+    x_own = r.x_own
+    x_own[0:tail, :] = hidden[0:tail, :]
+    x_own[tail:slot_rows, :] = jnp.concatenate(
+        [hidden[tail:token_rows, :].astype(HIGH), extra[...]], axis=0
+    ).astype(LOW)
+    weight = r.qkv_weight
+    w_own = r.w_own
+    lane_depth = lanes(depth) < HD
+    for pair in range(H // 2):
+        columns = slice(pair * 128, pair * 128 + 128)
+        query, key, value = (weight[n, :, columns].astype(HIGH) for n in range(3))
+        w_own[2 * pair, :, 0:128] = jnp.where(lane_depth, query, turn(value)).astype(LOW)
+        w_own[2 * pair + 1, :, 0:128] = jnp.where(lane_depth, turn(query), value).astype(LOW)
+        w_own[2 * pair, :, 128:256] = jnp.where(lane_depth, key, 0.0).astype(LOW)
+        w_own[2 * pair + 1, :, 128:256] = jnp.where(lane_depth, turn(key), 0.0).astype(LOW)
+    rel_own = r.rel_own
+    eye_depth = (
+        lax.broadcasted_iota(jnp.int32, (depth, depth), 0)
+        == lax.broadcasted_iota(jnp.int32, (depth, depth), 1)
+    ).astype(LOW)
+    for kind in range(3):
+        rel_own[:, kind * NB : (kind + 1) * NB] = dot(eye_depth, r.rel_tables[kind], NT).astype(LOW)
+    bias_columns = dot(eye_depth, r.qkv_bias[...], NT)
+    rel_own[:, 3 * NB : 4 * NB] = jnp.where(
+        lanes(depth) == 0, bias_columns[:, 0:1], jnp.where(lanes(depth) == 1, bias_columns[:, 1:2], 0.0)
+    ).astype(LOW)
+    own_x = local(x_own, x_all.at[own_slot], keep.at[4])
+    own_w = local(w_own.at[chip], w_all.at[me], keep.at[5])
+    own_x.start()
+    own_w.start()
+    meet()
+
+    to_chip = lax.div(me, 2)
+    parity = lax.rem(chip, 2)
+    rel_slot = rel_all.at[pl.ds(parity * depth, depth)]
+
+    def rel_each(act_remote, act_own):
+        for to_core in range(2):
+            itself = jnp.logical_and(to_chip == chip, core == to_core)
+            copy = lambda: remote(
+                rel_own, rel_slot, r.rel_send.at[to_core], r.rel_recv.at[parity], (to_core, to_chip)
+            )
+            pl.when(jnp.logical_not(itself))(lambda: act_remote(copy()))
+            if act_own is not None:
+                pl.when(itself)(act_own)
+
+    rel_each(
+        lambda copy: copy.start(), lambda: local(rel_own, rel_slot, r.rel_recv.at[parity]).start()
+    )
+
+    def w_copy(ahead):
+        to = lax.rem(chip + ahead, CHIPS)
+        return remote(
+            w_own.at[to], w_all.at[me], r.w_send.at[ahead], r.w_recv.at[chip], (core, to)
+        )
+
+    half = width // 2
+
+    def pick_x(part):
+        return lambda slot: x_all.at[
+            pl.ds(pl.multiple_of(slot * slot_rows, 16), slot_rows), pl.ds(part * half, half)
+        ]
+
+    x_plans = [
+        Gather(pick_x(part), r.x_send.at[part], r.x_recv.at[part], across)
+        for part, across in enumerate("xy")
+    ]
+
+    own_x.wait()
+    each(x_plans, Gather.own_line, 0)
+    each(x_plans, Gather.own_plane)
+    for ahead in range(1, CHIPS):
+        w_copy(ahead).start()
+    each(x_plans, Gather.own_line, 1)
+    each(x_plans, Gather.own_line, 2)
+    swaps = [
+        remote(
+            r.ffn_in.at[:, columns_of(other, half_hidden)],
+            w_in.at[core, chip],
+            r.pair_send.at[0],
+            r.pair_recv.at[0],
+            (other, chip),
+        ),
+        remote(
+            r.qkv_any.at[:, :, columns_of(other, half_width)],
+            w_qkv.at[:, core, chip],
+            r.pair_send.at[1],
+            r.pair_recv.at[1],
+            (other, chip),
+        ),
+    ]
+    for copy in swaps:
+        copy.start()
+    each(x_plans, Gather.side, None)
+    for line in range(3):
+        each(x_plans, Gather.line, line)
+        each(x_plans, Gather.side, line)
+
+    plan_out = Gather(lambda slot: w_out.at[slot], r.out_send, r.out_recv, "x")
+    plan_in = Gather(lambda slot: w_in.at[:, slot], r.in_send, r.in_recv, "x")
+    plan_down = Gather(lambda slot: w_down.at[slot], r.down_send, r.down_recv, "y")
+    plan_qkv = Gather(lambda slot: w_qkv.at[:, :, slot], r.qkv_send, r.qkv_recv, "y")
+    plans = (plan_out, plan_in, plan_down)
+    for copy in loads:
+        copy.wait()
+    for copy in swaps:
+        copy.wait()
+    each(plans, Gather.own_line, 0)
+    each(plans, Gather.own_plane)
+    each(plans, Gather.own_line, 1)
+    each(plans, Gather.own_line, 2)
+
+    own_w.wait()
+    for ahead in range(1, CHIPS):
+        came = lax.rem(chip + ahead, CHIPS)
+        remote(
+            w_own.at[0], w_all.at[core * CHIPS + came], r.w_send.at[0], r.w_recv.at[came], (core, came)
+        ).wait_recv()
+    mine = w_all.at[pl.ds(core * CHIPS, CHIPS)]
+    pair_w = remote(mine, mine, r.pair_send.at[2], r.pair_recv.at[2], (other, chip))
+    pair_w.start()
+    for slot in range(2):
+        local(rel_own, rel_all.at[pl.ds(slot * depth, depth)], r.rel_recv.at[slot]).wait()
+    each(x_plans, Gather.arrive)
+    keep_x = local(x_all, r.x_out, keep.at[6])
+    keep_x.start()
+    keep_rel = local(rel_all, r.rel_out, keep.at[7])
+    keep_rel.start()
+
+    meta, shares, bias_in = r.meta, r.shares, r.bias_in
+    eye = (
+        lax.broadcasted_iota(jnp.int32, (slot_rows, 256), 0)
+        == lax.broadcasted_iota(jnp.int32, (slot_rows, 256), 1)
+    ).astype(LOW)
+    shares[core] = jnp.zeros(shares.shape[1:], HIGH)
+    for slot in range(CHIPS):
+        end = (slot + 1) * slot_rows
+        labels = x_all[end - 16 : end, 0:256]
+        meta[end - slot_rows : end, 0:16] = dot(eye, labels, NT)
+        small = x_all[end - 16 : end, BRANCH_AT:768].astype(HIGH)[8:16]
+        target = slice(slot * depth // 128 * 128, slot * depth // 128 * 128 + 128)
+        for number in range(3):
+            piece = jnp.where(lanes(8) < depth, small[:, number * 128 : number * 128 + 128], 0.0)
+            if slot * depth % 128:
+                piece = pltpu.roll(piece, slot * depth % 128, 1)
+            shares[core, number, :, target] += piece
+        bias_in[:, slot * 128 : slot * 128 + 128] = small[0:1, 384:512]
+    pair_small = remote(
+        shares.at[core], shares.at[core], r.pair_send.at[3], r.pair_recv.at[3], (other, chip)
+    )
+    pair_small.start()
+    rel = rel_all[...]
+    table_t = rel[:, 0 : 3 * NB]
+    extra_columns = rel[:, 3 * NB : 4 * NB].astype(HIGH)
+    row_at = lax.broadcasted_iota(jnp.int32, (2 * depth, 128), 0)
+    column_at = lanes(2 * depth)
+    bias = column_sums(
+        jnp.where(row_at == column_at, extra_columns[:, 0:1], 0.0)
+        + jnp.where(row_at + 2 * depth == column_at, extra_columns[:, 1:2], 0.0)
+    )
+    lane = lanes(BLOCK)
+    first_half = lane < HD
+    scale = 1.0 / math.sqrt(4.0 * HD)
+    left, right, right_t = r.left, r.right, r.right_t
+    value, value_t, kept = r.value, r.value_t, r.kept
+    pair_w.wait()
+
+    def prepare(index, carry):
+        rows = pl.ds(pl.multiple_of(index * BLOCK, BLOCK), BLOCK)
+        at_steps(
+            index,
+            {
+                3: [lambda: each(plans, Gather.side, None)],
+                7: [lambda: each(plans, Gather.line, 0)],
+            },
+        )
+        projected = dot(x_all[rows, :], w_all[...].reshape(width, 4 * HD))
+        query_value = (projected[:, 0:128] + bias).astype(LOW).astype(HIGH)
+        key = projected[:, 128:256].astype(LOW).astype(HIGH)
+        query = query_value[:, 0:HD].astype(LOW)
+        tables = dot(query, table_t).astype(LOW).astype(HIGH)
+        ids = meta[rows, 8:12].astype(jnp.int32)
+        segment, order, box_x, box_y = ids[:, 0:1], ids[:, 1:2], ids[:, 2:3], ids[:, 3:4]
+
+        def selected(column, ids_of, values):
+            bucket = jnp.clip(ids_of - values, -(NB // 2), NB // 2 - 1) + NB // 2
+            return jnp.take_along_axis(tables[:, column * NB : (column + 1) * NB], bucket, axis=1)
+
+        wide = selected(0, order, lane)
+        narrow = jnp.where(first_half, selected(1, box_x, lane), selected(2, box_y, lane - HD))
+        label = lane - HD
+        query_side = jnp.where(
+            first_half,
+            query_value * scale,
+            jnp.where(jnp.logical_and(label != segment, label < 8), MASKED, 0.0),
+        )
+        key_side = jnp.where(first_half, key, (label == segment).astype(HIGH))
+        left[rows, 0:128] = (wide * scale).astype(LOW)
+        left[rows, 128:256] = (narrow * scale).astype(LOW)
+        left[rows, 256:384] = query_side.astype(LOW)
+        order_hot = (lane == order).astype(HIGH)
+        box_hot = (jnp.where(first_half, box_x, box_y + HD) == lane).astype(HIGH)
+        right[rows, 0:128] = order_hot.astype(LOW)
+        right[rows, 128:256] = box_hot.astype(LOW)
+        right[rows, 256:384] = key_side.astype(LOW)
+        right_t[0:128, rows] = order_hot.T.astype(LOW)
+        right_t[128:256, rows] = box_hot.T.astype(LOW)
+        right_t[256:384, rows] = key_side.T.astype(LOW)
+        held = jnp.where(first_half, turn(query_value), (label == 0).astype(HIGH))
+        value[rows, :] = held.astype(LOW)
+        value_t[:, rows] = held.T.astype(LOW)
+        return carry
+
+    lax.fori_loop(0, total // BLOCK, prepare, 0)
+    stash = [
+        local(held, out, keep.at[8 + k])
+        for k, (held, out) in enumerate(
+            (
+                (left, r.left_out),
+                (right, r.right_out),
+                (right_t, r.right_t_out),
+                (value_t, r.value_t_out),
+            )
+        )
+    ]
+    for copy in stash:
+        copy.start()
+
+    def attend(index, carry):
+        rows = pl.ds(pl.multiple_of(index * BLOCK, BLOCK), BLOCK)
+        at_steps(
+            index,
+            {
+                1: [lambda: each(plans, Gather.side, 0)],
+                4: [lambda: each(plans, Gather.line, 1)],
+                7: [lambda: each(plans, Gather.side, 1)],
+            },
+        )
+        logits = dot(left[rows, :], right_t[...])
+        top = jnp.max(logits, axis=1, keepdims=True)
+        weights = jnp.exp(logits - top).astype(LOW)
+        mixed = dot(weights, value[...])
+        row_sum = mixed[:, HD : HD + 1]
+        ids = meta[rows, 8:12]
+        facts = jnp.where(lane == HD, top + jnp.log(row_sum), ids[:, 3:4])
+        facts = jnp.where(lane == HD + 1, ids[:, 1:2], facts)
+        facts = jnp.where(lane == HD + 2, ids[:, 2:3], facts)
+        kept[rows, :] = jnp.where(first_half, mixed / row_sum, facts)
+        return carry
+
+    lax.fori_loop(0, total // BLOCK, attend, 0)
+    keep_facts = local(kept, r.kept_out, keep.at[12])
+    keep_facts.start()
+    message, context_in = r.message, r.context_in
+    for slot in range(CHIPS):
+        message[slot] = fold(kept[slot * slot_rows : (slot + 1) * slot_rows, :])
+    context_arrives, context_sent = to_tokens(message, context_in, r.msg_send, r.msg_recv)
+    each(plans, Gather.line, 2)
+    each(plans, Gather.side, 2)
+    plan_qkv.own_line(0)
+    plan_qkv.own_plane()
+    plan_qkv.own_line(1)
+    plan_qkv.own_line(2)
+    context_arrives()
+    pair_small.wait()
+
+    vectors = [
+        [jnp.concatenate([shares[0, number, k : k + 1], shares[1, number, k : k + 1]], axis=1) for k in range(2)]
+        for number in range(3)
+    ]
+    branch_bias, gains, shifts = vectors
+    context_wide, context, low_first = r.context_wide, r.context, r.low_first
+    act, slope, d_second, d_inner, d_branch = r.act, r.slope, r.d_second, r.d_inner, r.d_branch
+    out_part, in_part, g_small = r.out_part, r.in_part, r.g_small
+    own = pl.ds(pl.multiple_of(core * slot_rows, 16), slot_rows)
+    far = pl.ds(pl.multiple_of(other * slot_rows, 16), slot_rows)
+    tile = 512
+    half_slot = slot_rows // 2
+    count = [4]
+
+    def swap(source, target):
+        copy = remote(
+            source, target, r.pair_send.at[count[0]], r.pair_recv.at[count[0]], (other, chip)
+        )
+        count[0] += 1
+        copy.start()
+        return copy
+
+    left_half = lanes(half_slot) < HD
+    for group in range(2):
+        for pair in range(HALF // 2):
+            even = context_in[group * HALF + 2 * pair].astype(HIGH)[:half_slot]
+            odd = context_in[group * HALF + 2 * pair + 1].astype(HIGH)[:half_slot]
+            top = group * slot_rows
+            columns = slice(pair * 128, pair * 128 + 128)
+            context_wide[top : top + half_slot, columns] = jnp.where(left_half, even, turn(odd))
+            context_wide[top + half_slot : top + slot_rows, columns] = jnp.where(
+                left_half, turn(even), odd
+            )
+    context[...] = context_wide[...].astype(LOW)
+
+    def product(index, lhs, rhs):
+        out_part[index] = dot(lhs[far, :], rhs)
+        copy = swap(out_part.at[index], in_part.at[index])
+        mine = dot(lhs[own, :], rhs)
+        copy.wait()
+        return mine + in_part[index]
+
+    plan_out.arrive()
+    branch = product(0, context, w_out[...].reshape(half_width, width)) + branch_bias[0]
+    row_index = lax.broadcasted_iota(jnp.int32, (slot_rows, 1), 0)
+    tokens = row_index < token_rows
+    x_mine = jnp.where(tokens, x_own[...].astype(HIGH), 0.0)
+    first, normed1, inverse1 = normalize(x_mine + branch, gains[0], shifts[0])
+    low_first[own, :] = first.astype(LOW)
+    copy = swap(low_first.at[own], low_first.at[own])
+    plan_qkv.side(None)
+    plan_in.arrive()
+    copy.wait()
+
+    def widen(index, carry):
+        columns = pl.ds(pl.multiple_of(index * tile, tile), tile)
+        pre = dot(low_first[...], w_in[:, :, :, columns].reshape(width, tile)) + bias_in[:, columns]
+        found, derivative = gelu_parts(pre)
+        act[:, columns] = found.astype(LOW)
+        slope[:, columns] = derivative
+        return carry
+
+    lax.fori_loop(0, half_hidden // tile, widen, 0)
+    plan_down.arrive()
+    second = product(1, act, w_down[...].reshape(half_hidden, width)) + branch_bias[1]
+    plan_qkv.line(0)
+    plan_qkv.side(0)
+    result, normed2, inverse2 = normalize(first + second, gains[1], shifts[1])
+    r.hidden_out[...] = result[:token_rows].astype(LOW)
+    given = r.out_grad
+    upstream = jnp.concatenate(
+        [given[...].astype(HIGH), jnp.zeros((slot_rows - token_rows, width), HIGH)], axis=0
+    )
+    d_sum2 = normalize_back(upstream, normed2, inverse2, gains[1])
+    low_second = d_sum2.astype(LOW)
+    d_second[own, :] = low_second
+    copy = swap(d_second.at[own], d_second.at[own])
+    g_small[...] = jnp.zeros_like(g_small)
+    g_small[1:2, 0:width] = column_sums(low_second.astype(HIGH))
+    g_small[3:4, 0:width] = column_sums(upstream * normed2)
+    g_small[5:6, 0:width] = column_sums(upstream)
+    plan_qkv.line(1)
+    plan_qkv.side(1)
+    copy.wait()
+    g_down, g_in, g_out = r.g_down, r.g_in, r.g_out
+
+    def narrow_back(index, carry):
+        columns = pl.ds(pl.multiple_of(index * tile, tile), tile)
+        down = w_down[pl.ds(index * (tile // 128), tile // 128)].reshape(tile, width)
+        low = (dot(d_second[...], down, NT) * slope[:, columns]).astype(LOW)
+        d_inner[:, columns] = low
+        g_small[pl.ds(8, 1), columns] = column_sums(low.astype(HIGH))
+        g_down[columns, :] = dot(act[:, columns], d_second[...], TN).astype(LOW)
+        return carry
+
+    lax.fori_loop(0, half_hidden // tile, narrow_back, 0)
+    keep_down = local(g_down, r.g_down_out, keep.at[13])
+    keep_down.start()
+    plan_qkv.line(2)
+    plan_qkv.side(2)
+    w_in_all = w_in[...].reshape(width, half_hidden)
+    out_part[2] = dot(d_inner[far, :], w_in_all, NT)
+    copy = swap(out_part.at[2], in_part.at[2])
+    mine = dot(d_inner[own, :], w_in_all, NT)
+
+    def widen_grad(index, carry):
+        rows = pl.ds(pl.multiple_of(index * 256, 256), 256)
+        g_in[rows, :] = dot(low_first[:, rows], d_inner[...], TN).astype(LOW)
+        return carry
+
+    lax.fori_loop(0, width // 256, widen_grad, 0)
+    keep_in = local(g_in, r.g_in_out, keep.at[14])
+    keep_in.start()
+    copy.wait()
+    d_first = d_sum2 + mine + in_part[2]
+    d_sum1 = normalize_back(d_first, normed1, inverse1, gains[0])
+    r.d_sum1[...] = d_sum1
+    low_branch = d_sum1.astype(LOW)
+    d_branch[own, :] = low_branch
+    copy = swap(d_branch.at[own], d_branch.at[own])
+    g_small[0:1, 0:width] = column_sums(low_branch.astype(HIGH))
+    g_small[2:3, 0:width] = column_sums(d_first * normed1)
+    g_small[4:5, 0:width] = column_sums(d_first)
+    copy.wait()
+    w_out_all = w_out[...].reshape(half_width, width)
+    context_wide[...] = dot(d_branch[...], w_out_all, NT)
+    for group in range(2):
+        for pair in range(HALF // 2):
+            both = context_wide[
+                group * slot_rows : (group + 1) * slot_rows, pair * 128 : pair * 128 + 128
+            ]
+            r.d_message[group * HALF + 2 * pair] = fold(both)
+            r.d_message[group * HALF + 2 * pair + 1] = fold(turn(both))
+    g_out[...] = dot(context[...], d_branch[...], TN).astype(LOW)
+    plan_qkv.arrive()
+    keep_qkv = local(w_qkv, r.w_qkv_out, keep.at[15])
+    keep_qkv.start()
+
+    for ahead in range(1, CHIPS):
+        w_copy(ahead).wait_send()
+    rel_each(lambda copy: copy.wait_send(), None)
+    context_sent()
+    each(x_plans, Gather.finish)
+    each(plans + (plan_qkv,), Gather.finish)
+    for copy in stash + [keep_x, keep_rel, keep_facts, keep_down, keep_in, keep_qkv]:
+        copy.wait()
+
+
+def second_kernel(names, *refs):
+    r = types.SimpleNamespace(**dict(zip(names, refs)))
+    core, chip = place()
+    other = 1 - core
+    left, right, right_t, value_t, kept = r.left, r.right, r.right_t, r.value_t, r.kept
+    rel_all, x_all, w_qkv = r.rel_all, r.x_all, r.w_qkv
+    g_in, g_down, g_out = r.g_in, r.g_down, r.g_out
+    total, width = x_all.shape
+    slot_rows = total // CHIPS
+    half_slot = slot_rows // 2
+    half_width = width // 2
+    depth = w_qkv.shape[3]
+    token_rows = r.hidden_grad.shape[0]
+    scale = 1.0 / math.sqrt(4.0 * HD)
+    keep = r.keep_sem
+    loads = [
+        local(there, held, keep.at[k])
+        for k, (there, held) in enumerate(
+            (
+                (r.left_any, left),
+                (r.right_t_any, right_t),
+                (r.value_t_any, value_t),
+                (r.kept_any, kept),
+                (r.right_any, right),
+                (r.g_down_any, g_down),
+                (r.g_in_any, g_in),
+                (r.g_out_any, g_out),
+                (r.x_all_any, x_all),
+                (r.w_qkv_any, w_qkv),
+            )
+        )
+    ]
+    for copy in loads:
+        copy.start()
+    meet()
+    d_arrived = r.d_arrived
+    grad_arrives, grad_sent = to_heads(r.d_message, d_arrived, r.d_send, r.d_recv)
+    plan_down = Reduce(
+        r.g_down_any,
+        g_down,
+        lambda ref, slot: ref.at[slot],
+        [r.down_1, r.down_2, r.down_3],
+        r.down_send,
+        r.down_recv,
+        "y",
+    )
+    plan_in = Reduce(
+        r.g_in_any,
+        g_in,
+        lambda ref, slot: ref.at[:, slot],
+        [r.in_1, r.in_2, r.in_3],
+        r.in_send,
+        r.in_recv,
+        "x",
+    )
+    plan_out = Reduce(
+        r.g_out_any,
+        g_out,
+        lambda ref, slot: ref.at[slot],
+        [r.out_1, r.out_2, r.out_3],
+        r.out_send,
+        r.out_recv,
+        "y",
+    )
+    plans = (plan_down, plan_in, plan_out)
+
+    each(plans, Reduce.start, 2)
+    each(plans, Reduce.start, 1)
+
+    z, y, x = coordinates(chip)
+    small_sum, small_in = r.small_sum, r.small_in
+    small_sum[...] = r.g_small[...]
+
+    def small_copy(index, to_core, to_chip):
+        return remote(
+            small_sum, small_in.at[index], r.small_send.at[index], r.small_recv.at[index], (to_core, to_chip)
+        )
+
+    def small_turn(index):
+        if index == 0:
+            return [small_copy(0, other, chip)]
+        if index == 1:
+            return [small_copy(1, core, z * 4 + (1 - y) * 2 + x)]
+        if index == 2:
+            return [small_copy(2, core, z * 4 + y * 2 + 1 - x)]
+        return [
+            small_copy(2 + ahead, core, lax.rem(z + ahead, 4) * 4 + y * 2 + x) for ahead in (1, 2, 3)
+        ]
+
+    def small_start(index):
+        for copy in small_turn(index):
+            copy.start()
+
+    def small_end(index):
+        for copy in small_turn(index):
+            copy.wait()
+        if index == 0:
+            small_sum[0:8, :] += small_in[0, 0:8, :]
+        elif index < 3:
+            small_sum[...] += small_in[index]
+
+    small_start(0)
+    left_half = lanes(half_slot) < HD
+    d_context = r.d_context
+    grad_arrives()
+    for slot in range(CHIPS):
+        both = d_arrived[slot].astype(HIGH)[:half_slot]
+        top = slot * slot_rows
+        d_context[top : top + half_slot, :] = jnp.where(left_half, both, 0.0)
+        d_context[top + half_slot : top + slot_rows, :] = jnp.where(left_half, turn(both), 0.0)
+    table_t = rel_all[:, 0 : 3 * NB]
+    lane = lanes(BLOCK)
+    first_half = lane < HD
+    d_query, d_query_t, d_pair_t, rel_grad = r.d_query, r.d_query_t, r.d_pair_t, r.rel_grad
+    d_pair_t[...] = jnp.zeros_like(d_pair_t)
+    rel_grad[...] = jnp.zeros_like(rel_grad)
+    for copy in loads:
+        copy.wait()
+
+    def step(index, carry):
+        rows = pl.ds(pl.multiple_of(index * BLOCK, BLOCK), BLOCK)
+        at_steps(
+            index,
+            {
+                1: [
+                    lambda: each(plans, Reduce.side, 2),
+                    lambda: each(plans, Reduce.start, 0),
+                    lambda: small_end(0),
+                    lambda: small_start(1),
+                ],
+                2: [lambda: each(plans, Reduce.line, 2)],
+                4: [
+                    lambda: each(plans, Reduce.side, 1),
+                    lambda: each(plans, Reduce.start, None),
+                    lambda: small_end(1),
+                    lambda: small_start(2),
+                ],
+                5: [lambda: each(plans, Reduce.line, 1)],
+                7: [lambda: each(plans, Reduce.side, 0), lambda: small_end(2), lambda: small_start(3)],
+                8: [lambda: each(plans, Reduce.line, 0)],
+            },
+        )
+        facts = kept[rows, :]
+        grad = d_context[rows, :]
+        delta = jnp.sum(grad * facts, axis=1, keepdims=True)
+        probs = jnp.exp(dot(left[rows, :], right_t[...]) - facts[:, HD : HD + 1])
+        d_probs = dot(grad.astype(LOW), value_t[...])
+        d_logits = (probs * (d_probs - delta)).astype(LOW)
+        query_t = jnp.where(first_half, left[rows, 256:384].astype(HIGH), 0.0).T[0:HD]
+        d_pair_t[0:HD, :] += dot(grad.T[0:HD].astype(LOW), probs.astype(LOW))
+        d_pair_t[HD : 2 * HD, :] += dot(query_t.astype(LOW), d_logits)
+        back = dot(d_logits, right[...]) * scale
+        ids = facts.astype(jnp.int32)
+        order, box_x, box_y = (ids[:, HD + k : HD + k + 1] for k in (1, 2, 3))
+
+        def placed(column, ids_of, extent, start):
+            found_at = ids_of + NB // 2 - lane
+            found = jnp.take_along_axis(
+                back[:, column * 128 : column * 128 + 128], jnp.clip(found_at, 0, extent - 1) + start, axis=1
+            )
+            return jnp.where(jnp.logical_and(found_at >= 0, found_at < extent), found, 0.0)
+
+        wide = back[:, 0:128]
+        low_end = jnp.sum(jnp.where(lane >= order + NB // 2, wide, 0.0), axis=1, keepdims=True)
+        high_end = jnp.sum(jnp.where(lane <= order - (NB // 2 - 1), wide, 0.0), axis=1, keepdims=True)
+        first = placed(0, order, ORDER_RANGE, 0)
+        first = jnp.where(lane == 0, low_end, jnp.where(lane == NB - 1, high_end, first))
+        d_tables = jnp.concatenate(
+            [first, placed(1, box_x, BOX_RANGE, 0), placed(1, box_y, BOX_RANGE, BOX_RANGE)], axis=1
+        ).astype(LOW)
+        from_tables = dot(d_tables, table_t, NT)
+        d_query[rows, :] = jnp.where(
+            first_half,
+            back[:, 256:384] + jnp.concatenate([from_tables, from_tables], axis=1),
+            0.0,
+        )
+        d_query_t[0:HD, rows] = d_query[rows, :].T[0:HD].astype(LOW)
+        rel_grad[:, 0 : 3 * NB] += dot((query_t / scale).astype(LOW), d_tables)
+        return carry
+
+    lax.fori_loop(0, total // BLOCK, step, 0)
+    message = r.message
+    slot_lane = lanes(slot_rows) < HD
+    for slot in range(CHIPS):
+        top = slot * slot_rows
+        if slot % 8 == 0:
+            turned = d_pair_t[:, top : top + 8 * slot_rows].T
+        pair = turned[(slot % 8) * slot_rows : (slot % 8 + 1) * slot_rows]
+        message[slot, 0:slot_rows, :] = jnp.where(
+            slot_lane, d_query[top : top + slot_rows, :], pair
+        ).astype(LOW)
+        message[slot, slot_rows:, :] = fold(pair)
+    tokens_in = r.tokens_in
+    tokens_arrive, tokens_sent = to_tokens(message, tokens_in, r.msg_send, r.msg_recv)
+    each(plans, Reduce.side, None)
+
+    d_query_t[HD : 3 * HD, :] = d_pair_t[...].astype(LOW)
+    d_columns = d_query_t[...]
+    sums = jnp.sum(d_columns[0 : 2 * HD].astype(HIGH), axis=1, keepdims=True)
+    rel_grad[:, 3 * NB : 4 * NB] = jnp.where(
+        lanes(HD) == 0, sums[0:HD], jnp.where(lanes(HD) == 1, sums[HD : 2 * HD], 0.0)
+    )
+    rel_far, rel_sum = r.rel_far, r.rel_sum
+    rel_rows = pl.ds(pl.multiple_of(other * depth, 8), depth)
+    rel_pair = remote(
+        rel_grad.at[rel_rows], rel_far, r.pair_send.at[0], r.pair_recv.at[0], (other, chip)
+    )
+    rel_pair.start()
+    w_mine, w_far, w_low, w_came = r.w_mine, r.w_far, r.w_low, r.w_came
+    w_grad = dot(d_columns, x_all[...])
+    for part in range(2):
+        w_mine[part] = w_grad[:, part * half_width : (part + 1) * half_width]
+    w_pair = remote(
+        w_mine.at[other], w_far, r.pair_send.at[1], r.pair_recv.at[1], (other, chip)
+    )
+    w_pair.start()
+    rel_pair.wait()
+    rel_sum[...] = rel_grad[pl.ds(pl.multiple_of(core * depth, 8), depth), :] + rel_far[...]
+    rel_to = (lax.div(chip, HALF), lax.rem(2 * chip + core, CHIPS))
+    rel_here = jnp.logical_and(rel_to[0] == core, rel_to[1] == chip)
+    rel_came = r.rel_came
+    rel_copy = lambda: remote(rel_sum, rel_came, r.rel_send.at[0], r.rel_recv.at[0], rel_to)
+    own_rel = lambda: local(rel_sum, rel_came, r.rel_recv.at[0])
+    pl.when(rel_here)(lambda: own_rel().start())
+    pl.when(jnp.logical_not(rel_here))(lambda: rel_copy().start())
+    w_pair.wait()
+    w_sum = (w_mine[core] + w_far[...]).T
+    w_low[...] = jnp.zeros_like(w_low)
+    for slot in range(CHIPS):
+        w_low[slot, :, 0 : 3 * HD] = w_sum[slot * depth : (slot + 1) * depth].astype(LOW)
+
+    def w_copy(ahead):
+        to = lax.rem(chip + ahead, CHIPS)
+        return remote(w_low.at[to], w_came.at[chip], r.w_send.at[ahead], r.w_recv.at[chip], (core, to))
+
+    own_w = local(w_low.at[chip], w_came.at[chip], keep.at[10])
+    own_w.start()
+    for ahead in range(1, CHIPS):
+        w_copy(ahead).start()
+
+    wide, low = r.wide, r.low
+    tokens_arrive()
+    for group in range(2):
+        top = group * slot_rows
+        for pair in range(HALF // 2):
+            columns = slice(pair * 128, pair * 128 + 128)
+            even = tokens_in[group * HALF + 2 * pair].astype(HIGH)
+            odd = tokens_in[group * HALF + 2 * pair + 1].astype(HIGH)
+            even_main, odd_main = even[:slot_rows], odd[:slot_rows]
+            low[0, top : top + slot_rows, columns] = jnp.where(
+                slot_lane, even_main, turn(odd_main)
+            ).astype(LOW)
+            low[1, top : top + slot_rows, columns] = jnp.where(
+                slot_lane, turn(even_main), odd_main
+            ).astype(LOW)
+            even_last = even[slot_rows : slot_rows + half_slot]
+            odd_last = odd[slot_rows : slot_rows + half_slot]
+            wide[top : top + half_slot, columns] = jnp.where(left_half, even_last, turn(odd_last))
+            wide[top + half_slot : top + slot_rows, columns] = jnp.where(
+                left_half, turn(even_last), odd_last
+            )
+    low[2] = wide[...].astype(LOW)
+    own = pl.ds(pl.multiple_of(core * slot_rows, 16), slot_rows)
+    far = pl.ds(pl.multiple_of(other * slot_rows, 16), slot_rows)
+    weights = [w_qkv[n].reshape(width, half_width) for n in range(3)]
+
+    def part(rows):
+        return (
+            dot(low[0, rows, :], weights[0], NT)
+            + dot(low[1, rows, :], weights[1], NT)
+            + dot(low[2, rows, :], weights[2], NT)
+        )
+
+    out_part, in_part = r.out_part, r.in_part
+    out_part[...] = part(far)
+    x_pair = remote(out_part, in_part, r.pair_send.at[2], r.pair_recv.at[2], (other, chip))
+    x_pair.start()
+    mine = part(own) + r.d_sum1[...]
+    x_pair.wait()
+    r.hidden_grad[...] = (mine + in_part[...])[:token_rows].astype(LOW)
+
+    plan_down.finish(r.down_grad)
+    in_total, in_far = r.in_total, r.in_far
+    plan_in.finish(in_total)
+    in_pair = remote(
+        in_total.at[other], in_far, r.pair_send.at[3], r.pair_recv.at[3], (other, chip)
+    )
+    in_pair.start()
+    plan_out.finish(r.out_grad)
+    half_hidden = in_total.shape[2]
+    in_grad = r.in_grad
+    in_grad[:, columns_of(core, half_hidden)] = in_total[core]
+    small_end(3)
+    me = core * CHIPS + chip
+    small_all = lambda rows, columns: (
+        small_sum[rows, columns] + small_in[3, rows, columns] + small_in[4, rows, columns] + small_in[5, rows, columns]
+    )
+    strip = columns_of(lax.div(me * depth, 128), 128)
+    shares = pltpu.roll(small_all(pl.ds(0, 8), strip), 128 - lax.rem(me * depth, 128), 1)
+    for number, result in enumerate((r.branch_grad, r.gain_grad, r.shift_grad)):
+        result[...] = shares[2 * number : 2 * number + 2, 0:depth]
+    r.bias_grad[...] = small_all(pl.ds(8, 1), columns_of(chip, 128))
+    own_rel().wait()
+    pl.when(jnp.logical_not(rel_here))(lambda: rel_copy().wait_send())
+    tables = rel_came[...].T
+    for kind in range(3):
+        r.rel_tables_grad[kind] = tables[kind * NB : (kind + 1) * NB]
+    r.qkv_bias_grad[...] = tables[3 * NB : 3 * NB + 2]
+    own_w.wait()
+    for ahead in range(1, CHIPS):
+        came = lax.rem(chip + ahead, CHIPS)
+        remote(w_low.at[0], w_came.at[came], r.w_send.at[0], r.w_recv.at[came], (core, came)).wait_recv()
+        w_copy(ahead).wait_send()
+    lane_depth = lanes(depth) < HD
+    for pair in range(H // 2):
+        columns = slice(pair * 128, pair * 128 + 128)
+        even = w_came[2 * pair].astype(HIGH)
+        odd = w_came[2 * pair + 1].astype(HIGH)
+        w_out = r.qkv_grad
+        w_out[0, :, columns] = jnp.where(lane_depth, even[:, 0:128], turn(odd[:, 0:128]))
+        w_out[2, :, columns] = jnp.where(lane_depth, turn(even[:, 0:128]), odd[:, 0:128])
+        w_out[1, :, columns] = jnp.where(lane_depth, even[:, 128:256], turn(odd[:, 128:256]))
+    in_pair.wait()
+    in_grad[:, columns_of(other, half_hidden)] = in_far[...]
+    grad_sent()
+    tokens_sent()
+
+
+def call(kernel, name, number, inputs, outputs, scratch):
+    names = list(inputs) + list(outputs) + list(scratch)
+    results = pl.pallas_call(
+        functools.partial(kernel, names),
+        out_shape=[jax.ShapeDtypeStruct(shape, dtype) for shape, dtype, _ in outputs.values()],
+        in_specs=[pl.BlockSpec(memory_space=space) for _, space in inputs.values()],
+        out_specs=[pl.BlockSpec(memory_space=space) for _, _, space in outputs.values()],
+        scratch_shapes=list(scratch.values()),
+        compiler_params=pltpu.CompilerParams(
+            collective_id=number, has_side_effects=True, vmem_limit_bytes=VMEM_LIMIT
+        ),
+        name=name,
+    )(*(array for array, _ in inputs.values()))
+    return types.SimpleNamespace(**dict(zip(outputs, results)))
+
+
+def head_shards(
+    hidden_in,
+    segment_ids,
+    order_ids,
+    box_ids,
+    qkv_weight,
+    qkv_bias,
+    rel_tables,
+    out_weight,
+    branch_bias,
+    norm_gains,
+    norm_shifts,
+    ffn_in,
+    ffn_in_bias,
+    ffn_out,
+    out_grad,
+):
+    rows, width = hidden_in.shape
+    slot_rows = -(-rows // 16) * 16
+    total = CHIPS * slot_rows
+    depth = qkv_weight.shape[1]
+    hidden = ffn_in.shape[1]
+    half_hidden, half_width = hidden // 2, width // 2
+    down_rows = ffn_out.shape[0]
+    both = 2 * slot_rows
+    fold_rows = -(-(slot_rows // 2) // 16) * 16
+    any_, vmem, dma = pl.ANY, pltpu.VMEM, pltpu.SemaphoreType.DMA
+    message = (CHIPS, fold_rows, 128)
+    made = call(
+        first_kernel,
+        "forward_and_feed_forward",
+        0,
+        dict(
+            hidden_in=(hidden_in, vmem),
+            segment_ids=(segment_ids.reshape(1, rows), vmem),
+            order_ids=(order_ids.reshape(1, rows), vmem),
+            box_ids=(box_ids, vmem),
+            qkv_weight=(qkv_weight, vmem),
+            qkv_any=(qkv_weight, any_),
+            qkv_bias=(qkv_bias, vmem),
+            rel_tables=(rel_tables, vmem),
+            out_weight=(out_weight, any_),
+            branch_bias=(branch_bias, vmem),
+            norm_gains=(norm_gains, vmem),
+            norm_shifts=(norm_shifts, vmem),
+            ffn_in=(ffn_in, any_),
+            ffn_in_bias=(ffn_in_bias.reshape(1, down_rows), vmem),
+            ffn_out=(ffn_out, any_),
+            out_grad=(out_grad, vmem),
+        ),
+        dict(
+            hidden_out=((rows, width), LOW, vmem),
+            x_out=((total, width), LOW, any_),
+            rel_out=((2 * depth, 4 * NB), LOW, any_),
+            left_out=((total, 384), LOW, any_),
+            right_out=((total, 384), LOW, any_),
+            right_t_out=((384, total), LOW, any_),
+            value_t_out=((128, total), LOW, any_),
+            kept_out=((total, 128), HIGH, any_),
+            g_down_out=((half_hidden, width), LOW, any_),
+            g_in_out=((width, half_hidden), LOW, any_),
+            g_out=((half_width, width), LOW, vmem),
+            g_small=((16, half_hidden), HIGH, vmem),
+            d_sum1=((slot_rows, width), HIGH, vmem),
+            d_message=(message, LOW, vmem),
+            w_qkv_out=((3, 2, CHIPS, depth, half_width), LOW, any_),
+        ),
+        dict(
+            x_own=vmem((slot_rows, width), LOW),
+            x_vmem=vmem((total, width), LOW),
+            extra=vmem((slot_rows - rows, width), HIGH),
+            w_own=vmem((H, depth, 4 * HD), LOW),
+            w_all=vmem((2 * CHIPS, depth, 4 * HD), LOW),
+            rel_own=vmem((depth, 4 * NB), LOW),
+            rel_all=vmem((2 * depth, 4 * NB), LOW),
+            w_in=vmem((2, CHIPS, depth, half_hidden), LOW),
+            w_down=vmem((CHIPS, down_rows, width), LOW),
+            w_out=vmem((CHIPS, depth, width), LOW),
+            w_qkv=vmem((3, 2, CHIPS, depth, half_width), LOW),
+            meta=vmem((total, 128), HIGH),
+            shares=vmem((2, 3, 8, half_width), HIGH),
+            bias_in=vmem((1, half_hidden), HIGH),
+            left=vmem((total, 384), LOW),
+            right=vmem((total, 384), LOW),
+            right_t=vmem((384, total), LOW),
+            value=vmem((total, 128), LOW),
+            value_t=vmem((128, total), LOW),
+            kept=vmem((total, 128), HIGH),
+            message=vmem(message, LOW),
+            context_in=vmem(message, LOW),
+            context_wide=vmem((both, half_width), HIGH),
+            context=vmem((both, half_width), LOW),
+            low_first=vmem((both, width), LOW),
+            act=vmem((both, half_hidden), LOW),
+            slope=vmem((both, half_hidden), HIGH),
+            d_second=vmem((both, width), LOW),
+            d_inner=vmem((both, half_hidden), LOW),
+            d_branch=vmem((both, width), LOW),
+            g_down=vmem((half_hidden, width), LOW),
+            g_in=vmem((width, half_hidden), LOW),
+            out_part=vmem((3, slot_rows, width), HIGH),
+            in_part=vmem((3, slot_rows, width), HIGH),
+            keep_sem=dma((16,)),
+            x_send=dma((2, 16)),
+            x_recv=dma((2, 16)),
+            w_send=dma((16,)),
+            w_recv=dma((16,)),
+            rel_send=dma((2,)),
+            rel_recv=dma((2,)),
+            out_send=dma((16,)),
+            out_recv=dma((16,)),
+            in_send=dma((16,)),
+            in_recv=dma((16,)),
+            down_send=dma((16,)),
+            down_recv=dma((16,)),
+            qkv_send=dma((16,)),
+            qkv_recv=dma((16,)),
+            msg_send=dma((16,)),
+            msg_recv=dma((16,)),
+            pair_send=dma((10,)),
+            pair_recv=dma((10,)),
+        ),
+    )
+    g_down = made.g_down_out.reshape(CHIPS, down_rows, width)
+    g_in = made.g_in_out.reshape(2, CHIPS, depth, half_hidden)
+    g_out = made.g_out.reshape(CHIPS, depth, width)
+    out_message = (CHIPS, slot_rows + fold_rows, 128)
+    in_block, down_block, out_block = (2, depth, half_hidden), (down_rows, width), (depth, width)
+    ended = call(
+        second_kernel,
+        "backward_and_sums",
+        1,
+        dict(
+            left_any=(made.left_out, any_),
+            right_any=(made.right_out, any_),
+            right_t_any=(made.right_t_out, any_),
+            value_t_any=(made.value_t_out, any_),
+            kept_any=(made.kept_out, any_),
+            rel_all=(made.rel_out, vmem),
+            x_all_any=(made.x_out, any_),
+            w_qkv_any=(made.w_qkv_out, any_),
+            g_down_any=(g_down, any_),
+            g_in_any=(g_in, any_),
+            g_out_any=(g_out, any_),
+            g_small=(made.g_small, vmem),
+            d_sum1=(made.d_sum1, vmem),
+            d_message=(made.d_message, vmem),
+        ),
+        dict(
+            hidden_grad=((rows, width), LOW, vmem),
+            qkv_grad=((3, depth, width), HIGH, vmem),
+            qkv_bias_grad=((2, depth), HIGH, vmem),
+            rel_tables_grad=((3, NB, depth), HIGH, vmem),
+            out_grad=((depth, width), HIGH, vmem),
+            branch_grad=((2, depth), HIGH, vmem),
+            gain_grad=((2, depth), HIGH, vmem),
+            shift_grad=((2, depth), HIGH, vmem),
+            in_grad=((depth, hidden), HIGH, vmem),
+            bias_grad=((1, down_rows), HIGH, vmem),
+            down_grad=((down_rows, width), HIGH, vmem),
+        ),
+        dict(
+            left=vmem((total, 384), LOW),
+            right=vmem((total, 384), LOW),
+            right_t=vmem((384, total), LOW),
+            value_t=vmem((128, total), LOW),
+            kept=vmem((total, 128), HIGH),
+            x_all=vmem((total, width), LOW),
+            w_qkv=vmem((3, 2, CHIPS, depth, half_width), LOW),
+            g_down=vmem((CHIPS,) + down_block, LOW),
+            g_in=vmem((2, CHIPS, depth, half_hidden), LOW),
+            g_out=vmem((CHIPS,) + out_block, LOW),
+            in_1=vmem((8,) + in_block, LOW),
+            in_2=vmem((4,) + in_block, LOW),
+            in_3=vmem((3,) + in_block, LOW),
+            down_1=vmem((8,) + down_block, LOW),
+            down_2=vmem((4,) + down_block, LOW),
+            down_3=vmem((3,) + down_block, LOW),
+            out_1=vmem((8,) + out_block, LOW),
+            out_2=vmem((4,) + out_block, LOW),
+            out_3=vmem((3,) + out_block, LOW),
+            in_total=vmem(in_block, HIGH),
+            in_far=vmem((depth, half_hidden), HIGH),
+            small_sum=vmem((16, half_hidden), HIGH),
+            small_in=vmem((6, 16, half_hidden), HIGH),
+            d_arrived=vmem(message, LOW),
+            d_context=vmem((total, 128), HIGH),
+            d_query=vmem((total, 128), HIGH),
+            d_query_t=vmem((3 * HD, total), LOW),
+            d_pair_t=vmem((2 * HD, total), HIGH),
+            rel_grad=vmem((2 * depth, 4 * NB), HIGH),
+            rel_far=vmem((depth, 4 * NB), HIGH),
+            rel_sum=vmem((depth, 4 * NB), HIGH),
+            rel_came=vmem((depth, 4 * NB), HIGH),
+            message=vmem(out_message, LOW),
+            tokens_in=vmem(out_message, LOW),
+            w_mine=vmem((2, 3 * HD, half_width), HIGH),
+            w_far=vmem((3 * HD, half_width), HIGH),
+            w_low=vmem((CHIPS, depth, 4 * HD), LOW),
+            w_came=vmem((CHIPS, depth, 4 * HD), LOW),
+            wide=vmem((both, half_width), HIGH),
+            low=vmem((3, both, half_width), LOW),
+            out_part=vmem((slot_rows, width), HIGH),
+            in_part=vmem((slot_rows, width), HIGH),
+            keep_sem=dma((11,)),
+            d_send=dma((16,)),
+            d_recv=dma((16,)),
+            in_send=dma((16,)),
+            in_recv=dma((16,)),
+            down_send=dma((16,)),
+            down_recv=dma((16,)),
+            out_send=dma((16,)),
+            out_recv=dma((16,)),
+            small_send=dma((6,)),
+            small_recv=dma((6,)),
+            msg_send=dma((16,)),
+            msg_recv=dma((16,)),
+            w_send=dma((16,)),
+            w_recv=dma((16,)),
+            rel_send=dma((1,)),
+            rel_recv=dma((1,)),
+            pair_send=dma((4,)),
+            pair_recv=dma((4,)),
+        ),
+    )
+    return (
+        made.hidden_out,
+        ended.hidden_grad,
+        ended.qkv_grad,
+        ended.qkv_bias_grad,
+        ended.rel_tables_grad,
+        ended.out_grad,
+        ended.branch_grad,
+        ended.gain_grad,
+        ended.shift_grad,
+        ended.in_grad,
+        ended.bias_grad.reshape(down_rows),
+        ended.down_grad,
+    )
+
+
 def solution(mesh):
+    by_heads = mesh.shape["grp"] == 2 and mesh.shape["blk"] == CHIPS == H
     return jax.shard_map(
-        shards,
+        head_shards if by_heads else shards,
         mesh=mesh,
         in_specs=(
             P(("grp", "blk"), None),

time: 3220 us -> 338 us (0.10)
  waiting for transfers between devices: 2050 us -> 0 us
  blocking collectives: 476 us -> 0 us
  matrix products: 338 us -> 0 us
  Pallas kernels: 0 us -> 319 us
  local copies, waits for them, and re-layouts: 199 us -> 17 us
  other arithmetic: 130 us -> 0 us
    reduce_scatter x4 -> x0, waiting for transfers between devices: 1010 us -> none  [the longest x1 363 us: shards(): lax.psum_scatter(grad_w_down, ('grp', 'blk'), scatter_dimension=0, tiled=...]
    unnamed x20 -> x0, waiting for transfers between devices: 720 us -> none
    all_gather x7 -> x0, blocking collectives: 433 us -> none  [the longest x1 79.8 us: shards(): lax.all_gather(rel_tables, ('grp', 'blk'), axis=2, tiled=True)]
    dot_general x145 -> x0, matrix products: 338 us -> none  [the longest x20 56.1 us: block_logits(): jnp.einsum('thd,khd->htk', query_heads, key_heads, preferred_element_type...]
    pallas_call x0 -> x2, Pallas kernels: none -> 319 us  [call(): pl.pallas_call(functools.partial(kernel, names), out_shape=[jax.ShapeDtyp...]
    ppermute x64 -> x0, waiting for transfers between devices: 242 us -> none  [shifted(): lax.ppermute(x, axis, [(i, (i + by) % devices) for i in range(devices)])]
    while x261 -> x0, local copies, waits for them, and re-layouts: 93.3 us -> none
    convert_element_type x58 -> x0, other arithmetic: 80.6 us -> none  [the longest x16 42.6 us: cycle_turn(): carried.astype(jnp.bfloat16)]
  transfers between devices with their start and end apart: 79 -> 0, of which waited for: 26 -> 0; matrix products, arithmetic and copies ran while one was open for 17% -> 0% of each run, Pallas kernels for 0% -> 0%
where the time goes in v2:
time: 338 us; the launch traced here: 337 us
  Pallas kernels  319 us (94%)
  local copies, waits for them, and re-layouts  17 us (5%)
    pallas_call x2, Pallas kernels, call(): pl.pallas_call(functools.partial(kernel, names), out_shape=[jax.ShapeDtyp...  319 us
    unnamed x19, local copies, waits for them, and re-layouts  17 us

profile of v2, /device:TPU:1, one launch (start us, length us, event | category | flops | bytes accessed | tf_op | source)
XLA Modules:
  0.0 336.7 jit_solution(17601218811480440101)
XLA Ops:
  0.6 1.5 copy.27.refs_7_
  2.1 189.3 %forward_and_feed_forward.1 = (bf16[136,1024]{1,0:T(8,128)(2,1)}, bf16[2304,1024]{1,0:T(8,128)(2,1)}, bf16[64,512]{1,0:T(8,128)(2,1)}, bf16[2304,384]{1,0:T(8,12...) custom-call(bf16[136,1024]{1,0:T(8,128)(2,1)} %refs_0_.1, ...), custom_call_target="tpu_custom_call" | custom-call | tf_op jit(solution)/shard_map/forward_and_feed_forward/pallas_call | solution.py:1487
  191.5 0.0 copy-start.1
  191.5 129.8 %backward_and_sums.1 = (bf16[136,1024]{1,0:T(8,128)(2,1)}, f32[3,32,1024]{2,1,0:T(8,128)}, f32[2,32]{1,0:T(2,128)}, f32[3,128,32]{2,1,0:T(8,128)}, f32[32,1024]{...) custom-call(bf16[2304,384]{1,0:T(8,128)(2,1)} %get-tuple-element.39., ...), custom_call_target="tpu_custom_call" | custom-call | tf_op jit(solution)/shard_map/backward_and_sums/pallas_call | solution.py:1487
  321.2 0.0 copy-start.2
  321.2 0.0 copy-start
  321.3 1.7 copy.28
  323.0 0.0 copy-done.1
  323.0 0.7 copy.40
  323.7 1.7 copy.41
  325.4 1.8 copy.42
  327.1 1.2 copy.43
  328.3 1.6 copy.44
  329.9 1.2 copy.45
  331.1 1.2 copy.46
  332.4 1.2 copy.47
  333.6 1.9 copy.48
  335.4 0.0 copy-done.2
  335.4 0.5 copy.49
  335.9 0.0 copy-done
  335.9 0.8 copy.50
Async XLA Ops:
  191.5 131.5 %copy-start.1 = (bf16[136,1024]{1,0:T(8,128)(2,1)S(1)}, bf16[136,1024]{1,0:T(8,128)(2,1)}, u32[]{:S(2)}) copy-start(bf16[136,1024]{1,0:T(8,128)(2,1)} %get-tuple-element.88) | copy-start | bytes 835588
  321.2 14.2 %copy-start.2 = (f32[1,128]{1,0:T(1,128)S(1)}, f32[1,128]{1,0:T(1,128)}, u32[]{:S(2)}) copy-start(f32[1,128]{1,0:T(1,128)} %get-tuple-element.62) | copy-start | bytes 1540
  321.2 14.7 %copy-start = (f32[128,1024]{1,0:T(8,128)S(1)}, f32[128,1024]{1,0:T(8,128)}, u32[]{:S(2)}) copy-start(f32[128,1024]{1,0:T(8,128)} %get-tuple-element.99) | copy-start | bytes 1572868

commit v3 on v2

--- a/solution.py
+++ b/solution.py
@@ -506,10 +506,32 @@
         self.moves.all_sent()
 
 
+class GatherLate(Gather):
+    def first(self):
+        self.ship((0, 0, None), (1, 0, None))
+        self.ship((0, 0, None), (0, 1, None))
+
+    def second(self):
+        self.landed(1, 0, None)
+        self.ship((1, 0, None), (0, 1, None))
+
+    def third(self):
+        for far_p in (0, 1):
+            self.landed(far_p, 1, None)
+        for line in range(3):
+            for what in ((0, 0), (1, 0), (0, 1), (1, 1)):
+                self.ship(what + (None,), (0, 0, line))
+
+    def arrive(self):
+        for line in range(3):
+            for what in ((0, 0), (1, 0), (0, 1), (1, 1)):
+                self.landed(*what, line)
+
+
 class Reduce:
     def __init__(self, sent, own, pick, stages, send, recv, across):
         self.sent, self.own, self.pick, self.at = sent, own, pick, neighbours(across)
-        self.first, self.second, self.third = stages
+        self.first, self.second, self.third_in = stages
         self.moves = Shipments(send, recv)
 
     @staticmethod
@@ -560,7 +582,7 @@
         ahead = lambda: lax.rem(lax.div(self.at(0, 0, None), 4) - lax.div(self.at(0, 0, line), 4) + 4, 4) - 1
         self.moves.ship(
             lambda: self.first.at[index],
-            lambda: self.third.at[ahead()],
+            lambda: self.third_in.at[ahead()],
             lambda: 12 + ahead(),
             lambda: self.at(0, 0, line),
         )
@@ -568,8 +590,57 @@
     def finish(self, result):
         result[...] = self.line(None)
         for ahead in range(3):
-            self.landed(self.third.at[ahead], 12 + ahead)
-            result[...] += self.third[ahead].astype(HIGH)
+            self.landed(self.third_in.at[ahead], 12 + ahead)
+            result[...] += self.third_in[ahead].astype(HIGH)
+        self.moves.all_sent()
+
+
+class ReduceEarly(Reduce):
+    PLANE = ((0, 0), (1, 0), (0, 1), (1, 1))
+
+    def ahead(self, line):
+        return lax.rem(lax.div(self.at(0, 0, None), 4) - lax.div(self.at(0, 0, line), 4) + 4, 4) - 1
+
+    def start(self):
+        for line in (2, 1, 0):
+            for number, what in enumerate(self.PLANE):
+                index = lambda number=number, line=line: self.ahead(line) * 4 + number
+                self.moves.ship(
+                    lambda what=what, line=line: self.pick(self.sent, self.at(*what, line)),
+                    lambda index=index: self.first.at[index()],
+                    index,
+                    lambda line=line: self.at(0, 0, line),
+                )
+
+    def plane_sum(self, number):
+        total = self.mine(*self.PLANE[number], None)
+        for ahead in range(3):
+            index = ahead * 4 + number
+            self.landed(self.first.at[index], index)
+            total += self.first[index].astype(HIGH)
+        return total
+
+    def third(self):
+        for number, far_p in ((3, 1), (2, 0)):
+            self.first[number] = self.plane_sum(number).astype(LOW)
+            self.ship(
+                lambda number=number: self.first.at[number],
+                lambda far_p=far_p: self.second.at[far_p],
+                12 + far_p,
+                (0, 1, None),
+            )
+
+    def across(self):
+        total = self.plane_sum(1)
+        self.landed(self.second.at[1], 13)
+        self.first[1] = (total + self.second[1].astype(HIGH)).astype(LOW)
+        self.ship(lambda: self.first.at[1], lambda: self.third_in.at[0], 14, (1, 0, None))
+
+    def finish(self, result):
+        total = self.plane_sum(0)
+        self.landed(self.second.at[0], 12)
+        self.landed(self.third_in.at[0], 14)
+        result[...] = total + self.second[0].astype(HIGH) + self.third_in[0].astype(HIGH)
         self.moves.all_sent()
 
 
@@ -761,7 +832,7 @@
         == lax.broadcasted_iota(jnp.int32, (depth, depth), 1)
     ).astype(LOW)
     for kind in range(3):
-        rel_own[:, kind * NB : (kind + 1) * NB] = dot(eye_depth, r.rel_tables[kind], NT).astype(LOW)
+        rel_own[:, kind * NB : (kind + 1) * NB] = r.rel_tables[kind]
     bias_columns = dot(eye_depth, r.qkv_bias[...], NT)
     rel_own[:, 3 * NB : 4 * NB] = jnp.where(
         lanes(depth) == 0, bias_columns[:, 0:1], jnp.where(lanes(depth) == 1, bias_columns[:, 1:2], 0.0)
@@ -838,19 +909,29 @@
         each(x_plans, Gather.line, line)
         each(x_plans, Gather.side, line)
 
-    plan_out = Gather(lambda slot: w_out.at[slot], r.out_send, r.out_recv, "x")
-    plan_in = Gather(lambda slot: w_in.at[:, slot], r.in_send, r.in_recv, "x")
-    plan_down = Gather(lambda slot: w_down.at[slot], r.down_send, r.down_recv, "y")
+    half_tile = half_hidden // 2
+    plan_out = GatherLate(lambda slot: w_out.at[slot], r.out_send, r.out_recv, "x")
     plan_qkv = Gather(lambda slot: w_qkv.at[:, :, slot], r.qkv_send, r.qkv_recv, "y")
-    plans = (plan_out, plan_in, plan_down)
+
+    def halves(ref, wide, sends, recvs):
+        return [
+            Gather(
+                lambda slot, part=part: ref(slot, pl.ds(part * wide, wide)), sends.at[part], recvs.at[part], across
+            )
+            for part, across in enumerate("xy")
+        ]
+
+    plans_in = halves(lambda slot, columns: w_in.at[:, slot, :, columns], half_tile, r.in_send, r.in_recv)
+    plans_down = halves(lambda slot, columns: w_down.at[slot, :, columns], half, r.down_send, r.down_recv)
     for copy in loads:
         copy.wait()
     for copy in swaps:
         copy.wait()
-    each(plans, Gather.own_line, 0)
-    each(plans, Gather.own_plane)
-    each(plans, Gather.own_line, 1)
-    each(plans, Gather.own_line, 2)
+    each(plans_in, Gather.own_line, 0)
+    each(plans_in, Gather.own_plane)
+    plan_out.first()
+    each(plans_in, Gather.own_line, 1)
+    each(plans_in, Gather.own_line, 2)
 
     own_w.wait()
     for ahead in range(1, CHIPS):
@@ -912,8 +993,18 @@
         at_steps(
             index,
             {
-                3: [lambda: each(plans, Gather.side, None)],
-                7: [lambda: each(plans, Gather.line, 0)],
+                1: [
+                    lambda: each(plans_in, Gather.side, None),
+                    plan_out.second,
+                    lambda: each(plans_down, Gather.own_line, 0),
+                    lambda: each(plans_down, Gather.own_plane),
+                ],
+                4: [lambda: each(plans_in, Gather.line, 0), plan_out.third],
+                7: [
+                    lambda: each(plans_in, Gather.side, 0),
+                    lambda: each(plans_down, Gather.own_line, 1),
+                    lambda: each(plans_down, Gather.own_line, 2),
+                ],
             },
         )
         projected = dot(x_all[rows, :], w_all[...].reshape(width, 4 * HD))
@@ -973,9 +1064,9 @@
         at_steps(
             index,
             {
-                1: [lambda: each(plans, Gather.side, 0)],
-                4: [lambda: each(plans, Gather.line, 1)],
-                7: [lambda: each(plans, Gather.side, 1)],
+                0: [lambda: each(plans_in, Gather.line, 1), lambda: each(plans_down, Gather.side, None)],
+                3: [lambda: each(plans_in, Gather.side, 1)],
+                6: [lambda: each(plans_in, Gather.line, 2), lambda: each(plans_down, Gather.line, 0)],
             },
         )
         logits = dot(left[rows, :], right_t[...])
@@ -997,12 +1088,10 @@
     for slot in range(CHIPS):
         message[slot] = fold(kept[slot * slot_rows : (slot + 1) * slot_rows, :])
     context_arrives, context_sent = to_tokens(message, context_in, r.msg_send, r.msg_recv)
-    each(plans, Gather.line, 2)
-    each(plans, Gather.side, 2)
-    plan_qkv.own_line(0)
-    plan_qkv.own_plane()
-    plan_qkv.own_line(1)
-    plan_qkv.own_line(2)
+    each(plans_in, Gather.side, 2)
+    each(plans_down, Gather.side, 0)
+    each(plans_down, Gather.line, 1)
+    each(plans_down, Gather.side, 1)
     context_arrives()
     pair_small.wait()
 
@@ -1056,8 +1145,13 @@
     first, normed1, inverse1 = normalize(x_mine + branch, gains[0], shifts[0])
     low_first[own, :] = first.astype(LOW)
     copy = swap(low_first.at[own], low_first.at[own])
-    plan_qkv.side(None)
-    plan_in.arrive()
+    each(plans_down, Gather.line, 2)
+    each(plans_down, Gather.side, 2)
+    plan_qkv.own_line(0)
+    plan_qkv.own_plane()
+    plan_qkv.own_line(1)
+    plan_qkv.own_line(2)
+    each(plans_in, Gather.arrive)
     copy.wait()
 
     def widen(index, carry):
@@ -1069,7 +1163,8 @@
         return carry
 
     lax.fori_loop(0, half_hidden // tile, widen, 0)
-    plan_down.arrive()
+    plan_qkv.side(None)
+    each(plans_down, Gather.arrive)
     second = product(1, act, w_down[...].reshape(half_hidden, width)) + branch_bias[1]
     plan_qkv.line(0)
     plan_qkv.side(0)
@@ -1149,7 +1244,7 @@
     rel_each(lambda copy: copy.wait_send(), None)
     context_sent()
     each(x_plans, Gather.finish)
-    each(plans + (plan_qkv,), Gather.finish)
+    each(plans_in + plans_down + [plan_out, plan_qkv], Gather.finish)
     for copy in stash + [keep_x, keep_rel, keep_facts, keep_down, keep_in, keep_qkv]:
         copy.wait()
 
@@ -1209,7 +1304,7 @@
         r.in_recv,
         "x",
     )
-    plan_out = Reduce(
+    plan_out = ReduceEarly(
         r.g_out_any,
         g_out,
         lambda ref, slot: ref.at[slot],
@@ -1218,7 +1313,8 @@
         r.out_recv,
         "y",
     )
-    plans = (plan_down, plan_in, plan_out)
+    plans = (plan_down, plan_in)
+    plan_out.start()
 
     each(plans, Reduce.start, 2)
     each(plans, Reduce.start, 1)
@@ -1284,14 +1380,14 @@
                     lambda: small_end(0),
                     lambda: small_start(1),
                 ],
-                2: [lambda: each(plans, Reduce.line, 2)],
+                2: [lambda: each(plans, Reduce.line, 2), plan_out.third],
                 4: [
                     lambda: each(plans, Reduce.side, 1),
                     lambda: each(plans, Reduce.start, None),
                     lambda: small_end(1),
                     lambda: small_start(2),
                 ],
-                5: [lambda: each(plans, Reduce.line, 1)],
+                5: [lambda: each(plans, Reduce.line, 1), plan_out.across],
                 7: [lambda: each(plans, Reduce.side, 0), lambda: small_end(2), lambda: small_start(3)],
                 8: [lambda: each(plans, Reduce.line, 0)],
             },
@@ -1458,10 +1554,9 @@
     r.bias_grad[...] = small_all(pl.ds(8, 1), columns_of(chip, 128))
     own_rel().wait()
     pl.when(jnp.logical_not(rel_here))(lambda: rel_copy().wait_send())
-    tables = rel_came[...].T
     for kind in range(3):
-        r.rel_tables_grad[kind] = tables[kind * NB : (kind + 1) * NB]
-    r.qkv_bias_grad[...] = tables[3 * NB : 3 * NB + 2]
+        r.rel_tables_grad[kind] = rel_came[:, kind * NB : (kind + 1) * NB]
+    r.qkv_bias_grad[...] = rel_came[:, 3 * NB : 4 * NB].T[0:2]
     own_w.wait()
     for ahead in range(1, CHIPS):
         came = lax.rem(chip + ahead, CHIPS)
@@ -1480,6 +1575,19 @@
     in_grad[:, columns_of(other, half_hidden)] = in_far[...]
     grad_sent()
     tokens_sent()
+
+
+def hand_over(count, *refs):
+    for source, target in zip(refs[:count], refs[count:]):
+        target[...] = source[...]
+
+
+def handed_over(arrays):
+    return pl.pallas_call(
+        functools.partial(hand_over, len(arrays)),
+        out_shape=[jax.ShapeDtypeStruct(array.shape, array.dtype) for array in arrays],
+        name="hand_over",
+    )(*arrays)
 
 
 def call(kernel, name, number, inputs, outputs, scratch):
@@ -1538,7 +1646,7 @@
             qkv_weight=(qkv_weight, vmem),
             qkv_any=(qkv_weight, any_),
             qkv_bias=(qkv_bias, vmem),
-            rel_tables=(rel_tables, vmem),
+            rel_tables=(rel_tables.transpose(0, 2, 1), vmem),
             out_weight=(out_weight, any_),
             branch_bias=(branch_bias, vmem),
             norm_gains=(norm_gains, vmem),
@@ -1609,10 +1717,10 @@
             rel_recv=dma((2,)),
             out_send=dma((16,)),
             out_recv=dma((16,)),
-            in_send=dma((16,)),
-            in_recv=dma((16,)),
-            down_send=dma((16,)),
-            down_recv=dma((16,)),
+            in_send=dma((2, 16)),
+            in_recv=dma((2, 16)),
+            down_send=dma((2, 16)),
+            down_recv=dma((2, 16)),
             qkv_send=dma((16,)),
             qkv_recv=dma((16,)),
             msg_send=dma((16,)),
@@ -1650,7 +1758,7 @@
             hidden_grad=((rows, width), LOW, vmem),
             qkv_grad=((3, depth, width), HIGH, vmem),
             qkv_bias_grad=((2, depth), HIGH, vmem),
-            rel_tables_grad=((3, NB, depth), HIGH, vmem),
+            rel_tables_grad=((3, depth, NB), HIGH, vmem),
             out_grad=((depth, width), HIGH, vmem),
             branch_grad=((2, depth), HIGH, vmem),
             gain_grad=((2, depth), HIGH, vmem),
@@ -1676,9 +1784,9 @@
             down_1=vmem((8,) + down_block, LOW),
             down_2=vmem((4,) + down_block, LOW),
             down_3=vmem((3,) + down_block, LOW),
-            out_1=vmem((8,) + out_block, LOW),
-            out_2=vmem((4,) + out_block, LOW),
-            out_3=vmem((3,) + out_block, LOW),
+            out_1=vmem((12,) + out_block, LOW),
+            out_2=vmem((2,) + out_block, LOW),
+            out_3=vmem((1,) + out_block, LOW),
             in_total=vmem(in_block, HIGH),
             in_far=vmem((depth, half_hidden), HIGH),
             small_sum=vmem((16, half_hidden), HIGH),
@@ -1723,20 +1831,25 @@
             pair_recv=dma((4,)),
         ),
     )
-    return (
-        made.hidden_out,
-        ended.hidden_grad,
-        ended.qkv_grad,
-        ended.qkv_bias_grad,
-        ended.rel_tables_grad,
-        ended.out_grad,
-        ended.branch_grad,
-        ended.gain_grad,
-        ended.shift_grad,
-        ended.in_grad,
-        ended.bias_grad.reshape(down_rows),
-        ended.down_grad,
-    )
+    results = list(handed_over(
+        [
+            made.hidden_out,
+            ended.hidden_grad,
+            ended.qkv_grad,
+            ended.qkv_bias_grad,
+            ended.rel_tables_grad,
+            ended.out_grad,
+            ended.branch_grad,
+            ended.gain_grad,
+            ended.shift_grad,
+            ended.in_grad,
+            ended.bias_grad,
+            ended.down_grad,
+        ]
+    ))
+    results[4] = results[4].transpose(0, 2, 1)
+    results[10] = results[10].reshape(down_rows)
+    return tuple(results)
 
 
 def solution(mesh):

time: 338 us -> 318 us (0.941)
  local copies, waits for them, and re-layouts: 17 us -> 0 us
    unnamed x19 -> x0, local copies, waits for them, and re-layouts: 17 us -> none
    pallas_call x2, Pallas kernels: 319 us -> 314 us  [call(): pl.pallas_call(functools.partial(kernel, names), out_shape=[jax.ShapeDtyp...]
where the time goes in v3:
time: 318 us; the launch traced here: 317 us
  Pallas kernels  317 us (100%)
    pallas_call x2, Pallas kernels, call(): pl.pallas_call(functools.partial(kernel, names), out_shape=[jax.ShapeDtyp...  314 us

profile of v3, /device:TPU:1, one launch (start us, length us, event | category | flops | bytes accessed | tf_op | source)
XLA Modules:
  0.0 317.2 jit_solution(5633202115376350560)
XLA Ops:
  0.7 188.7 %forward_and_feed_forward.1 = (bf16[136,1024]{1,0:T(8,128)(2,1)}, bf16[2304,1024]{1,0:T(8,128)(2,1)}, bf16[64,512]{1,0:T(8,128)(2,1)}, bf16[2304,384]{1,0:T(8,12...) custom-call(bf16[136,1024]{1,0:T(8,128)(2,1)} %refs_0_.1, ...), custom_call_target="tpu_custom_call" | custom-call | tf_op jit(solution)/shard_map/forward_and_feed_forward/pallas_call | solution.py:1595
  189.3 124.9 %backward_and_sums.1 = (bf16[136,1024]{1,0:T(8,128)(2,1)}, f32[3,32,1024]{2,1,0:T(8,128)}, f32[2,32]{1,0:T(2,128)}, f32[3,32,128]{2,1,0:T(8,128)}, f32[32,1024]{...) custom-call(bf16[2304,384]{1,0:T(8,128)(2,1)} %get-tuple-element.51., ...), custom_call_target="tpu_custom_call" | custom-call | tf_op jit(solution)/shard_map/backward_and_sums/pallas_call | solution.py:1595
  314.2 3.0 hand_over.1

commit v4 on v3

--- a/solution.py
+++ b/solution.py
@@ -461,8 +461,8 @@
     def landed(self, target, recv_index, near):
         remote(target, target, self.send.at[0], self.recv.at[recv_index], (self.core, near)).wait_recv()
 
-    def all_sent(self):
-        assert len(self.made) == 15
+    def all_sent(self, count=15):
+        assert len(self.made) == count
         for make in self.made:
             make().wait_send()
 
@@ -644,15 +644,106 @@
         self.moves.all_sent()
 
 
+def cube_of(order):
+    core, chip = place()
+    z, y, x = coordinates(chip)
+
+    def at(*flips):
+        far = dict(zip(order, flips))
+        plane = z + 1 - 2 * lax.rem(z, 2) if far["z"] else z
+        return plane * 4 + (1 - y if far["y"] else y) * 2 + (1 - x if far["x"] else x)
+
+    return at
+
+
+class CubeGather:
+    def __init__(self, pick, send, recv, order):
+        self.pick, self.at = pick, cube_of(order)
+        self.moves = Shipments(send, recv)
+
+    def ship(self, what, to):
+        slot = lambda: lax.rem(self.at(*what), HALF)
+        ref = lambda: self.pick(slot())
+        self.moves.ship(ref, ref, slot, lambda: self.at(*to))
+
+    def landed(self, *what):
+        slot = lax.rem(self.at(*what), HALF)
+        self.moves.landed(self.pick(slot), slot, self.at(1, 0, 0))
+
+    def own(self):
+        for to in ((1, 0, 0), (0, 1, 0), (0, 0, 1)):
+            self.ship((0, 0, 0), to)
+
+    def one(self):
+        self.landed(1, 0, 0)
+        self.ship((1, 0, 0), (0, 1, 0))
+        self.ship((1, 0, 0), (0, 0, 1))
+
+    def two(self):
+        for what in ((0, 1, 0), (1, 1, 0)):
+            self.landed(*what)
+            self.ship(what, (0, 0, 1))
+
+    def arrive(self):
+        for what in ((0, 0, 1), (1, 0, 1), (0, 1, 1), (1, 1, 1)):
+            self.landed(*what)
+
+    def finish(self):
+        self.moves.all_sent(7)
+
+
+class CubeReduce:
+    def __init__(self, pick, stage, send, recv, order):
+        self.pick, self.stage, self.at = pick, stage, cube_of(order)
+        self.moves = Shipments(send, recv)
+
+    def ship(self, source, index, to):
+        self.moves.ship(source, lambda: self.stage.at[index], lambda: index, lambda: self.at(*to))
+
+    def mine(self, *what):
+        return self.pick(lax.rem(self.at(*what), HALF))
+
+    def term(self, index):
+        self.moves.landed(self.stage.at[index], index, self.at(1, 0, 0))
+        return self.stage[index].astype(HIGH)
+
+    def own(self):
+        for index, (one, two) in enumerate(((1, 1), (0, 1), (1, 0), (0, 0))):
+            self.ship(lambda one=one, two=two: self.mine(one, two, 1), index, (0, 0, 1))
+
+    def one(self):
+        for index, one in ((0, 1), (1, 0)):
+            total = self.mine(one, 1, 0)[...].astype(HIGH) + self.term(index)
+            self.stage[index] = total.astype(LOW)
+            self.ship(lambda index=index: self.stage.at[index], 4 + index, (0, 1, 0))
+
+    def two(self):
+        total = self.mine(1, 0, 0)[...].astype(HIGH) + self.term(2) + self.term(4)
+        self.stage[2] = total.astype(LOW)
+        self.ship(lambda: self.stage.at[2], 6, (1, 0, 0))
+
+    def arrive(self):
+        return self.mine(0, 0, 0)[...].astype(HIGH) + self.term(3) + self.term(5) + self.term(6)
+
+    def finish(self):
+        self.moves.all_sent(7)
+
+
 def each(plans, act, *arguments):
     for plan in plans:
         act(plan, *arguments)
 
 
+def unit():
+    core, chip = place()
+    return lax.div(chip, HALF), lax.rem(chip, HALF), core
+
+
 def to_tokens(source, target, send, recv):
     core, chip = place()
-    to_core = lax.div(chip, HALF)
-    mine = core * HALF + lax.rem(chip, HALF)
+    group, position, _ = unit()
+    to_core = lax.div(position, 4)
+    mine = group * HALF + 2 * lax.rem(position, 4) + core
     here = to_core == core
 
     def copy_to(ahead):
@@ -680,31 +771,29 @@
 
 def to_heads(source, target, send, recv):
     core, chip = place()
-    here = lax.div(chip, HALF) == core
-
-    def copy_to(group, ahead):
-        head = lax.rem(chip + ahead, HALF)
+    group, position, _ = unit()
+    here = lax.div(position, 4) == core
+    start = 2 * lax.rem(position, 4) + core
+
+    def copy_to(turn_group, ahead):
+        to_group = lax.rem(group + turn_group, 2)
+        head = lax.rem(start + ahead, HALF)
         return remote(
-            source.at[group * HALF + head],
+            source.at[to_group * HALF + head],
             target.at[chip],
-            send.at[group * HALF + ahead],
+            send.at[turn_group * HALF + ahead],
             recv.at[chip],
-            (group, core * HALF + head),
+            (lax.rem(head, 2), to_group * HALF + core * 4 + lax.div(head, 2)),
         )
 
     def every(act):
-        for group in range(2):
-            for ahead in range(HALF):
-                if ahead == 0:
-                    itself = jnp.logical_and(here, core == group)
-                    pl.when(jnp.logical_not(itself))(lambda: act(copy_to(group, 0)))
-                else:
-                    act(copy_to(group, ahead))
+        pl.when(jnp.logical_not(here))(lambda: act(copy_to(0, 0)))
+        for turn_group in range(2):
+            for ahead in range(0 if turn_group else 1, HALF):
+                act(copy_to(turn_group, ahead))
 
     pl.when(here)(
-        lambda: local(
-            source.at[core * HALF + lax.rem(chip, HALF)], target.at[chip], recv.at[chip]
-        ).start()
+        lambda: local(source.at[group * HALF + start], target.at[chip], recv.at[chip]).start()
     )
     every(lambda copy: copy.start())
 
@@ -773,20 +862,21 @@
     return pl.ds(pl.multiple_of(half * width, 128), width)
 
 
-LABEL_AT, BRANCH_AT, GAIN_AT, SHIFT_AT, BIAS_AT = 0, 256, 384, 512, 640
+GAIN_AT, SHIFT_AT, BIAS_AT = 128, 256, 384
 
 
 def first_kernel(names, *refs):
     r = types.SimpleNamespace(**dict(zip(names, refs)))
-    hidden, x_all, w_all, rel_all = r.hidden_in, r.x_vmem, r.w_all, r.rel_all
+    hidden, x_all, w_all, rel_all = r.hidden_in, r.x_all, r.w_all, r.rel_all
     token_rows, width = hidden.shape
-    total = x_all.shape[0]
-    slot_rows = total // CHIPS
+    slot_rows = x_all.shape[1]
+    total = CHIPS * slot_rows
     depth = r.out_weight.shape[0]
-    w_in, w_down, w_out, w_qkv = r.w_in, r.w_down, r.w_out, r.w_qkv
+    w_in, w_down, w_out = r.w_in, r.w_down, r.w_out
     half_hidden = w_in.shape[3]
     half_width = width // 2
     core, chip = place()
+    group, position, _ = unit()
     other = 1 - core
     me = core * CHIPS + chip
     keep = r.keep_sem
@@ -794,22 +884,17 @@
     loads = [
         local(r.ffn_in.at[:, columns_of(core, half_hidden)], w_in.at[core, chip], keep.at[0]),
         local(r.ffn_out, w_down.at[chip], keep.at[1]),
-        local(r.out_weight, w_out.at[chip], keep.at[2]),
-        local(r.qkv_any.at[:, :, columns_of(core, half_width)], w_qkv.at[:, core, chip], keep.at[3]),
+        local(r.out_weight, w_out.at[chip, pl.ds(0, depth)], keep.at[2]),
     ]
     for copy in loads:
         copy.start()
 
-    own_slot = pl.ds(pl.multiple_of(chip * slot_rows, 16), slot_rows)
     extra = r.extra
     extra[...] = jnp.zeros_like(extra)
     extra[0:1, 0:256] = jnp.full((1, 256), 4.0, HIGH)
     extra[0:1, 0:token_rows] = r.segment_ids[...].astype(HIGH)
     extra[1:2, 0:token_rows] = r.order_ids[...].astype(HIGH)
     extra[2:4, 0:token_rows] = r.box_ids[...].astype(HIGH)
-    for start, pair in ((BRANCH_AT, r.branch_bias), (GAIN_AT, r.norm_gains), (SHIFT_AT, r.norm_shifts)):
-        extra[0:2, start : start + depth] = pair[...].astype(HIGH)
-    extra[0:1, BIAS_AT : BIAS_AT + 128] = r.ffn_in_bias[...].astype(HIGH)
     tail = token_rows - token_rows % 16
     x_own = r.x_own
     x_own[0:tail, :] = hidden[0:tail, :]
@@ -817,41 +902,49 @@
         [hidden[tail:token_rows, :].astype(HIGH), extra[...]], axis=0
     ).astype(LOW)
     weight = r.qkv_weight
-    w_own = r.w_own
-    lane_depth = lanes(depth) < HD
-    for pair in range(H // 2):
-        columns = slice(pair * 128, pair * 128 + 128)
-        query, key, value = (weight[n, :, columns].astype(HIGH) for n in range(3))
-        w_own[2 * pair, :, 0:128] = jnp.where(lane_depth, query, turn(value)).astype(LOW)
-        w_own[2 * pair + 1, :, 0:128] = jnp.where(lane_depth, turn(query), value).astype(LOW)
-        w_own[2 * pair, :, 128:256] = jnp.where(lane_depth, key, 0.0).astype(LOW)
-        w_own[2 * pair + 1, :, 128:256] = jnp.where(lane_depth, turn(key), 0.0).astype(LOW)
     rel_own = r.rel_own
+    for kind in range(3):
+        rel_own[:, kind * NB : (kind + 1) * NB] = r.rel_tables[kind]
     eye_depth = (
         lax.broadcasted_iota(jnp.int32, (depth, depth), 0)
         == lax.broadcasted_iota(jnp.int32, (depth, depth), 1)
     ).astype(LOW)
-    for kind in range(3):
-        rel_own[:, kind * NB : (kind + 1) * NB] = r.rel_tables[kind]
     bias_columns = dot(eye_depth, r.qkv_bias[...], NT)
     rel_own[:, 3 * NB : 4 * NB] = jnp.where(
         lanes(depth) == 0, bias_columns[:, 0:1], jnp.where(lanes(depth) == 1, bias_columns[:, 1:2], 0.0)
     ).astype(LOW)
-    own_x = local(x_own, x_all.at[own_slot], keep.at[4])
-    own_w = local(w_own.at[chip], w_all.at[me], keep.at[5])
-    own_x.start()
-    own_w.start()
+    small_own = r.small_own
+    small_own[...] = jnp.zeros_like(small_own)
+    small_own[0:2, 0:depth] = r.branch_bias[...]
+    small_own[0:2, GAIN_AT : GAIN_AT + depth] = r.norm_gains[...]
+    small_own[0:2, SHIFT_AT : SHIFT_AT + depth] = r.norm_shifts[...]
+    small_own[0:1, BIAS_AT : BIAS_AT + 128] = r.ffn_in_bias[...]
+    loads += [
+        local(small_own, w_out.at[chip, pl.ds(depth, 16)], keep.at[3]),
+        local(weight.at[:, :, columns_of(position, 128)], w_all.at[:, core, chip], keep.at[4]),
+    ]
+    for copy in loads[3:]:
+        copy.start()
     meet()
 
-    to_chip = lax.div(me, 2)
+    at_home = group == core
+    away = lax.rem(chip + HALF, CHIPS)
+    x_slot = x_all.at[position]
+    home = lambda: local(x_own, x_slot, r.home_sem.at[1])
+    abroad = lambda: remote(x_own, x_slot, r.home_sem.at[0], r.home_sem.at[1], (other, away))
+    pl.when(at_home)(lambda: home().start())
+    pl.when(jnp.logical_not(at_home))(lambda: abroad().start())
+
+    rel_head = core * HALF + lax.div(chip, 2)
     parity = lax.rem(chip, 2)
     rel_slot = rel_all.at[pl.ds(parity * depth, depth)]
 
     def rel_each(act_remote, act_own):
-        for to_core in range(2):
-            itself = jnp.logical_and(to_chip == chip, core == to_core)
+        for to_group in range(2):
+            to = (lax.rem(rel_head, 2), to_group * HALF + lax.div(rel_head, 2))
+            itself = jnp.logical_and(to[0] == core, to[1] == chip)
             copy = lambda: remote(
-                rel_own, rel_slot, r.rel_send.at[to_core], r.rel_recv.at[parity], (to_core, to_chip)
+                rel_own, rel_slot, r.rel_send.at[to_group], r.rel_recv.at[parity], to
             )
             pl.when(jnp.logical_not(itself))(lambda: act_remote(copy()))
             if act_own is not None:
@@ -864,54 +957,42 @@
     def w_copy(ahead):
         to = lax.rem(chip + ahead, CHIPS)
         return remote(
-            w_own.at[to], w_all.at[me], r.w_send.at[ahead], r.w_recv.at[chip], (core, to)
-        )
-
-    half = width // 2
-
-    def pick_x(part):
-        return lambda slot: x_all.at[
-            pl.ds(pl.multiple_of(slot * slot_rows, 16), slot_rows), pl.ds(part * half, half)
-        ]
-
-    x_plans = [
-        Gather(pick_x(part), r.x_send.at[part], r.x_recv.at[part], across)
-        for part, across in enumerate("xy")
-    ]
-
-    own_x.wait()
-    each(x_plans, Gather.own_line, 0)
-    each(x_plans, Gather.own_plane)
+            weight.at[:, :, columns_of(lax.rem(to, HALF), 128)],
+            w_all.at[:, core, chip],
+            r.w_send.at[ahead],
+            r.w_recv.at[chip],
+            (core, to),
+        )
+
     for ahead in range(1, CHIPS):
         w_copy(ahead).start()
-    each(x_plans, Gather.own_line, 1)
-    each(x_plans, Gather.own_line, 2)
-    swaps = [
-        remote(
-            r.ffn_in.at[:, columns_of(other, half_hidden)],
-            w_in.at[core, chip],
-            r.pair_send.at[0],
-            r.pair_recv.at[0],
-            (other, chip),
-        ),
-        remote(
-            r.qkv_any.at[:, :, columns_of(other, half_width)],
-            w_qkv.at[:, core, chip],
-            r.pair_send.at[1],
-            r.pair_recv.at[1],
-            (other, chip),
-        ),
+    swap_in = remote(
+        r.ffn_in.at[:, columns_of(other, half_hidden)],
+        w_in.at[core, chip],
+        r.pair_send.at[0],
+        r.pair_recv.at[0],
+        (other, chip),
+    )
+    swap_in.start()
+
+    third = slot_rows // 3
+    x_plans = [
+        CubeGather(
+            lambda slot, part=part: x_all.at[slot, pl.ds(part * third, third)],
+            r.x_send.at[part],
+            r.x_recv.at[part],
+            order,
+        )
+        for part, order in enumerate(("xyz", "yzx", "zxy"))
     ]
-    for copy in swaps:
-        copy.start()
-    each(x_plans, Gather.side, None)
-    for line in range(3):
-        each(x_plans, Gather.line, line)
-        each(x_plans, Gather.side, line)
-
+    home().wait()
+    each(x_plans, CubeGather.own)
+    each(x_plans, CubeGather.one)
+    each(x_plans, CubeGather.two)
+
+    half = width // 2
     half_tile = half_hidden // 2
     plan_out = GatherLate(lambda slot: w_out.at[slot], r.out_send, r.out_recv, "x")
-    plan_qkv = Gather(lambda slot: w_qkv.at[:, :, slot], r.qkv_send, r.qkv_recv, "y")
 
     def halves(ref, wide, sends, recvs):
         return [
@@ -925,68 +1006,101 @@
     plans_down = halves(lambda slot, columns: w_down.at[slot, :, columns], half, r.down_send, r.down_recv)
     for copy in loads:
         copy.wait()
-    for copy in swaps:
-        copy.wait()
+    swap_in.wait()
     each(plans_in, Gather.own_line, 0)
     each(plans_in, Gather.own_plane)
     plan_out.first()
     each(plans_in, Gather.own_line, 1)
     each(plans_in, Gather.own_line, 2)
 
-    own_w.wait()
     for ahead in range(1, CHIPS):
         came = lax.rem(chip + ahead, CHIPS)
         remote(
-            w_own.at[0], w_all.at[core * CHIPS + came], r.w_send.at[0], r.w_recv.at[came], (core, came)
+            weight.at[:, :, pl.ds(0, 128)], w_all.at[:, core, came], r.w_send.at[0], r.w_recv.at[came], (core, came)
         ).wait_recv()
-    mine = w_all.at[pl.ds(core * CHIPS, CHIPS)]
-    pair_w = remote(mine, mine, r.pair_send.at[2], r.pair_recv.at[2], (other, chip))
+    pair_w = remote(w_all.at[:, core], w_all.at[:, core], r.pair_send.at[1], r.pair_recv.at[1], (other, chip))
     pair_w.start()
     for slot in range(2):
         local(rel_own, rel_all.at[pl.ds(slot * depth, depth)], r.rel_recv.at[slot]).wait()
-    each(x_plans, Gather.arrive)
+    pair_bias = remote(
+        rel_all.at[:, pl.ds(3 * NB, NB)], r.bias_far, r.pair_send.at[2], r.pair_recv.at[2], (other, chip)
+    )
+    pair_bias.start()
+    each(x_plans, CubeGather.arrive)
+
+    labels = r.labels
+    first_slot = core * HALF
+    label_part = x_all.at[:, pl.ds(slot_rows - 16, 16), pl.ds(0, 256)]
+    label_slots = labels.at[pl.ds(first_slot, HALF)]
+    pair_label = remote(label_part, label_slots, r.pair_send.at[3], r.pair_recv.at[3], (other, chip))
+    pair_label.start()
+    own_label = local(label_part, label_slots, keep.at[5])
+    own_label.start()
     keep_x = local(x_all, r.x_out, keep.at[6])
     keep_x.start()
     keep_rel = local(rel_all, r.rel_out, keep.at[7])
     keep_rel.start()
-
-    meta, shares, bias_in = r.meta, r.shares, r.bias_in
+    pair_w.wait()
+    pair_bias.wait()
+    keep_w = local(w_all, r.w_all_out, keep.at[15])
+    keep_w.start()
+
+    head_rows = 2 * depth
+    row_at = lax.broadcasted_iota(jnp.int32, (head_rows, 128), 0)
+    column_at = lanes(head_rows)
+
+    def bias_row(columns, number):
+        column = columns[:, number : number + 1]
+        return column_sums(jnp.where(row_at == column_at, column, 0.0))
+
+    rel = rel_all[...]
+    bias_near = rel[:, 3 * NB : 4 * NB].astype(HIGH)
+    bias_far = r.bias_far[...].astype(HIGH)
+    bias_query, bias_value = (
+        bias_row(bias_near, number) + turn(bias_row(bias_far, number)) for number in range(2)
+    )
+    weights = [w_all[n].reshape(width, 128) for n in range(3)]
+    near, far_part = r.near, r.far_part
+    pair_rows = 2 * slot_rows
+    pair_half = lanes(pair_rows) < HD
+
+    for pair in range(HALF // 2):
+        tokens = x_all[2 * pair : 2 * pair + 2].reshape(pair_rows, width)
+        query, key, value_rows = (
+            pltpu.roll(dot(tokens, weights[n]), core * HD, 1) for n in range(3)
+        )
+        query, value_rows = query + bias_query, value_rows + bias_value
+        rows = pl.ds(pl.multiple_of(core * HALF * slot_rows, 16) + pair * pair_rows, pair_rows)
+        near[rows, 0:128] = jnp.where(pair_half, query, turn(value_rows)).astype(LOW)
+        near[rows, 128:256] = key.astype(LOW)
+        far_rows = slice(pair * pair_rows, (pair + 1) * pair_rows)
+        far_part[far_rows, 0:128] = jnp.where(pair_half, turn(query), value_rows).astype(LOW)
+        far_part[far_rows, 128:256] = turn(key).astype(LOW)
+    pair_qkv = remote(
+        far_part,
+        near.at[pl.ds(pl.multiple_of(core * HALF * slot_rows, 16), HALF * slot_rows)],
+        r.pair_send.at[4],
+        r.pair_recv.at[4],
+        (other, chip),
+    )
+    pair_qkv.start()
+
+    meta = r.meta
     eye = (
         lax.broadcasted_iota(jnp.int32, (slot_rows, 256), 0)
         == lax.broadcasted_iota(jnp.int32, (slot_rows, 256), 1)
     ).astype(LOW)
-    shares[core] = jnp.zeros(shares.shape[1:], HIGH)
+    pair_label.wait()
+    own_label.wait()
     for slot in range(CHIPS):
-        end = (slot + 1) * slot_rows
-        labels = x_all[end - 16 : end, 0:256]
-        meta[end - slot_rows : end, 0:16] = dot(eye, labels, NT)
-        small = x_all[end - 16 : end, BRANCH_AT:768].astype(HIGH)[8:16]
-        target = slice(slot * depth // 128 * 128, slot * depth // 128 * 128 + 128)
-        for number in range(3):
-            piece = jnp.where(lanes(8) < depth, small[:, number * 128 : number * 128 + 128], 0.0)
-            if slot * depth % 128:
-                piece = pltpu.roll(piece, slot * depth % 128, 1)
-            shares[core, number, :, target] += piece
-        bias_in[:, slot * 128 : slot * 128 + 128] = small[0:1, 384:512]
-    pair_small = remote(
-        shares.at[core], shares.at[core], r.pair_send.at[3], r.pair_recv.at[3], (other, chip)
-    )
-    pair_small.start()
-    rel = rel_all[...]
+        meta[slot * slot_rows : (slot + 1) * slot_rows, 0:16] = dot(eye, labels[slot], NT)
     table_t = rel[:, 0 : 3 * NB]
-    extra_columns = rel[:, 3 * NB : 4 * NB].astype(HIGH)
-    row_at = lax.broadcasted_iota(jnp.int32, (2 * depth, 128), 0)
-    column_at = lanes(2 * depth)
-    bias = column_sums(
-        jnp.where(row_at == column_at, extra_columns[:, 0:1], 0.0)
-        + jnp.where(row_at + 2 * depth == column_at, extra_columns[:, 1:2], 0.0)
-    )
     lane = lanes(BLOCK)
     first_half = lane < HD
     scale = 1.0 / math.sqrt(4.0 * HD)
     left, right, right_t = r.left, r.right, r.right_t
     value, value_t, kept = r.value, r.value_t, r.kept
-    pair_w.wait()
+    pair_qkv.wait()
 
     def prepare(index, carry):
         rows = pl.ds(pl.multiple_of(index * BLOCK, BLOCK), BLOCK)
@@ -1007,11 +1121,9 @@
                 ],
             },
         )
-        projected = dot(x_all[rows, :], w_all[...].reshape(width, 4 * HD))
-        query_value = (projected[:, 0:128] + bias).astype(LOW).astype(HIGH)
-        key = projected[:, 128:256].astype(LOW).astype(HIGH)
-        query = query_value[:, 0:HD].astype(LOW)
-        tables = dot(query, table_t).astype(LOW).astype(HIGH)
+        query_value = near[rows, 0:128].astype(HIGH)
+        key = near[rows, 128:256].astype(HIGH)
+        tables = dot(near[rows, 0:128][:, 0:HD], table_t).astype(LOW).astype(HIGH)
         ids = meta[rows, 8:12].astype(jnp.int32)
         segment, order, box_x, box_y = ids[:, 0:1], ids[:, 1:2], ids[:, 2:3], ids[:, 3:4]
 
@@ -1092,22 +1204,35 @@
     each(plans_down, Gather.side, 0)
     each(plans_down, Gather.line, 1)
     each(plans_down, Gather.side, 1)
+
+    plan_out.arrive()
+    keep_out = local(w_out, r.w_out_out, keep.at[13])
+    keep_out.start()
+    shares, bias_in = r.shares, r.bias_in
+    shares[core] = jnp.zeros(shares.shape[1:], HIGH)
+    for slot in range(CHIPS):
+        small = w_out[slot, depth : depth + 16, 0 : BIAS_AT + 128].astype(HIGH)[0:8]
+        target = slice(slot * depth // 128 * 128, slot * depth // 128 * 128 + 128)
+        for number in range(3):
+            piece = jnp.where(lanes(8) < depth, small[:, number * 128 : number * 128 + 128], 0.0)
+            if slot * depth % 128:
+                piece = pltpu.roll(piece, slot * depth % 128, 1)
+            shares[core, number, :, target] += piece
+        bias_in[:, slot * 128 : slot * 128 + 128] = small[0:1, BIAS_AT : BIAS_AT + 128]
+    pair_small = remote(
+        shares.at[core], shares.at[core], r.pair_send.at[5], r.pair_recv.at[5], (other, chip)
+    )
+    pair_small.start()
     context_arrives()
-    pair_small.wait()
-
-    vectors = [
-        [jnp.concatenate([shares[0, number, k : k + 1], shares[1, number, k : k + 1]], axis=1) for k in range(2)]
-        for number in range(3)
-    ]
-    branch_bias, gains, shifts = vectors
+
     context_wide, context, low_first = r.context_wide, r.context, r.low_first
-    act, slope, d_second, d_inner, d_branch = r.act, r.slope, r.d_second, r.d_inner, r.d_branch
+    act, slope = r.act, r.slope
     out_part, in_part, g_small = r.out_part, r.in_part, r.g_small
     own = pl.ds(pl.multiple_of(core * slot_rows, 16), slot_rows)
     far = pl.ds(pl.multiple_of(other * slot_rows, 16), slot_rows)
     tile = 512
     half_slot = slot_rows // 2
-    count = [4]
+    count = [6]
 
     def swap(source, target):
         copy = remote(
@@ -1118,17 +1243,19 @@
         return copy
 
     left_half = lanes(half_slot) < HD
-    for group in range(2):
+    for slot_group in range(2):
         for pair in range(HALF // 2):
-            even = context_in[group * HALF + 2 * pair].astype(HIGH)[:half_slot]
-            odd = context_in[group * HALF + 2 * pair + 1].astype(HIGH)[:half_slot]
-            top = group * slot_rows
+            even = context_in[slot_group * HALF + 2 * pair].astype(HIGH)[:half_slot]
+            odd = context_in[slot_group * HALF + 2 * pair + 1].astype(HIGH)[:half_slot]
+            top = slot_group * slot_rows
             columns = slice(pair * 128, pair * 128 + 128)
             context_wide[top : top + half_slot, columns] = jnp.where(left_half, even, turn(odd))
             context_wide[top + half_slot : top + slot_rows, columns] = jnp.where(
                 left_half, turn(even), odd
             )
     context[...] = context_wide[...].astype(LOW)
+    keep_context = local(context, r.context_out, keep.at[14])
+    keep_context.start()
 
     def product(index, lhs, rhs):
         out_part[index] = dot(lhs[far, :], rhs)
@@ -1137,22 +1264,29 @@
         copy.wait()
         return mine + in_part[index]
 
-    plan_out.arrive()
-    branch = product(0, context, w_out[...].reshape(half_width, width)) + branch_bias[0]
+    pair_small.wait()
+    branch_bias, gains, shifts = (
+        [jnp.concatenate([shares[0, number, k : k + 1], shares[1, number, k : k + 1]], axis=1) for k in range(2)]
+        for number in range(3)
+    )
+    for k in range(2):
+        r.gains_out[k : k + 1, :] = gains[k]
+    branch = product(0, context, w_out[:, 0:depth, :].reshape(half_width, width)) + branch_bias[0]
     row_index = lax.broadcasted_iota(jnp.int32, (slot_rows, 1), 0)
-    tokens = row_index < token_rows
-    x_mine = jnp.where(tokens, x_own[...].astype(HIGH), 0.0)
+    x_mine = jnp.where(row_index < token_rows, x_own[...].astype(HIGH), 0.0)
     first, normed1, inverse1 = normalize(x_mine + branch, gains[0], shifts[0])
     low_first[own, :] = first.astype(LOW)
     copy = swap(low_first.at[own], low_first.at[own])
+    r.normed1[...] = normed1
+    r.inverse1[...] = jnp.broadcast_to(inverse1, r.inverse1.shape)
     each(plans_down, Gather.line, 2)
     each(plans_down, Gather.side, 2)
-    plan_qkv.own_line(0)
-    plan_qkv.own_plane()
-    plan_qkv.own_line(1)
-    plan_qkv.own_line(2)
     each(plans_in, Gather.arrive)
+    keep_in = local(w_in, r.w_in_out, keep.at[16])
+    keep_in.start()
     copy.wait()
+    keep_first = local(low_first, r.low_first_out, keep.at[17])
+    keep_first.start()
 
     def widen(index, carry):
         columns = pl.ds(pl.multiple_of(index * tile, tile), tile)
@@ -1163,104 +1297,66 @@
         return carry
 
     lax.fori_loop(0, half_hidden // tile, widen, 0)
-    plan_qkv.side(None)
+    keep_act = local(act, r.act_out, keep.at[18])
+    keep_act.start()
+    keep_slope = local(slope, r.slope_out, keep.at[19])
+    keep_slope.start()
     each(plans_down, Gather.arrive)
+    keep_down = local(w_down, r.w_down_out, keep.at[20])
+    keep_down.start()
     second = product(1, act, w_down[...].reshape(half_hidden, width)) + branch_bias[1]
-    plan_qkv.line(0)
-    plan_qkv.side(0)
     result, normed2, inverse2 = normalize(first + second, gains[1], shifts[1])
     r.hidden_out[...] = result[:token_rows].astype(LOW)
-    given = r.out_grad
     upstream = jnp.concatenate(
-        [given[...].astype(HIGH), jnp.zeros((slot_rows - token_rows, width), HIGH)], axis=0
+        [r.out_grad[...].astype(HIGH), jnp.zeros((slot_rows - token_rows, width), HIGH)], axis=0
     )
     d_sum2 = normalize_back(upstream, normed2, inverse2, gains[1])
+    r.d_sum2[...] = d_sum2
     low_second = d_sum2.astype(LOW)
-    d_second[own, :] = low_second
-    copy = swap(d_second.at[own], d_second.at[own])
+    r.d_second_out[...] = low_second
     g_small[...] = jnp.zeros_like(g_small)
     g_small[1:2, 0:width] = column_sums(low_second.astype(HIGH))
     g_small[3:4, 0:width] = column_sums(upstream * normed2)
     g_small[5:6, 0:width] = column_sums(upstream)
-    plan_qkv.line(1)
-    plan_qkv.side(1)
-    copy.wait()
-    g_down, g_in, g_out = r.g_down, r.g_in, r.g_out
-
-    def narrow_back(index, carry):
-        columns = pl.ds(pl.multiple_of(index * tile, tile), tile)
-        down = w_down[pl.ds(index * (tile // 128), tile // 128)].reshape(tile, width)
-        low = (dot(d_second[...], down, NT) * slope[:, columns]).astype(LOW)
-        d_inner[:, columns] = low
-        g_small[pl.ds(8, 1), columns] = column_sums(low.astype(HIGH))
-        g_down[columns, :] = dot(act[:, columns], d_second[...], TN).astype(LOW)
-        return carry
-
-    lax.fori_loop(0, half_hidden // tile, narrow_back, 0)
-    keep_down = local(g_down, r.g_down_out, keep.at[13])
-    keep_down.start()
-    plan_qkv.line(2)
-    plan_qkv.side(2)
-    w_in_all = w_in[...].reshape(width, half_hidden)
-    out_part[2] = dot(d_inner[far, :], w_in_all, NT)
-    copy = swap(out_part.at[2], in_part.at[2])
-    mine = dot(d_inner[own, :], w_in_all, NT)
-
-    def widen_grad(index, carry):
-        rows = pl.ds(pl.multiple_of(index * 256, 256), 256)
-        g_in[rows, :] = dot(low_first[:, rows], d_inner[...], TN).astype(LOW)
-        return carry
-
-    lax.fori_loop(0, width // 256, widen_grad, 0)
-    keep_in = local(g_in, r.g_in_out, keep.at[14])
-    keep_in.start()
-    copy.wait()
-    d_first = d_sum2 + mine + in_part[2]
-    d_sum1 = normalize_back(d_first, normed1, inverse1, gains[0])
-    r.d_sum1[...] = d_sum1
-    low_branch = d_sum1.astype(LOW)
-    d_branch[own, :] = low_branch
-    copy = swap(d_branch.at[own], d_branch.at[own])
-    g_small[0:1, 0:width] = column_sums(low_branch.astype(HIGH))
-    g_small[2:3, 0:width] = column_sums(d_first * normed1)
-    g_small[4:5, 0:width] = column_sums(d_first)
-    copy.wait()
-    w_out_all = w_out[...].reshape(half_width, width)
-    context_wide[...] = dot(d_branch[...], w_out_all, NT)
-    for group in range(2):
-        for pair in range(HALF // 2):
-            both = context_wide[
-                group * slot_rows : (group + 1) * slot_rows, pair * 128 : pair * 128 + 128
-            ]
-            r.d_message[group * HALF + 2 * pair] = fold(both)
-            r.d_message[group * HALF + 2 * pair + 1] = fold(turn(both))
-    g_out[...] = dot(context[...], d_branch[...], TN).astype(LOW)
-    plan_qkv.arrive()
-    keep_qkv = local(w_qkv, r.w_qkv_out, keep.at[15])
-    keep_qkv.start()
 
     for ahead in range(1, CHIPS):
         w_copy(ahead).wait_send()
     rel_each(lambda copy: copy.wait_send(), None)
+    pl.when(jnp.logical_not(at_home))(lambda: abroad().wait_send())
     context_sent()
-    each(x_plans, Gather.finish)
-    each(plans_in + plans_down + [plan_out, plan_qkv], Gather.finish)
-    for copy in stash + [keep_x, keep_rel, keep_facts, keep_down, keep_in, keep_qkv]:
+    each(x_plans, CubeGather.finish)
+    each(plans_in + plans_down + [plan_out], Gather.finish)
+    for copy in stash + [
+        keep_x,
+        keep_rel,
+        keep_w,
+        keep_facts,
+        keep_out,
+        keep_context,
+        keep_in,
+        keep_first,
+        keep_act,
+        keep_slope,
+        keep_down,
+    ]:
         copy.wait()
 
 
 def second_kernel(names, *refs):
     r = types.SimpleNamespace(**dict(zip(names, refs)))
     core, chip = place()
+    group, position, _ = unit()
     other = 1 - core
     left, right, right_t, value_t, kept = r.left, r.right, r.right_t, r.value_t, r.kept
-    rel_all, x_all, w_qkv = r.rel_all, r.x_all, r.w_qkv
-    g_in, g_down, g_out = r.g_in, r.g_down, r.g_out
-    total, width = x_all.shape
-    slot_rows = total // CHIPS
+    rel_all, x_all, w_all = r.rel_all, r.x_all, r.w_all
+    w_in, w_down, w_out = r.w_in, r.w_down, r.w_out
+    slot_rows, width = x_all.shape[1:]
+    total = CHIPS * slot_rows
+    half_total = HALF * slot_rows
     half_slot = slot_rows // 2
+    half_hidden = w_in.shape[3]
     half_width = width // 2
-    depth = w_qkv.shape[3]
+    depth = r.g_out.shape[1]
     token_rows = r.hidden_grad.shape[0]
     scale = 1.0 / math.sqrt(4.0 * HD)
     keep = r.keep_sem
@@ -1268,27 +1364,45 @@
         local(there, held, keep.at[k])
         for k, (there, held) in enumerate(
             (
+                (r.w_down_any, w_down),
+                (r.act_any, r.act),
+                (r.slope_any, r.slope),
+                (r.w_in_any, w_in),
+                (r.low_first_any, r.low_first),
+                (r.w_out_any, w_out),
+                (r.context_any, r.context),
                 (r.left_any, left),
                 (r.right_t_any, right_t),
                 (r.value_t_any, value_t),
                 (r.kept_any, kept),
                 (r.right_any, right),
-                (r.g_down_any, g_down),
-                (r.g_in_any, g_in),
-                (r.g_out_any, g_out),
-                (r.x_all_any, x_all),
-                (r.w_qkv_any, w_qkv),
+                (r.x_any, x_all),
+                (r.w_all_any, w_all),
             )
         )
     ]
     for copy in loads:
         copy.start()
     meet()
-    d_arrived = r.d_arrived
-    grad_arrives, grad_sent = to_heads(r.d_message, d_arrived, r.d_send, r.d_recv)
+    count = [0]
+
+    def swap(source, target):
+        copy = remote(
+            source, target, r.pair_send.at[count[0]], r.pair_recv.at[count[0]], (other, chip)
+        )
+        count[0] += 1
+        copy.start()
+        return copy
+
+    own = pl.ds(pl.multiple_of(core * slot_rows, 16), slot_rows)
+    far = pl.ds(pl.multiple_of(other * slot_rows, 16), slot_rows)
+    act, slope, low_first, context = r.act, r.slope, r.low_first, r.context
+    d_second, d_branch, context_wide = r.d_second, r.d_branch, r.context_wide
+    d_inner = act
+    out_part, in_part, small_sum = r.out_part, r.in_part, r.small_sum
     plan_down = Reduce(
-        r.g_down_any,
-        g_down,
+        w_down,
+        w_down,
         lambda ref, slot: ref.at[slot],
         [r.down_1, r.down_2, r.down_3],
         r.down_send,
@@ -1296,8 +1410,8 @@
         "y",
     )
     plan_in = Reduce(
-        r.g_in_any,
-        g_in,
+        w_in,
+        w_in,
         lambda ref, slot: ref.at[:, slot],
         [r.in_1, r.in_2, r.in_3],
         r.in_send,
@@ -1305,8 +1419,8 @@
         "x",
     )
     plan_out = ReduceEarly(
-        r.g_out_any,
-        g_out,
+        r.g_out,
+        r.g_out,
         lambda ref, slot: ref.at[slot],
         [r.out_1, r.out_2, r.out_3],
         r.out_send,
@@ -1314,14 +1428,77 @@
         "y",
     )
     plans = (plan_down, plan_in)
+
+    d_second[own, :] = r.d_second_own[...]
+    copy = swap(r.d_second_own, d_second.at[own])
+    small_sum[...] = r.g_small[...]
+    for load in loads[0:3]:
+        load.wait()
+    copy.wait()
+    tile = 512
+    slots = tile // w_down.shape[1]
+
+    def narrow_back(index, carry):
+        columns = pl.ds(pl.multiple_of(index * tile, tile), tile)
+        rows = pl.ds(index * slots, slots)
+        low = (dot(d_second[...], w_down[rows].reshape(tile, width), NT) * slope[:, columns]).astype(LOW)
+        small_sum[pl.ds(8, 1), columns] = column_sums(low.astype(HIGH))
+        w_down[rows] = (
+            dot(act[:, columns], d_second[...], TN).astype(LOW).reshape(slots, tile // slots, width)
+        )
+        d_inner[:, columns] = low
+        return carry
+
+    lax.fori_loop(0, half_hidden // tile, narrow_back, 0)
+    plan_down.start(2)
+    for load in loads[3:5]:
+        load.wait()
+    w_in_all = w_in[...].reshape(width, half_hidden)
+    out_part[...] = dot(d_inner[far, :], w_in_all, NT)
+    copy = swap(out_part, in_part)
+    mine = dot(d_inner[own, :], w_in_all, NT)
+    slots_in = 256 // depth
+
+    def widen_grad(index, carry):
+        rows = pl.ds(pl.multiple_of(index * 256, 256), 256)
+        parts = CHIPS // slots_in
+        w_in[lax.div(index, parts), pl.ds(lax.rem(index, parts) * slots_in, slots_in)] = (
+            dot(low_first[:, rows], d_inner[...], TN).astype(LOW).reshape(slots_in, depth, half_hidden)
+        )
+        return carry
+
+    lax.fori_loop(0, width // 256, widen_grad, 0)
+    plan_in.start(2)
+    copy.wait()
+    d_sum2, gains = r.d_sum2, r.gains
+    d_first = d_sum2[...] + mine + in_part[...]
+    d_sum1 = normalize_back(d_first, r.normed1[...], r.inverse1[:, 0:1], gains[0:1])
+    low_branch = d_sum1.astype(LOW)
+    d_branch[own, :] = low_branch
+    copy = swap(d_branch.at[own], d_branch.at[own])
+    r.d_sum1[...] = d_sum1
+    small_sum[0:1, 0:width] = column_sums(low_branch.astype(HIGH))
+    small_sum[2:3, 0:width] = column_sums(d_first * r.normed1[...])
+    small_sum[4:5, 0:width] = column_sums(d_first)
+    for load in loads[5:7]:
+        load.wait()
+    copy.wait()
+    context_wide[...] = dot(d_branch[...], w_out[:, 0:depth, :].reshape(half_width, width), NT)
+    for slot_group in range(2):
+        for pair in range(HALF // 2):
+            both = context_wide[
+                slot_group * slot_rows : (slot_group + 1) * slot_rows, pair * 128 : pair * 128 + 128
+            ]
+            r.d_message[slot_group * HALF + 2 * pair] = fold(both)
+            r.d_message[slot_group * HALF + 2 * pair + 1] = fold(turn(both))
+    d_arrived = r.d_arrived
+    grad_arrives, grad_sent = to_heads(r.d_message, d_arrived, r.d_send, r.d_recv)
+    r.g_out[...] = dot(context[...], d_branch[...], TN).astype(LOW).reshape(r.g_out.shape)
+    each(plans, Reduce.start, 1)
     plan_out.start()
 
-    each(plans, Reduce.start, 2)
-    each(plans, Reduce.start, 1)
-
     z, y, x = coordinates(chip)
-    small_sum, small_in = r.small_sum, r.small_in
-    small_sum[...] = r.g_small[...]
+    small_in = r.small_in
 
     def small_copy(index, to_core, to_chip):
         return remote(
@@ -1352,6 +1529,7 @@
             small_sum[...] += small_in[index]
 
     small_start(0)
+    each(plans, Reduce.side, 2)
     left_half = lanes(half_slot) < HD
     d_context = r.d_context
     grad_arrives()
@@ -1363,33 +1541,33 @@
     table_t = rel_all[:, 0 : 3 * NB]
     lane = lanes(BLOCK)
     first_half = lane < HD
-    d_query, d_query_t, d_pair_t, rel_grad = r.d_query, r.d_query_t, r.d_pair_t, r.rel_grad
+    d_heads, d_pair_t, rel_grad = r.d_heads, r.d_pair_t, r.rel_grad
     d_pair_t[...] = jnp.zeros_like(d_pair_t)
     rel_grad[...] = jnp.zeros_like(rel_grad)
-    for copy in loads:
-        copy.wait()
+    for load in loads[7:]:
+        load.wait()
 
     def step(index, carry):
         rows = pl.ds(pl.multiple_of(index * BLOCK, BLOCK), BLOCK)
         at_steps(
             index,
             {
-                1: [
-                    lambda: each(plans, Reduce.side, 2),
+                0: [
+                    lambda: each(plans, Reduce.line, 2),
                     lambda: each(plans, Reduce.start, 0),
                     lambda: small_end(0),
                     lambda: small_start(1),
                 ],
-                2: [lambda: each(plans, Reduce.line, 2), plan_out.third],
-                4: [
+                2: [plan_out.third],
+                3: [
                     lambda: each(plans, Reduce.side, 1),
                     lambda: each(plans, Reduce.start, None),
                     lambda: small_end(1),
                     lambda: small_start(2),
                 ],
-                5: [lambda: each(plans, Reduce.line, 1), plan_out.across],
-                7: [lambda: each(plans, Reduce.side, 0), lambda: small_end(2), lambda: small_start(3)],
-                8: [lambda: each(plans, Reduce.line, 0)],
+                5: [plan_out.across],
+                6: [lambda: each(plans, Reduce.side, 0)],
+                8: [lambda: each(plans, Reduce.line, 1), lambda: small_end(2), lambda: small_start(3)],
             },
         )
         facts = kept[rows, :]
@@ -1399,8 +1577,8 @@
         d_probs = dot(grad.astype(LOW), value_t[...])
         d_logits = (probs * (d_probs - delta)).astype(LOW)
         query_t = jnp.where(first_half, left[rows, 256:384].astype(HIGH), 0.0).T[0:HD]
-        d_pair_t[0:HD, :] += dot(grad.T[0:HD].astype(LOW), probs.astype(LOW))
-        d_pair_t[HD : 2 * HD, :] += dot(query_t.astype(LOW), d_logits)
+        d_pair_t[0:HD, :] += dot(query_t.astype(LOW), d_logits)
+        d_pair_t[HD : 2 * HD, :] += dot(grad.T[0:HD].astype(LOW), probs.astype(LOW))
         back = dot(d_logits, right[...]) * scale
         ids = facts.astype(jnp.int32)
         order, box_x, box_y = (ids[:, HD + k : HD + k + 1] for k in (1, 2, 3))
@@ -1421,125 +1599,104 @@
             [first, placed(1, box_x, BOX_RANGE, 0), placed(1, box_y, BOX_RANGE, BOX_RANGE)], axis=1
         ).astype(LOW)
         from_tables = dot(d_tables, table_t, NT)
-        d_query[rows, :] = jnp.where(
-            first_half,
-            back[:, 256:384] + jnp.concatenate([from_tables, from_tables], axis=1),
-            0.0,
-        )
-        d_query_t[0:HD, rows] = d_query[rows, :].T[0:HD].astype(LOW)
+        d_query = back[:, 256:384] + jnp.concatenate([from_tables, from_tables], axis=1)
+        d_heads[0, :, rows] = d_query.T[0:HD].astype(LOW)
         rel_grad[:, 0 : 3 * NB] += dot((query_t / scale).astype(LOW), d_tables)
         return carry
 
     lax.fori_loop(0, total // BLOCK, step, 0)
-    message = r.message
-    slot_lane = lanes(slot_rows) < HD
-    for slot in range(CHIPS):
-        top = slot * slot_rows
-        if slot % 8 == 0:
-            turned = d_pair_t[:, top : top + 8 * slot_rows].T
-        pair = turned[(slot % 8) * slot_rows : (slot % 8 + 1) * slot_rows]
-        message[slot, 0:slot_rows, :] = jnp.where(
-            slot_lane, d_query[top : top + slot_rows, :], pair
-        ).astype(LOW)
-        message[slot, slot_rows:, :] = fold(pair)
-    tokens_in = r.tokens_in
-    tokens_arrive, tokens_sent = to_tokens(message, tokens_in, r.msg_send, r.msg_recv)
-    each(plans, Reduce.side, None)
-
-    d_query_t[HD : 3 * HD, :] = d_pair_t[...].astype(LOW)
-    d_columns = d_query_t[...]
-    sums = jnp.sum(d_columns[0 : 2 * HD].astype(HIGH), axis=1, keepdims=True)
+
+    d_heads[1] = d_pair_t[0:HD, :].astype(LOW)
+    d_heads[2] = d_pair_t[HD : 2 * HD, :].astype(LOW)
+    d_both = r.d_both
+    near_part = pl.ds(pl.multiple_of(core * half_total, 128), half_total)
+    far_part = pl.ds(pl.multiple_of(other * half_total, 128), half_total)
+    copy = swap(d_heads.at[:, :, far_part], d_both.at[:, core])
+    d_both[:, core] = d_heads[:, :, near_part]
+    sums = [jnp.sum(d_heads[n].astype(HIGH), axis=1, keepdims=True) for n in (0, 2)]
     rel_grad[:, 3 * NB : 4 * NB] = jnp.where(
-        lanes(HD) == 0, sums[0:HD], jnp.where(lanes(HD) == 1, sums[HD : 2 * HD], 0.0)
-    )
-    rel_far, rel_sum = r.rel_far, r.rel_sum
-    rel_rows = pl.ds(pl.multiple_of(other * depth, 8), depth)
-    rel_pair = remote(
-        rel_grad.at[rel_rows], rel_far, r.pair_send.at[0], r.pair_recv.at[0], (other, chip)
-    )
-    rel_pair.start()
+        lanes(HD) == 0, sums[0], jnp.where(lanes(HD) == 1, sums[1], 0.0)
+    )
+    head = 2 * position + core
+    rel_came = r.rel_came
+
+    def rel_each(act_remote, act_own):
+        for side in range(2):
+            to = (lax.div(position, 4), lax.rem(2 * head + side, CHIPS))
+            itself = jnp.logical_and(to[0] == core, to[1] == chip)
+            source = rel_grad.at[pl.ds(side * depth, depth)]
+            act = lambda: act_remote(
+                remote(source, rel_came.at[group], r.rel_send.at[side], r.rel_recv.at[group], to)
+            )
+            pl.when(jnp.logical_not(itself))(act)
+            if act_own:
+                pl.when(itself)(lambda: local(source, rel_came.at[group], r.rel_recv.at[group]).start())
+
+    rel_each(lambda copy: copy.start(), True)
+    copy.wait()
+    d_columns = d_both[...].reshape(6 * HD, half_total)
+
+    w_heads = jnp.concatenate([w_all[n].reshape(width, 128) for n in range(3)], axis=1)
+    d_rows = d_columns.T
+    d_x = r.d_x
+    pair_rows = 2 * slot_rows
+    for pair in range(HALF // 2):
+        d_x[2 * pair : 2 * pair + 2] = (
+            dot(d_rows[pair * pair_rows : (pair + 1) * pair_rows], w_heads, NT)
+            .astype(LOW)
+            .reshape(2, slot_rows, width)
+        )
+    third = slot_rows // 3
+    x_plans = [
+        CubeReduce(
+            lambda slot, part=part: d_x.at[slot, pl.ds(part * third, third)],
+            r.x_stage.at[part],
+            r.x_send.at[part],
+            r.x_recv.at[part],
+            order,
+        )
+        for part, order in enumerate(("xyz", "yzx", "zxy"))
+    ]
+    each(x_plans, CubeReduce.own)
+
+    w_grad = dot(d_columns, x_all[...].reshape(half_total, width))
     w_mine, w_far, w_low, w_came = r.w_mine, r.w_far, r.w_low, r.w_came
-    w_grad = dot(d_columns, x_all[...])
     for part in range(2):
         w_mine[part] = w_grad[:, part * half_width : (part + 1) * half_width]
-    w_pair = remote(
-        w_mine.at[other], w_far, r.pair_send.at[1], r.pair_recv.at[1], (other, chip)
-    )
-    w_pair.start()
-    rel_pair.wait()
-    rel_sum[...] = rel_grad[pl.ds(pl.multiple_of(core * depth, 8), depth), :] + rel_far[...]
-    rel_to = (lax.div(chip, HALF), lax.rem(2 * chip + core, CHIPS))
-    rel_here = jnp.logical_and(rel_to[0] == core, rel_to[1] == chip)
-    rel_came = r.rel_came
-    rel_copy = lambda: remote(rel_sum, rel_came, r.rel_send.at[0], r.rel_recv.at[0], rel_to)
-    own_rel = lambda: local(rel_sum, rel_came, r.rel_recv.at[0])
-    pl.when(rel_here)(lambda: own_rel().start())
-    pl.when(jnp.logical_not(rel_here))(lambda: rel_copy().start())
-    w_pair.wait()
+    copy = swap(w_mine.at[other], w_far)
+    each(x_plans, CubeReduce.one)
+    copy.wait()
     w_sum = (w_mine[core] + w_far[...]).T
-    w_low[...] = jnp.zeros_like(w_low)
     for slot in range(CHIPS):
-        w_low[slot, :, 0 : 3 * HD] = w_sum[slot * depth : (slot + 1) * depth].astype(LOW)
+        w_low[slot] = w_sum[slot * depth : (slot + 1) * depth].astype(LOW)
 
     def w_copy(ahead):
         to = lax.rem(chip + ahead, CHIPS)
         return remote(w_low.at[to], w_came.at[chip], r.w_send.at[ahead], r.w_recv.at[chip], (core, to))
 
-    own_w = local(w_low.at[chip], w_came.at[chip], keep.at[10])
+    own_w = local(w_low.at[chip], w_came.at[chip], keep.at[14])
     own_w.start()
     for ahead in range(1, CHIPS):
         w_copy(ahead).start()
-
-    wide, low = r.wide, r.low
-    tokens_arrive()
-    for group in range(2):
-        top = group * slot_rows
-        for pair in range(HALF // 2):
-            columns = slice(pair * 128, pair * 128 + 128)
-            even = tokens_in[group * HALF + 2 * pair].astype(HIGH)
-            odd = tokens_in[group * HALF + 2 * pair + 1].astype(HIGH)
-            even_main, odd_main = even[:slot_rows], odd[:slot_rows]
-            low[0, top : top + slot_rows, columns] = jnp.where(
-                slot_lane, even_main, turn(odd_main)
-            ).astype(LOW)
-            low[1, top : top + slot_rows, columns] = jnp.where(
-                slot_lane, turn(even_main), odd_main
-            ).astype(LOW)
-            even_last = even[slot_rows : slot_rows + half_slot]
-            odd_last = odd[slot_rows : slot_rows + half_slot]
-            wide[top : top + half_slot, columns] = jnp.where(left_half, even_last, turn(odd_last))
-            wide[top + half_slot : top + slot_rows, columns] = jnp.where(
-                left_half, turn(even_last), odd_last
-            )
-    low[2] = wide[...].astype(LOW)
-    own = pl.ds(pl.multiple_of(core * slot_rows, 16), slot_rows)
-    far = pl.ds(pl.multiple_of(other * slot_rows, 16), slot_rows)
-    weights = [w_qkv[n].reshape(width, half_width) for n in range(3)]
-
-    def part(rows):
-        return (
-            dot(low[0, rows, :], weights[0], NT)
-            + dot(low[1, rows, :], weights[1], NT)
-            + dot(low[2, rows, :], weights[2], NT)
-        )
-
-    out_part, in_part = r.out_part, r.in_part
-    out_part[...] = part(far)
-    x_pair = remote(out_part, in_part, r.pair_send.at[2], r.pair_recv.at[2], (other, chip))
-    x_pair.start()
-    mine = part(own) + r.d_sum1[...]
-    x_pair.wait()
-    r.hidden_grad[...] = (mine + in_part[...])[:token_rows].astype(LOW)
-
-    plan_down.finish(r.down_grad)
+    each(x_plans, CubeReduce.two)
+    each(plans, Reduce.line, 0)
+    each(plans, Reduce.side, None)
+    x_total, x_came = r.x_total, r.x_came
+    for part, plan in enumerate(x_plans):
+        x_total[part * third : (part + 1) * third] = plan.arrive().astype(LOW)
+    at_home = group == core
+    home = lambda: local(x_total, x_came, r.home_sem.at[1])
+    abroad = lambda: remote(
+        x_total, x_came, r.home_sem.at[0], r.home_sem.at[1], (other, lax.rem(chip + HALF, CHIPS))
+    )
+    pl.when(at_home)(lambda: home().start())
+    pl.when(jnp.logical_not(at_home))(lambda: abroad().start())
+
     in_total, in_far = r.in_total, r.in_far
     plan_in.finish(in_total)
-    in_pair = remote(
-        in_total.at[other], in_far, r.pair_send.at[3], r.pair_recv.at[3], (other, chip)
-    )
-    in_pair.start()
+    in_pair = swap(in_total.at[other], in_far)
+    plan_down.finish(r.down_grad)
     plan_out.finish(r.out_grad)
-    half_hidden = in_total.shape[2]
     in_grad = r.in_grad
     in_grad[:, columns_of(core, half_hidden)] = in_total[core]
     small_end(3)
@@ -1552,29 +1709,29 @@
     for number, result in enumerate((r.branch_grad, r.gain_grad, r.shift_grad)):
         result[...] = shares[2 * number : 2 * number + 2, 0:depth]
     r.bias_grad[...] = small_all(pl.ds(8, 1), columns_of(chip, 128))
-    own_rel().wait()
-    pl.when(jnp.logical_not(rel_here))(lambda: rel_copy().wait_send())
+    for slot in range(2):
+        local(rel_grad.at[pl.ds(0, depth)], rel_came.at[slot], r.rel_recv.at[slot]).wait()
+    rel_each(lambda copy: copy.wait_send(), False)
+    rel_total = rel_came[0] + rel_came[1]
     for kind in range(3):
-        r.rel_tables_grad[kind] = rel_came[:, kind * NB : (kind + 1) * NB]
-    r.qkv_bias_grad[...] = rel_came[:, 3 * NB : 4 * NB].T[0:2]
+        r.rel_tables_grad[kind] = rel_total[:, kind * NB : (kind + 1) * NB]
+    r.qkv_bias_grad[...] = rel_total[:, 3 * NB : 4 * NB].T[0:2]
     own_w.wait()
     for ahead in range(1, CHIPS):
         came = lax.rem(chip + ahead, CHIPS)
         remote(w_low.at[0], w_came.at[came], r.w_send.at[0], r.w_recv.at[came], (core, came)).wait_recv()
         w_copy(ahead).wait_send()
-    lane_depth = lanes(depth) < HD
-    for pair in range(H // 2):
-        columns = slice(pair * 128, pair * 128 + 128)
-        even = w_came[2 * pair].astype(HIGH)
-        odd = w_came[2 * pair + 1].astype(HIGH)
-        w_out = r.qkv_grad
-        w_out[0, :, columns] = jnp.where(lane_depth, even[:, 0:128], turn(odd[:, 0:128]))
-        w_out[2, :, columns] = jnp.where(lane_depth, turn(even[:, 0:128]), odd[:, 0:128])
-        w_out[1, :, columns] = jnp.where(lane_depth, even[:, 128:256], turn(odd[:, 128:256]))
+    for pair in range(HALF):
+        both = w_came[pair].astype(HIGH) + w_came[HALF + pair].astype(HIGH)
+        for n in range(3):
+            r.qkv_grad[n, :, pair * 128 : pair * 128 + 128] = both[:, n * 128 : n * 128 + 128]
+    home().wait()
+    pl.when(jnp.logical_not(at_home))(lambda: abroad().wait_send())
+    r.hidden_grad[...] = (r.d_sum1[...] + x_came[...].astype(HIGH))[:token_rows].astype(LOW)
     in_pair.wait()
     in_grad[:, columns_of(other, half_hidden)] = in_far[...]
     grad_sent()
-    tokens_sent()
+    each(x_plans, CubeReduce.finish)
 
 
 def hand_over(count, *refs):
@@ -1624,7 +1781,7 @@
     out_grad,
 ):
     rows, width = hidden_in.shape
-    slot_rows = -(-rows // 16) * 16
+    slot_rows = -(-rows // 48) * 48
     total = CHIPS * slot_rows
     depth = qkv_weight.shape[1]
     hidden = ffn_in.shape[1]
@@ -1634,9 +1791,12 @@
     fold_rows = -(-(slot_rows // 2) // 16) * 16
     any_, vmem, dma = pl.ANY, pltpu.VMEM, pltpu.SemaphoreType.DMA
     message = (CHIPS, fold_rows, 128)
+    x_block, w_block = (HALF, slot_rows, width), (3, 2, CHIPS, depth, 128)
+    in_all, down_all = (2, CHIPS, depth, half_hidden), (CHIPS, down_rows, width)
+    out_all = (CHIPS, depth + 16, width)
     made = call(
         first_kernel,
-        "forward_and_feed_forward",
+        "forward_pass",
         0,
         dict(
             hidden_in=(hidden_in, vmem),
@@ -1644,7 +1804,6 @@
             order_ids=(order_ids.reshape(1, rows), vmem),
             box_ids=(box_ids, vmem),
             qkv_weight=(qkv_weight, vmem),
-            qkv_any=(qkv_weight, any_),
             qkv_bias=(qkv_bias, vmem),
             rel_tables=(rel_tables.transpose(0, 2, 1), vmem),
             out_weight=(out_weight, any_),
@@ -1658,33 +1817,43 @@
         ),
         dict(
             hidden_out=((rows, width), LOW, vmem),
-            x_out=((total, width), LOW, any_),
+            x_out=(x_block, LOW, any_),
+            w_all_out=(w_block, LOW, any_),
             rel_out=((2 * depth, 4 * NB), LOW, any_),
             left_out=((total, 384), LOW, any_),
             right_out=((total, 384), LOW, any_),
             right_t_out=((384, total), LOW, any_),
             value_t_out=((128, total), LOW, any_),
             kept_out=((total, 128), HIGH, any_),
-            g_down_out=((half_hidden, width), LOW, any_),
-            g_in_out=((width, half_hidden), LOW, any_),
-            g_out=((half_width, width), LOW, vmem),
+            w_in_out=(in_all, LOW, any_),
+            w_down_out=(down_all, LOW, any_),
+            w_out_out=(out_all, LOW, any_),
+            context_out=((both, half_width), LOW, any_),
+            low_first_out=((both, width), LOW, any_),
+            act_out=((both, half_hidden), LOW, any_),
+            slope_out=((both, half_hidden), HIGH, any_),
+            normed1=((slot_rows, width), HIGH, vmem),
+            inverse1=((slot_rows, 128), HIGH, vmem),
+            d_sum2=((slot_rows, width), HIGH, vmem),
+            d_second_out=((slot_rows, width), LOW, vmem),
+            gains_out=((2, width), HIGH, vmem),
             g_small=((16, half_hidden), HIGH, vmem),
-            d_sum1=((slot_rows, width), HIGH, vmem),
-            d_message=(message, LOW, vmem),
-            w_qkv_out=((3, 2, CHIPS, depth, half_width), LOW, any_),
         ),
         dict(
             x_own=vmem((slot_rows, width), LOW),
-            x_vmem=vmem((total, width), LOW),
+            x_all=vmem(x_block, LOW),
             extra=vmem((slot_rows - rows, width), HIGH),
-            w_own=vmem((H, depth, 4 * HD), LOW),
-            w_all=vmem((2 * CHIPS, depth, 4 * HD), LOW),
+            small_own=vmem((16, width), LOW),
+            w_all=vmem(w_block, LOW),
             rel_own=vmem((depth, 4 * NB), LOW),
             rel_all=vmem((2 * depth, 4 * NB), LOW),
-            w_in=vmem((2, CHIPS, depth, half_hidden), LOW),
-            w_down=vmem((CHIPS, down_rows, width), LOW),
-            w_out=vmem((CHIPS, depth, width), LOW),
-            w_qkv=vmem((3, 2, CHIPS, depth, half_width), LOW),
+            bias_far=vmem((2 * depth, NB), LOW),
+            labels=vmem((CHIPS, 16, 256), LOW),
+            near=vmem((total, 256), LOW),
+            far_part=vmem((total // 2, 256), LOW),
+            w_in=vmem(in_all, LOW),
+            w_down=vmem(down_all, LOW),
+            w_out=vmem(out_all, LOW),
             meta=vmem((total, 128), HIGH),
             shares=vmem((2, 3, 8, half_width), HIGH),
             bias_in=vmem((1, half_hidden), HIGH),
@@ -1701,16 +1870,12 @@
             low_first=vmem((both, width), LOW),
             act=vmem((both, half_hidden), LOW),
             slope=vmem((both, half_hidden), HIGH),
-            d_second=vmem((both, width), LOW),
-            d_inner=vmem((both, half_hidden), LOW),
-            d_branch=vmem((both, width), LOW),
-            g_down=vmem((half_hidden, width), LOW),
-            g_in=vmem((width, half_hidden), LOW),
-            out_part=vmem((3, slot_rows, width), HIGH),
-            in_part=vmem((3, slot_rows, width), HIGH),
-            keep_sem=dma((16,)),
-            x_send=dma((2, 16)),
-            x_recv=dma((2, 16)),
+            out_part=vmem((2, slot_rows, width), HIGH),
+            in_part=vmem((2, slot_rows, width), HIGH),
+            keep_sem=dma((21,)),
+            home_sem=dma((2,)),
+            x_send=dma((3, 8)),
+            x_recv=dma((3, 8)),
             w_send=dma((16,)),
             w_recv=dma((16,)),
             rel_send=dma((2,)),
@@ -1721,22 +1886,16 @@
             in_recv=dma((2, 16)),
             down_send=dma((2, 16)),
             down_recv=dma((2, 16)),
-            qkv_send=dma((16,)),
-            qkv_recv=dma((16,)),
             msg_send=dma((16,)),
             msg_recv=dma((16,)),
-            pair_send=dma((10,)),
-            pair_recv=dma((10,)),
+            pair_send=dma((9,)),
+            pair_recv=dma((9,)),
         ),
     )
-    g_down = made.g_down_out.reshape(CHIPS, down_rows, width)
-    g_in = made.g_in_out.reshape(2, CHIPS, depth, half_hidden)
-    g_out = made.g_out.reshape(CHIPS, depth, width)
-    out_message = (CHIPS, slot_rows + fold_rows, 128)
     in_block, down_block, out_block = (2, depth, half_hidden), (down_rows, width), (depth, width)
     ended = call(
         second_kernel,
-        "backward_and_sums",
+        "backward_pass",
         1,
         dict(
             left_any=(made.left_out, any_),
@@ -1745,14 +1904,21 @@
             value_t_any=(made.value_t_out, any_),
             kept_any=(made.kept_out, any_),
             rel_all=(made.rel_out, vmem),
-            x_all_any=(made.x_out, any_),
-            w_qkv_any=(made.w_qkv_out, any_),
-            g_down_any=(g_down, any_),
-            g_in_any=(g_in, any_),
-            g_out_any=(g_out, any_),
+            x_any=(made.x_out, any_),
+            w_all_any=(made.w_all_out, any_),
+            w_in_any=(made.w_in_out, any_),
+            w_down_any=(made.w_down_out, any_),
+            w_out_any=(made.w_out_out, any_),
+            context_any=(made.context_out, any_),
+            low_first_any=(made.low_first_out, any_),
+            act_any=(made.act_out, any_),
+            slope_any=(made.slope_out, any_),
+            normed1=(made.normed1, vmem),
+            inverse1=(made.inverse1, vmem),
+            d_sum2=(made.d_sum2, vmem),
+            d_second_own=(made.d_second_out, vmem),
+            gains=(made.gains_out, vmem),
             g_small=(made.g_small, vmem),
-            d_sum1=(made.d_sum1, vmem),
-            d_message=(made.d_message, vmem),
         ),
         dict(
             hidden_grad=((rows, width), LOW, vmem),
@@ -1773,11 +1939,22 @@
             right_t=vmem((384, total), LOW),
             value_t=vmem((128, total), LOW),
             kept=vmem((total, 128), HIGH),
-            x_all=vmem((total, width), LOW),
-            w_qkv=vmem((3, 2, CHIPS, depth, half_width), LOW),
-            g_down=vmem((CHIPS,) + down_block, LOW),
-            g_in=vmem((2, CHIPS, depth, half_hidden), LOW),
+            x_all=vmem(x_block, LOW),
+            w_all=vmem(w_block, LOW),
+            w_in=vmem(in_all, LOW),
+            w_down=vmem(down_all, LOW),
+            w_out=vmem(out_all, LOW),
             g_out=vmem((CHIPS,) + out_block, LOW),
+            context=vmem((both, half_width), LOW),
+            context_wide=vmem((both, half_width), HIGH),
+            low_first=vmem((both, width), LOW),
+            act=vmem((both, half_hidden), LOW),
+            slope=vmem((both, half_hidden), HIGH),
+            d_second=vmem((both, width), LOW),
+            d_branch=vmem((both, width), LOW),
+            d_sum1=vmem((slot_rows, width), HIGH),
+            out_part=vmem((slot_rows, width), HIGH),
+            in_part=vmem((slot_rows, width), HIGH),
             in_1=vmem((8,) + in_block, LOW),
             in_2=vmem((4,) + in_block, LOW),
             in_3=vmem((3,) + in_block, LOW),
@@ -1791,26 +1968,24 @@
             in_far=vmem((depth, half_hidden), HIGH),
             small_sum=vmem((16, half_hidden), HIGH),
             small_in=vmem((6, 16, half_hidden), HIGH),
+            d_message=vmem(message, LOW),
             d_arrived=vmem(message, LOW),
             d_context=vmem((total, 128), HIGH),
-            d_query=vmem((total, 128), HIGH),
-            d_query_t=vmem((3 * HD, total), LOW),
+            d_heads=vmem((3, HD, total), LOW),
             d_pair_t=vmem((2 * HD, total), HIGH),
+            d_both=vmem((3, 2, HD, total // 2), LOW),
+            d_x=vmem(x_block, LOW),
+            x_stage=vmem((3, 7, slot_rows // 3, width), LOW),
+            x_total=vmem((slot_rows, width), LOW),
+            x_came=vmem((slot_rows, width), LOW),
             rel_grad=vmem((2 * depth, 4 * NB), HIGH),
-            rel_far=vmem((depth, 4 * NB), HIGH),
-            rel_sum=vmem((depth, 4 * NB), HIGH),
-            rel_came=vmem((depth, 4 * NB), HIGH),
-            message=vmem(out_message, LOW),
-            tokens_in=vmem(out_message, LOW),
-            w_mine=vmem((2, 3 * HD, half_width), HIGH),
-            w_far=vmem((3 * HD, half_width), HIGH),
-            w_low=vmem((CHIPS, depth, 4 * HD), LOW),
-            w_came=vmem((CHIPS, depth, 4 * HD), LOW),
-            wide=vmem((both, half_width), HIGH),
-            low=vmem((3, both, half_width), LOW),
-            out_part=vmem((slot_rows, width), HIGH),
-            in_part=vmem((slot_rows, width), HIGH),
-            keep_sem=dma((11,)),
+            rel_came=vmem((2, depth, 4 * NB), HIGH),
+            w_mine=vmem((2, 6 * HD, half_width), HIGH),
+            w_far=vmem((6 * HD, half_width), HIGH),
+            w_low=vmem((CHIPS, depth, 6 * HD), LOW),
+            w_came=vmem((CHIPS, depth, 6 * HD), LOW),
+            keep_sem=dma((15,)),
+            home_sem=dma((2,)),
             d_send=dma((16,)),
             d_recv=dma((16,)),
             in_send=dma((16,)),
@@ -1821,32 +1996,34 @@
             out_recv=dma((16,)),
             small_send=dma((6,)),
             small_recv=dma((6,)),
-            msg_send=dma((16,)),
-            msg_recv=dma((16,)),
+            x_send=dma((3, 8)),
+            x_recv=dma((3, 8)),
             w_send=dma((16,)),
             w_recv=dma((16,)),
-            rel_send=dma((1,)),
-            rel_recv=dma((1,)),
-            pair_send=dma((4,)),
-            pair_recv=dma((4,)),
+            rel_send=dma((2,)),
+            rel_recv=dma((2,)),
+            pair_send=dma((6,)),
+            pair_recv=dma((6,)),
         ),
     )
-    results = list(handed_over(
-        [
-            made.hidden_out,
-            ended.hidden_grad,
-            ended.qkv_grad,
-            ended.qkv_bias_grad,
-            ended.rel_tables_grad,
-            ended.out_grad,
-            ended.branch_grad,
-            ended.gain_grad,
-            ended.shift_grad,
-            ended.in_grad,
-            ended.bias_grad,
-            ended.down_grad,
-        ]
-    ))
+    results = list(
+        handed_over(
+            [
+                made.hidden_out,
+                ended.hidden_grad,
+                ended.qkv_grad,
+                ended.qkv_bias_grad,
+                ended.rel_tables_grad,
+                ended.out_grad,
+                ended.branch_grad,
+                ended.gain_grad,
+                ended.shift_grad,
+                ended.in_grad,
+                ended.bias_grad,
+                ended.down_grad,
+            ]
+        )
+    )
     results[4] = results[4].transpose(0, 2, 1)
     results[10] = results[10].reshape(down_rows)
     return tuple(results)

time: 318 us -> 296 us (0.931)
  Pallas kernels: 317 us -> 295 us
    pallas_call x2, Pallas kernels: 314 us -> 292 us  [call(): pl.pallas_call(functools.partial(kernel, names), out_shape=[jax.ShapeDtyp...]
where the time goes in v4:
time: 296 us
  Pallas kernels  295 us (100%)
    pallas_call x2, Pallas kernels, call(): pl.pallas_call(functools.partial(kernel, names), out_shape=[jax.ShapeDtyp...  292 us

profile of v4, /device:TPU:1, one launch (start us, length us, event | category | flops | bytes accessed | tf_op | source)
XLA Modules:
  0.0 295.7 jit_solution(12461730953842970529)
XLA Ops:
  0.7 145.0 %forward_pass.1 = (bf16[136,1024]{1,0:T(8,128)(2,1)}, bf16[8,144,1024]{2,1,0:T(8,128)(2,1)}, bf16[3,2,16,32,128]{4,3,2,1,0:T(8,128)(2,1)}, bf16[64,512]{1,0:T(8,...) custom-call(bf16[136,1024]{1,0:T(8,128)(2,1)} %refs_0_.1, ...), custom_call_target="tpu_custom_call" | custom-call | tf_op jit(solution)/shard_map/forward_pass/pallas_call | solution.py:1752
  145.6 147.0 %backward_pass.1 = (bf16[136,1024]{1,0:T(8,128)(2,1)}, f32[3,32,1024]{2,1,0:T(8,128)}, f32[2,32]{1,0:T(2,128)}, f32[3,32,128]{2,1,0:T(8,128)}, f32[32,1024]{1,0:...) custom-call(bf16[2304,384]{1,0:T(8,128)(2,1)} %get-tuple-element.58., ...), custom_call_target="tpu_custom_call" | custom-call | tf_op jit(solution)/shard_map/backward_pass/pallas_call | solution.py:1752
  292.7 3.0 %hand_over.1 = (bf16[136,1024]{1,0:T(8,128)(2,1)}, bf16[136,1024]{1,0:T(8,128)(2,1)}, f32[3,32,1024]{2,1,0:T(8,128)}, f32[2,32]{1,0:T(2,128)}, f32[3,32,128]{2,1...) custom-call(bf16[136,1024]{1,0:T(8,128)(2,1)} %get-tuple-element.57., ...), custom_call_target="tpu_custom_call" | custom-call | tf_op jit(solution)/shard_map/hand_over/pallas_call | solution.py:1743

commit v5 on v4

--- a/solution.py
+++ b/solution.py
@@ -395,7 +395,7 @@
     return lax.div(chip, 4), lax.rem(lax.div(chip, 2), 2), lax.rem(chip, 2)
 
 
-def meet():
+def greet_all():
     core, chip = place()
     me = core * CHIPS + chip
     barrier = pltpu.get_barrier_semaphore()
@@ -411,7 +411,10 @@
         return carry
 
     lax.fori_loop(1, 2 * CHIPS, greet, 0)
-    pl.semaphore_wait(barrier, 2 * CHIPS - 1)
+
+
+def await_all():
+    pl.semaphore_wait(pltpu.get_barrier_semaphore(), 2 * CHIPS - 1)
 
 
 def remote(source, target, send, recv, device):
@@ -429,10 +432,18 @@
     return pltpu.make_async_copy(source, target, sem)
 
 
+MIRROR = 3
+
+
+def in_the_middle():
+    z, _, _ = coordinates(lax.axis_index("blk"))
+    return jnp.logical_and(z > 0, z < 3)
+
+
 def neighbours(across):
     core, chip = place()
     z, y, x = coordinates(chip)
-    planes = (z + 1 - 2 * lax.rem(z, 2), 2 - lax.div(z, 2), 3 - 3 * lax.div(z, 2))
+    planes = (z + 1 - 2 * lax.rem(z, 2), 2 - lax.div(z, 2), 3 - 3 * lax.div(z, 2), 3 - z)
 
     def slot(far_p, far_q, line):
         far_y, far_x = (far_q, far_p) if across == "x" else (far_p, far_q)
@@ -447,7 +458,7 @@
         self.send, self.recv, self.made = send, recv, []
         self.core = lax.axis_index("grp")
 
-    def ship(self, source, target, recv_index, to):
+    def ship(self, source, target, recv_index, to, when=None):
         index = len(self.made)
 
         def make():
@@ -455,34 +466,48 @@
                 source(), target(), self.send.at[index], self.recv.at[recv_index()], (self.core, to())
             )
 
-        self.made.append(make)
-        make().start()
+        self.made.append((make, when))
+        self.on(when, lambda: make().start())
+
+    @staticmethod
+    def on(when, act):
+        if when is None:
+            act()
+        else:
+            pl.when(when)(act)
 
     def landed(self, target, recv_index, near):
         remote(target, target, self.send.at[0], self.recv.at[recv_index], (self.core, near)).wait_recv()
 
-    def all_sent(self, count=15):
+    def all_sent(self, count):
         assert len(self.made) == count
-        for make in self.made:
-            make().wait_send()
+        for make, when in self.made:
+            self.on(when, lambda make=make: make().wait_send())
 
 
 class Gather:
     def __init__(self, pick, send, recv, across):
         self.pick, self.at = pick, neighbours(across)
         self.moves = Shipments(send, recv)
-
-    def ship(self, what, to):
+        self.middle = in_the_middle()
+
+    def ship(self, what, to, when=None):
         slot = lambda: self.at(*what)
         ref = lambda: self.pick(slot())
-        self.moves.ship(ref, ref, slot, lambda: self.at(*to))
+        self.moves.ship(ref, ref, slot, lambda: self.at(*to), when)
 
     def landed(self, *what):
         slot = self.at(*what)
         self.moves.landed(self.pick(slot), slot, self.at(1, 0, None))
 
-    def own_line(self, line):
-        self.ship((0, 0, None), (0, 0, line))
+    def pass_on(self, what, line):
+        self.ship(what, (0, 0, MIRROR if line == 0 else 0), self.middle)
+
+    def own_line(self, number):
+        if number == 0:
+            self.ship((0, 0, None), (0, 0, 0))
+        else:
+            self.ship((0, 0, None), (0, 0, MIRROR), self.middle)
 
     def own_plane(self):
         self.ship((0, 0, None), (1, 0, None))
@@ -490,6 +515,7 @@
 
     def line(self, line):
         self.landed(0, 0, line)
+        self.pass_on((0, 0, line), line)
         self.ship((0, 0, line), (1, 0, None))
         self.ship((0, 0, line), (0, 1, None))
 
@@ -503,13 +529,14 @@
                 self.landed(far_p, 1, line)
 
     def finish(self):
-        self.moves.all_sent()
+        self.moves.all_sent(17)
 
 
 class GatherLate(Gather):
+    PLANE = ((0, 0), (1, 0), (0, 1), (1, 1))
+
     def first(self):
-        self.ship((0, 0, None), (1, 0, None))
-        self.ship((0, 0, None), (0, 1, None))
+        self.own_plane()
 
     def second(self):
         self.landed(1, 0, None)
@@ -518,14 +545,18 @@
     def third(self):
         for far_p in (0, 1):
             self.landed(far_p, 1, None)
-        for line in range(3):
-            for what in ((0, 0), (1, 0), (0, 1), (1, 1)):
-                self.ship(what + (None,), (0, 0, line))
-
-    def arrive(self):
-        for line in range(3):
-            for what in ((0, 0), (1, 0), (0, 1), (1, 1)):
-                self.landed(*what, line)
+        for what in self.PLANE:
+            self.ship(what + (None,), (0, 0, 0))
+        for what in self.PLANE:
+            self.ship(what + (None,), (0, 0, MIRROR), self.middle)
+
+    def late_line(self, line):
+        for what in self.PLANE:
+            self.landed(*what, line)
+            self.pass_on(what + (line,), line)
+
+    def finish(self):
+        self.moves.all_sent(23)
 
 
 class Reduce:
@@ -592,7 +623,7 @@
         for ahead in range(3):
             self.landed(self.third_in.at[ahead], 12 + ahead)
             result[...] += self.third_in[ahead].astype(HIGH)
-        self.moves.all_sent()
+        self.moves.all_sent(15)
 
 
 class ReduceEarly(Reduce):
@@ -641,7 +672,7 @@
         self.landed(self.second.at[0], 12)
         self.landed(self.third_in.at[0], 14)
         result[...] = total + self.second[0].astype(HIGH) + self.third_in[0].astype(HIGH)
-        self.moves.all_sent()
+        self.moves.all_sent(15)
 
 
 def cube_of(order):
@@ -880,6 +911,8 @@
     other = 1 - core
     me = core * CHIPS + chip
     keep = r.keep_sem
+
+    greet_all()
 
     loads = [
         local(r.ffn_in.at[:, columns_of(core, half_hidden)], w_in.at[core, chip], keep.at[0]),
@@ -925,7 +958,7 @@
     ]
     for copy in loads[3:]:
         copy.start()
-    meet()
+    await_all()
 
     at_home = group == core
     away = lax.rem(chip + HALF, CHIPS)
@@ -964,8 +997,6 @@
             (core, to),
         )
 
-    for ahead in range(1, CHIPS):
-        w_copy(ahead).start()
     swap_in = remote(
         r.ffn_in.at[:, columns_of(other, half_hidden)],
         w_in.at[core, chip],
@@ -985,11 +1016,6 @@
         )
         for part, order in enumerate(("xyz", "yzx", "zxy"))
     ]
-    home().wait()
-    each(x_plans, CubeGather.own)
-    each(x_plans, CubeGather.one)
-    each(x_plans, CubeGather.two)
-
     half = width // 2
     half_tile = half_hidden // 2
     plan_out = GatherLate(lambda slot: w_out.at[slot], r.out_send, r.out_recv, "x")
@@ -1004,15 +1030,25 @@
 
     plans_in = halves(lambda slot, columns: w_in.at[:, slot, :, columns], half_tile, r.in_send, r.in_recv)
     plans_down = halves(lambda slot, columns: w_down.at[slot, :, columns], half, r.down_send, r.down_recv)
+
+    for ahead in range(1, CHIPS):
+        w_copy(ahead).start()
     for copy in loads:
         copy.wait()
+    each(plans_down, Gather.own_plane)
     swap_in.wait()
-    each(plans_in, Gather.own_line, 0)
     each(plans_in, Gather.own_plane)
     plan_out.first()
-    each(plans_in, Gather.own_line, 1)
-    each(plans_in, Gather.own_line, 2)
-
+    each(plans_in, Gather.own_line, 0)
+    home().wait()
+    each(x_plans, CubeGather.own)
+    each(x_plans, CubeGather.one)
+    each(plans_down, Gather.own_line, 1)
+    plan_out.second()
+    each(x_plans, CubeGather.two)
+    each(plans_down, Gather.own_line, 0)
+    plan_out.third()
+    each(plans_in, Gather.line, 0)
     for ahead in range(1, CHIPS):
         came = lax.rem(chip + ahead, CHIPS)
         remote(
@@ -1101,24 +1137,16 @@
     left, right, right_t = r.left, r.right, r.right_t
     value, value_t, kept = r.value, r.value_t, r.kept
     pair_qkv.wait()
+    each(plans_in, Gather.own_line, 1)
+    each(plans_in, Gather.side, None)
 
     def prepare(index, carry):
         rows = pl.ds(pl.multiple_of(index * BLOCK, BLOCK), BLOCK)
         at_steps(
             index,
             {
-                1: [
-                    lambda: each(plans_in, Gather.side, None),
-                    plan_out.second,
-                    lambda: each(plans_down, Gather.own_line, 0),
-                    lambda: each(plans_down, Gather.own_plane),
-                ],
-                4: [lambda: each(plans_in, Gather.line, 0), plan_out.third],
-                7: [
-                    lambda: each(plans_in, Gather.side, 0),
-                    lambda: each(plans_down, Gather.own_line, 1),
-                    lambda: each(plans_down, Gather.own_line, 2),
-                ],
+                3: [lambda: each(plans_down, Gather.side, None), lambda: each(plans_down, Gather.line, 1)],
+                4: [lambda: each(plans_in, Gather.side, 0), lambda: each(plans_down, Gather.line, 0)],
             },
         )
         query_value = near[rows, 0:128].astype(HIGH)
@@ -1176,9 +1204,9 @@
         at_steps(
             index,
             {
-                0: [lambda: each(plans_in, Gather.line, 1), lambda: each(plans_down, Gather.side, None)],
-                3: [lambda: each(plans_in, Gather.side, 1)],
-                6: [lambda: each(plans_in, Gather.line, 2), lambda: each(plans_down, Gather.line, 0)],
+                1: [lambda: each(plans_in, Gather.line, 2)],
+                5: [lambda: each(plans_in, Gather.line, 1)],
+                6: [lambda: plan_out.late_line(0)],
             },
         )
         logits = dot(left[rows, :], right_t[...])
@@ -1200,12 +1228,13 @@
     for slot in range(CHIPS):
         message[slot] = fold(kept[slot * slot_rows : (slot + 1) * slot_rows, :])
     context_arrives, context_sent = to_tokens(message, context_in, r.msg_send, r.msg_recv)
-    each(plans_in, Gather.side, 2)
+    each(plans_down, Gather.side, 1)
+    each(plans_down, Gather.line, 2)
+    plan_out.late_line(1)
     each(plans_down, Gather.side, 0)
-    each(plans_down, Gather.line, 1)
-    each(plans_down, Gather.side, 1)
-
-    plan_out.arrive()
+    each(plans_in, Gather.side, 1)
+    plan_out.late_line(2)
+
     keep_out = local(w_out, r.w_out_out, keep.at[13])
     keep_out.start()
     shares, bias_in = r.shares, r.bias_in
@@ -1223,7 +1252,9 @@
         shares.at[core], shares.at[core], r.pair_send.at[5], r.pair_recv.at[5], (other, chip)
     )
     pair_small.start()
+    each(plans_in, Gather.side, 2)
     context_arrives()
+    each(plans_down, Gather.side, 2)
 
     context_wide, context, low_first = r.context_wide, r.context, r.low_first
     act, slope = r.act, r.slope
@@ -1279,8 +1310,6 @@
     copy = swap(low_first.at[own], low_first.at[own])
     r.normed1[...] = normed1
     r.inverse1[...] = jnp.broadcast_to(inverse1, r.inverse1.shape)
-    each(plans_down, Gather.line, 2)
-    each(plans_down, Gather.side, 2)
     each(plans_in, Gather.arrive)
     keep_in = local(w_in, r.w_in_out, keep.at[16])
     keep_in.start()
@@ -1315,9 +1344,9 @@
     low_second = d_sum2.astype(LOW)
     r.d_second_out[...] = low_second
     g_small[...] = jnp.zeros_like(g_small)
-    g_small[1:2, 0:width] = column_sums(low_second.astype(HIGH))
-    g_small[3:4, 0:width] = column_sums(upstream * normed2)
-    g_small[5:6, 0:width] = column_sums(upstream)
+    g_small[1:2, :] = column_sums(low_second.astype(HIGH))
+    g_small[3:4, :] = column_sums(upstream * normed2)
+    g_small[5:6, :] = column_sums(upstream)
 
     for ahead in range(1, CHIPS):
         w_copy(ahead).wait_send()
@@ -1325,7 +1354,8 @@
     pl.when(jnp.logical_not(at_home))(lambda: abroad().wait_send())
     context_sent()
     each(x_plans, CubeGather.finish)
-    each(plans_in + plans_down + [plan_out], Gather.finish)
+    each(plans_in + plans_down, Gather.finish)
+    plan_out.finish()
     for copy in stash + [
         keep_x,
         keep_rel,
@@ -1383,7 +1413,8 @@
     ]
     for copy in loads:
         copy.start()
-    meet()
+    greet_all()
+    await_all()
     count = [0]
 
     def swap(source, target):
@@ -1427,7 +1458,6 @@
         r.out_recv,
         "y",
     )
-    plans = (plan_down, plan_in)
 
     d_second[own, :] = r.d_second_own[...]
     copy = swap(r.d_second_own, d_second.at[own])
@@ -1442,7 +1472,15 @@
         columns = pl.ds(pl.multiple_of(index * tile, tile), tile)
         rows = pl.ds(index * slots, slots)
         low = (dot(d_second[...], w_down[rows].reshape(tile, width), NT) * slope[:, columns]).astype(LOW)
-        small_sum[pl.ds(8, 1), columns] = column_sums(low.astype(HIGH))
+        turns = width // tile
+        bias_sums = column_sums(low.astype(HIGH))
+        bias_columns = pl.ds(pl.multiple_of(lax.rem(index, turns) * tile, tile), tile)
+        for row in range(half_hidden // width):
+
+            @pl.when(lax.div(index, turns) == row)
+            def _():
+                small_sum[6 + row : 7 + row, bias_columns] = bias_sums
+
         w_down[rows] = (
             dot(act[:, columns], d_second[...], TN).astype(LOW).reshape(slots, tile // slots, width)
         )
@@ -1468,7 +1506,6 @@
         return carry
 
     lax.fori_loop(0, width // 256, widen_grad, 0)
-    plan_in.start(2)
     copy.wait()
     d_sum2, gains = r.d_sum2, r.gains
     d_first = d_sum2[...] + mine + in_part[...]
@@ -1477,9 +1514,9 @@
     d_branch[own, :] = low_branch
     copy = swap(d_branch.at[own], d_branch.at[own])
     r.d_sum1[...] = d_sum1
-    small_sum[0:1, 0:width] = column_sums(low_branch.astype(HIGH))
-    small_sum[2:3, 0:width] = column_sums(d_first * r.normed1[...])
-    small_sum[4:5, 0:width] = column_sums(d_first)
+    small_sum[0:1, :] = column_sums(low_branch.astype(HIGH))
+    small_sum[2:3, :] = column_sums(d_first * r.normed1[...])
+    small_sum[4:5, :] = column_sums(d_first)
     for load in loads[5:7]:
         load.wait()
     copy.wait()
@@ -1494,8 +1531,6 @@
     d_arrived = r.d_arrived
     grad_arrives, grad_sent = to_heads(r.d_message, d_arrived, r.d_send, r.d_recv)
     r.g_out[...] = dot(context[...], d_branch[...], TN).astype(LOW).reshape(r.g_out.shape)
-    each(plans, Reduce.start, 1)
-    plan_out.start()
 
     z, y, x = coordinates(chip)
     small_in = r.small_in
@@ -1524,15 +1559,22 @@
         for copy in small_turn(index):
             copy.wait()
         if index == 0:
-            small_sum[0:8, :] += small_in[0, 0:8, :]
+            small_sum[0:6, :] += small_in[0, 0:6, :]
         elif index < 3:
             small_sum[...] += small_in[index]
 
     small_start(0)
-    each(plans, Reduce.side, 2)
+    plan_down.side(2)
+    plan_down.start(1)
+    small_end(0)
+    plan_in.start(2)
     left_half = lanes(half_slot) < HD
     d_context = r.d_context
     grad_arrives()
+    plan_down.start(0)
+    plan_out.start()
+    small_start(1)
+    plan_in.start(0)
     for slot in range(CHIPS):
         both = d_arrived[slot].astype(HIGH)[:half_slot]
         top = slot * slot_rows
@@ -1552,22 +1594,13 @@
         at_steps(
             index,
             {
-                0: [
-                    lambda: each(plans, Reduce.line, 2),
-                    lambda: each(plans, Reduce.start, 0),
-                    lambda: small_end(0),
-                    lambda: small_start(1),
-                ],
-                2: [plan_out.third],
-                3: [
-                    lambda: each(plans, Reduce.side, 1),
-                    lambda: each(plans, Reduce.start, None),
-                    lambda: small_end(1),
-                    lambda: small_start(2),
-                ],
-                5: [plan_out.across],
-                6: [lambda: each(plans, Reduce.side, 0)],
-                8: [lambda: each(plans, Reduce.line, 1), lambda: small_end(2), lambda: small_start(3)],
+                1: [lambda: plan_in.side(2), lambda: plan_in.start(1)],
+                2: [lambda: plan_down.line(2), lambda: small_end(1), lambda: plan_down.side(0)],
+                3: [lambda: plan_in.side(0)],
+                5: [lambda: plan_in.line(2)],
+                6: [lambda: plan_in.line(0), lambda: plan_in.side(1)],
+                7: [lambda: plan_down.start(None)],
+                8: [lambda: plan_in.start(None)],
             },
         )
         facts = kept[rows, :]
@@ -1605,6 +1638,9 @@
         return carry
 
     lax.fori_loop(0, total // BLOCK, step, 0)
+    small_start(2)
+    plan_in.line(1)
+    plan_down.line(0)
 
     d_heads[1] = d_pair_t[0:HD, :].astype(LOW)
     d_heads[2] = d_pair_t[HD : 2 * HD, :].astype(LOW)
@@ -1657,14 +1693,21 @@
         )
         for part, order in enumerate(("xyz", "yzx", "zxy"))
     ]
+    plan_down.side(1)
     each(x_plans, CubeReduce.own)
+    small_end(2)
+    plan_down.line(1)
+    plan_out.third()
+    plan_out.across()
 
     w_grad = dot(d_columns, x_all[...].reshape(half_total, width))
     w_mine, w_far, w_low, w_came = r.w_mine, r.w_far, r.w_low, r.w_came
     for part in range(2):
         w_mine[part] = w_grad[:, part * half_width : (part + 1) * half_width]
     copy = swap(w_mine.at[other], w_far)
+    plan_in.side(None)
     each(x_plans, CubeReduce.one)
+    plan_down.side(None)
     copy.wait()
     w_sum = (w_mine[core] + w_far[...]).T
     for slot in range(CHIPS):
@@ -1679,8 +1722,12 @@
     for ahead in range(1, CHIPS):
         w_copy(ahead).start()
     each(x_plans, CubeReduce.two)
-    each(plans, Reduce.line, 0)
-    each(plans, Reduce.side, None)
+    plan_down.finish(r.down_grad)
+    small_start(3)
+    plan_out.finish(r.out_grad)
+    in_total, in_far = r.in_total, r.in_far
+    plan_in.finish(in_total)
+    in_pair = swap(in_total.at[other], in_far)
     x_total, x_came = r.x_total, r.x_came
     for part, plan in enumerate(x_plans):
         x_total[part * third : (part + 1) * third] = plan.arrive().astype(LOW)
@@ -1692,11 +1739,6 @@
     pl.when(at_home)(lambda: home().start())
     pl.when(jnp.logical_not(at_home))(lambda: abroad().start())
 
-    in_total, in_far = r.in_total, r.in_far
-    plan_in.finish(in_total)
-    in_pair = swap(in_total.at[other], in_far)
-    plan_down.finish(r.down_grad)
-    plan_out.finish(r.out_grad)
     in_grad = r.in_grad
     in_grad[:, columns_of(core, half_hidden)] = in_total[core]
     small_end(3)
@@ -1708,7 +1750,8 @@
     shares = pltpu.roll(small_all(pl.ds(0, 8), strip), 128 - lax.rem(me * depth, 128), 1)
     for number, result in enumerate((r.branch_grad, r.gain_grad, r.shift_grad)):
         result[...] = shares[2 * number : 2 * number + 2, 0:depth]
-    r.bias_grad[...] = small_all(pl.ds(8, 1), columns_of(chip, 128))
+    bias_strip = small_all(pl.ds(0, 8), columns_of(position, 128))
+    r.bias_grad[...] = jnp.where(group == 0, bias_strip[6:7], bias_strip[7:8])
     for slot in range(2):
         local(rel_grad.at[pl.ds(0, depth)], rel_came.at[slot], r.rel_recv.at[slot]).wait()
     rel_each(lambda copy: copy.wait_send(), False)
@@ -1837,7 +1880,7 @@
             d_sum2=((slot_rows, width), HIGH, vmem),
             d_second_out=((slot_rows, width), LOW, vmem),
             gains_out=((2, width), HIGH, vmem),
-            g_small=((16, half_hidden), HIGH, vmem),
+            g_small=((8, width), HIGH, vmem),
         ),
         dict(
             x_own=vmem((slot_rows, width), LOW),
@@ -1880,11 +1923,11 @@
             w_recv=dma((16,)),
             rel_send=dma((2,)),
             rel_recv=dma((2,)),
-            out_send=dma((16,)),
+            out_send=dma((24,)),
             out_recv=dma((16,)),
-            in_send=dma((2, 16)),
+            in_send=dma((2, 18)),
             in_recv=dma((2, 16)),
-            down_send=dma((2, 16)),
+            down_send=dma((2, 18)),
             down_recv=dma((2, 16)),
             msg_send=dma((16,)),
             msg_recv=dma((16,)),
@@ -1966,8 +2009,8 @@
             out_3=vmem((1,) + out_block, LOW),
             in_total=vmem(in_block, HIGH),
             in_far=vmem((depth, half_hidden), HIGH),
-            small_sum=vmem((16, half_hidden), HIGH),
-            small_in=vmem((6, 16, half_hidden), HIGH),
+            small_sum=vmem((8, width), HIGH),
+            small_in=vmem((6, 8, width), HIGH),
             d_message=vmem(message, LOW),
             d_arrived=vmem(message, LOW),
             d_context=vmem((total, 128), HIGH),

time: 296 us -> 250 us (0.84)
  Pallas kernels: 295 us -> 249 us
    pallas_call x2, Pallas kernels: 292 us -> 246 us  [call(): pl.pallas_call(functools.partial(kernel, names), out_shape=[jax.ShapeDtyp...]
where the time goes in v5:
time: 250 us
  Pallas kernels  249 us (100%)
    pallas_call x2, Pallas kernels, call(): pl.pallas_call(functools.partial(kernel, names), out_shape=[jax.ShapeDtyp...  246 us

profile of v5, /device:TPU:1, one launch (start us, length us, event | category | flops | bytes accessed | tf_op | source)
XLA Modules:
  0.0 250.1 jit_solution(18112882805306193181)
XLA Ops:
  0.7 116.9 %forward_pass.1 = (bf16[136,1024]{1,0:T(8,128)(2,1)}, bf16[8,144,1024]{2,1,0:T(8,128)(2,1)}, bf16[3,2,16,32,128]{4,3,2,1,0:T(8,128)(2,1)}, bf16[64,512]{1,0:T(8,...) custom-call(bf16[136,1024]{1,0:T(8,128)(2,1)} %refs_0_.1, ...), custom_call_target="tpu_custom_call" | custom-call | tf_op jit(solution)/shard_map/forward_pass/pallas_call | solution.py:1795
  117.6 129.5 %backward_pass.1 = (bf16[136,1024]{1,0:T(8,128)(2,1)}, f32[3,32,1024]{2,1,0:T(8,128)}, f32[2,32]{1,0:T(2,128)}, f32[3,32,128]{2,1,0:T(8,128)}, f32[32,1024]{1,0:...) custom-call(bf16[2304,384]{1,0:T(8,128)(2,1)} %get-tuple-element.58., ...), custom_call_target="tpu_custom_call" | custom-call | tf_op jit(solution)/shard_map/backward_pass/pallas_call | solution.py:1795
  247.1 3.0 %hand_over.1 = (bf16[136,1024]{1,0:T(8,128)(2,1)}, bf16[136,1024]{1,0:T(8,128)(2,1)}, f32[3,32,1024]{2,1,0:T(8,128)}, f32[2,32]{1,0:T(2,128)}, f32[3,32,128]{2,1...) custom-call(bf16[136,1024]{1,0:T(8,128)(2,1)} %get-tuple-element.57., ...), custom_call_target="tpu_custom_call" | custom-call | tf_op jit(solution)/shard_map/hand_over/pallas_call | solution.py:1786

commit v6 on v5

--- a/solution.py
+++ b/solution.py
@@ -896,7 +896,7 @@
 GAIN_AT, SHIFT_AT, BIAS_AT = 128, 256, 384
 
 
-def first_kernel(names, *refs):
+def layer_kernel(names, *refs):
     r = types.SimpleNamespace(**dict(zip(names, refs)))
     hidden, x_all, w_all, rel_all = r.hidden_in, r.x_all, r.w_all, r.rel_all
     token_rows, width = hidden.shape
@@ -1063,6 +1063,7 @@
     )
     pair_bias.start()
     each(x_plans, CubeGather.arrive)
+    pl.when(jnp.logical_not(at_home))(lambda: abroad().wait_send())
 
     labels = r.labels
     first_slot = core * HALF
@@ -1072,14 +1073,8 @@
     pair_label.start()
     own_label = local(label_part, label_slots, keep.at[5])
     own_label.start()
-    keep_x = local(x_all, r.x_out, keep.at[6])
-    keep_x.start()
-    keep_rel = local(rel_all, r.rel_out, keep.at[7])
-    keep_rel.start()
     pair_w.wait()
     pair_bias.wait()
-    keep_w = local(w_all, r.w_all_out, keep.at[15])
-    keep_w.start()
 
     head_rows = 2 * depth
     row_at = lax.broadcasted_iota(jnp.int32, (head_rows, 128), 0)
@@ -1185,20 +1180,6 @@
         return carry
 
     lax.fori_loop(0, total // BLOCK, prepare, 0)
-    stash = [
-        local(held, out, keep.at[8 + k])
-        for k, (held, out) in enumerate(
-            (
-                (left, r.left_out),
-                (right, r.right_out),
-                (right_t, r.right_t_out),
-                (value_t, r.value_t_out),
-            )
-        )
-    ]
-    for copy in stash:
-        copy.start()
-
     def attend(index, carry):
         rows = pl.ds(pl.multiple_of(index * BLOCK, BLOCK), BLOCK)
         at_steps(
@@ -1222,8 +1203,6 @@
         return carry
 
     lax.fori_loop(0, total // BLOCK, attend, 0)
-    keep_facts = local(kept, r.kept_out, keep.at[12])
-    keep_facts.start()
     message, context_in = r.message, r.context_in
     for slot in range(CHIPS):
         message[slot] = fold(kept[slot * slot_rows : (slot + 1) * slot_rows, :])
@@ -1235,8 +1214,6 @@
     each(plans_in, Gather.side, 1)
     plan_out.late_line(2)
 
-    keep_out = local(w_out, r.w_out_out, keep.at[13])
-    keep_out.start()
     shares, bias_in = r.shares, r.bias_in
     shares[core] = jnp.zeros(shares.shape[1:], HIGH)
     for slot in range(CHIPS):
@@ -1258,7 +1235,7 @@
 
     context_wide, context, low_first = r.context_wide, r.context, r.low_first
     act, slope = r.act, r.slope
-    out_part, in_part, g_small = r.out_part, r.in_part, r.g_small
+    out_part, in_part = r.out_part, r.in_part
     own = pl.ds(pl.multiple_of(core * slot_rows, 16), slot_rows)
     far = pl.ds(pl.multiple_of(other * slot_rows, 16), slot_rows)
     tile = 512
@@ -1285,37 +1262,27 @@
                 left_half, turn(even), odd
             )
     context[...] = context_wide[...].astype(LOW)
-    keep_context = local(context, r.context_out, keep.at[14])
-    keep_context.start()
-
-    def product(index, lhs, rhs):
-        out_part[index] = dot(lhs[far, :], rhs)
-        copy = swap(out_part.at[index], in_part.at[index])
+
+    def product(lhs, rhs):
+        out_part[...] = dot(lhs[far, :], rhs)
+        copy = swap(out_part, in_part)
         mine = dot(lhs[own, :], rhs)
         copy.wait()
-        return mine + in_part[index]
+        return mine + in_part[...]
 
     pair_small.wait()
     branch_bias, gains, shifts = (
         [jnp.concatenate([shares[0, number, k : k + 1], shares[1, number, k : k + 1]], axis=1) for k in range(2)]
         for number in range(3)
     )
-    for k in range(2):
-        r.gains_out[k : k + 1, :] = gains[k]
-    branch = product(0, context, w_out[:, 0:depth, :].reshape(half_width, width)) + branch_bias[0]
+    branch = product(context, w_out[:, 0:depth, :].reshape(half_width, width)) + branch_bias[0]
     row_index = lax.broadcasted_iota(jnp.int32, (slot_rows, 1), 0)
     x_mine = jnp.where(row_index < token_rows, x_own[...].astype(HIGH), 0.0)
     first, normed1, inverse1 = normalize(x_mine + branch, gains[0], shifts[0])
     low_first[own, :] = first.astype(LOW)
     copy = swap(low_first.at[own], low_first.at[own])
-    r.normed1[...] = normed1
-    r.inverse1[...] = jnp.broadcast_to(inverse1, r.inverse1.shape)
     each(plans_in, Gather.arrive)
-    keep_in = local(w_in, r.w_in_out, keep.at[16])
-    keep_in.start()
     copy.wait()
-    keep_first = local(low_first, r.low_first_out, keep.at[17])
-    keep_first.start()
 
     def widen(index, carry):
         columns = pl.ds(pl.multiple_of(index * tile, tile), tile)
@@ -1326,146 +1293,55 @@
         return carry
 
     lax.fori_loop(0, half_hidden // tile, widen, 0)
-    keep_act = local(act, r.act_out, keep.at[18])
-    keep_act.start()
-    keep_slope = local(slope, r.slope_out, keep.at[19])
-    keep_slope.start()
     each(plans_down, Gather.arrive)
-    keep_down = local(w_down, r.w_down_out, keep.at[20])
-    keep_down.start()
-    second = product(1, act, w_down[...].reshape(half_hidden, width)) + branch_bias[1]
+    second = product(act, w_down[...].reshape(half_hidden, width)) + branch_bias[1]
     result, normed2, inverse2 = normalize(first + second, gains[1], shifts[1])
     r.hidden_out[...] = result[:token_rows].astype(LOW)
     upstream = jnp.concatenate(
         [r.out_grad[...].astype(HIGH), jnp.zeros((slot_rows - token_rows, width), HIGH)], axis=0
     )
     d_sum2 = normalize_back(upstream, normed2, inverse2, gains[1])
-    r.d_sum2[...] = d_sum2
     low_second = d_sum2.astype(LOW)
-    r.d_second_out[...] = low_second
-    g_small[...] = jnp.zeros_like(g_small)
-    g_small[1:2, :] = column_sums(low_second.astype(HIGH))
-    g_small[3:4, :] = column_sums(upstream * normed2)
-    g_small[5:6, :] = column_sums(upstream)
-
-    for ahead in range(1, CHIPS):
-        w_copy(ahead).wait_send()
-    rel_each(lambda copy: copy.wait_send(), None)
-    pl.when(jnp.logical_not(at_home))(lambda: abroad().wait_send())
-    context_sent()
-    each(x_plans, CubeGather.finish)
-    each(plans_in + plans_down, Gather.finish)
-    plan_out.finish()
-    for copy in stash + [
-        keep_x,
-        keep_rel,
-        keep_w,
-        keep_facts,
-        keep_out,
-        keep_context,
-        keep_in,
-        keep_first,
-        keep_act,
-        keep_slope,
-        keep_down,
-    ]:
-        copy.wait()
-
-
-def second_kernel(names, *refs):
-    r = types.SimpleNamespace(**dict(zip(names, refs)))
-    core, chip = place()
-    group, position, _ = unit()
-    other = 1 - core
-    left, right, right_t, value_t, kept = r.left, r.right, r.right_t, r.value_t, r.kept
-    rel_all, x_all, w_all = r.rel_all, r.x_all, r.w_all
-    w_in, w_down, w_out = r.w_in, r.w_down, r.w_out
-    slot_rows, width = x_all.shape[1:]
-    total = CHIPS * slot_rows
+    d_second, small_sum = r.d_second, r.small_sum
+    d_second[own, :] = low_second
+    copy = swap(d_second.at[own], d_second.at[own])
+    small_sum[...] = jnp.zeros_like(small_sum)
+    small_sum[1:2, :] = column_sums(low_second.astype(HIGH))
+    small_sum[3:4, :] = column_sums(upstream * normed2)
+    small_sum[5:6, :] = column_sums(upstream)
+
     half_total = HALF * slot_rows
-    half_slot = slot_rows // 2
-    half_hidden = w_in.shape[3]
-    half_width = width // 2
-    depth = r.g_out.shape[1]
-    token_rows = r.hidden_grad.shape[0]
-    scale = 1.0 / math.sqrt(4.0 * HD)
-    keep = r.keep_sem
-    loads = [
-        local(there, held, keep.at[k])
-        for k, (there, held) in enumerate(
-            (
-                (r.w_down_any, w_down),
-                (r.act_any, r.act),
-                (r.slope_any, r.slope),
-                (r.w_in_any, w_in),
-                (r.low_first_any, r.low_first),
-                (r.w_out_any, w_out),
-                (r.context_any, r.context),
-                (r.left_any, left),
-                (r.right_t_any, right_t),
-                (r.value_t_any, value_t),
-                (r.kept_any, kept),
-                (r.right_any, right),
-                (r.x_any, x_all),
-                (r.w_all_any, w_all),
-            )
-        )
-    ]
-    for copy in loads:
-        copy.start()
-    greet_all()
-    await_all()
-    count = [0]
-
-    def swap(source, target):
-        copy = remote(
-            source, target, r.pair_send.at[count[0]], r.pair_recv.at[count[0]], (other, chip)
-        )
-        count[0] += 1
-        copy.start()
-        return copy
-
-    own = pl.ds(pl.multiple_of(core * slot_rows, 16), slot_rows)
-    far = pl.ds(pl.multiple_of(other * slot_rows, 16), slot_rows)
-    act, slope, low_first, context = r.act, r.slope, r.low_first, r.context
-    d_second, d_branch, context_wide = r.d_second, r.d_branch, r.context_wide
-    d_inner = act
-    out_part, in_part, small_sum = r.out_part, r.in_part, r.small_sum
-    plan_down = Reduce(
+    sum_down = Reduce(
         w_down,
         w_down,
         lambda ref, slot: ref.at[slot],
         [r.down_1, r.down_2, r.down_3],
-        r.down_send,
-        r.down_recv,
+        r.g_down_send,
+        r.g_down_recv,
         "y",
     )
-    plan_in = Reduce(
+    sum_in = Reduce(
         w_in,
         w_in,
         lambda ref, slot: ref.at[:, slot],
         [r.in_1, r.in_2, r.in_3],
-        r.in_send,
-        r.in_recv,
+        r.g_in_send,
+        r.g_in_recv,
         "x",
     )
-    plan_out = ReduceEarly(
+    sum_out = ReduceEarly(
         r.g_out,
         r.g_out,
         lambda ref, slot: ref.at[slot],
         [r.out_1, r.out_2, r.out_3],
-        r.out_send,
-        r.out_recv,
+        r.g_out_send,
+        r.g_out_recv,
         "y",
     )
 
-    d_second[own, :] = r.d_second_own[...]
-    copy = swap(r.d_second_own, d_second.at[own])
-    small_sum[...] = r.g_small[...]
-    for load in loads[0:3]:
-        load.wait()
+    d_inner = act
+    each(plans_in + plans_down, Gather.finish)
     copy.wait()
-    tile = 512
     slots = tile // w_down.shape[1]
 
     def narrow_back(index, carry):
@@ -1488,9 +1364,7 @@
         return carry
 
     lax.fori_loop(0, half_hidden // tile, narrow_back, 0)
-    plan_down.start(2)
-    for load in loads[3:5]:
-        load.wait()
+    sum_down.start(2)
     w_in_all = w_in[...].reshape(width, half_hidden)
     out_part[...] = dot(d_inner[far, :], w_in_all, NT)
     copy = swap(out_part, in_part)
@@ -1507,29 +1381,27 @@
 
     lax.fori_loop(0, width // 256, widen_grad, 0)
     copy.wait()
-    d_sum2, gains = r.d_sum2, r.gains
-    d_first = d_sum2[...] + mine + in_part[...]
-    d_sum1 = normalize_back(d_first, r.normed1[...], r.inverse1[:, 0:1], gains[0:1])
+    d_first = d_sum2 + mine + in_part[...]
+    d_sum1 = normalize_back(d_first, normed1, inverse1, gains[0])
     low_branch = d_sum1.astype(LOW)
+    d_branch = d_second
     d_branch[own, :] = low_branch
     copy = swap(d_branch.at[own], d_branch.at[own])
-    r.d_sum1[...] = d_sum1
+    out_part[...] = d_sum1
     small_sum[0:1, :] = column_sums(low_branch.astype(HIGH))
-    small_sum[2:3, :] = column_sums(d_first * r.normed1[...])
+    small_sum[2:3, :] = column_sums(d_first * normed1)
     small_sum[4:5, :] = column_sums(d_first)
-    for load in loads[5:7]:
-        load.wait()
     copy.wait()
     context_wide[...] = dot(d_branch[...], w_out[:, 0:depth, :].reshape(half_width, width), NT)
+    d_message, d_arrived = context_in, r.d_arrived
     for slot_group in range(2):
         for pair in range(HALF // 2):
             both = context_wide[
                 slot_group * slot_rows : (slot_group + 1) * slot_rows, pair * 128 : pair * 128 + 128
             ]
-            r.d_message[slot_group * HALF + 2 * pair] = fold(both)
-            r.d_message[slot_group * HALF + 2 * pair + 1] = fold(turn(both))
-    d_arrived = r.d_arrived
-    grad_arrives, grad_sent = to_heads(r.d_message, d_arrived, r.d_send, r.d_recv)
+            d_message[slot_group * HALF + 2 * pair] = fold(both)
+            d_message[slot_group * HALF + 2 * pair + 1] = fold(turn(both))
+    grad_arrives, grad_sent = to_heads(d_message, d_arrived, r.d_send, r.d_recv)
     r.g_out[...] = dot(context[...], d_branch[...], TN).astype(LOW).reshape(r.g_out.shape)
 
     z, y, x = coordinates(chip)
@@ -1564,43 +1436,37 @@
             small_sum[...] += small_in[index]
 
     small_start(0)
-    plan_down.side(2)
-    plan_down.start(1)
+    sum_down.side(2)
+    sum_down.start(1)
     small_end(0)
-    plan_in.start(2)
-    left_half = lanes(half_slot) < HD
-    d_context = r.d_context
+    sum_in.start(2)
+    d_context = meta
     grad_arrives()
-    plan_down.start(0)
-    plan_out.start()
+    sum_down.start(0)
+    sum_out.start()
     small_start(1)
-    plan_in.start(0)
+    sum_in.start(0)
     for slot in range(CHIPS):
         both = d_arrived[slot].astype(HIGH)[:half_slot]
         top = slot * slot_rows
         d_context[top : top + half_slot, :] = jnp.where(left_half, both, 0.0)
         d_context[top + half_slot : top + slot_rows, :] = jnp.where(left_half, turn(both), 0.0)
-    table_t = rel_all[:, 0 : 3 * NB]
-    lane = lanes(BLOCK)
-    first_half = lane < HD
     d_heads, d_pair_t, rel_grad = r.d_heads, r.d_pair_t, r.rel_grad
     d_pair_t[...] = jnp.zeros_like(d_pair_t)
     rel_grad[...] = jnp.zeros_like(rel_grad)
-    for load in loads[7:]:
-        load.wait()
 
     def step(index, carry):
         rows = pl.ds(pl.multiple_of(index * BLOCK, BLOCK), BLOCK)
         at_steps(
             index,
             {
-                1: [lambda: plan_in.side(2), lambda: plan_in.start(1)],
-                2: [lambda: plan_down.line(2), lambda: small_end(1), lambda: plan_down.side(0)],
-                3: [lambda: plan_in.side(0)],
-                5: [lambda: plan_in.line(2)],
-                6: [lambda: plan_in.line(0), lambda: plan_in.side(1)],
-                7: [lambda: plan_down.start(None)],
-                8: [lambda: plan_in.start(None)],
+                1: [lambda: sum_in.side(2), lambda: sum_in.start(1)],
+                2: [lambda: sum_down.line(2), lambda: small_end(1), lambda: sum_down.side(0)],
+                3: [lambda: sum_in.side(0)],
+                5: [lambda: sum_in.line(2)],
+                6: [lambda: sum_in.line(0), lambda: sum_in.side(1)],
+                7: [lambda: sum_down.start(None)],
+                8: [lambda: sum_in.start(None)],
             },
         )
         facts = kept[rows, :]
@@ -1639,8 +1505,8 @@
 
     lax.fori_loop(0, total // BLOCK, step, 0)
     small_start(2)
-    plan_in.line(1)
-    plan_down.line(0)
+    sum_in.line(1)
+    sum_down.line(0)
 
     d_heads[1] = d_pair_t[0:HD, :].astype(LOW)
     d_heads[2] = d_pair_t[HD : 2 * HD, :].astype(LOW)
@@ -1656,88 +1522,97 @@
     head = 2 * position + core
     rel_came = r.rel_came
 
-    def rel_each(act_remote, act_own):
+    def d_rel_each(act_remote, act_own):
         for side in range(2):
             to = (lax.div(position, 4), lax.rem(2 * head + side, CHIPS))
             itself = jnp.logical_and(to[0] == core, to[1] == chip)
             source = rel_grad.at[pl.ds(side * depth, depth)]
             act = lambda: act_remote(
-                remote(source, rel_came.at[group], r.rel_send.at[side], r.rel_recv.at[group], to)
+                remote(source, rel_came.at[group], r.d_rel_send.at[side], r.d_rel_recv.at[group], to)
             )
             pl.when(jnp.logical_not(itself))(act)
             if act_own:
-                pl.when(itself)(lambda: local(source, rel_came.at[group], r.rel_recv.at[group]).start())
-
-    rel_each(lambda copy: copy.start(), True)
+                pl.when(itself)(lambda: local(source, rel_came.at[group], r.d_rel_recv.at[group]).start())
+
+    d_rel_each(lambda copy: copy.start(), True)
     copy.wait()
     d_columns = d_both[...].reshape(6 * HD, half_total)
 
+    w_grad = dot(d_columns, x_all[...].reshape(half_total, width))
+
     w_heads = jnp.concatenate([w_all[n].reshape(width, 128) for n in range(3)], axis=1)
     d_rows = d_columns.T
-    d_x = r.d_x
-    pair_rows = 2 * slot_rows
+    d_x = x_all
+    each(x_plans, CubeGather.finish)
     for pair in range(HALF // 2):
         d_x[2 * pair : 2 * pair + 2] = (
             dot(d_rows[pair * pair_rows : (pair + 1) * pair_rows], w_heads, NT)
             .astype(LOW)
             .reshape(2, slot_rows, width)
         )
-    third = slot_rows // 3
-    x_plans = [
+    d_x_plans = [
         CubeReduce(
             lambda slot, part=part: d_x.at[slot, pl.ds(part * third, third)],
             r.x_stage.at[part],
-            r.x_send.at[part],
-            r.x_recv.at[part],
+            r.d_x_send.at[part],
+            r.d_x_recv.at[part],
             order,
         )
         for part, order in enumerate(("xyz", "yzx", "zxy"))
     ]
-    plan_down.side(1)
-    each(x_plans, CubeReduce.own)
+    sum_down.side(1)
+    each(d_x_plans, CubeReduce.own)
     small_end(2)
-    plan_down.line(1)
-    plan_out.third()
-    plan_out.across()
-
-    w_grad = dot(d_columns, x_all[...].reshape(half_total, width))
-    w_mine, w_far, w_low, w_came = r.w_mine, r.w_far, r.w_low, r.w_came
+    sum_down.line(1)
+    sum_out.third()
+    sum_out.across()
+
+    w_mine, w_far, w_low, w_came = slope, r.w_far, r.w_low, r.w_came
+    w_rows = 3 * HD
     for part in range(2):
-        w_mine[part] = w_grad[:, part * half_width : (part + 1) * half_width]
-    copy = swap(w_mine.at[other], w_far)
-    plan_in.side(None)
-    each(x_plans, CubeReduce.one)
-    plan_down.side(None)
-    copy.wait()
-    w_sum = (w_mine[core] + w_far[...]).T
+        w_mine[0:w_rows, part * width : (part + 1) * width] = w_grad[part * w_rows : (part + 1) * w_rows]
+
+    def w_columns(part, half):
+        return pl.ds(pl.multiple_of(part * width + half * half_width, 128), half_width)
+
+    w_swaps = [
+        swap(w_mine.at[pl.ds(0, w_rows), w_columns(part, other)], w_far.at[part]) for part in range(2)
+    ]
+    sum_in.side(None)
+    each(d_x_plans, CubeReduce.one)
+    sum_down.side(None)
+    for copy in w_swaps:
+        copy.wait()
+    w_sum = jnp.concatenate(
+        [(w_mine[0:w_rows, w_columns(part, core)] + w_far[part]).T for part in range(2)], axis=1
+    )
     for slot in range(CHIPS):
         w_low[slot] = w_sum[slot * depth : (slot + 1) * depth].astype(LOW)
 
-    def w_copy(ahead):
+    def d_w_copy(ahead):
         to = lax.rem(chip + ahead, CHIPS)
-        return remote(w_low.at[to], w_came.at[chip], r.w_send.at[ahead], r.w_recv.at[chip], (core, to))
-
-    own_w = local(w_low.at[chip], w_came.at[chip], keep.at[14])
-    own_w.start()
+        return remote(w_low.at[to], w_came.at[chip], r.d_w_send.at[ahead], r.d_w_recv.at[chip], (core, to))
+
+    own_d_w = local(w_low.at[chip], w_came.at[chip], keep.at[6])
+    own_d_w.start()
     for ahead in range(1, CHIPS):
-        w_copy(ahead).start()
-    each(x_plans, CubeReduce.two)
-    plan_down.finish(r.down_grad)
+        d_w_copy(ahead).start()
+    each(d_x_plans, CubeReduce.two)
+    sum_down.finish(r.down_grad)
     small_start(3)
-    plan_out.finish(r.out_grad)
+    sum_out.finish(r.out_w_grad)
     in_total, in_far = r.in_total, r.in_far
-    plan_in.finish(in_total)
+    sum_in.finish(in_total)
     in_pair = swap(in_total.at[other], in_far)
-    x_total, x_came = r.x_total, r.x_came
-    for part, plan in enumerate(x_plans):
+    x_total, x_came = x_own, r.x_came
+    for part, plan in enumerate(d_x_plans):
         x_total[part * third : (part + 1) * third] = plan.arrive().astype(LOW)
-    at_home = group == core
-    home = lambda: local(x_total, x_came, r.home_sem.at[1])
-    abroad = lambda: remote(
-        x_total, x_came, r.home_sem.at[0], r.home_sem.at[1], (other, lax.rem(chip + HALF, CHIPS))
-    )
-    pl.when(at_home)(lambda: home().start())
-    pl.when(jnp.logical_not(at_home))(lambda: abroad().start())
+    back = lambda: local(x_total, x_came, r.back_sem.at[1])
+    back_abroad = lambda: remote(
+        x_total, x_came, r.back_sem.at[0], r.back_sem.at[1], (other, lax.rem(chip + HALF, CHIPS))
+    )
+    pl.when(at_home)(lambda: back().start())
+    pl.when(jnp.logical_not(at_home))(lambda: back_abroad().start())
 
     in_grad = r.in_grad
     in_grad[:, columns_of(core, half_hidden)] = in_total[core]
@@ -1753,28 +1628,33 @@
     bias_strip = small_all(pl.ds(0, 8), columns_of(position, 128))
     r.bias_grad[...] = jnp.where(group == 0, bias_strip[6:7], bias_strip[7:8])
     for slot in range(2):
-        local(rel_grad.at[pl.ds(0, depth)], rel_came.at[slot], r.rel_recv.at[slot]).wait()
-    rel_each(lambda copy: copy.wait_send(), False)
+        local(rel_grad.at[pl.ds(0, depth)], rel_came.at[slot], r.d_rel_recv.at[slot]).wait()
+    d_rel_each(lambda copy: copy.wait_send(), False)
     rel_total = rel_came[0] + rel_came[1]
     for kind in range(3):
         r.rel_tables_grad[kind] = rel_total[:, kind * NB : (kind + 1) * NB]
     r.qkv_bias_grad[...] = rel_total[:, 3 * NB : 4 * NB].T[0:2]
-    own_w.wait()
+    own_d_w.wait()
     for ahead in range(1, CHIPS):
         came = lax.rem(chip + ahead, CHIPS)
-        remote(w_low.at[0], w_came.at[came], r.w_send.at[0], r.w_recv.at[came], (core, came)).wait_recv()
-        w_copy(ahead).wait_send()
+        remote(w_low.at[0], w_came.at[came], r.d_w_send.at[0], r.d_w_recv.at[came], (core, came)).wait_recv()
+        d_w_copy(ahead).wait_send()
     for pair in range(HALF):
         both = w_came[pair].astype(HIGH) + w_came[HALF + pair].astype(HIGH)
         for n in range(3):
             r.qkv_grad[n, :, pair * 128 : pair * 128 + 128] = both[:, n * 128 : n * 128 + 128]
-    home().wait()
-    pl.when(jnp.logical_not(at_home))(lambda: abroad().wait_send())
-    r.hidden_grad[...] = (r.d_sum1[...] + x_came[...].astype(HIGH))[:token_rows].astype(LOW)
+    back().wait()
+    pl.when(jnp.logical_not(at_home))(lambda: back_abroad().wait_send())
+    r.hidden_grad[...] = (out_part[...] + x_came[...].astype(HIGH))[:token_rows].astype(LOW)
     in_pair.wait()
     in_grad[:, columns_of(other, half_hidden)] = in_far[...]
     grad_sent()
-    each(x_plans, CubeReduce.finish)
+    each(d_x_plans, CubeReduce.finish)
+    for ahead in range(1, CHIPS):
+        w_copy(ahead).wait_send()
+    rel_each(lambda copy: copy.wait_send(), None)
+    context_sent()
+    plan_out.finish()
 
 
 def hand_over(count, *refs):
@@ -1837,9 +1717,10 @@
     x_block, w_block = (HALF, slot_rows, width), (3, 2, CHIPS, depth, 128)
     in_all, down_all = (2, CHIPS, depth, half_hidden), (CHIPS, down_rows, width)
     out_all = (CHIPS, depth + 16, width)
+    in_block, down_block, out_block = (2, depth, half_hidden), (down_rows, width), (depth, width)
     made = call(
-        first_kernel,
-        "forward_pass",
+        layer_kernel,
+        "layer",
         0,
         dict(
             hidden_in=(hidden_in, vmem),
@@ -1860,27 +1741,17 @@
         ),
         dict(
             hidden_out=((rows, width), LOW, vmem),
-            x_out=(x_block, LOW, any_),
-            w_all_out=(w_block, LOW, any_),
-            rel_out=((2 * depth, 4 * NB), LOW, any_),
-            left_out=((total, 384), LOW, any_),
-            right_out=((total, 384), LOW, any_),
-            right_t_out=((384, total), LOW, any_),
-            value_t_out=((128, total), LOW, any_),
-            kept_out=((total, 128), HIGH, any_),
-            w_in_out=(in_all, LOW, any_),
-            w_down_out=(down_all, LOW, any_),
-            w_out_out=(out_all, LOW, any_),
-            context_out=((both, half_width), LOW, any_),
-            low_first_out=((both, width), LOW, any_),
-            act_out=((both, half_hidden), LOW, any_),
-            slope_out=((both, half_hidden), HIGH, any_),
-            normed1=((slot_rows, width), HIGH, vmem),
-            inverse1=((slot_rows, 128), HIGH, vmem),
-            d_sum2=((slot_rows, width), HIGH, vmem),
-            d_second_out=((slot_rows, width), LOW, vmem),
-            gains_out=((2, width), HIGH, vmem),
-            g_small=((8, width), HIGH, vmem),
+            hidden_grad=((rows, width), LOW, vmem),
+            qkv_grad=((3, depth, width), HIGH, vmem),
+            qkv_bias_grad=((2, depth), HIGH, vmem),
+            rel_tables_grad=((3, depth, NB), HIGH, vmem),
+            out_w_grad=((depth, width), HIGH, vmem),
+            branch_grad=((2, depth), HIGH, vmem),
+            gain_grad=((2, depth), HIGH, vmem),
+            shift_grad=((2, depth), HIGH, vmem),
+            in_grad=((depth, hidden), HIGH, vmem),
+            bias_grad=((1, down_rows), HIGH, vmem),
+            down_grad=((down_rows, width), HIGH, vmem),
         ),
         dict(
             x_own=vmem((slot_rows, width), LOW),
@@ -1913,10 +1784,37 @@
             low_first=vmem((both, width), LOW),
             act=vmem((both, half_hidden), LOW),
             slope=vmem((both, half_hidden), HIGH),
-            out_part=vmem((2, slot_rows, width), HIGH),
-            in_part=vmem((2, slot_rows, width), HIGH),
-            keep_sem=dma((21,)),
+            out_part=vmem((slot_rows, width), HIGH),
+            in_part=vmem((slot_rows, width), HIGH),
+            d_second=vmem((both, width), LOW),
+            g_out=vmem((CHIPS,) + out_block, LOW),
+            in_1=vmem((8,) + in_block, LOW),
+            in_2=vmem((4,) + in_block, LOW),
+            in_3=vmem((3,) + in_block, LOW),
+            down_1=vmem((8,) + down_block, LOW),
+            down_2=vmem((4,) + down_block, LOW),
+            down_3=vmem((3,) + down_block, LOW),
+            out_1=vmem((12,) + out_block, LOW),
+            out_2=vmem((2,) + out_block, LOW),
+            out_3=vmem((1,) + out_block, LOW),
+            in_total=vmem(in_block, HIGH),
+            in_far=vmem((depth, half_hidden), HIGH),
+            small_sum=vmem((8, width), HIGH),
+            small_in=vmem((6, 8, width), HIGH),
+            d_arrived=vmem(message, LOW),
+            d_heads=vmem((3, HD, total), LOW),
+            d_pair_t=vmem((2 * HD, total), HIGH),
+            d_both=vmem((3, 2, HD, total // 2), LOW),
+            x_stage=vmem((3, 7, slot_rows // 3, width), LOW),
+            x_came=vmem((slot_rows, width), LOW),
+            rel_grad=vmem((2 * depth, 4 * NB), HIGH),
+            rel_came=vmem((2, depth, 4 * NB), HIGH),
+            w_far=vmem((2, 3 * HD, half_width), HIGH),
+            w_low=vmem((CHIPS, depth, 6 * HD), LOW),
+            w_came=vmem((CHIPS, depth, 6 * HD), LOW),
+            keep_sem=dma((7,)),
             home_sem=dma((2,)),
+            back_sem=dma((2,)),
             x_send=dma((3, 8)),
             x_recv=dma((3, 8)),
             w_send=dma((16,)),
@@ -1931,139 +1829,41 @@
             down_recv=dma((2, 16)),
             msg_send=dma((16,)),
             msg_recv=dma((16,)),
-            pair_send=dma((9,)),
-            pair_recv=dma((9,)),
-        ),
-    )
-    in_block, down_block, out_block = (2, depth, half_hidden), (down_rows, width), (depth, width)
-    ended = call(
-        second_kernel,
-        "backward_pass",
-        1,
-        dict(
-            left_any=(made.left_out, any_),
-            right_any=(made.right_out, any_),
-            right_t_any=(made.right_t_out, any_),
-            value_t_any=(made.value_t_out, any_),
-            kept_any=(made.kept_out, any_),
-            rel_all=(made.rel_out, vmem),
-            x_any=(made.x_out, any_),
-            w_all_any=(made.w_all_out, any_),
-            w_in_any=(made.w_in_out, any_),
-            w_down_any=(made.w_down_out, any_),
-            w_out_any=(made.w_out_out, any_),
-            context_any=(made.context_out, any_),
-            low_first_any=(made.low_first_out, any_),
-            act_any=(made.act_out, any_),
-            slope_any=(made.slope_out, any_),
-            normed1=(made.normed1, vmem),
-            inverse1=(made.inverse1, vmem),
-            d_sum2=(made.d_sum2, vmem),
-            d_second_own=(made.d_second_out, vmem),
-            gains=(made.gains_out, vmem),
-            g_small=(made.g_small, vmem),
-        ),
-        dict(
-            hidden_grad=((rows, width), LOW, vmem),
-            qkv_grad=((3, depth, width), HIGH, vmem),
-            qkv_bias_grad=((2, depth), HIGH, vmem),
-            rel_tables_grad=((3, depth, NB), HIGH, vmem),
-            out_grad=((depth, width), HIGH, vmem),
-            branch_grad=((2, depth), HIGH, vmem),
-            gain_grad=((2, depth), HIGH, vmem),
-            shift_grad=((2, depth), HIGH, vmem),
-            in_grad=((depth, hidden), HIGH, vmem),
-            bias_grad=((1, down_rows), HIGH, vmem),
-            down_grad=((down_rows, width), HIGH, vmem),
-        ),
-        dict(
-            left=vmem((total, 384), LOW),
-            right=vmem((total, 384), LOW),
-            right_t=vmem((384, total), LOW),
-            value_t=vmem((128, total), LOW),
-            kept=vmem((total, 128), HIGH),
-            x_all=vmem(x_block, LOW),
-            w_all=vmem(w_block, LOW),
-            w_in=vmem(in_all, LOW),
-            w_down=vmem(down_all, LOW),
-            w_out=vmem(out_all, LOW),
-            g_out=vmem((CHIPS,) + out_block, LOW),
-            context=vmem((both, half_width), LOW),
-            context_wide=vmem((both, half_width), HIGH),
-            low_first=vmem((both, width), LOW),
-            act=vmem((both, half_hidden), LOW),
-            slope=vmem((both, half_hidden), HIGH),
-            d_second=vmem((both, width), LOW),
-            d_branch=vmem((both, width), LOW),
-            d_sum1=vmem((slot_rows, width), HIGH),
-            out_part=vmem((slot_rows, width), HIGH),
-            in_part=vmem((slot_rows, width), HIGH),
-            in_1=vmem((8,) + in_block, LOW),
-            in_2=vmem((4,) + in_block, LOW),
-            in_3=vmem((3,) + in_block, LOW),
-            down_1=vmem((8,) + down_block, LOW),
-            down_2=vmem((4,) + down_block, LOW),
-            down_3=vmem((3,) + down_block, LOW),
-            out_1=vmem((12,) + out_block, LOW),
-            out_2=vmem((2,) + out_block, LOW),
-            out_3=vmem((1,) + out_block, LOW),
-            in_total=vmem(in_block, HIGH),
-            in_far=vmem((depth, half_hidden), HIGH),
-            small_sum=vmem((8, width), HIGH),
-            small_in=vmem((6, 8, width), HIGH),
-            d_message=vmem(message, LOW),
-            d_arrived=vmem(message, LOW),
-            d_context=vmem((total, 128), HIGH),
-            d_heads=vmem((3, HD, total), LOW),
-            d_pair_t=vmem((2 * HD, total), HIGH),
-            d_both=vmem((3, 2, HD, total // 2), LOW),
-            d_x=vmem(x_block, LOW),
-            x_stage=vmem((3, 7, slot_rows // 3, width), LOW),
-            x_total=vmem((slot_rows, width), LOW),
-            x_came=vmem((slot_rows, width), LOW),
-            rel_grad=vmem((2 * depth, 4 * NB), HIGH),
-            rel_came=vmem((2, depth, 4 * NB), HIGH),
-            w_mine=vmem((2, 6 * HD, half_width), HIGH),
-            w_far=vmem((6 * HD, half_width), HIGH),
-            w_low=vmem((CHIPS, depth, 6 * HD), LOW),
-            w_came=vmem((CHIPS, depth, 6 * HD), LOW),
-            keep_sem=dma((15,)),
-            home_sem=dma((2,)),
             d_send=dma((16,)),
             d_recv=dma((16,)),
-            in_send=dma((16,)),
-            in_recv=dma((16,)),
-            down_send=dma((16,)),
-            down_recv=dma((16,)),
-            out_send=dma((16,)),
-            out_recv=dma((16,)),
+            g_in_send=dma((16,)),
+            g_in_recv=dma((16,)),
+            g_down_send=dma((16,)),
+            g_down_recv=dma((16,)),
+            g_out_send=dma((16,)),
+            g_out_recv=dma((16,)),
             small_send=dma((6,)),
             small_recv=dma((6,)),
-            x_send=dma((3, 8)),
-            x_recv=dma((3, 8)),
-            w_send=dma((16,)),
-            w_recv=dma((16,)),
-            rel_send=dma((2,)),
-            rel_recv=dma((2,)),
-            pair_send=dma((6,)),
-            pair_recv=dma((6,)),
+            d_x_send=dma((3, 8)),
+            d_x_recv=dma((3, 8)),
+            d_w_send=dma((16,)),
+            d_w_recv=dma((16,)),
+            d_rel_send=dma((2,)),
+            d_rel_recv=dma((2,)),
+            pair_send=dma((16,)),
+            pair_recv=dma((16,)),
         ),
     )
     results = list(
         handed_over(
             [
                 made.hidden_out,
-                ended.hidden_grad,
-                ended.qkv_grad,
-                ended.qkv_bias_grad,
-                ended.rel_tables_grad,
-                ended.out_grad,
-                ended.branch_grad,
-                ended.gain_grad,
-                ended.shift_grad,
-                ended.in_grad,
-                ended.bias_grad,
-                ended.down_grad,
+                made.hidden_grad,
+                made.qkv_grad,
+                made.qkv_bias_grad,
+                made.rel_tables_grad,
+                made.out_w_grad,
+                made.branch_grad,
+                made.gain_grad,
+                made.shift_grad,
+                made.in_grad,
+                made.bias_grad,
+                made.down_grad,
             ]
         )
     )

time: 250 us -> 242 us (0.968)
  Pallas kernels: 249 us -> 241 us
    pallas_call x2 -> x1, Pallas kernels: 246 us -> 238 us  [call(): pl.pallas_call(functools.partial(kernel, names), out_shape=[jax.ShapeDtyp...]
where the time goes in v6:
time: 242 us
  Pallas kernels  241 us (100%)
    pallas_call x1, Pallas kernels, call(): pl.pallas_call(functools.partial(kernel, names), out_shape=[jax.ShapeDtyp...  238 us

profile of v6, /device:TPU:1, one launch (start us, length us, event | category | flops | bytes accessed | tf_op | source)
XLA Modules:
  0.0 242.1 jit_solution(7477826285257212361)
XLA Ops:
  0.7 238.4 %layer.1 = (bf16[136,1024]{1,0:T(8,128)(2,1)}, bf16[136,1024]{1,0:T(8,128)(2,1)}, f32[3,32,1024]{2,1,0:T(8,128)}, f32[2,32]{1,0:T(2,128)}, f32[3,32,128]{2,1,0:T...) custom-call(bf16[136,1024]{1,0:T(8,128)(2,1)} %refs_0_.1, ...), custom_call_target="tpu_custom_call" | custom-call | tf_op jit(solution)/shard_map/layer/pallas_call | solution.py:1675
  239.1 3.0 %hand_over.1 = (bf16[136,1024]{1,0:T(8,128)(2,1)}, bf16[136,1024]{1,0:T(8,128)(2,1)}, f32[3,32,1024]{2,1,0:T(8,128)}, f32[2,32]{1,0:T(2,128)}, f32[3,32,128]{2,1...) custom-call(bf16[136,1024]{1,0:T(8,128)(2,1)} %get-tuple-element.36., ...), custom_call_target="tpu_custom_call" | custom-call | tf_op jit(solution)/shard_map/hand_over/pallas_call | solution.py:1666

commit v7 on v6

--- a/solution.py
+++ b/solution.py
@@ -455,113 +455,116 @@
 
 class Shipments:
     def __init__(self, send, recv):
-        self.send, self.recv, self.made = send, recv, []
+        self.send, self.recv = send, recv
         self.core = lax.axis_index("grp")
 
-    def ship(self, source, target, recv_index, to, when=None):
-        index = len(self.made)
-
-        def make():
-            return remote(
-                source(), target(), self.send.at[index], self.recv.at[recv_index()], (self.core, to())
-            )
-
-        self.made.append((make, when))
-        self.on(when, lambda: make().start())
-
-    @staticmethod
-    def on(when, act):
+    def ship(self, source, target, kind, recv_index, to, when=None):
+        start = lambda: remote(
+            source, target, self.send.at[kind], self.recv.at[recv_index], (self.core, to)
+        ).start()
         if when is None:
-            act()
+            start()
         else:
-            pl.when(when)(act)
-
-    def landed(self, target, recv_index, near):
-        remote(target, target, self.send.at[0], self.recv.at[recv_index], (self.core, near)).wait_recv()
-
-    def all_sent(self, count):
-        assert len(self.made) == count
-        for make, when in self.made:
-            self.on(when, lambda make=make: make().wait_send())
+            pl.when(when)(start)
+
+    def landed(self, target, recv_index):
+        local(target, target, self.recv.at[recv_index]).wait()
+
+    def all_sent(self, bytes_of, kind):
+        local(bytes_of, bytes_of, self.send.at[kind]).wait()
 
 
 class Gather:
+    SENDS, RECEIVES = 2, 9
+
     def __init__(self, pick, send, recv, across):
         self.pick, self.at = pick, neighbours(across)
         self.moves = Shipments(send, recv)
         self.middle = in_the_middle()
 
-    def ship(self, what, to, when=None):
-        slot = lambda: self.at(*what)
-        ref = lambda: self.pick(slot())
-        self.moves.ship(ref, ref, slot, lambda: self.at(*to), when)
-
-    def landed(self, *what):
-        slot = self.at(*what)
-        self.moves.landed(self.pick(slot), slot, self.at(1, 0, None))
-
-    def pass_on(self, what, line):
-        self.ship(what, (0, 0, MIRROR if line == 0 else 0), self.middle)
+    def ship(self, what, kind, recv_index, to, when=None):
+        ref = self.pick(self.at(*what))
+        self.moves.ship(ref, ref, kind, recv_index, self.at(*to), when)
+
+    def plane(self, line):
+        return lax.div(self.at(0, 0, line), 4)
+
+    def along_z(self, line, to, when=None):
+        self.ship((0, 0, line), 0, self.plane(line), (0, 0, to), when)
+
+    def along_p(self, line):
+        self.ship((0, 0, line), 1, 4 + self.plane(line), (1, 0, None))
+
+    def along_q(self, far_p, line):
+        self.ship((far_p, 0, line), 1, 8, (0, 1, None))
 
     def own_line(self, number):
         if number == 0:
-            self.ship((0, 0, None), (0, 0, 0))
+            self.along_z(None, 0)
         else:
-            self.ship((0, 0, None), (0, 0, MIRROR), self.middle)
+            self.along_z(None, MIRROR, self.middle)
 
     def own_plane(self):
-        self.ship((0, 0, None), (1, 0, None))
-        self.ship((0, 0, None), (0, 1, None))
+        self.along_p(None)
+        self.along_q(0, None)
 
     def line(self, line):
-        self.landed(0, 0, line)
-        self.pass_on((0, 0, line), line)
-        self.ship((0, 0, line), (1, 0, None))
-        self.ship((0, 0, line), (0, 1, None))
+        self.moves.landed(self.pick(self.at(0, 0, line)), self.plane(line))
+        self.along_z(line, MIRROR if line == 0 else 0, self.middle)
+        self.along_p(line)
+        self.along_q(0, line)
 
     def side(self, line):
-        self.landed(1, 0, line)
-        self.ship((1, 0, line), (0, 1, None))
+        self.moves.landed(self.pick(self.at(1, 0, line)), 4 + self.plane(line))
+        self.along_q(1, line)
 
     def arrive(self):
-        for line in (None, 0, 1, 2):
-            for far_p in (0, 1):
-                self.landed(far_p, 1, line)
+        self.moves.landed(self.pick(pl.ds(0, 8)), 8)
 
     def finish(self):
-        self.moves.all_sent(17)
+        self.moves.all_sent(self.pick(pl.ds(0, 12)), 1)
+        pl.when(self.middle)(lambda: self.moves.all_sent(self.pick(pl.ds(0, 5)), 0))
+        pl.when(jnp.logical_not(self.middle))(lambda: self.moves.all_sent(self.pick(pl.ds(0, 1)), 0))
 
 
 class GatherLate(Gather):
-    PLANE = ((0, 0), (1, 0), (0, 1), (1, 1))
+    SENDS, RECEIVES = 3, 6
+
+    def plane_slots(self, line):
+        return self.pick(pl.ds(self.plane(line) * 4, 4))
 
     def first(self):
-        self.own_plane()
+        self.ship((0, 0, None), 0, 4, (1, 0, None))
+        self.ship((0, 0, None), 0, 5, (0, 1, None))
 
     def second(self):
-        self.landed(1, 0, None)
-        self.ship((1, 0, None), (0, 1, None))
+        self.moves.landed(self.pick(self.at(1, 0, None)), 4)
+        self.ship((1, 0, None), 0, 5, (0, 1, None))
+
+    def pass_plane(self, line, kind, to, when=None):
+        slots = self.plane_slots(line)
+        self.moves.ship(slots, slots, kind, self.plane(line), self.at(0, 0, to), when)
 
     def third(self):
-        for far_p in (0, 1):
-            self.landed(far_p, 1, None)
-        for what in self.PLANE:
-            self.ship(what + (None,), (0, 0, 0))
-        for what in self.PLANE:
-            self.ship(what + (None,), (0, 0, MIRROR), self.middle)
+        self.moves.landed(self.pick(pl.ds(0, 2)), 5)
+        self.pass_plane(None, 1, 0)
+        self.pass_plane(None, 2, MIRROR, self.middle)
 
     def late_line(self, line):
-        for what in self.PLANE:
-            self.landed(*what, line)
-            self.pass_on(what + (line,), line)
+        self.moves.landed(self.plane_slots(line), self.plane(line))
+        self.pass_plane(line, 2, MIRROR if line == 0 else 0, self.middle)
 
     def finish(self):
-        self.moves.all_sent(23)
+        self.moves.all_sent(self.pick(pl.ds(0, 3)), 0)
+        self.moves.all_sent(self.pick(pl.ds(0, 4)), 1)
+        pl.when(self.middle)(lambda: self.moves.all_sent(self.pick(pl.ds(0, 16)), 2))
 
 
 class Reduce:
-    def __init__(self, sent, own, pick, stages, send, recv, across):
-        self.sent, self.own, self.pick, self.at = sent, own, pick, neighbours(across)
+    SENDS, RECEIVES = 1, 15
+
+    def __init__(self, held, pick, stages, send, recv, across):
+        self.held, self.pick, self.at = held, pick, neighbours(across)
         self.first, self.second, self.third_in = stages
         self.moves = Shipments(send, recv)
 
@@ -569,110 +572,99 @@
     def number(line):
         return 3 if line is None else line
 
-    def ship(self, source, target, index, to):
-        self.moves.ship(source, target, lambda: index, lambda: self.at(*to))
-
-    def landed(self, target, index):
-        self.moves.landed(target, index, self.at(1, 0, None))
+    def mine(self, *what):
+        return self.pick(self.held, self.at(*what))
+
+    def term(self, stage, index, recv_index):
+        self.moves.landed(stage.at[index], recv_index)
+        return stage[index].astype(HIGH)
 
     def start(self, line):
         for far_p in (1, 0):
             index = self.number(line) * 2 + far_p
-            self.ship(
-                lambda far_p=far_p: self.pick(self.sent, self.at(far_p, 1, line)),
-                lambda index=index: self.first.at[index],
-                index,
-                (0, 1, None),
+            self.moves.ship(
+                self.mine(far_p, 1, line), self.first.at[index], 0, index, self.at(0, 1, None)
             )
-
-    def mine(self, *what):
-        return self.pick(self.own, self.at(*what))[...].astype(HIGH)
 
     def side(self, line):
         number = self.number(line)
         index = number * 2 + 1
-        self.landed(self.first.at[index], index)
-        self.first[index] = (self.first[index].astype(HIGH) + self.mine(1, 0, line)).astype(LOW)
-        self.ship(
-            lambda: self.first.at[index], lambda: self.second.at[number], 8 + number, (1, 0, None)
+        total = self.term(self.first, index, index) + self.mine(1, 0, line)[...].astype(HIGH)
+        self.first[index] = total.astype(LOW)
+        self.moves.ship(
+            self.first.at[index], self.second.at[number], 0, 8 + number, self.at(1, 0, None)
         )
 
     def line(self, line):
         number = self.number(line)
         index = number * 2
-        self.landed(self.first.at[index], index)
-        self.landed(self.second.at[number], 8 + number)
         total = (
-            self.first[index].astype(HIGH)
-            + self.second[number].astype(HIGH)
-            + self.mine(0, 0, line)
+            self.term(self.first, index, index)
+            + self.term(self.second, number, 8 + number)
+            + self.mine(0, 0, line)[...].astype(HIGH)
         )
         if line is None:
             return total
         self.first[index] = total.astype(LOW)
-        ahead = lambda: lax.rem(lax.div(self.at(0, 0, None), 4) - lax.div(self.at(0, 0, line), 4) + 4, 4) - 1
+        ahead = self.ahead(line)
         self.moves.ship(
-            lambda: self.first.at[index],
-            lambda: self.third_in.at[ahead()],
-            lambda: 12 + ahead(),
-            lambda: self.at(0, 0, line),
-        )
-
-    def finish(self, result):
-        result[...] = self.line(None)
-        for ahead in range(3):
-            self.landed(self.third_in.at[ahead], 12 + ahead)
-            result[...] += self.third_in[ahead].astype(HIGH)
-        self.moves.all_sent(15)
-
-
-class ReduceEarly(Reduce):
-    PLANE = ((0, 0), (1, 0), (0, 1), (1, 1))
+            self.first.at[index], self.third_in.at[ahead], 0, 12 + ahead, self.at(0, 0, line)
+        )
 
     def ahead(self, line):
         return lax.rem(lax.div(self.at(0, 0, None), 4) - lax.div(self.at(0, 0, line), 4) + 4, 4) - 1
 
+    def finish(self, result):
+        total = self.line(None)
+        for ahead in range(3):
+            total += self.term(self.third_in, ahead, 12 + ahead)
+        result[...] = total
+        self.moves.all_sent(self.pick(self.held, pl.ds(0, 15)), 0)
+
+
+class ReduceEarly(Reduce):
+    SENDS, RECEIVES = 1, 6
+
     def start(self):
         for line in (2, 1, 0):
-            for number, what in enumerate(self.PLANE):
-                index = lambda number=number, line=line: self.ahead(line) * 4 + number
-                self.moves.ship(
-                    lambda what=what, line=line: self.pick(self.sent, self.at(*what, line)),
-                    lambda index=index: self.first.at[index()],
-                    index,
-                    lambda line=line: self.at(0, 0, line),
-                )
-
-    def plane_sum(self, number):
-        total = self.mine(*self.PLANE[number], None)
+            plane = lax.div(self.at(0, 0, line), 4)
+            ahead = self.ahead(line)
+            self.moves.ship(
+                self.pick(self.held, pl.ds(plane * 4, 4)),
+                self.first.at[ahead],
+                0,
+                ahead,
+                self.at(0, 0, line),
+            )
+
+    def plane_sum(self, *what):
+        slot = self.at(*what, None)
+        total = self.pick(self.held, slot)[...].astype(HIGH)
         for ahead in range(3):
-            index = ahead * 4 + number
-            self.landed(self.first.at[index], index)
-            total += self.first[index].astype(HIGH)
+            total += self.first[ahead, lax.rem(slot, 4)].astype(HIGH)
         return total
 
+    def plane_ref(self, *what):
+        return self.first.at[0, lax.rem(self.at(*what, None), 4)]
+
     def third(self):
-        for number, far_p in ((3, 1), (2, 0)):
-            self.first[number] = self.plane_sum(number).astype(LOW)
-            self.ship(
-                lambda number=number: self.first.at[number],
-                lambda far_p=far_p: self.second.at[far_p],
-                12 + far_p,
-                (0, 1, None),
-            )
+        for ahead in range(3):
+            self.moves.landed(self.first.at[ahead], ahead)
+        for far_p in (1, 0):
+            ref = self.plane_ref(far_p, 1)
+            ref[...] = self.plane_sum(far_p, 1).astype(LOW)
+            self.moves.ship(ref, self.second.at[far_p], 0, 3 + far_p, self.at(0, 1, None))
 
     def across(self):
-        total = self.plane_sum(1)
-        self.landed(self.second.at[1], 13)
-        self.first[1] = (total + self.second[1].astype(HIGH)).astype(LOW)
-        self.ship(lambda: self.first.at[1], lambda: self.third_in.at[0], 14, (1, 0, None))
+        ref = self.plane_ref(1, 0)
+        ref[...] = (self.plane_sum(1, 0) + self.term(self.second, 1, 4)).astype(LOW)
+        self.moves.ship(ref, self.third_in.at[0], 0, 5, self.at(1, 0, None))
 
     def finish(self, result):
-        total = self.plane_sum(0)
-        self.landed(self.second.at[0], 12)
-        self.landed(self.third_in.at[0], 14)
-        result[...] = total + self.second[0].astype(HIGH) + self.third_in[0].astype(HIGH)
-        self.moves.all_sent(15)
+        result[...] = (
+            self.plane_sum(0, 0) + self.term(self.second, 0, 3) + self.term(self.third_in, 0, 5)
+        )
+        self.moves.all_sent(self.pick(self.held, pl.ds(0, 15)), 0)
 
 
 def cube_of(order):
@@ -688,76 +680,77 @@
 
 
 class CubeGather:
+    SENDS, RECEIVES = 1, 4
+
     def __init__(self, pick, send, recv, order):
         self.pick, self.at = pick, cube_of(order)
         self.moves = Shipments(send, recv)
 
-    def ship(self, what, to):
-        slot = lambda: lax.rem(self.at(*what), HALF)
-        ref = lambda: self.pick(slot())
-        self.moves.ship(ref, ref, slot, lambda: self.at(*to))
-
-    def landed(self, *what):
-        slot = lax.rem(self.at(*what), HALF)
-        self.moves.landed(self.pick(slot), slot, self.at(1, 0, 0))
+    def ref(self, *what):
+        return self.pick(lax.rem(self.at(*what), HALF))
+
+    def ship(self, what, recv_index, to):
+        self.moves.ship(self.ref(*what), self.ref(*what), 0, recv_index, self.at(*to))
 
     def own(self):
-        for to in ((1, 0, 0), (0, 1, 0), (0, 0, 1)):
-            self.ship((0, 0, 0), to)
+        self.ship((0, 0, 0), 0, (1, 0, 0))
+        self.ship((0, 0, 0), 1, (0, 1, 0))
+        self.ship((0, 0, 0), 3, (0, 0, 1))
 
     def one(self):
-        self.landed(1, 0, 0)
-        self.ship((1, 0, 0), (0, 1, 0))
-        self.ship((1, 0, 0), (0, 0, 1))
+        self.moves.landed(self.ref(1, 0, 0), 0)
+        self.ship((1, 0, 0), 2, (0, 1, 0))
+        self.ship((1, 0, 0), 3, (0, 0, 1))
 
     def two(self):
-        for what in ((0, 1, 0), (1, 1, 0)):
-            self.landed(*what)
-            self.ship(what, (0, 0, 1))
+        for one in range(2):
+            self.moves.landed(self.ref(one, 1, 0), 1 + one)
+            self.ship((one, 1, 0), 3, (0, 0, 1))
 
     def arrive(self):
-        for what in ((0, 0, 1), (1, 0, 1), (0, 1, 1), (1, 1, 1)):
-            self.landed(*what)
+        self.moves.landed(self.pick(pl.ds(0, 4)), 3)
 
     def finish(self):
-        self.moves.all_sent(7)
+        self.moves.all_sent(self.pick(pl.ds(0, 7)), 0)
 
 
 class CubeReduce:
+    SENDS, RECEIVES = 1, 7
+
     def __init__(self, pick, stage, send, recv, order):
         self.pick, self.stage, self.at = pick, stage, cube_of(order)
         self.moves = Shipments(send, recv)
 
     def ship(self, source, index, to):
-        self.moves.ship(source, lambda: self.stage.at[index], lambda: index, lambda: self.at(*to))
+        self.moves.ship(source, self.stage.at[index], 0, index, self.at(*to))
 
     def mine(self, *what):
         return self.pick(lax.rem(self.at(*what), HALF))
 
     def term(self, index):
-        self.moves.landed(self.stage.at[index], index, self.at(1, 0, 0))
+        self.moves.landed(self.stage.at[index], index)
         return self.stage[index].astype(HIGH)
 
     def own(self):
         for index, (one, two) in enumerate(((1, 1), (0, 1), (1, 0), (0, 0))):
-            self.ship(lambda one=one, two=two: self.mine(one, two, 1), index, (0, 0, 1))
+            self.ship(self.mine(one, two, 1), index, (0, 0, 1))
 
     def one(self):
         for index, one in ((0, 1), (1, 0)):
             total = self.mine(one, 1, 0)[...].astype(HIGH) + self.term(index)
             self.stage[index] = total.astype(LOW)
-            self.ship(lambda index=index: self.stage.at[index], 4 + index, (0, 1, 0))
+            self.ship(self.stage.at[index], 4 + index, (0, 1, 0))
 
     def two(self):
         total = self.mine(1, 0, 0)[...].astype(HIGH) + self.term(2) + self.term(4)
         self.stage[2] = total.astype(LOW)
-        self.ship(lambda: self.stage.at[2], 6, (1, 0, 0))
+        self.ship(self.stage.at[2], 6, (1, 0, 0))
 
     def arrive(self):
         return self.mine(0, 0, 0)[...].astype(HIGH) + self.term(3) + self.term(5) + self.term(6)
 
     def finish(self):
-        self.moves.all_sent(7)
+        self.moves.all_sent(self.stage, 0)
 
 
 def each(plans, act, *arguments):
@@ -768,6 +761,12 @@
 def unit():
     core, chip = place()
     return lax.div(chip, HALF), lax.rem(chip, HALF), core
+
+
+def all_but_one(source, send, itself):
+    most = source.at[pl.ds(0, CHIPS - 1)]
+    pl.when(itself)(lambda: local(most, most, send.at[0]).wait())
+    pl.when(jnp.logical_not(itself))(lambda: local(source, source, send.at[0]).wait())
 
 
 def to_tokens(source, target, send, recv):
@@ -780,24 +779,15 @@
     def copy_to(ahead):
         chip_to = lax.rem(chip + ahead, CHIPS)
         return remote(
-            source.at[chip_to], target.at[mine], send.at[ahead], recv.at[mine], (to_core, chip_to)
-        )
-
-    pl.when(here)(lambda: local(source.at[chip], target.at[mine], recv.at[mine]).start())
+            source.at[chip_to], target.at[mine], send.at[0], recv.at[0], (to_core, chip_to)
+        )
+
+    pl.when(here)(lambda: local(source.at[chip], target.at[mine], recv.at[0]).start())
     pl.when(jnp.logical_not(here))(lambda: copy_to(0).start())
     for ahead in range(1, CHIPS):
         copy_to(ahead).start()
-
-    def arrive():
-        for slot in range(CHIPS):
-            local(source.at[slot], target.at[slot], recv.at[slot]).wait()
-
-    def finish():
-        pl.when(jnp.logical_not(here))(lambda: copy_to(0).wait_send())
-        for ahead in range(1, CHIPS):
-            copy_to(ahead).wait_send()
-
-    return arrive, finish
+    arrive = lambda: local(target, target, recv.at[0]).wait()
+    return arrive, lambda: all_but_one(source, send, here)
 
 
 def to_heads(source, target, send, recv):
@@ -812,27 +802,18 @@
         return remote(
             source.at[to_group * HALF + head],
             target.at[chip],
-            send.at[turn_group * HALF + ahead],
-            recv.at[chip],
+            send.at[0],
+            recv.at[0],
             (lax.rem(head, 2), to_group * HALF + core * 4 + lax.div(head, 2)),
         )
 
-    def every(act):
-        pl.when(jnp.logical_not(here))(lambda: act(copy_to(0, 0)))
-        for turn_group in range(2):
-            for ahead in range(0 if turn_group else 1, HALF):
-                act(copy_to(turn_group, ahead))
-
-    pl.when(here)(
-        lambda: local(source.at[group * HALF + start], target.at[chip], recv.at[chip]).start()
-    )
-    every(lambda copy: copy.start())
-
-    def arrive():
-        for slot in range(CHIPS):
-            local(source.at[slot], target.at[slot], recv.at[slot]).wait()
-
-    return arrive, lambda: every(lambda copy: copy.wait_send())
+    pl.when(here)(lambda: local(source.at[group * HALF + start], target.at[chip], recv.at[0]).start())
+    pl.when(jnp.logical_not(here))(lambda: copy_to(0, 0).start())
+    for turn_group in range(2):
+        for ahead in range(0 if turn_group else 1, HALF):
+            copy_to(turn_group, ahead).start()
+    arrive = lambda: local(target, target, recv.at[0]).wait()
+    return arrive, lambda: all_but_one(source, send, here)
 
 
 def lanes(rows, width=128):
@@ -992,8 +973,8 @@
         return remote(
             weight.at[:, :, columns_of(lax.rem(to, HALF), 128)],
             w_all.at[:, core, chip],
-            r.w_send.at[ahead],
-            r.w_recv.at[chip],
+            r.w_send.at[0],
+            r.w_recv.at[0],
             (core, to),
         )
 
@@ -1049,11 +1030,8 @@
     each(plans_down, Gather.own_line, 0)
     plan_out.third()
     each(plans_in, Gather.line, 0)
-    for ahead in range(1, CHIPS):
-        came = lax.rem(chip + ahead, CHIPS)
-        remote(
-            weight.at[:, :, pl.ds(0, 128)], w_all.at[:, core, came], r.w_send.at[0], r.w_recv.at[came], (core, came)
-        ).wait_recv()
+    w_most = w_all.at[:, core, pl.ds(0, CHIPS - 1)]
+    local(w_most, w_most, r.w_recv.at[0]).wait()
     pair_w = remote(w_all.at[:, core], w_all.at[:, core], r.pair_send.at[1], r.pair_recv.at[1], (other, chip))
     pair_w.start()
     for slot in range(2):
@@ -1311,26 +1289,36 @@
     small_sum[5:6, :] = column_sums(upstream)
 
     half_total = HALF * slot_rows
-    sum_down = Reduce(
+    def half_sums(ref, pick, wide, stages, sends, recvs):
+        return [
+            Reduce(
+                ref,
+                lambda held, slot, part=part: pick(held, slot, pl.ds(part * wide, wide)),
+                [stage.at[part] for stage in stages],
+                sends.at[part],
+                recvs.at[part],
+                across,
+            )
+            for part, across in enumerate("xy")
+        ]
+
+    sums_down = half_sums(
         w_down,
-        w_down,
-        lambda ref, slot: ref.at[slot],
-        [r.down_1, r.down_2, r.down_3],
+        lambda held, slot, columns: held.at[slot, :, columns],
+        half,
+        (r.down_1, r.down_2, r.down_3),
         r.g_down_send,
         r.g_down_recv,
-        "y",
-    )
-    sum_in = Reduce(
+    )
+    sums_in = half_sums(
         w_in,
-        w_in,
-        lambda ref, slot: ref.at[:, slot],
-        [r.in_1, r.in_2, r.in_3],
+        lambda held, slot, columns: held.at[:, slot, :, columns],
+        half_tile,
+        (r.in_1, r.in_2, r.in_3),
         r.g_in_send,
         r.g_in_recv,
-        "x",
     )
     sum_out = ReduceEarly(
-        r.g_out,
         r.g_out,
         lambda ref, slot: ref.at[slot],
         [r.out_1, r.out_2, r.out_3],
@@ -1364,7 +1352,7 @@
         return carry
 
     lax.fori_loop(0, half_hidden // tile, narrow_back, 0)
-    sum_down.start(2)
+    each(sums_down, Reduce.start, 1)
     w_in_all = w_in[...].reshape(width, half_hidden)
     out_part[...] = dot(d_inner[far, :], w_in_all, NT)
     copy = swap(out_part, in_part)
@@ -1435,17 +1423,19 @@
         elif index < 3:
             small_sum[...] += small_in[index]
 
+    each(sums_down, Reduce.start, None)
+    each(sums_in, Reduce.start, 2)
+    each(sums_down, Reduce.side, 1)
     small_start(0)
-    sum_down.side(2)
-    sum_down.start(1)
+    each(sums_down, Reduce.start, 2)
     small_end(0)
-    sum_in.start(2)
+    small_start(1)
+    sum_out.start()
+    each(sums_down, Reduce.side, 2)
+    each(sums_down, Reduce.start, 0)
+    each(sums_in, Reduce.side, 2)
     d_context = meta
     grad_arrives()
-    sum_down.start(0)
-    sum_out.start()
-    small_start(1)
-    sum_in.start(0)
     for slot in range(CHIPS):
         both = d_arrived[slot].astype(HIGH)[:half_slot]
         top = slot * slot_rows
@@ -1460,13 +1450,26 @@
         at_steps(
             index,
             {
-                1: [lambda: sum_in.side(2), lambda: sum_in.start(1)],
-                2: [lambda: sum_down.line(2), lambda: small_end(1), lambda: sum_down.side(0)],
-                3: [lambda: sum_in.side(0)],
-                5: [lambda: sum_in.line(2)],
-                6: [lambda: sum_in.line(0), lambda: sum_in.side(1)],
-                7: [lambda: sum_down.start(None)],
-                8: [lambda: sum_in.start(None)],
+                1: [lambda: small_end(1)],
+                2: [
+                    lambda: small_start(2),
+                    lambda: each(sums_in, Reduce.start, None),
+                    lambda: each(sums_down, Reduce.line, 2),
+                ],
+                3: [
+                    lambda: each(sums_down, Reduce.side, 0),
+                    lambda: each(sums_in, Reduce.start, 1),
+                    lambda: small_end(2),
+                    lambda: each(sums_in, Reduce.line, 2),
+                ],
+                4: [lambda: small_start(3)],
+                6: [lambda: each(sums_down, Reduce.line, 0), lambda: each(sums_in, Reduce.side, 1)],
+                7: [
+                    lambda: each(sums_in, Reduce.start, 0),
+                    lambda: each(sums_down, Reduce.line, 1),
+                    sum_out.third,
+                ],
+                8: [lambda: each(sums_in, Reduce.line, 1)],
             },
         )
         facts = kept[rows, :]
@@ -1504,9 +1507,6 @@
         return carry
 
     lax.fori_loop(0, total // BLOCK, step, 0)
-    small_start(2)
-    sum_in.line(1)
-    sum_down.line(0)
 
     d_heads[1] = d_pair_t[0:HD, :].astype(LOW)
     d_heads[2] = d_pair_t[HD : 2 * HD, :].astype(LOW)
@@ -1560,12 +1560,8 @@
         )
         for part, order in enumerate(("xyz", "yzx", "zxy"))
     ]
-    sum_down.side(1)
     each(d_x_plans, CubeReduce.own)
-    small_end(2)
-    sum_down.line(1)
-    sum_out.third()
-    sum_out.across()
+    small_end(3)
 
     w_mine, w_far, w_low, w_came = slope, r.w_far, r.w_low, r.w_came
     w_rows = 3 * HD
@@ -1578,9 +1574,8 @@
     w_swaps = [
         swap(w_mine.at[pl.ds(0, w_rows), w_columns(part, other)], w_far.at[part]) for part in range(2)
     ]
-    sum_in.side(None)
+    each(sums_in, Reduce.side, 0)
     each(d_x_plans, CubeReduce.one)
-    sum_down.side(None)
     for copy in w_swaps:
         copy.wait()
     w_sum = jnp.concatenate(
@@ -1591,32 +1586,43 @@
 
     def d_w_copy(ahead):
         to = lax.rem(chip + ahead, CHIPS)
-        return remote(w_low.at[to], w_came.at[chip], r.d_w_send.at[ahead], r.d_w_recv.at[chip], (core, to))
+        return remote(w_low.at[to], w_came.at[chip], r.d_w_send.at[0], r.d_w_recv.at[0], (core, to))
 
     own_d_w = local(w_low.at[chip], w_came.at[chip], keep.at[6])
     own_d_w.start()
     for ahead in range(1, CHIPS):
         d_w_copy(ahead).start()
+    sum_out.across()
     each(d_x_plans, CubeReduce.two)
-    sum_down.finish(r.down_grad)
-    small_start(3)
+    each(sums_in, Reduce.line, 0)
+    each(sums_down, Reduce.side, None)
+    each(sums_in, Reduce.side, None)
+    x_total, x_came = x_own, r.x_came
+    back_part = lambda part: pl.ds(part * third, third)
+    back = lambda part: local(
+        x_total.at[back_part(part)], x_came.at[back_part(part)], r.back_recv.at[part]
+    )
+    back_abroad = lambda part: remote(
+        x_total.at[back_part(part)],
+        x_came.at[back_part(part)],
+        r.back_send.at[part],
+        r.back_recv.at[part],
+        (other, away),
+    )
+    for part, plan in enumerate(d_x_plans):
+        x_total[part * third : (part + 1) * third] = plan.arrive().astype(LOW)
+        pl.when(at_home)(lambda: back(part).start())
+        pl.when(jnp.logical_not(at_home))(lambda: back_abroad(part).start())
+    for part, plan in enumerate(sums_down):
+        plan.finish(r.down_grad.at[:, pl.ds(part * half, half)])
     sum_out.finish(r.out_w_grad)
     in_total, in_far = r.in_total, r.in_far
-    sum_in.finish(in_total)
+    for part, plan in enumerate(sums_in):
+        plan.finish(in_total.at[:, :, pl.ds(part * half_tile, half_tile)])
     in_pair = swap(in_total.at[other], in_far)
-    x_total, x_came = x_own, r.x_came
-    for part, plan in enumerate(d_x_plans):
-        x_total[part * third : (part + 1) * third] = plan.arrive().astype(LOW)
-    back = lambda: local(x_total, x_came, r.back_sem.at[1])
-    back_abroad = lambda: remote(
-        x_total, x_came, r.back_sem.at[0], r.back_sem.at[1], (other, lax.rem(chip + HALF, CHIPS))
-    )
-    pl.when(at_home)(lambda: back().start())
-    pl.when(jnp.logical_not(at_home))(lambda: back_abroad().start())
 
     in_grad = r.in_grad
     in_grad[:, columns_of(core, half_hidden)] = in_total[core]
-    small_end(3)
     me = core * CHIPS + chip
     small_all = lambda rows, columns: (
         small_sum[rows, columns] + small_in[3, rows, columns] + small_in[4, rows, columns] + small_in[5, rows, columns]
@@ -1635,23 +1641,22 @@
         r.rel_tables_grad[kind] = rel_total[:, kind * NB : (kind + 1) * NB]
     r.qkv_bias_grad[...] = rel_total[:, 3 * NB : 4 * NB].T[0:2]
     own_d_w.wait()
-    for ahead in range(1, CHIPS):
-        came = lax.rem(chip + ahead, CHIPS)
-        remote(w_low.at[0], w_came.at[came], r.d_w_send.at[0], r.d_w_recv.at[came], (core, came)).wait_recv()
-        d_w_copy(ahead).wait_send()
+    w_came_most = w_came.at[pl.ds(0, CHIPS - 1)]
+    local(w_came_most, w_came_most, r.d_w_recv.at[0]).wait()
+    local(w_came_most, w_came_most, r.d_w_send.at[0]).wait()
     for pair in range(HALF):
         both = w_came[pair].astype(HIGH) + w_came[HALF + pair].astype(HIGH)
         for n in range(3):
             r.qkv_grad[n, :, pair * 128 : pair * 128 + 128] = both[:, n * 128 : n * 128 + 128]
-    back().wait()
-    pl.when(jnp.logical_not(at_home))(lambda: back_abroad().wait_send())
+    for part in range(3):
+        back(part).wait()
+        pl.when(jnp.logical_not(at_home))(lambda: back_abroad(part).wait_send())
     r.hidden_grad[...] = (out_part[...] + x_came[...].astype(HIGH))[:token_rows].astype(LOW)
     in_pair.wait()
     in_grad[:, columns_of(other, half_hidden)] = in_far[...]
     grad_sent()
     each(d_x_plans, CubeReduce.finish)
-    for ahead in range(1, CHIPS):
-        w_copy(ahead).wait_send()
+    local(w_most, w_most, r.w_send.at[0]).wait()
     rel_each(lambda copy: copy.wait_send(), None)
     context_sent()
     plan_out.finish()
@@ -1717,7 +1722,8 @@
     x_block, w_block = (HALF, slot_rows, width), (3, 2, CHIPS, depth, 128)
     in_all, down_all = (2, CHIPS, depth, half_hidden), (CHIPS, down_rows, width)
     out_all = (CHIPS, depth + 16, width)
-    in_block, down_block, out_block = (2, depth, half_hidden), (down_rows, width), (depth, width)
+    in_half, down_half = (2, depth, half_hidden // 2), (down_rows, half_width)
+    in_block, out_block = (2, depth, half_hidden), (depth, width)
     made = call(
         layer_kernel,
         "layer",
@@ -1788,13 +1794,13 @@
             in_part=vmem((slot_rows, width), HIGH),
             d_second=vmem((both, width), LOW),
             g_out=vmem((CHIPS,) + out_block, LOW),
-            in_1=vmem((8,) + in_block, LOW),
-            in_2=vmem((4,) + in_block, LOW),
-            in_3=vmem((3,) + in_block, LOW),
-            down_1=vmem((8,) + down_block, LOW),
-            down_2=vmem((4,) + down_block, LOW),
-            down_3=vmem((3,) + down_block, LOW),
-            out_1=vmem((12,) + out_block, LOW),
+            in_1=vmem((2, 8) + in_half, LOW),
+            in_2=vmem((2, 4) + in_half, LOW),
+            in_3=vmem((2, 3) + in_half, LOW),
+            down_1=vmem((2, 8) + down_half, LOW),
+            down_2=vmem((2, 4) + down_half, LOW),
+            down_3=vmem((2, 3) + down_half, LOW),
+            out_1=vmem((3, 4) + out_block, LOW),
             out_2=vmem((2,) + out_block, LOW),
             out_3=vmem((1,) + out_block, LOW),
             in_total=vmem(in_block, HIGH),
@@ -1814,35 +1820,36 @@
             w_came=vmem((CHIPS, depth, 6 * HD), LOW),
             keep_sem=dma((7,)),
             home_sem=dma((2,)),
-            back_sem=dma((2,)),
-            x_send=dma((3, 8)),
-            x_recv=dma((3, 8)),
-            w_send=dma((16,)),
-            w_recv=dma((16,)),
+            back_send=dma((3,)),
+            back_recv=dma((3,)),
+            x_send=dma((3, CubeGather.SENDS)),
+            x_recv=dma((3, CubeGather.RECEIVES)),
+            w_send=dma((1,)),
+            w_recv=dma((1,)),
             rel_send=dma((2,)),
             rel_recv=dma((2,)),
-            out_send=dma((24,)),
-            out_recv=dma((16,)),
-            in_send=dma((2, 18)),
-            in_recv=dma((2, 16)),
-            down_send=dma((2, 18)),
-            down_recv=dma((2, 16)),
-            msg_send=dma((16,)),
-            msg_recv=dma((16,)),
-            d_send=dma((16,)),
-            d_recv=dma((16,)),
-            g_in_send=dma((16,)),
-            g_in_recv=dma((16,)),
-            g_down_send=dma((16,)),
-            g_down_recv=dma((16,)),
-            g_out_send=dma((16,)),
-            g_out_recv=dma((16,)),
+            out_send=dma((GatherLate.SENDS,)),
+            out_recv=dma((GatherLate.RECEIVES,)),
+            in_send=dma((2, Gather.SENDS)),
+            in_recv=dma((2, Gather.RECEIVES)),
+            down_send=dma((2, Gather.SENDS)),
+            down_recv=dma((2, Gather.RECEIVES)),
+            msg_send=dma((1,)),
+            msg_recv=dma((1,)),
+            d_send=dma((1,)),
+            d_recv=dma((1,)),
+            g_in_send=dma((2, Reduce.SENDS)),
+            g_in_recv=dma((2, Reduce.RECEIVES)),
+            g_down_send=dma((2, Reduce.SENDS)),
+            g_down_recv=dma((2, Reduce.RECEIVES)),
+            g_out_send=dma((ReduceEarly.SENDS,)),
+            g_out_recv=dma((ReduceEarly.RECEIVES,)),
             small_send=dma((6,)),
             small_recv=dma((6,)),
-            d_x_send=dma((3, 8)),
-            d_x_recv=dma((3, 8)),
-            d_w_send=dma((16,)),
-            d_w_recv=dma((16,)),
+            d_x_send=dma((3, CubeReduce.SENDS)),
+            d_x_recv=dma((3, CubeReduce.RECEIVES)),
+            d_w_send=dma((1,)),
+            d_w_recv=dma((1,)),
             d_rel_send=dma((2,)),
             d_rel_recv=dma((2,)),
             pair_send=dma((16,)),

time: 242 us -> 235 us (0.971)
  Pallas kernels: 241 us -> 234 us
    pallas_call x1, Pallas kernels: 238 us -> 231 us  [call(): pl.pallas_call(functools.partial(kernel, names), out_shape=[jax.ShapeDtyp...]
where the time goes in v7:
time: 235 us
  Pallas kernels  234 us (100%)
    pallas_call x1, Pallas kernels, call(): pl.pallas_call(functools.partial(kernel, names), out_shape=[jax.ShapeDtyp...  231 us

profile of v7, /device:TPU:1, one launch (start us, length us, event | category | flops | bytes accessed | tf_op | source)
XLA Modules:
  0.0 234.7 jit_solution(11003886378635618812)
XLA Ops:
  0.7 231.0 %layer.1 = (bf16[136,1024]{1,0:T(8,128)(2,1)}, bf16[136,1024]{1,0:T(8,128)(2,1)}, f32[3,32,1024]{2,1,0:T(8,128)}, f32[2,32]{1,0:T(2,128)}, f32[3,32,128]{2,1,0:T...) custom-call(bf16[136,1024]{1,0:T(8,128)(2,1)} %refs_0_.1, ...), custom_call_target="tpu_custom_call" | custom-call | tf_op jit(solution)/shard_map/layer/pallas_call | solution.py:1680
  231.7 3.0 %hand_over.1 = (bf16[136,1024]{1,0:T(8,128)(2,1)}, bf16[136,1024]{1,0:T(8,128)(2,1)}, f32[3,32,1024]{2,1,0:T(8,128)}, f32[2,32]{1,0:T(2,128)}, f32[3,32,128]{2,1...) custom-call(bf16[136,1024]{1,0:T(8,128)(2,1)} %get-tuple-element.36., ...), custom_call_target="tpu_custom_call" | custom-call | tf_op jit(solution)/shard_map/hand_over/pallas_call | solution.py:1671

commit v8 on v7

--- a/solution.py
+++ b/solution.py
@@ -572,6 +572,9 @@
     def number(line):
         return 3 if line is None else line
 
+    def plane(self, line):
+        return lax.div(self.at(0, 0, line), 4)
+
     def mine(self, *what):
         return self.pick(self.held, self.at(*what))
 
@@ -612,7 +615,7 @@
         )
 
     def ahead(self, line):
-        return lax.rem(lax.div(self.at(0, 0, None), 4) - lax.div(self.at(0, 0, line), 4) + 4, 4) - 1
+        return lax.rem(self.plane(None) - self.plane(line) + 4, 4) - 1
 
     def finish(self, result):
         total = self.line(None)
@@ -627,10 +630,9 @@
 
     def start(self):
         for line in (2, 1, 0):
-            plane = lax.div(self.at(0, 0, line), 4)
             ahead = self.ahead(line)
             self.moves.ship(
-                self.pick(self.held, pl.ds(plane * 4, 4)),
+                self.pick(self.held, pl.ds(self.plane(line) * 4, 4)),
                 self.first.at[ahead],
                 0,
                 ahead,
@@ -872,9 +874,6 @@
 
 def columns_of(half, width):
     return pl.ds(pl.multiple_of(half * width, 128), width)
-
-
-GAIN_AT, SHIFT_AT, BIAS_AT = 128, 256, 384
 
 
 def layer_kernel(names, *refs):
@@ -898,7 +897,7 @@
     loads = [
         local(r.ffn_in.at[:, columns_of(core, half_hidden)], w_in.at[core, chip], keep.at[0]),
         local(r.ffn_out, w_down.at[chip], keep.at[1]),
-        local(r.out_weight, w_out.at[chip, pl.ds(0, depth)], keep.at[2]),
+        local(r.out_weight, w_out.at[chip], keep.at[2]),
     ]
     for copy in loads:
         copy.start()
@@ -927,14 +926,14 @@
     rel_own[:, 3 * NB : 4 * NB] = jnp.where(
         lanes(depth) == 0, bias_columns[:, 0:1], jnp.where(lanes(depth) == 1, bias_columns[:, 1:2], 0.0)
     ).astype(LOW)
-    small_own = r.small_own
-    small_own[...] = jnp.zeros_like(small_own)
-    small_own[0:2, 0:depth] = r.branch_bias[...]
-    small_own[0:2, GAIN_AT : GAIN_AT + depth] = r.norm_gains[...]
-    small_own[0:2, SHIFT_AT : SHIFT_AT + depth] = r.norm_shifts[...]
-    small_own[0:1, BIAS_AT : BIAS_AT + 128] = r.ffn_in_bias[...]
+    small_wide, small_own, small_all = r.small_wide, r.small_own, r.small_all
+    small_wide[...] = jnp.zeros_like(small_wide)
+    for number, pair in enumerate((r.branch_bias, r.norm_gains, r.norm_shifts)):
+        small_wide[2 * number : 2 * number + 2, 0:depth] = pair[...].astype(HIGH)
+    small_wide[6:7, :] = r.ffn_in_bias[...].astype(HIGH)
+    small_own[...] = small_wide[...].astype(LOW)
     loads += [
-        local(small_own, w_out.at[chip, pl.ds(depth, 16)], keep.at[3]),
+        local(small_own, small_all.at[chip], keep.at[3]),
         local(weight.at[:, :, columns_of(position, 128)], w_all.at[:, core, chip], keep.at[4]),
     ]
     for copy in loads[3:]:
@@ -999,7 +998,10 @@
     ]
     half = width // 2
     half_tile = half_hidden // 2
-    plan_out = GatherLate(lambda slot: w_out.at[slot], r.out_send, r.out_recv, "x")
+    plans_out = [
+        GatherLate(lambda slot: w_out.at[slot], r.out_send.at[0], r.out_recv.at[0], "x"),
+        GatherLate(lambda slot: small_all.at[slot], r.out_send.at[1], r.out_recv.at[1], "y"),
+    ]
 
     def halves(ref, wide, sends, recvs):
         return [
@@ -1012,24 +1014,22 @@
     plans_in = halves(lambda slot, columns: w_in.at[:, slot, :, columns], half_tile, r.in_send, r.in_recv)
     plans_down = halves(lambda slot, columns: w_down.at[slot, :, columns], half, r.down_send, r.down_recv)
 
-    for ahead in range(1, CHIPS):
-        w_copy(ahead).start()
     for copy in loads:
         copy.wait()
     each(plans_down, Gather.own_plane)
+    each(plans_out, GatherLate.first)
     swap_in.wait()
     each(plans_in, Gather.own_plane)
-    plan_out.first()
     each(plans_in, Gather.own_line, 0)
+    for ahead in range(1, CHIPS):
+        w_copy(ahead).start()
+    each(plans_out, GatherLate.second)
+    each(plans_in, Gather.own_line, 1)
     home().wait()
     each(x_plans, CubeGather.own)
     each(x_plans, CubeGather.one)
-    each(plans_down, Gather.own_line, 1)
-    plan_out.second()
     each(x_plans, CubeGather.two)
     each(plans_down, Gather.own_line, 0)
-    plan_out.third()
-    each(plans_in, Gather.line, 0)
     w_most = w_all.at[:, core, pl.ds(0, CHIPS - 1)]
     local(w_most, w_most, r.w_recv.at[0]).wait()
     pair_w = remote(w_all.at[:, core], w_all.at[:, core], r.pair_send.at[1], r.pair_recv.at[1], (other, chip))
@@ -1040,6 +1040,9 @@
         rel_all.at[:, pl.ds(3 * NB, NB)], r.bias_far, r.pair_send.at[2], r.pair_recv.at[2], (other, chip)
     )
     pair_bias.start()
+    each(plans_down, Gather.side, None)
+    each(plans_out, GatherLate.third)
+    each(plans_in, Gather.line, 0)
     each(x_plans, CubeGather.arrive)
     pl.when(jnp.logical_not(at_home))(lambda: abroad().wait_send())
 
@@ -1110,16 +1113,15 @@
     left, right, right_t = r.left, r.right, r.right_t
     value, value_t, kept = r.value, r.value_t, r.kept
     pair_qkv.wait()
-    each(plans_in, Gather.own_line, 1)
-    each(plans_in, Gather.side, None)
 
     def prepare(index, carry):
         rows = pl.ds(pl.multiple_of(index * BLOCK, BLOCK), BLOCK)
         at_steps(
             index,
             {
-                3: [lambda: each(plans_down, Gather.side, None), lambda: each(plans_down, Gather.line, 1)],
-                4: [lambda: each(plans_in, Gather.side, 0), lambda: each(plans_down, Gather.line, 0)],
+                1: [lambda: each(plans_down, Gather.own_line, 1), lambda: each(plans_down, Gather.line, 0)],
+                3: [lambda: each(plans_in, Gather.line, 1)],
+                8: [lambda: each(plans_in, Gather.line, 2)],
             },
         )
         query_value = near[rows, 0:128].astype(HIGH)
@@ -1163,9 +1165,9 @@
         at_steps(
             index,
             {
-                1: [lambda: each(plans_in, Gather.line, 2)],
-                5: [lambda: each(plans_in, Gather.line, 1)],
-                6: [lambda: plan_out.late_line(0)],
+                2: [lambda: each(plans_in, Gather.side, None)],
+                4: [lambda: each(plans_down, Gather.line, 1)],
+                8: [lambda: each(plans_down, Gather.line, 2)],
             },
         )
         logits = dot(left[rows, :], right_t[...])
@@ -1181,35 +1183,36 @@
         return carry
 
     lax.fori_loop(0, total // BLOCK, attend, 0)
+    each(plans_out, GatherLate.late_line, 0)
     message, context_in = r.message, r.context_in
     for slot in range(CHIPS):
         message[slot] = fold(kept[slot * slot_rows : (slot + 1) * slot_rows, :])
     context_arrives, context_sent = to_tokens(message, context_in, r.msg_send, r.msg_recv)
+    each(plans_in, Gather.side, 1)
+    each(plans_in, Gather.side, 2)
+    each(plans_out, GatherLate.late_line, 1)
+    each(plans_in, Gather.side, 0)
     each(plans_down, Gather.side, 1)
-    each(plans_down, Gather.line, 2)
-    plan_out.late_line(1)
     each(plans_down, Gather.side, 0)
-    each(plans_in, Gather.side, 1)
-    plan_out.late_line(2)
+    each(plans_out, GatherLate.late_line, 2)
+    each(plans_down, Gather.side, 2)
 
     shares, bias_in = r.shares, r.bias_in
     shares[core] = jnp.zeros(shares.shape[1:], HIGH)
+    share = jnp.logical_and(lanes(8) < depth, lax.broadcasted_iota(jnp.int32, (8, 128), 0) < 6)
     for slot in range(CHIPS):
-        small = w_out[slot, depth : depth + 16, 0 : BIAS_AT + 128].astype(HIGH)[0:8]
+        small = small_all[slot].astype(HIGH)[0:8]
         target = slice(slot * depth // 128 * 128, slot * depth // 128 * 128 + 128)
-        for number in range(3):
-            piece = jnp.where(lanes(8) < depth, small[:, number * 128 : number * 128 + 128], 0.0)
-            if slot * depth % 128:
-                piece = pltpu.roll(piece, slot * depth % 128, 1)
-            shares[core, number, :, target] += piece
-        bias_in[:, slot * 128 : slot * 128 + 128] = small[0:1, BIAS_AT : BIAS_AT + 128]
+        piece = jnp.where(share, small, 0.0)
+        if slot * depth % 128:
+            piece = pltpu.roll(piece, slot * depth % 128, 1)
+        shares[core, :, target] += piece
+        bias_in[:, slot * 128 : slot * 128 + 128] = small[6:7]
     pair_small = remote(
         shares.at[core], shares.at[core], r.pair_send.at[5], r.pair_recv.at[5], (other, chip)
     )
     pair_small.start()
-    each(plans_in, Gather.side, 2)
     context_arrives()
-    each(plans_down, Gather.side, 2)
 
     context_wide, context, low_first = r.context_wide, r.context, r.low_first
     act, slope = r.act, r.slope
@@ -1242,18 +1245,18 @@
     context[...] = context_wide[...].astype(LOW)
 
     def product(lhs, rhs):
-        out_part[...] = dot(lhs[far, :], rhs)
+        out_part[...] = dot(lhs[far, :], rhs).astype(LOW)
         copy = swap(out_part, in_part)
         mine = dot(lhs[own, :], rhs)
         copy.wait()
-        return mine + in_part[...]
+        return mine + in_part[...].astype(HIGH)
 
     pair_small.wait()
     branch_bias, gains, shifts = (
-        [jnp.concatenate([shares[0, number, k : k + 1], shares[1, number, k : k + 1]], axis=1) for k in range(2)]
-        for number in range(3)
-    )
-    branch = product(context, w_out[:, 0:depth, :].reshape(half_width, width)) + branch_bias[0]
+        [jnp.concatenate([shares[g, row : row + 1] for g in range(2)], axis=1) for row in (first_row, first_row + 1)]
+        for first_row in (0, 2, 4)
+    )
+    branch = product(context, w_out[...].reshape(half_width, width)) + branch_bias[0]
     row_index = lax.broadcasted_iota(jnp.int32, (slot_rows, 1), 0)
     x_mine = jnp.where(row_index < token_rows, x_own[...].astype(HIGH), 0.0)
     first, normed1, inverse1 = normalize(x_mine + branch, gains[0], shifts[0])
@@ -1332,16 +1335,19 @@
     copy.wait()
     slots = tile // w_down.shape[1]
 
-    def narrow_back(index, carry):
-        columns = pl.ds(pl.multiple_of(index * tile, tile), tile)
-        rows = pl.ds(index * slots, slots)
+    turns = width // tile
+    z, y, x = coordinates(chip)
+    assert slots == 4
+    for line in (1, None, 2, 0):
+        plane = sums_down[0].plane(line)
+        columns = pl.ds(pl.multiple_of(plane * tile, tile), tile)
+        rows = pl.ds(plane * slots, slots)
         low = (dot(d_second[...], w_down[rows].reshape(tile, width), NT) * slope[:, columns]).astype(LOW)
-        turns = width // tile
         bias_sums = column_sums(low.astype(HIGH))
-        bias_columns = pl.ds(pl.multiple_of(lax.rem(index, turns) * tile, tile), tile)
+        bias_columns = pl.ds(pl.multiple_of(lax.rem(plane, turns) * tile, tile), tile)
         for row in range(half_hidden // width):
 
-            @pl.when(lax.div(index, turns) == row)
+            @pl.when(lax.div(plane, turns) == row)
             def _():
                 small_sum[6 + row : 7 + row, bias_columns] = bias_sums
 
@@ -1349,12 +1355,11 @@
             dot(act[:, columns], d_second[...], TN).astype(LOW).reshape(slots, tile // slots, width)
         )
         d_inner[:, columns] = low
-        return carry
-
-    lax.fori_loop(0, half_hidden // tile, narrow_back, 0)
-    each(sums_down, Reduce.start, 1)
+        if line == 1:
+            each(sums_down, Reduce.start, 1)
+    each(sums_down, Reduce.start, None)
     w_in_all = w_in[...].reshape(width, half_hidden)
-    out_part[...] = dot(d_inner[far, :], w_in_all, NT)
+    out_part[...] = dot(d_inner[far, :], w_in_all, NT).astype(LOW)
     copy = swap(out_part, in_part)
     mine = dot(d_inner[own, :], w_in_all, NT)
     slots_in = 256 // depth
@@ -1369,18 +1374,18 @@
 
     lax.fori_loop(0, width // 256, widen_grad, 0)
     copy.wait()
-    d_first = d_sum2 + mine + in_part[...]
+    d_first = d_sum2 + mine + in_part[...].astype(HIGH)
     d_sum1 = normalize_back(d_first, normed1, inverse1, gains[0])
     low_branch = d_sum1.astype(LOW)
     d_branch = d_second
     d_branch[own, :] = low_branch
     copy = swap(d_branch.at[own], d_branch.at[own])
-    out_part[...] = d_sum1
+    r.d_sum1[...] = d_sum1
     small_sum[0:1, :] = column_sums(low_branch.astype(HIGH))
     small_sum[2:3, :] = column_sums(d_first * normed1)
     small_sum[4:5, :] = column_sums(d_first)
     copy.wait()
-    context_wide[...] = dot(d_branch[...], w_out[:, 0:depth, :].reshape(half_width, width), NT)
+    context_wide[...] = dot(d_branch[...], w_out[...].reshape(half_width, width), NT)
     d_message, d_arrived = context_in, r.d_arrived
     for slot_group in range(2):
         for pair in range(HALF // 2):
@@ -1392,7 +1397,6 @@
     grad_arrives, grad_sent = to_heads(d_message, d_arrived, r.d_send, r.d_recv)
     r.g_out[...] = dot(context[...], d_branch[...], TN).astype(LOW).reshape(r.g_out.shape)
 
-    z, y, x = coordinates(chip)
     small_in = r.small_in
 
     def small_copy(index, to_core, to_chip):
@@ -1423,17 +1427,16 @@
         elif index < 3:
             small_sum[...] += small_in[index]
 
-    each(sums_down, Reduce.start, None)
-    each(sums_in, Reduce.start, 2)
     each(sums_down, Reduce.side, 1)
     small_start(0)
+    small_end(0)
     each(sums_down, Reduce.start, 2)
-    small_end(0)
+    sum_out.start()
+    each(sums_in, Reduce.start, 2)
     small_start(1)
-    sum_out.start()
     each(sums_down, Reduce.side, 2)
+    each(sums_in, Reduce.side, 2)
     each(sums_down, Reduce.start, 0)
-    each(sums_in, Reduce.side, 2)
     d_context = meta
     grad_arrives()
     for slot in range(CHIPS):
@@ -1450,26 +1453,30 @@
         at_steps(
             index,
             {
-                1: [lambda: small_end(1)],
-                2: [
+                1: [
+                    lambda: small_end(1),
+                    lambda: each(sums_in, Reduce.start, 1),
+                    lambda: each(sums_down, Reduce.side, None),
+                    lambda: each(sums_down, Reduce.side, 0),
+                    lambda: each(sums_down, Reduce.line, 2),
                     lambda: small_start(2),
+                ],
+                2: [lambda: each(sums_in, Reduce.line, 2)],
+                4: [
                     lambda: each(sums_in, Reduce.start, None),
-                    lambda: each(sums_down, Reduce.line, 2),
+                    sum_out.third,
+                    lambda: each(sums_down, Reduce.line, 1),
                 ],
-                3: [
-                    lambda: each(sums_down, Reduce.side, 0),
-                    lambda: each(sums_in, Reduce.start, 1),
+                5: [
                     lambda: small_end(2),
-                    lambda: each(sums_in, Reduce.line, 2),
+                    lambda: each(sums_in, Reduce.side, 1),
+                    lambda: each(sums_down, Reduce.line, 0),
                 ],
-                4: [lambda: small_start(3)],
-                6: [lambda: each(sums_down, Reduce.line, 0), lambda: each(sums_in, Reduce.side, 1)],
-                7: [
+                8: [
                     lambda: each(sums_in, Reduce.start, 0),
-                    lambda: each(sums_down, Reduce.line, 1),
-                    sum_out.third,
+                    lambda: small_start(3),
+                    lambda: each(sums_in, Reduce.line, 1),
                 ],
-                8: [lambda: each(sums_in, Reduce.line, 1)],
             },
         )
         facts = kept[rows, :]
@@ -1519,6 +1526,8 @@
     rel_grad[:, 3 * NB : 4 * NB] = jnp.where(
         lanes(HD) == 0, sums[0], jnp.where(lanes(HD) == 1, sums[1], 0.0)
     )
+    rel_low = r.rel_low
+    rel_low[...] = rel_grad[...].astype(LOW)
     head = 2 * position + core
     rel_came = r.rel_came
 
@@ -1526,7 +1535,7 @@
         for side in range(2):
             to = (lax.div(position, 4), lax.rem(2 * head + side, CHIPS))
             itself = jnp.logical_and(to[0] == core, to[1] == chip)
-            source = rel_grad.at[pl.ds(side * depth, depth)]
+            source = rel_low.at[pl.ds(side * depth, depth)]
             act = lambda: act_remote(
                 remote(source, rel_came.at[group], r.d_rel_send.at[side], r.d_rel_recv.at[group], to)
             )
@@ -1561,7 +1570,6 @@
         for part, order in enumerate(("xyz", "yzx", "zxy"))
     ]
     each(d_x_plans, CubeReduce.own)
-    small_end(3)
 
     w_mine, w_far, w_low, w_came = slope, r.w_far, r.w_low, r.w_came
     w_rows = 3 * HD
@@ -1574,7 +1582,7 @@
     w_swaps = [
         swap(w_mine.at[pl.ds(0, w_rows), w_columns(part, other)], w_far.at[part]) for part in range(2)
     ]
-    each(sums_in, Reduce.side, 0)
+    sum_out.across()
     each(d_x_plans, CubeReduce.one)
     for copy in w_swaps:
         copy.wait()
@@ -1592,11 +1600,14 @@
     own_d_w.start()
     for ahead in range(1, CHIPS):
         d_w_copy(ahead).start()
-    sum_out.across()
+    sum_out.finish(r.out_w_grad)
+    each(sums_in, Reduce.side, 0)
+    for part, plan in enumerate(sums_down):
+        plan.finish(r.down_grad.at[:, pl.ds(part * half, half)])
     each(d_x_plans, CubeReduce.two)
     each(sums_in, Reduce.line, 0)
-    each(sums_down, Reduce.side, None)
     each(sums_in, Reduce.side, None)
+    small_end(3)
     x_total, x_came = x_own, r.x_came
     back_part = lambda part: pl.ds(part * third, third)
     back = lambda part: local(
@@ -1613,9 +1624,6 @@
         x_total[part * third : (part + 1) * third] = plan.arrive().astype(LOW)
         pl.when(at_home)(lambda: back(part).start())
         pl.when(jnp.logical_not(at_home))(lambda: back_abroad(part).start())
-    for part, plan in enumerate(sums_down):
-        plan.finish(r.down_grad.at[:, pl.ds(part * half, half)])
-    sum_out.finish(r.out_w_grad)
     in_total, in_far = r.in_total, r.in_far
     for part, plan in enumerate(sums_in):
         plan.finish(in_total.at[:, :, pl.ds(part * half_tile, half_tile)])
@@ -1624,19 +1632,19 @@
     in_grad = r.in_grad
     in_grad[:, columns_of(core, half_hidden)] = in_total[core]
     me = core * CHIPS + chip
-    small_all = lambda rows, columns: (
+    small_total = lambda rows, columns: (
         small_sum[rows, columns] + small_in[3, rows, columns] + small_in[4, rows, columns] + small_in[5, rows, columns]
     )
     strip = columns_of(lax.div(me * depth, 128), 128)
-    shares = pltpu.roll(small_all(pl.ds(0, 8), strip), 128 - lax.rem(me * depth, 128), 1)
+    shares = pltpu.roll(small_total(pl.ds(0, 8), strip), 128 - lax.rem(me * depth, 128), 1)
     for number, result in enumerate((r.branch_grad, r.gain_grad, r.shift_grad)):
         result[...] = shares[2 * number : 2 * number + 2, 0:depth]
-    bias_strip = small_all(pl.ds(0, 8), columns_of(position, 128))
+    bias_strip = small_total(pl.ds(0, 8), columns_of(position, 128))
     r.bias_grad[...] = jnp.where(group == 0, bias_strip[6:7], bias_strip[7:8])
     for slot in range(2):
-        local(rel_grad.at[pl.ds(0, depth)], rel_came.at[slot], r.d_rel_recv.at[slot]).wait()
+        local(rel_low.at[pl.ds(0, depth)], rel_came.at[slot], r.d_rel_recv.at[slot]).wait()
     d_rel_each(lambda copy: copy.wait_send(), False)
-    rel_total = rel_came[0] + rel_came[1]
+    rel_total = rel_came[0].astype(HIGH) + rel_came[1].astype(HIGH)
     for kind in range(3):
         r.rel_tables_grad[kind] = rel_total[:, kind * NB : (kind + 1) * NB]
     r.qkv_bias_grad[...] = rel_total[:, 3 * NB : 4 * NB].T[0:2]
@@ -1651,7 +1659,7 @@
     for part in range(3):
         back(part).wait()
         pl.when(jnp.logical_not(at_home))(lambda: back_abroad(part).wait_send())
-    r.hidden_grad[...] = (out_part[...] + x_came[...].astype(HIGH))[:token_rows].astype(LOW)
+    r.hidden_grad[...] = (r.d_sum1[...] + x_came[...].astype(HIGH))[:token_rows].astype(LOW)
     in_pair.wait()
     in_grad[:, columns_of(other, half_hidden)] = in_far[...]
     grad_sent()
@@ -1659,7 +1667,7 @@
     local(w_most, w_most, r.w_send.at[0]).wait()
     rel_each(lambda copy: copy.wait_send(), None)
     context_sent()
-    plan_out.finish()
+    each(plans_out, GatherLate.finish)
 
 
 def hand_over(count, *refs):
@@ -1721,7 +1729,7 @@
     message = (CHIPS, fold_rows, 128)
     x_block, w_block = (HALF, slot_rows, width), (3, 2, CHIPS, depth, 128)
     in_all, down_all = (2, CHIPS, depth, half_hidden), (CHIPS, down_rows, width)
-    out_all = (CHIPS, depth + 16, width)
+    out_all = (CHIPS, depth, width)
     in_half, down_half = (2, depth, half_hidden // 2), (down_rows, half_width)
     in_block, out_block = (2, depth, half_hidden), (depth, width)
     made = call(
@@ -1763,7 +1771,9 @@
             x_own=vmem((slot_rows, width), LOW),
             x_all=vmem(x_block, LOW),
             extra=vmem((slot_rows - rows, width), HIGH),
-            small_own=vmem((16, width), LOW),
+            small_wide=vmem((16, 128), HIGH),
+            small_own=vmem((16, 128), LOW),
+            small_all=vmem((CHIPS, 16, 128), LOW),
             w_all=vmem(w_block, LOW),
             rel_own=vmem((depth, 4 * NB), LOW),
             rel_all=vmem((2 * depth, 4 * NB), LOW),
@@ -1775,7 +1785,7 @@
             w_down=vmem(down_all, LOW),
             w_out=vmem(out_all, LOW),
             meta=vmem((total, 128), HIGH),
-            shares=vmem((2, 3, 8, half_width), HIGH),
+            shares=vmem((2, 8, half_width), HIGH),
             bias_in=vmem((1, half_hidden), HIGH),
             left=vmem((total, 384), LOW),
             right=vmem((total, 384), LOW),
@@ -1790,8 +1800,9 @@
             low_first=vmem((both, width), LOW),
             act=vmem((both, half_hidden), LOW),
             slope=vmem((both, half_hidden), HIGH),
-            out_part=vmem((slot_rows, width), HIGH),
-            in_part=vmem((slot_rows, width), HIGH),
+            out_part=vmem((slot_rows, width), LOW),
+            in_part=vmem((slot_rows, width), LOW),
+            d_sum1=vmem((slot_rows, width), HIGH),
             d_second=vmem((both, width), LOW),
             g_out=vmem((CHIPS,) + out_block, LOW),
             in_1=vmem((2, 8) + in_half, LOW),
@@ -1814,7 +1825,8 @@
             x_stage=vmem((3, 7, slot_rows // 3, width), LOW),
             x_came=vmem((slot_rows, width), LOW),
             rel_grad=vmem((2 * depth, 4 * NB), HIGH),
-            rel_came=vmem((2, depth, 4 * NB), HIGH),
+            rel_low=vmem((2 * depth, 4 * NB), LOW),
+            rel_came=vmem((2, depth, 4 * NB), LOW),
             w_far=vmem((2, 3 * HD, half_width), HIGH),
             w_low=vmem((CHIPS, depth, 6 * HD), LOW),
             w_came=vmem((CHIPS, depth, 6 * HD), LOW),
@@ -1828,8 +1840,8 @@
             w_recv=dma((1,)),
             rel_send=dma((2,)),
             rel_recv=dma((2,)),
-            out_send=dma((GatherLate.SENDS,)),
-            out_recv=dma((GatherLate.RECEIVES,)),
+            out_send=dma((2, GatherLate.SENDS)),
+            out_recv=dma((2, GatherLate.RECEIVES)),
             in_send=dma((2, Gather.SENDS)),
             in_recv=dma((2, Gather.RECEIVES)),
             down_send=dma((2, Gather.SENDS)),

time: 235 us -> 229 us (0.974)
  Pallas kernels: 234 us -> 228 us
    pallas_call x1, Pallas kernels: 231 us -> 225 us  [call(): pl.pallas_call(functools.partial(kernel, names), out_shape=[jax.ShapeDtyp...]
where the time goes in v8:
time: 229 us
  Pallas kernels  228 us (100%)
    pallas_call x1, Pallas kernels, call(): pl.pallas_call(functools.partial(kernel, names), out_shape=[jax.ShapeDtyp...  225 us

profile of v8, /device:TPU:1, one launch (start us, length us, event | category | flops | bytes accessed | tf_op | source)
XLA Modules:
  0.0 228.6 jit_solution(8084248688937330023)
XLA Ops:
  0.7 224.9 %layer.1 = (bf16[136,1024]{1,0:T(8,128)(2,1)}, bf16[136,1024]{1,0:T(8,128)(2,1)}, f32[3,32,1024]{2,1,0:T(8,128)}, f32[2,32]{1,0:T(2,128)}, f32[3,32,128]{2,1,0:T...) custom-call(bf16[136,1024]{1,0:T(8,128)(2,1)} %refs_0_.1, ...), custom_call_target="tpu_custom_call" | custom-call | tf_op jit(solution)/shard_map/layer/pallas_call | solution.py:1688
  225.6 3.0 %hand_over.1 = (bf16[136,1024]{1,0:T(8,128)(2,1)}, bf16[136,1024]{1,0:T(8,128)(2,1)}, f32[3,32,1024]{2,1,0:T(8,128)}, f32[2,32]{1,0:T(2,128)}, f32[3,32,128]{2,1...) custom-call(bf16[136,1024]{1,0:T(8,128)(2,1)} %get-tuple-element.36., ...), custom_call_target="tpu_custom_call" | custom-call | tf_op jit(solution)/shard_map/hand_over/pallas_call | solution.py:1679

commit v9 on v8

--- a/solution.py
+++ b/solution.py
@@ -563,8 +563,8 @@
 class Reduce:
     SENDS, RECEIVES = 1, 15
 
-    def __init__(self, held, pick, stages, send, recv, across):
-        self.held, self.pick, self.at = held, pick, neighbours(across)
+    def __init__(self, pick, stages, send, recv, across):
+        self.pick, self.at = pick, neighbours(across)
         self.first, self.second, self.third_in = stages
         self.moves = Shipments(send, recv)
 
@@ -576,7 +576,7 @@
         return lax.div(self.at(0, 0, line), 4)
 
     def mine(self, *what):
-        return self.pick(self.held, self.at(*what))
+        return self.pick(self.at(*what))
 
     def term(self, stage, index, recv_index):
         self.moves.landed(stage.at[index], recv_index)
@@ -622,7 +622,7 @@
         for ahead in range(3):
             total += self.term(self.third_in, ahead, 12 + ahead)
         result[...] = total
-        self.moves.all_sent(self.pick(self.held, pl.ds(0, 15)), 0)
+        self.moves.all_sent(self.pick(pl.ds(0, 15)), 0)
 
 
 class ReduceEarly(Reduce):
@@ -632,7 +632,7 @@
         for line in (2, 1, 0):
             ahead = self.ahead(line)
             self.moves.ship(
-                self.pick(self.held, pl.ds(self.plane(line) * 4, 4)),
+                self.pick(pl.ds(self.plane(line) * 4, 4)),
                 self.first.at[ahead],
                 0,
                 ahead,
@@ -641,7 +641,7 @@
 
     def plane_sum(self, *what):
         slot = self.at(*what, None)
-        total = self.pick(self.held, slot)[...].astype(HIGH)
+        total = self.pick(slot)[...].astype(HIGH)
         for ahead in range(3):
             total += self.first[ahead, lax.rem(slot, 4)].astype(HIGH)
         return total
@@ -666,7 +666,7 @@
         result[...] = (
             self.plane_sum(0, 0) + self.term(self.second, 0, 3) + self.term(self.third_in, 0, 5)
         )
-        self.moves.all_sent(self.pick(self.held, pl.ds(0, 15)), 0)
+        self.moves.all_sent(self.pick(pl.ds(0, 15)), 0)
 
 
 def cube_of(order):
@@ -996,23 +996,26 @@
         )
         for part, order in enumerate(("xyz", "yzx", "zxy"))
     ]
-    half = width // 2
-    half_tile = half_hidden // 2
+    half_down = w_down.shape[1] // 2
     plans_out = [
         GatherLate(lambda slot: w_out.at[slot], r.out_send.at[0], r.out_recv.at[0], "x"),
         GatherLate(lambda slot: small_all.at[slot], r.out_send.at[1], r.out_recv.at[1], "y"),
     ]
 
-    def halves(ref, wide, sends, recvs):
+    def in_half(slot, part):
+        return w_in.at[part, slot]
+
+    def down_half(slot, part):
+        return w_down.at[slot, pl.ds(part * half_down, half_down)]
+
+    def halves(pick, sends, recvs):
         return [
-            Gather(
-                lambda slot, part=part: ref(slot, pl.ds(part * wide, wide)), sends.at[part], recvs.at[part], across
-            )
+            Gather(functools.partial(pick, part=part), sends.at[part], recvs.at[part], across)
             for part, across in enumerate("xy")
         ]
 
-    plans_in = halves(lambda slot, columns: w_in.at[:, slot, :, columns], half_tile, r.in_send, r.in_recv)
-    plans_down = halves(lambda slot, columns: w_down.at[slot, :, columns], half, r.down_send, r.down_recv)
+    plans_in = halves(in_half, r.in_send, r.in_recv)
+    plans_down = halves(down_half, r.down_send, r.down_recv)
 
     for copy in loads:
         copy.wait()
@@ -1292,11 +1295,10 @@
     small_sum[5:6, :] = column_sums(upstream)
 
     half_total = HALF * slot_rows
-    def half_sums(ref, pick, wide, stages, sends, recvs):
+    def half_sums(pick, stages, sends, recvs):
         return [
             Reduce(
-                ref,
-                lambda held, slot, part=part: pick(held, slot, pl.ds(part * wide, wide)),
+                functools.partial(pick, part=part),
                 [stage.at[part] for stage in stages],
                 sends.at[part],
                 recvs.at[part],
@@ -1305,25 +1307,10 @@
             for part, across in enumerate("xy")
         ]
 
-    sums_down = half_sums(
-        w_down,
-        lambda held, slot, columns: held.at[slot, :, columns],
-        half,
-        (r.down_1, r.down_2, r.down_3),
-        r.g_down_send,
-        r.g_down_recv,
-    )
-    sums_in = half_sums(
-        w_in,
-        lambda held, slot, columns: held.at[:, slot, :, columns],
-        half_tile,
-        (r.in_1, r.in_2, r.in_3),
-        r.g_in_send,
-        r.g_in_recv,
-    )
+    sums_down = half_sums(down_half, (r.down_1, r.down_2, r.down_3), r.g_down_send, r.g_down_recv)
+    sums_in = half_sums(in_half, (r.in_1, r.in_2, r.in_3), r.g_in_send, r.g_in_recv)
     sum_out = ReduceEarly(
-        r.g_out,
-        lambda ref, slot: ref.at[slot],
+        lambda slot: r.g_out.at[slot],
         [r.out_1, r.out_2, r.out_3],
         r.g_out_send,
         r.g_out_recv,
@@ -1603,7 +1590,7 @@
     sum_out.finish(r.out_w_grad)
     each(sums_in, Reduce.side, 0)
     for part, plan in enumerate(sums_down):
-        plan.finish(r.down_grad.at[:, pl.ds(part * half, half)])
+        plan.finish(r.down_grad.at[pl.ds(part * half_down, half_down)])
     each(d_x_plans, CubeReduce.two)
     each(sums_in, Reduce.line, 0)
     each(sums_in, Reduce.side, None)
@@ -1626,7 +1613,7 @@
         pl.when(jnp.logical_not(at_home))(lambda: back_abroad(part).start())
     in_total, in_far = r.in_total, r.in_far
     for part, plan in enumerate(sums_in):
-        plan.finish(in_total.at[:, :, pl.ds(part * half_tile, half_tile)])
+        plan.finish(in_total.at[part])
     in_pair = swap(in_total.at[other], in_far)
 
     in_grad = r.in_grad
@@ -1671,14 +1658,27 @@
 
 
 def hand_over(count, *refs):
-    for source, target in zip(refs[:count], refs[count:]):
-        target[...] = source[...]
+    sources, targets, held, sem = refs[:count], refs[count : 2 * count], refs[2 * count : 3 * count], refs[3 * count]
+    loads = [local(source, here, sem.at[0, k]) for k, (source, here) in enumerate(zip(sources, held))]
+    stores = [local(here, target, sem.at[1, k]) for k, (here, target) in enumerate(zip(held, targets))]
+    for copy in loads:
+        copy.start()
+    for load, store in zip(loads, stores):
+        load.wait()
+        store.start()
+    for copy in stores:
+        copy.wait()
 
 
 def handed_over(arrays):
+    count = len(arrays)
     return pl.pallas_call(
-        functools.partial(hand_over, len(arrays)),
+        functools.partial(hand_over, count),
         out_shape=[jax.ShapeDtypeStruct(array.shape, array.dtype) for array in arrays],
+        in_specs=[pl.BlockSpec(memory_space=pl.ANY)] * count,
+        out_specs=[pl.BlockSpec(memory_space=pl.ANY)] * count,
+        scratch_shapes=[pltpu.VMEM(array.shape, array.dtype) for array in arrays]
+        + [pltpu.SemaphoreType.DMA((2, count))],
         name="hand_over",
     )(*arrays)
 
@@ -1730,7 +1730,7 @@
     x_block, w_block = (HALF, slot_rows, width), (3, 2, CHIPS, depth, 128)
     in_all, down_all = (2, CHIPS, depth, half_hidden), (CHIPS, down_rows, width)
     out_all = (CHIPS, depth, width)
-    in_half, down_half = (2, depth, half_hidden // 2), (down_rows, half_width)
+    in_half, down_half = (depth, half_hidden), (down_rows // 2, width)
     in_block, out_block = (2, depth, half_hidden), (depth, width)
     made = call(
         layer_kernel,

time: 229 us -> 229 us (level)
  no operation moved by 1% of the time
where the time goes in v9:
time: 229 us; the launch traced here: 228 us
  Pallas kernels  227 us (99%)
    pallas_call x1, Pallas kernels, call(): pl.pallas_call(functools.partial(kernel, names), out_shape=[jax.ShapeDtyp...  225 us

profile of v9, /device:TPU:1, one launch (start us, length us, event | category | flops | bytes accessed | tf_op | source)
XLA Modules:
  0.0 228.3 jit_solution(8606963131610623980)
XLA Ops:
  0.7 224.8 %layer.1 = (bf16[136,1024]{1,0:T(8,128)(2,1)}, bf16[136,1024]{1,0:T(8,128)(2,1)}, f32[3,32,1024]{2,1,0:T(8,128)}, f32[2,32]{1,0:T(2,128)}, f32[3,32,128]{2,1,0:T...) custom-call(bf16[136,1024]{1,0:T(8,128)(2,1)} %refs_0_.1, ...), custom_call_target="tpu_custom_call" | custom-call | tf_op jit(solution)/shard_map/layer/pallas_call | solution.py:1688
  225.5 2.6 %hand_over.1 = (bf16[136,1024]{1,0:T(8,128)(2,1)}, bf16[136,1024]{1,0:T(8,128)(2,1)}, f32[3,32,1024]{2,1,0:T(8,128)}, f32[2,32]{1,0:T(2,128)}, f32[3,32,128]{2,1...) custom-call(bf16[136,1024]{1,0:T(8,128)(2,1)} %get-tuple-element.36., ...), custom_call_target="tpu_custom_call" | custom-call | tf_op jit(solution)/shard_map/hand_over/pallas_call | solution.py:1675
